TPU v7x, 32 devices: a whole 2x2x4 slice. The times are simulated.
32 devices in a mesh: grp: 2 (over y), seq: 4 (over z), ch: 4 (over x, core).
Axes of the slice: x: 2, y: 2, z: 4, core: 2. Of those that a mesh axis runs over, the one named last changes fastest.
Arguments:
- x_saved: bfloat16 [8192, 1536], P(('grp', 'seq'), 'ch'), parts along dimension 0, may hold values from -6 to 6
- pre_act: bfloat16 [8192, 1536], P(('grp', 'seq'), 'ch'), parts along dimension 0, may hold values from -6 to 6
- out_grad: bfloat16 [4096, 1536], P(('grp', 'seq'), 'ch'), parts along dimension 0, may hold values from -6 to 6
- conv_w: bfloat16 [1536, 5, 1536], P(None, None, 'ch'), may hold values from -0.0625 to 0.0625
- coverage_obs: float32 [8, 8, 8, 1536], P(('grp', 'seq'), None, None, 'ch'), parts along dimension 0, may hold values from 1 to 8
- owners: int32 [32], P('grp'), parts along dimension 0, may hold values from 0 to 3, as said below
- exon_blocks: int32 [32, 2], P('grp'), parts along dimension 0, may hold values from 0 to 255, as said below
Outputs:
- in_grad: bfloat16 [8192, 1536], P(('grp', 'seq'), 'ch'), parts along dimension 0
- w_grad: bfloat16 [3072, 5, 1536], P(('grp', 'seq'), None, 'ch'), parts along dimension 0
There are 2 independent parts, one for each index of `grp`. A program takes and returns all parts, laid end to end along the dimension named above; an argument that names none is the same for every part. Nothing has to cross between parts.
Inputs may be any that keep to these rules, and one draw needn't show every extreme that they name: `owners`: no device owns more than 8 transcripts, and some device owns exactly 8. `exon_blocks`: block b holds pooled rows 8 * b to 8 * b + 7, which lie on device b // 64 of seq; the 2 exon blocks of one transcript lie on 2 different devices, and for some owner device one device holds exon blocks of all its transcripts.
All inputs are finite; a program needn't handle non-finite values.
Results may differ from a plain program's by a relative error of at most 0.0095.
Values may be sent and summed in bfloat16 or wider, within the bound.
No kernel may reach another device: no remote copies, remote signals or barrier semaphores. Data moves between devices by JAX's collectives and lax.ppermute only.
A program may use at most 64 MiB of HBM per device.

v0:
```python
import jax
import jax.numpy as jnp
from jax import lax
from jax.sharding import PartitionSpec as P


def with_halo(block, sides, width):
    for axis, dim in sides:
        count = lax.axis_size(axis)
        forward = [(i, i + 1) for i in range(count - 1)]
        backward = [(target, source) for source, target in forward]
        low = lax.ppermute(
            lax.slice_in_dim(block, block.shape[dim] - width, None, axis=dim), axis, forward
        )
        high = lax.ppermute(lax.slice_in_dim(block, 0, width, axis=dim), axis, backward)
        block = jnp.concatenate([low, block, high], axis=dim)
    return block


def gelu_pair(value):
    normal_cdf = 0.5 * (1.0 + jax.scipy.special.erf(value * 0.7071067811865476))
    density = jnp.exp(-0.5 * value * value) * 0.3989422804014327
    return (value * normal_cdf, normal_cdf + value * density)


def local(x_saved, pre_act, out_grad, conv_w, coverage_obs, owners, exon_blocks):
    rows = x_saved.shape[0]
    width = x_saved.shape[1]
    kernel = conv_w.shape[1]
    nseq = lax.axis_size("seq")
    mine = lax.axis_index("seq")
    most = coverage_obs.shape[1]
    block = coverage_obs.shape[2]
    nblocks = rows // 2 // block
    counts = owners.shape[0]
    act, slope = gelu_pair(pre_act.astype(jnp.float32))
    pooled = (0.5 * jnp.sum(act.reshape(rows // 2, 2, width), axis=1)).astype(jnp.bfloat16)
    order = jnp.arange(counts, dtype=jnp.int32)
    same = owners[:, None] == owners[None, :]
    rank = jnp.sum((same & (order[:, None] < order[None, :])).astype(jnp.int32), axis=0)
    dest = jnp.arange(nseq, dtype=jnp.int32)
    slots = jnp.arange(most, dtype=jnp.int32)
    route = (owners[None, None, :] == dest[:, None, None]) & (
        rank[None, None, :] == slots[None, :, None]
    )
    route = route.astype(jnp.float32).reshape(nseq * most, counts)
    on_mine = exon_blocks // nblocks == mine
    holds = jnp.any(on_mine, axis=1)
    local_block = jnp.sum(jnp.where(on_mine, exon_blocks % nblocks, 0), axis=1)
    select = (
        holds[:, None] & (local_block[:, None] == jnp.arange(nblocks, dtype=jnp.int32)[None, :])
    ).astype(jnp.float32)
    picker = jnp.dot(route, select, precision=lax.Precision.HIGHEST).astype(jnp.bfloat16)
    pieces = pooled.reshape(nblocks, block * width)
    outgoing = jnp.dot(picker, pieces, preferred_element_type=jnp.float32).astype(jnp.bfloat16)
    outgoing = outgoing.reshape(nseq, most, block, width)
    arrived = lax.all_to_all(outgoing, "seq", split_axis=0, concat_axis=0, tiled=True)
    coverage = jnp.sum(arrived.astype(jnp.float32), axis=0)
    splice = jnp.tanh(coverage - coverage_obs[0]).astype(jnp.bfloat16)
    spread = jnp.broadcast_to(splice[None], (nseq, most, block, width))
    returned = lax.all_to_all(spread, "seq", split_axis=0, concat_axis=0, tiled=True)
    returned = returned.reshape(nseq * most, block * width)
    gained = jnp.dot(picker.T, returned, preferred_element_type=jnp.float32).reshape(
        rows // 2, width
    )
    pooled_grad = out_grad.astype(jnp.float32) + gained
    pre_grad = (jnp.repeat(pooled_grad, 2, axis=0) * 0.5 * slope).astype(jnp.bfloat16)
    x_rim = with_halo(x_saved, (("seq", 0),), 2)
    rimmed = with_halo(pre_grad, (("seq", 0),), 2)
    grad_rim = lax.all_gather(rimmed, "ch", axis=1, tiled=True)
    total = jnp.zeros((rows, width), jnp.float32)
    for tap in range(kernel):
        total = total + jnp.dot(
            grad_rim[4 - tap : 4 - tap + rows],
            conv_w[:, tap, :],
            preferred_element_type=jnp.float32,
        )
    in_grad = total.astype(jnp.bfloat16)
    inner = grad_rim[2 : 2 + rows]
    terms = [
        jnp.dot(inner.T, x_rim[tap : tap + rows], preferred_element_type=jnp.float32)
        for tap in range(kernel)
    ]
    w_grad = lax.psum_scatter(
        jnp.stack(terms, axis=1).astype(jnp.bfloat16), "seq", scatter_dimension=0, tiled=True
    )
    return (in_grad, w_grad)


def solution(mesh):
    in_specs = (
        P(("grp", "seq"), "ch"),
        P(("grp", "seq"), "ch"),
        P(("grp", "seq"), "ch"),
        P(None, None, "ch"),
        P(("grp", "seq"), None, None, "ch"),
        P("grp"),
        P("grp", None),
    )
    out_specs = (P(("grp", "seq"), "ch"), P(("grp", "seq"), None, "ch"))
    return jax.shard_map(local, mesh=mesh, in_specs=in_specs, out_specs=out_specs, check_vma=False)
```

profile of v0, /device:TPU:0, one launch (start us, length us, event | category | flops | bytes accessed | tf_op | source)
XLA Modules:
  0.0 216.2 jit_solution(1048674728044450605)
XLA Ops:
  7.2 0.8 convert_reduce_fusion.1
  8.0 0.7 iota_compare_fusion.3
  8.7 0.7 fusion.69
  9.4 0.7 fusion.65
  10.1 1.4 convert_multiply_fusion.3
  11.6 0.9 reshape.79
  12.5 1.9 reduce_sum.40
  15.0 13.7 %all_to_all.10 = bf16[4,8,8,384]{3,1,2,0:T(8,128)(2,1)S(1)} all-to-all(bf16[4,8,8,384]{3,1,2,0:T(8,128)(2,1)S(1)} %bitcast.59), channel_id=1, replica_groups=mesh['grp'=2,'seq'=4,'ch'=4] {'seq'}, dimensions={0} | all-to-all | bytes 393216 | tf_op jit(solution)/shard_map/all_to_all | solution.py:57
  28.9 9.9 %all_to_all.11 = bf16[4,8,8,384]{3,2,1,0:T(8,128)(2,1)S(1)} all-to-all(bf16[4,8,8,384]{3,2,1,0:T(8,128)(2,1)S(1)} %broadcast_in_dim.8), channel_id=1, replica_groups=mesh['grp'=2,'seq'=4,'ch'=4] {'seq'}, dimensions={0} | all-to-all | bytes 393216 | tf_op jit(solution)/shard_map/all_to_all | solution.py:61
  39.9 1.1 mul.55
  41.0 1.9 fusion.25
  42.9 2.3 %collective-permute-start = (bf16[2,384]{1,0:T(2,128)(2,1)S(1)}, bf16[2,384]{1,0:T(2,128)(2,1)S(1)}, u32[]{:S(2)}, u32[]{:S(2)}) collective-permute-start(bf16[2,384]{1,0:T(2,128)(2,1)S(1)} %get-tuple-element.7), channel_id=1, source_target_pairs={{0,4},{4,8},{8,12},{1,5},{5,9},{9,13},{2,6},{6,10},{10,14},{3,7},{... | collective-permute-start | bytes 4616 | tf_op jit(solution)/shard_map/ppermute | solution.py:12
  45.2 1.3 collective-permute-start.1
  46.5 4.2 %collective-permute-done.1 = bf16[2,384]{1,0:T(2,128)(2,1)S(1)} collective-permute-done((bf16[2,384]{1,0:T(2,128)(2,1)S(1)}, bf16[2,384]{1,0:T(2,128)(2,1)S(1)}, u32[]{:S(2)}, u32[]{:S(2)}) %collective-permute-start.1) | collective-permute-done | bytes 1568 | tf_op jit(solution)/shard_map/ppermute | solution.py:15
  50.7 6.1 %concatenate.12 = bf16[1028,384]{1,0:T(8,128)(2,1)} concatenate(bf16[2,384]{1,0:T(2,128)(2,1)S(1)} %collective-permute-done, bf16[1024,384]{1,0:T(8,128)(2,1)S(1)} %fusion.25, bf16[2,384]{1,0:T(2,128)(2,1)S(1)} %collective-permute-done.1), dimensions={0} | concatenate | bytes 1579008 | tf_op jit(solution)/shard_map/concatenate | solution.py:16
  56.9 2.3 %collective-permute-start.2 = (bf16[2,384]{1,0:T(2,128)(2,1)S(1)}, bf16[2,384]{1,0:T(2,128)(2,1)S(1)}, u32[]{:S(2)}, u32[]{:S(2)}) collective-permute-start(bf16[2,384]{1,0:T(2,128)(2,1)S(1)} %get-tuple-element.5), channel_id=1, source_target_pairs={{0,4},{4,8},{8,12},{1,5},{5,9},{9,13},{2,6},{6,10},{10,14},{3,7},{... | collective-permute-start | bytes 4616 | tf_op jit(solution)/shard_map/ppermute | solution.py:12
  59.2 1.5 collective-permute-start.3
  60.7 1.0 constant_dynamic-update-slice_fusion.1
  61.6 3.0 %collective-permute-done.3 = bf16[2,384]{1,0:T(2,128)(2,1)S(1)} collective-permute-done((bf16[2,384]{1,0:T(2,128)(2,1)S(1)}, bf16[2,384]{1,0:T(2,128)(2,1)S(1)}, u32[]{:S(2)}, u32[]{:S(2)}) %collective-permute-start.3) | collective-permute-done | bytes 1568 | tf_op jit(solution)/shard_map/ppermute | solution.py:15
  64.6 0.6 constant_dynamic-update-slice_fusion
  65.2 19.5 %all-gather.2.cloned.1.call-done = bf16[1028,1536]{1,0:T(8,128)(2,1)} async-done(((bf16[1028,384]{1,0:T(8,128)(2,1)}), bf16[1028,1536]{1,0:T(8,128)(2,1)}) %all-gather.2.cloned.1.call-update) | async-done | bytes 3158032 | tf_op jit(solution)/shard_map/all_gather | solution.py:70
  84.7 5.1 %fusion.9 = bf16[1536,5,384]{2,0,1:T(8,128)(2,1)} fusion(bf16[1028,1536]{1,0:T(8,128)(2,1)} %all-gather.2.cloned.1.call-done, bf16[2,384]{1,0:T(2,128)(2,1)S(1)} %collective-permute-done.2, bf16[1024,384]{1,0:T(8,128)(2,1)} %param.7), kind=kOutput, calls=%fused_computation.20 | convolution fusion | flops 1210122240 | bytes 5113344 | tf_op jit(solution)/shard_map/dot_general | solution.py:81
  89.8 4.1 %fusion.11 = bf16[1536,5,384]{2,0,1:T(8,128)(2,1)} fusion(bf16[1536,5,384]{2,0,1:T(8,128)(2,1)} %fusion.9, bf16[1028,1536]{1,0:T(8,128)(2,1)S(1)} %copy-done, bf16[1024,384]{1,0:T(8,128)(2,1)} %param.7, bf16[2,384]{1,0:T(2,128)(2,1)S(1)} %collective-permute-done.2), kind=kOutput, calls=%fused_computation.22 | convolution fusion | flops 1210122240 | bytes 5113344 | tf_op jit(solution)/shard_map/dot_general | solution.py:81
  93.9 2.9 %fusion.13 = bf16[1536,5,384]{2,0,1:T(8,128)(2,1)} fusion(bf16[1536,5,384]{2,0,1:T(8,128)(2,1)} %fusion.11, bf16[1024,384]{1,0:T(8,128)(2,1)S(1)} %copy-done.2, bf16[1028,1536]{1,0:T(8,128)(2,1)S(1)} %copy-done), kind=kOutput, calls=%fused_computation.24 | convolution fusion | flops 1208549376 | bytes 5111808 | tf_op jit(solution)/shard_map/dot_general | solution.py:81
  96.8 4.0 %fusion.15 = bf16[1536,5,384]{2,0,1:T(8,128)(2,1)} fusion(bf16[1536,5,384]{2,0,1:T(8,128)(2,1)} %fusion.13, bf16[1028,1536]{1,0:T(8,128)(2,1)S(1)} %copy-done, bf16[1026,384]{1,0:T(8,128)(2,1)} %constant_dynamic-update-slice_fusion), kind=kOutput, calls=%fused_computation.26 | convolution fusion | flops 1208549376 | bytes 5111808 | tf_op jit(solution)/shard_map/dot_general | solution.py:81
  100.8 4.0 %fusion.17 = bf16[1536,5,384]{2,0,1:T(8,128)(2,1)} fusion(bf16[1536,5,384]{2,0,1:T(8,128)(2,1)} %fusion.15, bf16[1028,1536]{1,0:T(8,128)(2,1)S(1)} %copy-done, bf16[1026,384]{1,0:T(8,128)(2,1)} %constant_dynamic-update-slice_fusion), kind=kOutput, calls=%fused_computation.28 | convolution fusion | flops 1208549376 | bytes 5111808 | tf_op jit(solution)/shard_map/dot_general | solution.py:81
  104.9 3.2 %fusion.2 = f32[1024,384]{1,0:T(8,128)S(1)} fusion(bf16[1028,1536]{1,0:T(8,128)(2,1)S(1)} %copy-done, bf16[1536,5,384]{2,0,1:T(8,128)(2,1)} %param.10), kind=kOutput, calls=%fused_computation.3 | convolution fusion | flops 1207959552 | bytes 5898240 | tf_op jit(solution)/shard_map/dot_general | solution.py:73
  108.1 3.4 %fusion.31 = f32[1024,384]{1,0:T(8,128)S(1)} fusion(bf16[1028,1536]{1,0:T(8,128)(2,1)S(1)} %copy-done, bf16[1536,5,384]{2,0,1:T(8,128)(2,1)} %param.10), kind=kOutput, calls=%fused_computation.43 | convolution fusion | flops 1207959552 | bytes 5898240 | tf_op jit(solution)/shard_map/dot_general | solution.py:73
  111.6 1.8 fusion.4
  113.3 1.8 fusion.6
  115.1 2.7 %add_convert_fusion = bf16[1024,384]{1,0:T(8,128)(2,1)} fusion(f32[1024,384]{1,0:T(8,128)S(1)} %fusion.2, f32[1024,384]{1,0:T(8,128)S(1)} %fusion.31, f32[1024,384]{1,0:T(8,128)S(1)} %fusion.6, f32[1024,384]{1,0:T(8,128)S(1)} %fusion.4, bf16[1536,5,384]{2,0,1:T(8,128)(2,1)S(1)} %bitcast.62, bf16[1028,1536]{1,0:T(8,128)(2,1)S(1)} %copy-done), kind=kOutput, calls=%fused_computation.37 | convolution fusion | flops 1209925632 | bytes 11403264 | tf_op jit(solution)/shard_map/dot_general | solution.py:73
  117.9 91.5 %reduce-scatter.2.cloned.1.call-done = bf16[384,5,384]{2,0,1:T(8,128)(2,1)} async-done(((bf16[1536,5,384]{2,0,1:T(8,128)(2,1)}), bf16[384,5,384]{2,0,1:T(8,128)(2,1)}) %reduce-scatter.2.cloned.1.call-update) | async-done | bytes 1474576 | tf_op jit(solution)/shard_map/reduce_scatter | solution.py:84
  (37 shorter events, 1.9 us)
Async XLA Ops:
  7.2 77.5 %all-gather.2.cloned.1.call-start = ((), (), s32[]{:S(2)}) async-start(), calls=%async_computation.3 | async-start | bytes 3962880 | tf_op jit(solution)/shard_map/all_gather | solution.py:70
  12.5 16.3 %copy-start.4 = (f32[1,8,8,384]{3,2,1,0:T(8,128)S(1)}, f32[1,8,8,384]{3,2,1,0:T(8,128)}, u32[]{:S(2)}) copy-start(f32[1,8,8,384]{3,2,1,0:T(8,128)} %param.11) | copy-start | bytes 294916
  15.0 24.2 %copy-start.3 = (bf16[512,384]{1,0:T(8,128)(2,1)S(1)}, bf16[512,384]{1,0:T(8,128)(2,1)}, u32[]{:S(2)}) copy-start(bf16[512,384]{1,0:T(8,128)(2,1)} %param.9) | copy-start | bytes 1179652
  41.0 15.9 %copy-start.1 = (bf16[1024,384]{1,0:T(8,128)(2,1)S(1)}, bf16[1024,384]{1,0:T(8,128)(2,1)}, u32[]{:S(2)}) copy-start(bf16[1024,384]{1,0:T(8,128)(2,1)} %param.7) | copy-start | bytes 2359300
  42.9 3.6 %collective-permute-start = (bf16[2,384]{1,0:T(2,128)(2,1)S(1)}, bf16[2,384]{1,0:T(2,128)(2,1)S(1)}, u32[]{:S(2)}, u32[]{:S(2)}) collective-permute-start(bf16[2,384]{1,0:T(2,128)(2,1)S(1)} %get-tuple-element.7), channel_id=1, source_target_pairs={{0,4},{4,8},{8,12},{1,5},{5,9},{9,13},{2,6},{6,10},{10,14},{3,7},{... | collective-permute-start | bytes 4616 | tf_op jit(solution)/shard_map/ppermute | solution.py:12
  45.2 5.5 %collective-permute-start.1 = (bf16[2,384]{1,0:T(2,128)(2,1)S(1)}, bf16[2,384]{1,0:T(2,128)(2,1)S(1)}, u32[]{:S(2)}, u32[]{:S(2)}) collective-permute-start(bf16[2,384]{1,0:T(2,128)(2,1)S(1)} %get-tuple-element.6), channel_id=1, source_target_pairs={{4,0},{8,4},{12,8},{5,1},{9,5},{13,9},{6,2},{10,6},{14,10},{7,3},{... | collective-permute-start | bytes 4616 | tf_op jit(solution)/shard_map/ppermute | solution.py:15
  56.8 152.6 %reduce-scatter.2.cloned.1.call-start = ((), (), s32[]{:S(2)}) async-start(), calls=%async_computation.4 | async-start | bytes 7372800 | tf_op jit(solution)/shard_map/reduce_scatter | solution.py:84
  56.9 8.3 %collective-permute-start.2 = (bf16[2,384]{1,0:T(2,128)(2,1)S(1)}, bf16[2,384]{1,0:T(2,128)(2,1)S(1)}, u32[]{:S(2)}, u32[]{:S(2)}) collective-permute-start(bf16[2,384]{1,0:T(2,128)(2,1)S(1)} %get-tuple-element.5), channel_id=1, source_target_pairs={{0,4},{4,8},{8,12},{1,5},{5,9},{9,13},{2,6},{6,10},{10,14},{3,7},{... | collective-permute-start | bytes 4616 | tf_op jit(solution)/shard_map/ppermute | solution.py:12
  59.2 5.5 %collective-permute-start.3 = (bf16[2,384]{1,0:T(2,128)(2,1)S(1)}, bf16[2,384]{1,0:T(2,128)(2,1)S(1)}, u32[]{:S(2)}, u32[]{:S(2)}) collective-permute-start(bf16[2,384]{1,0:T(2,128)(2,1)S(1)} %get-tuple-element.4), channel_id=1, source_target_pairs={{4,0},{8,4},{12,8},{5,1},{9,5},{13,9},{6,2},{10,6},{14,10},{7,3},{... | collective-permute-start | bytes 4616 | tf_op jit(solution)/shard_map/ppermute | solution.py:15
  84.7 5.1 %copy-start = (bf16[1028,1536]{1,0:T(8,128)(2,1)S(1)}, bf16[1028,1536]{1,0:T(8,128)(2,1)}, u32[]{:S(2)}) copy-start(bf16[1028,1536]{1,0:T(8,128)(2,1)} %all-gather.2.cloned.1.call-done) | copy-start | bytes 9474052
  89.8 4.1 %copy-start.2 = (bf16[1024,384]{1,0:T(8,128)(2,1)S(1)}, bf16[1024,384]{1,0:T(8,128)(2,1)}, u32[]{:S(2)}) copy-start(bf16[1024,384]{1,0:T(8,128)(2,1)} %param.7) | copy-start | bytes 2359300
  104.9 6.7 %slice-start = ((s8[5898240]{0:T(1024)(128)(4,1)}), s8[4194304]{0:T(1024)(128)(4,1)S(1)}, s32[]{:S(2)}) async-start(s8[5898240]{0:T(1024)(128)(4,1)} %bitcast.61), calls=%async_computation.5 | async-start | bytes 8388608
  108.1 3.4 %slice-start.1 = ((s8[5898240]{0:T(1024)(128)(4,1)}), s8[1703936]{0:T(1024)(128)(4,1)S(1)}, s32[]{:S(2)}) async-start(s8[5898240]{0:T(1024)(128)(4,1)} %bitcast.61), calls=%async_computation.6 | async-start | bytes 3407872
Sparse Core Ops, SparseCore 0:
  56.9 27.7 all-gather.1
  105.0 104.3 reduce-scatter.1
where the time goes:
time: 217 us; the launch traced here: 216 us
  waiting for transfers between devices  118 us (54%)
  matrix products  33.7 us (16%)
  blocking collectives  23.6 us (11%)
  between operations  14.3 us (7%)
  local copies, waits for them, and re-layouts  10.6 us (5%)
  other arithmetic  8.31 us (4%)
  starting transfers between devices  7.41 us (3%)
    reduce_scatter x1, waiting for transfers between devices, local(): lax.psum_scatter(jnp.stack(terms, axis=1).astype(jnp.bfloat16), 'seq', sc...  91.5 us
    dot_general x5, matrix products, local(): jnp.dot(inner.T, x_rim[tap:tap + rows], preferred_element_type=jnp.float32)  20.1 us
    all_gather x1, waiting for transfers between devices, local(): grad_rim = lax.all_gather(rimmed, 'ch', axis=1, tiled=True)  19.5 us
    all_to_all x1, blocking collectives, local(): lax.all_to_all(outgoing, 'seq', split_axis=0, concat_axis=0, tiled=True)  13.7 us
    dot_general x5, matrix products, local(): jnp.dot(grad_rim[4 - tap:4 - tap + rows], conv_w[:, tap, :], preferred_el...  12.9 us
    all_to_all x1, blocking collectives, local(): lax.all_to_all(spread, 'seq', split_axis=0, concat_axis=0, tiled=True)  9.89 us
    ppermute x2, waiting for transfers between devices, with_halo(): lax.ppermute(lax.slice_in_dim(block, 0, width, axis=dim), axis, backward)  7.17 us
    concatenate x2, local copies, waits for them, and re-layouts, with_halo(): block = jnp.concatenate([low, block, high], axis=dim)  6.68 us
  transfers between devices with their start and end apart: 6, of which 4 were waited for; matrix products, arithmetic and copies ran while one was open for 7% of the time, Pallas kernels for 0%

commit v1 on v0

v1 whole, which is shorter than its diff:
```python
import functools

import jax
import jax.numpy as jnp
from jax import lax
from jax.experimental import pallas as pl
from jax.experimental.pallas import tpu as pltpu
from jax.sharding import PartitionSpec as P

PAD = 16
MIB = 1024 * 1024


def swap(block, axis, flip):
    count = lax.axis_size(axis)
    return lax.ppermute(block, axis, [(i, i ^ flip) for i in range(count)])


def shift(block, axis, step, first=0):
    count = lax.axis_size(axis)
    if step > 0:
        pairs = [(i, i + 1) for i in range(first, count - 1)]
    else:
        pairs = [(i + 1, i) for i in range(count - 1 - first)]
    return lax.ppermute(block, axis, pairs)


def gelu_pair(value):
    normal_cdf = 0.5 * (1.0 + jax.scipy.special.erf(value * 0.7071067811865476))
    density = jnp.exp(-0.5 * value * value) * 0.3989422804014327
    return (value * normal_cdf, normal_cdf + value * density)


def pad_offsets(values):
    return jnp.stack([jnp.asarray(v, jnp.int32) for v in values])


def input_kernel(taps, tile, offs, *refs, pieces):
    parts, (low, high, weights, out, wide, wbuf, sems) = refs[:pieces], refs[pieces:]
    rows = parts[0].shape[0]
    half = taps // 2
    copies = []
    base = 0
    for e in range(pieces):
        span = parts[e].shape[1]
        src = weights.at[:, pl.ds(pl.multiple_of(offs[e], 16), span), :]
        copy = pltpu.make_async_copy(src, wbuf.at[:, pl.ds(base, span), :], sems.at[e])
        copy.start()
        copies.append(copy)
        base += span
    base = 0
    for e in range(pieces):
        span = parts[e].shape[1]
        wide[pl.ds(0, PAD), pl.ds(base, span)] = low[:, pl.ds(base, span)]
        wide[pl.ds(PAD, rows), pl.ds(base, span)] = parts[e][...]
        wide[pl.ds(PAD + rows, PAD), pl.ds(base, span)] = high[:, pl.ds(base, span)]
        base += span
    for copy in copies:
        copy.wait()

    def body(step, carry):
        start = pl.multiple_of(step * tile, tile)
        block = wide[pl.ds(start, tile + 2 * PAD), :]
        total = None
        for tap in range(taps):
            term = jnp.dot(block, wbuf[tap], preferred_element_type=jnp.float32)
            first = PAD + half - tap
            term = term[first : first + tile]
            total = term if total is None else total + term
        out[pl.ds(start, tile), :] = total.astype(out.dtype)
        return carry

    lax.fori_loop(0, rows // tile, body, 0)


def input_gradient(parts, low, high, weights, offs):
    taps, chans, width = weights.shape
    rows = parts[0].shape[0]
    tile = min(256, rows)
    vmem = pl.BlockSpec(memory_space=pltpu.VMEM)
    return pl.pallas_call(
        functools.partial(input_kernel, taps, tile, pieces=len(parts)),
        out_shape=jax.ShapeDtypeStruct((rows, width), jnp.bfloat16),
        in_specs=[pl.BlockSpec(memory_space=pltpu.SMEM)]
        + [vmem] * (len(parts) + 2)
        + [pl.BlockSpec(memory_space=pl.ANY)],
        out_specs=vmem,
        scratch_shapes=[
            pltpu.VMEM((rows + 2 * PAD, chans), jnp.bfloat16),
            pltpu.VMEM((taps, chans, width), jnp.bfloat16),
            pltpu.SemaphoreType.DMA((len(parts),)),
        ],
        cost_estimate=pl.CostEstimate(
            flops=2 * rows * chans * width * taps,
            bytes_accessed=2 * (rows * chans + taps * chans * width + rows * width),
            transcendentals=0,
        ),
        compiler_params=pltpu.CompilerParams(vmem_limit_bytes=32 * MIB),
    )(offs, *parts, low, high, weights)


def weight_kernel(taps, tile, rows, offs, *refs, nx, ng):
    xs, gs = refs[:nx], refs[nx : nx + ng]
    out, xbuf, gbuf, acc, sems = refs[nx + ng :]
    half = taps // 2

    def copy(at):
        if at < nx:
            src, dst, extra = xs[at], xbuf, PAD
        else:
            src, dst, extra = gs[at - nx], gbuf, 0
        row = pl.multiple_of(offs[at] + extra, 16)
        return pltpu.make_async_copy(src, dst.at[pl.ds(row, src.shape[0]), :], sems.at[at])

    for at in range(nx + ng):

        @pl.when(offs[at] >= 0)
        def _():
            copy(at).start()

    zeros = jnp.zeros((PAD, xbuf.shape[1]), xbuf.dtype)
    xbuf[pl.ds(0, PAD), :] = zeros
    xbuf[pl.ds(PAD + rows, PAD), :] = zeros
    acc[...] = jnp.zeros_like(acc)
    for at in range(nx + ng):

        @pl.when(offs[at] >= 0)
        def _():
            copy(at).wait()

    def body(step, carry):
        start = pl.multiple_of(step * tile, tile)
        grad = gbuf[pl.ds(start, tile), :].T
        block = xbuf[pl.ds(start, tile + 2 * PAD), :].astype(jnp.float32)
        for tap in range(taps):
            first = PAD - half + tap
            moved = block[first : first + tile].astype(jnp.bfloat16)
            acc[tap] += jnp.dot(grad, moved, preferred_element_type=jnp.float32)
        return carry

    lax.fori_loop(0, rows // tile, body, 0)
    out[...] = acc[...].astype(out.dtype)


def weight_gradient(xs, gs, offs, taps, rows):
    width, chunk = xs[0].shape[1], gs[0].shape[1]
    tile = min(512, rows)
    some = pl.BlockSpec(memory_space=pl.ANY)
    return pl.pallas_call(
        functools.partial(weight_kernel, taps, tile, rows, nx=len(xs), ng=len(gs)),
        out_shape=jax.ShapeDtypeStruct((taps, chunk, width), jnp.bfloat16),
        in_specs=[pl.BlockSpec(memory_space=pltpu.SMEM)] + [some] * (len(xs) + len(gs)),
        out_specs=pl.BlockSpec(memory_space=pltpu.VMEM),
        scratch_shapes=[
            pltpu.VMEM((rows + 2 * PAD, width), jnp.bfloat16),
            pltpu.VMEM((rows, chunk), jnp.bfloat16),
            pltpu.VMEM((taps, chunk, width), jnp.float32),
            pltpu.SemaphoreType.DMA((len(xs) + len(gs),)),
        ],
        cost_estimate=pl.CostEstimate(
            flops=2 * rows * chunk * width * taps,
            bytes_accessed=2 * rows * (chunk + width),
            transcendentals=0,
        ),
        compiler_params=pltpu.CompilerParams(vmem_limit_bytes=40 * MIB),
    )(offs, *xs, *gs)


def local(x_saved, pre_act, out_grad, conv_w, coverage_obs, owners, exon_blocks):
    rows = x_saved.shape[0]
    width = x_saved.shape[1]
    taps = conv_w.shape[1]
    nseq = lax.axis_size("seq")
    nch = lax.axis_size("ch")
    mine = lax.axis_index("seq")
    place = lax.axis_index("ch")
    chunk = conv_w.shape[0] // nseq
    most = coverage_obs.shape[1]
    block = coverage_obs.shape[2]
    nblocks = rows // 2 // block
    counts = owners.shape[0]
    direct = nseq == nch and nseq <= 4 and chunk == width and width % 128 == 0

    if direct:
        xs, x_offs = [x_saved], [mine * rows]
        up = down = x_saved
        for hop in range(1, nseq):
            up = shift(up, "seq", 1, hop - 1)
            down = shift(down, "seq", -1, hop - 1)
            xs += [up, down]
            x_offs += [
                jnp.where(mine >= hop, (mine - hop) * rows, -1),
                jnp.where(mine + hop < nseq, (mine + hop) * rows, -1),
            ]
    else:
        xs, x_offs = [lax.all_gather(x_saved, "seq", axis=0, tiled=True)], [0]

    act, slope = gelu_pair(pre_act.astype(jnp.float32))
    pooled = (0.5 * jnp.sum(act.reshape(rows // 2, 2, width), axis=1)).astype(jnp.bfloat16)
    order = jnp.arange(counts, dtype=jnp.int32)
    same = owners[:, None] == owners[None, :]
    rank = jnp.sum((same & (order[:, None] < order[None, :])).astype(jnp.int32), axis=0)
    dest = jnp.arange(nseq, dtype=jnp.int32)
    if direct:
        dest = dest ^ mine
    slots = jnp.arange(most, dtype=jnp.int32)
    route = (owners[None, None, :] == dest[:, None, None]) & (
        rank[None, None, :] == slots[None, :, None]
    )
    route = route.astype(jnp.float32).reshape(nseq * most, counts)
    on_mine = exon_blocks // nblocks == mine
    holds = jnp.any(on_mine, axis=1)
    local_block = jnp.sum(jnp.where(on_mine, exon_blocks % nblocks, 0), axis=1)
    select = (
        holds[:, None] & (local_block[:, None] == jnp.arange(nblocks, dtype=jnp.int32)[None, :])
    ).astype(jnp.float32)
    picker = jnp.dot(route, select, precision=lax.Precision.HIGHEST).astype(jnp.bfloat16)
    pieces = pooled.reshape(nblocks, block * width)
    outgoing = jnp.dot(picker, pieces, preferred_element_type=jnp.float32).astype(jnp.bfloat16)
    outgoing = outgoing.reshape(nseq, most, block, width)
    if direct:
        arrived = [outgoing[0]] + [swap(outgoing[d], "seq", d) for d in range(1, nseq)]
        coverage = functools.reduce(jnp.add, [a.astype(jnp.float32) for a in arrived])
    else:
        arrived = lax.all_to_all(outgoing, "seq", split_axis=0, concat_axis=0, tiled=True)
        coverage = jnp.sum(arrived.astype(jnp.float32), axis=0)
    splice = jnp.tanh(coverage - coverage_obs[0]).astype(jnp.bfloat16)
    if direct:
        returned = jnp.stack([splice] + [swap(splice, "seq", d) for d in range(1, nseq)])
    else:
        returned = lax.all_gather(splice, "seq", axis=0, tiled=False)
    returned = returned.reshape(nseq * most, block * width)
    gained = jnp.dot(picker.T, returned, preferred_element_type=jnp.float32).reshape(
        rows // 2, width
    )
    pooled_grad = out_grad.astype(jnp.float32) + gained
    pre_grad = (jnp.repeat(pooled_grad, 2, axis=0) * 0.5 * slope).astype(jnp.bfloat16)

    if direct:
        parts = [pre_grad]
        flip = nch // 2
        while flip:
            parts = parts + [swap(p, "ch", flip) for p in parts]
            flip //= 2
        tags = [0]
        flip = nch // 2
        while flip:
            tags = tags + [t | flip for t in tags]
            flip //= 2
        w_offs = [(place ^ t) * width for t in tags]
        quarter = rows // nch
        slices = [lax.dynamic_slice_in_dim(p, place * quarter, quarter, axis=0) for p in parts]

        def chosen(flipped, options):
            want = mine ^ flipped ^ place
            picked = options[0]
            for t, option in zip(tags[1:], options[1:]):
                picked = jnp.where(want == t, option, picked)
            return picked

        gs, g_offs = [chosen(0, parts)], [mine * rows]
        for d in range(1, nseq):
            got = [swap(chosen(d, slices), "seq", d)]
            flip = nch // 2
            while flip:
                got = got + [swap(p, "ch", flip) for p in got]
                flip //= 2
            gs += got
            g_offs += [(mine ^ d) * rows + (place ^ t) * quarter for t in tags]
    else:
        whole = lax.all_gather(pre_grad, "ch", axis=1, tiled=True)
        parts, w_offs = [whole], [0]
        blocks = whole.reshape(rows, nseq, chunk).transpose(1, 0, 2)
        gs = [lax.all_to_all(blocks, "seq", 0, 0, tiled=True).reshape(nseq * rows, chunk)]
        g_offs = [0]
    low = shift(jnp.concatenate([p[rows - PAD :] for p in parts], axis=1), "seq", 1)
    high = shift(jnp.concatenate([p[:PAD] for p in parts], axis=1), "seq", -1)

    weights = conv_w.transpose(1, 0, 2)
    in_grad = input_gradient(parts, low, high, weights, pad_offsets(w_offs))
    w_grad = weight_gradient(xs, gs, pad_offsets(x_offs + g_offs), taps, nseq * rows)
    return (in_grad, w_grad.transpose(1, 0, 2))


def solution(mesh):
    in_specs = (
        P(("grp", "seq"), "ch"),
        P(("grp", "seq"), "ch"),
        P(("grp", "seq"), "ch"),
        P(None, None, "ch"),
        P(("grp", "seq"), None, None, "ch"),
        P("grp"),
        P("grp", None),
    )
    out_specs = (P(("grp", "seq"), "ch"), P(("grp", "seq"), None, "ch"))
    return jax.shard_map(local, mesh=mesh, in_specs=in_specs, out_specs=out_specs, check_vma=False)
```

time: 217 us -> 138 us (0.64)
  waiting for transfers between devices: 118 us -> 44.9 us
  starting transfers between devices: 7.41 us -> 46.4 us
  matrix products: 33.7 us -> 0.66 us
  Pallas kernels: 0 us -> 27.2 us
  blocking collectives: 23.6 us -> 0 us
  between operations: 14.3 us -> 1.22 us
  local copies, waits for them, and re-layouts: 10.6 us -> 6.92 us
    reduce_scatter x1 -> x0, waiting for transfers between devices: 91.5 us -> none  [local(): lax.psum_scatter(jnp.stack(terms, axis=1).astype(jnp.bfloat16), 'seq', sc...]
    ppermute x4 -> x29, starting transfers between devices: 7.33 us -> 46.4 us  [the longest x21 32.5 us: swap(): return lax.ppermute(block, axis, [(i, i ^ flip) for i in range(count)])]
    ppermute x4 -> x29, waiting for transfers between devices: 7.18 us -> 44.9 us  [the longest x21 34.3 us: swap(): return lax.ppermute(block, axis, [(i, i ^ flip) for i in range(count)])]
    dot_general x10 -> x0, matrix products: 33.1 us -> none  [the longest x5 20.1 us: local(): jnp.dot(inner.T, x_rim[tap:tap + rows], preferred_element_type=jnp.float32)]
    pallas_call x0 -> x2, Pallas kernels: none -> 27.2 us  [the longest x1 14.6 us: weight_gradient(): pl.pallas_call(functools.partial(weight_kernel, taps, tile, rows, nx=len(...]
    all_to_all x2 -> x0, blocking collectives: 23.6 us -> none  [the longest x1 13.7 us: local(): lax.all_to_all(outgoing, 'seq', split_axis=0, concat_axis=0, tiled=True)]
    all_gather x1 -> x0, waiting for transfers between devices: 19.5 us -> none  [local(): grad_rim = lax.all_gather(rimmed, 'ch', axis=1, tiled=True)]
    concatenate x2 -> x0, local copies, waits for them, and re-layouts: 6.68 us -> none  [with_halo(): block = jnp.concatenate([low, block, high], axis=dim)]
  transfers between devices with their start and end apart: 6 -> 29, of which waited for: 4 -> 12; matrix products, arithmetic and copies ran while one was open for 7% -> 1% of each run, Pallas kernels for 0% -> 9%
where the time goes in v1:
time: 138 us; the launch traced here: 137 us
  starting transfers between devices  46.4 us (34%)
  waiting for transfers between devices  44.9 us (33%)
  Pallas kernels  27.2 us (20%)
  other arithmetic  10.1 us (7%)
  local copies, waits for them, and re-layouts  6.92 us (5%)
    ppermute x21, waiting for transfers between devices, swap(): return lax.ppermute(block, axis, [(i, i ^ flip) for i in range(count)])  34.3 us
    ppermute x21, starting transfers between devices, swap(): return lax.ppermute(block, axis, [(i, i ^ flip) for i in range(count)])  32.5 us
    pallas_call x1, Pallas kernels, weight_gradient(): pl.pallas_call(functools.partial(weight_kernel, taps, tile, rows, nx=len(...  14.6 us
    ppermute x8, starting transfers between devices, shift(): return lax.ppermute(block, axis, pairs)  13.9 us
    pallas_call x1, Pallas kernels, input_gradient(): pl.pallas_call(functools.partial(input_kernel, taps, tile, pieces=len(par...  12.6 us
    ppermute x8, waiting for transfers between devices, shift(): return lax.ppermute(block, axis, pairs)  10.5 us
    unnamed x19, local copies, waits for them, and re-layouts  3.9 us
  transfers between devices with their start and end apart: 29, of which 12 were waited for; matrix products, arithmetic and copies ran while one was open for 1% of the time, Pallas kernels for 9%

profile of v1, /device:TPU:0, one launch (start us, length us, event | category | flops | bytes accessed | tf_op | source)
XLA Modules:
  0.0 137.4 jit_solution(5309404733000428689)
XLA Ops:
  3.6 1.4 %convert_multiply_fusion.3 = f32[1024,384]{1,0:T(8,128)S(1)} fusion(bf16[1024,384]{1,0:T(8,128)(2,1)} %param.8), kind=kLoop, calls=%fused_computation.4 | loop fusion | flops 1966080 | bytes 2359296 | tf_op jit(solution)/shard_map/mul | solution.py:31
  5.1 0.9 reshape.98
  6.0 1.9 %reduce_sum.29 = f32[512,384]{1,0:T(8,128)S(1)} reduce(f32[512,2,384]{2,1,0:T(2,128)S(1)} %reshape.98, f32[]{:T(128)} %constant.62.clone.1), dimensions={1}, to_apply=%region_3.4 | reduce | flops 196608 | bytes 2359300 | tf_op jit(solution)/shard_map/reduce_sum | solution.py:199
  8.6 5.1 %collective-permute-start.2 = (bf16[8,8,384]{2,1,0:T(8,128)(2,1)S(1)}, bf16[8,8,384]{2,1,0:T(8,128)(2,1)S(1)}, u32[]{:S(2)}, u32[]{:S(2)}) collective-permute-start(bf16[8,8,384]{2,1,0:T(8,128)(2,1)S(1)} %copy.16), channel_id=1, source_target_pairs={{0,12},{4,8},{8,4},{12,0},{1,13},{5,9},{9,5},{13,1},{2,14},{6,10},... | collective-permute-start | bytes 147464 | tf_op jit(solution)/shard_map/ppermute | solution.py:16
  14.4 1.4 %collective-permute-done.2 = bf16[8,8,384]{2,1,0:T(8,128)(2,1)S(1)} collective-permute-done((bf16[8,8,384]{2,1,0:T(8,128)(2,1)S(1)}, bf16[8,8,384]{2,1,0:T(8,128)(2,1)S(1)}, u32[]{:S(2)}, u32[]{:S(2)}) %collective-permute-start.2) | collective-permute-done | bytes 49184 | tf_op jit(solution)/shard_map/ppermute | solution.py:16
  15.8 2.9 %collective-permute-done.1 = bf16[8,8,384]{2,1,0:T(8,128)(2,1)S(1)} collective-permute-done((bf16[8,8,384]{2,1,0:T(8,128)(2,1)S(1)}, bf16[8,8,384]{2,1,0:T(8,128)(2,1)S(1)}, u32[]{:S(2)}, u32[]{:S(2)}) %collective-permute-start.1) | collective-permute-done | bytes 49184 | tf_op jit(solution)/shard_map/ppermute | solution.py:16
  18.8 2.1 %collective-permute-start.5 = (bf16[8,8,384]{2,1,0:T(8,128)(2,1)S(1)}, bf16[8,8,384]{2,1,0:T(8,128)(2,1)S(1)}, u32[]{:S(2)}, u32[]{:S(2)}) collective-permute-start(bf16[8,8,384]{2,1,0:T(8,128)(2,1)S(1)} %fusion.9), channel_id=1, source_target_pairs={{0,12},{4,8},{8,4},{12,0},{1,13},{5,9},{9,5},{13,1},{2,14},{6,10},... | collective-permute-start | bytes 147464 | tf_op jit(solution)/shard_map/ppermute | solution.py:16
  21.1 2.2 %collective-permute-start.3 = (bf16[8,8,384]{2,1,0:T(8,128)(2,1)S(1)}, bf16[8,8,384]{2,1,0:T(8,128)(2,1)S(1)}, u32[]{:S(2)}, u32[]{:S(2)}) collective-permute-start(bf16[8,8,384]{2,1,0:T(8,128)(2,1)S(1)} %fusion.9), channel_id=1, source_target_pairs={{0,4},{4,0},{8,12},{12,8},{1,5},{5,1},{9,13},{13,9},{2,6},{6,2},{1... | collective-permute-start | bytes 147464 | tf_op jit(solution)/shard_map/ppermute | solution.py:16
  23.3 1.7 %collective-permute-done.5 = bf16[8,8,384]{2,1,0:T(8,128)(2,1)S(1)} collective-permute-done((bf16[8,8,384]{2,1,0:T(8,128)(2,1)S(1)}, bf16[8,8,384]{2,1,0:T(8,128)(2,1)S(1)}, u32[]{:S(2)}, u32[]{:S(2)}) %collective-permute-start.5) | collective-permute-done | bytes 49184 | tf_op jit(solution)/shard_map/ppermute | solution.py:16
  25.0 1.4 %collective-permute-done.4 = bf16[8,8,384]{2,1,0:T(8,128)(2,1)S(1)} collective-permute-done((bf16[8,8,384]{2,1,0:T(8,128)(2,1)S(1)}, bf16[8,8,384]{2,1,0:T(8,128)(2,1)S(1)}, u32[]{:S(2)}, u32[]{:S(2)}) %collective-permute-start.4) | collective-permute-done | bytes 49184 | tf_op jit(solution)/shard_map/ppermute | solution.py:16
  28.1 1.1 mul.135
  29.2 1.8 %fusion.7.refs_0_ = bf16[1024,384]{1,0:T(8,128)(2,1)S(1)} fusion(f32[1024,384]{1,0:T(8,128)S(1)} %mul.135, bf16[1024,384]{1,0:T(8,128)(2,1)} %param.8), kind=kLoop, calls=%fused_computation.13 | loop fusion | flops 4325376 | bytes 3145728 | tf_op jit(solution)/shard_map/convert_element_type | solution.py:237
  31.0 1.6 %collective-permute-start.6 = (bf16[1024,384]{1,0:T(8,128)(2,1)S(1)}, bf16[1024,384]{1,0:T(8,128)(2,1)S(1)}, u32[]{:S(2)}, u32[]{:S(2)}) collective-permute-start(bf16[1024,384]{1,0:T(8,128)(2,1)S(1)} %fusion.7.refs_0_), channel_id=1, source_target_pairs={{0,2},{1,3},{2,0},{3,1},{4,6},{5,7},{6,4},{7,5},{8,10},{9,11},{10,... | collective-permute-start | bytes 2359304 | tf_op jit(solution)/shard_map/ppermute | solution.py:16
  32.6 3.7 %collective-permute-start.11 = (bf16[1024,384]{1,0:T(8,128)(2,1)}, bf16[1024,384]{1,0:T(8,128)(2,1)}, u32[]{:S(2)}, u32[]{:S(2)}) collective-permute-start(bf16[1024,384]{1,0:T(8,128)(2,1)} %refs_0_.1), channel_id=1, source_target_pairs={{0,4},{4,8},{8,12},{1,5},{5,9},{9,13},{2,6},{6,10},{10,14},{3,7},{... | collective-permute-start | bytes 2359304 | tf_op jit(solution)/shard_map/ppermute | solution.py:25
  36.3 1.3 collective-permute-start.12
  37.7 11.1 %collective-permute-done.6.refs_1_ = bf16[1024,384]{1,0:T(8,128)(2,1)S(1)} collective-permute-done((bf16[1024,384]{1,0:T(8,128)(2,1)S(1)}, bf16[1024,384]{1,0:T(8,128)(2,1)S(1)}, u32[]{:S(2)}, u32[]{:S(2)}) %collective-permute-start.6) | collective-permute-done | bytes 786464 | tf_op jit(solution)/shard_map/ppermute | solution.py:16
  48.8 1.4 %collective-permute-done.11.refs_1_ = bf16[1024,384]{1,0:T(8,128)(2,1)} collective-permute-done((bf16[1024,384]{1,0:T(8,128)(2,1)}, bf16[1024,384]{1,0:T(8,128)(2,1)}, u32[]{:S(2)}, u32[]{:S(2)}) %collective-permute-start.11) | collective-permute-done | bytes 786464 | tf_op jit(solution)/shard_map/ppermute | solution.py:25
  51.0 4.3 %collective-permute-done.12.refs_2_ = bf16[1024,384]{1,0:T(8,128)(2,1)} collective-permute-done((bf16[1024,384]{1,0:T(8,128)(2,1)}, bf16[1024,384]{1,0:T(8,128)(2,1)}, u32[]{:S(2)}, u32[]{:S(2)}) %collective-permute-start.12) | collective-permute-done | bytes 786464 | tf_op jit(solution)/shard_map/ppermute | solution.py:25
  55.3 1.3 collective-permute-start.14
  57.5 2.6 %collective-permute-start.17 = (bf16[256,384]{1,0:T(8,128)(2,1)S(1)}, bf16[256,384]{1,0:T(8,128)(2,1)S(1)}, u32[]{:S(2)}, u32[]{:S(2)}) collective-permute-start(bf16[256,384]{1,0:T(8,128)(2,1)S(1)} %get-tuple-element.6), channel_id=1, source_target_pairs={{0,4},{4,0},{8,12},{12,8},{1,5},{5,1},{9,13},{13,9},{2,6},{6,2},{1... | collective-permute-start | bytes 589832 | tf_op jit(solution)/shard_map/ppermute | solution.py:16
  60.1 3.5 %collective-permute-start.9 = (bf16[16,1536]{1,0:T(8,128)(2,1)S(1)}, bf16[16,1536]{1,0:T(8,128)(2,1)S(1)}, u32[]{:S(2)}, u32[]{:S(2)}) collective-permute-start(bf16[16,1536]{1,0:T(8,128)(2,1)S(1)} %pad_maximum_fusion), channel_id=1, source_target_pairs={{0,4},{4,8},{8,12},{1,5},{5,9},{9,13},{2,6},{6,10},{10,14},{3,7},{... | collective-permute-start | bytes 147464 | tf_op jit(solution)/shard_map/ppermute | solution.py:25
  63.6 14.4 %collective-permute-start.25 = (bf16[256,384]{1,0:T(8,128)(2,1)}, bf16[256,384]{1,0:T(8,128)(2,1)}, u32[]{:S(2)}, u32[]{:S(2)}) collective-permute-start(bf16[256,384]{1,0:T(8,128)(2,1)} %get-tuple-element.4), channel_id=1, source_target_pairs={{0,12},{4,8},{8,4},{12,0},{1,13},{5,9},{9,5},{13,1},{2,14},{6,10},... | collective-permute-start | bytes 589832 | tf_op jit(solution)/shard_map/ppermute | solution.py:16
  78.1 5.6 %collective-permute-done.17.refs_8_ = bf16[256,384]{1,0:T(8,128)(2,1)S(1)} collective-permute-done((bf16[256,384]{1,0:T(8,128)(2,1)S(1)}, bf16[256,384]{1,0:T(8,128)(2,1)S(1)}, u32[]{:S(2)}, u32[]{:S(2)}) %collective-permute-start.17) | collective-permute-done | bytes 196640 | tf_op jit(solution)/shard_map/ppermute | solution.py:16
  84.2 3.6 %collective-permute-done.21.refs_12_ = bf16[256,384]{1,0:T(8,128)(2,1)S(1)} collective-permute-done((bf16[256,384]{1,0:T(8,128)(2,1)S(1)}, bf16[256,384]{1,0:T(8,128)(2,1)S(1)}, u32[]{:S(2)}, u32[]{:S(2)}) %collective-permute-start.21) | collective-permute-done | bytes 196640 | tf_op jit(solution)/shard_map/ppermute | solution.py:16
  87.9 1.5 %collective-permute-start.22 = (bf16[256,384]{1,0:T(8,128)(2,1)S(1)}, bf16[256,384]{1,0:T(8,128)(2,1)}, u32[]{:S(2)}, u32[]{:S(2)}) collective-permute-start(bf16[256,384]{1,0:T(8,128)(2,1)S(1)} %collective-permute-done.21.refs_12_), channel_id=1, source_target_pairs={{0,2},{1,3},{2,0},{3,1},{4,6},{5,7},{6,4},{7,5},{8,10},{9,11},{10,... | collective-permute-start | bytes 589832 | tf_op jit(solution)/shard_map/ppermute | solution.py:16
  90.6 1.3 collective-permute-start.10
  92.1 4.8 %collective-permute-done.10.refs_5_ = bf16[16,1536]{1,0:T(8,128)(2,1)} collective-permute-done((bf16[16,1536]{1,0:T(8,128)(2,1)}, bf16[16,1536]{1,0:T(8,128)(2,1)}, u32[]{:S(2)}, u32[]{:S(2)}) %collective-permute-start.10) | collective-permute-done | bytes 49184 | tf_op jit(solution)/shard_map/ppermute | solution.py:25
  97.6 1.5 %collective-permute-start.16 = (bf16[1024,384]{1,0:T(8,128)(2,1)}, bf16[1024,384]{1,0:T(8,128)(2,1)S(1)}, u32[]{:S(2)}, u32[]{:S(2)}) collective-permute-start(bf16[1024,384]{1,0:T(8,128)(2,1)} %copy-done.3), channel_id=1, source_target_pairs={{4,0},{5,1},{6,2},{7,3},{20,16},{21,17},{22,18},{23,19}} | collective-permute-start | bytes 2359304 | tf_op jit(solution)/shard_map/ppermute | solution.py:25
  100.7 6.0 %collective-permute-done.26.refs_17_ = bf16[256,384]{1,0:T(8,128)(2,1)S(1)} collective-permute-done((bf16[256,384]{1,0:T(8,128)(2,1)}, bf16[256,384]{1,0:T(8,128)(2,1)S(1)}, u32[]{:S(2)}, u32[]{:S(2)}) %collective-permute-start.26) | collective-permute-done | bytes 196640 | tf_op jit(solution)/shard_map/ppermute | solution.py:16
  107.2 2.7 %copy-done = bf16[1536,5,384]{2,0,1:T(8,128)(2,1)S(1)} copy-done((bf16[1536,5,384]{2,0,1:T(8,128)(2,1)S(1)}, bf16[1536,5,384]{2,0,1:T(8,128)(2,1)}, u32[]{:S(2)}) %copy-start) | copy-done | bytes 5898264
  109.9 12.6 %shard_map.86 = bf16[1024,384]{1,0:T(8,128)(2,1)} custom-call(s32[4]{0:T(128)S(1)} %pad_add_fusion.offs, bf16[1024,384]{1,0:T(8,128)(2,1)S(1)} %fusion.7.refs_0_, bf16[1024,384]{1,0:T(8,128)(2,1)S(1)} %collective-permute-done.6.refs_1_, bf16[1024,384]{1,0:T(8,128)(2,1)S(1)} %collective-permute-done.7.refs_2_, ...), custom_call_target="tpu_custom_call" | custom-call | flops 6039797760 | bytes 9830400 | tf_op jit(solution)/shard_map/pallas_call | solution.py:81
  122.6 14.6 %shard_map.87 = bf16[5,384,384]{2,1,0:T(8,128)(2,1)} custom-call(s32[20]{0:T(128)S(1)} %stack.120.offs, bf16[1024,384]{1,0:T(8,128)(2,1)} %refs_0_.1, bf16[1024,384]{1,0:T(8,128)(2,1)} %collective-permute-done.11.refs_1_, bf16[1024,384]{1,0:T(8,128)(2,1)} %collective-permute-done.12.refs_2_, bf16[1024,384]{1,0:T(8,128)(2,1)S(1)} %copy-done.2, ...), custom_call_target="tpu_custom_call" | custom-call | flops 6039797760 | bytes 6291456 | tf_op jit(solution)/shard_map/pallas_call | solution.py:149
  (83 shorter events, 12.7 us)
Async XLA Ops:
  8.6 7.2 %collective-permute-start.2 = (bf16[8,8,384]{2,1,0:T(8,128)(2,1)S(1)}, bf16[8,8,384]{2,1,0:T(8,128)(2,1)S(1)}, u32[]{:S(2)}, u32[]{:S(2)}) collective-permute-start(bf16[8,8,384]{2,1,0:T(8,128)(2,1)S(1)} %copy.16), channel_id=1, source_target_pairs={{0,12},{4,8},{8,4},{12,0},{1,13},{5,9},{9,5},{13,1},{2,14},{6,10},... | collective-permute-start | bytes 147464 | tf_op jit(solution)/shard_map/ppermute | solution.py:16
  13.7 5.1 %collective-permute-start.1 = (bf16[8,8,384]{2,1,0:T(8,128)(2,1)S(1)}, bf16[8,8,384]{2,1,0:T(8,128)(2,1)S(1)}, u32[]{:S(2)}, u32[]{:S(2)}) collective-permute-start(bf16[8,8,384]{2,1,0:T(8,128)(2,1)S(1)} %copy.15), channel_id=1, source_target_pairs={{0,8},{4,12},{8,0},{12,4},{1,9},{5,13},{9,1},{13,5},{2,10},{6,14},... | collective-permute-start | bytes 147464 | tf_op jit(solution)/shard_map/ppermute | solution.py:16
  13.8 5.0 %collective-permute-start = (bf16[8,8,384]{2,1,0:T(8,128)(2,1)S(1)}, bf16[8,8,384]{2,1,0:T(8,128)(2,1)S(1)}, u32[]{:S(2)}, u32[]{:S(2)}) collective-permute-start(bf16[8,8,384]{2,1,0:T(8,128)(2,1)S(1)} %copy.13), channel_id=1, source_target_pairs={{0,4},{4,0},{8,12},{12,8},{1,5},{5,1},{9,13},{13,9},{2,6},{6,2},{1... | collective-permute-start | bytes 147464 | tf_op jit(solution)/shard_map/ppermute | solution.py:16
  18.8 6.2 %collective-permute-start.5 = (bf16[8,8,384]{2,1,0:T(8,128)(2,1)S(1)}, bf16[8,8,384]{2,1,0:T(8,128)(2,1)S(1)}, u32[]{:S(2)}, u32[]{:S(2)}) collective-permute-start(bf16[8,8,384]{2,1,0:T(8,128)(2,1)S(1)} %fusion.9), channel_id=1, source_target_pairs={{0,12},{4,8},{8,4},{12,0},{1,13},{5,9},{9,5},{13,1},{2,14},{6,10},... | collective-permute-start | bytes 147464 | tf_op jit(solution)/shard_map/ppermute | solution.py:16
  20.9 5.5 %collective-permute-start.4 = (bf16[8,8,384]{2,1,0:T(8,128)(2,1)S(1)}, bf16[8,8,384]{2,1,0:T(8,128)(2,1)S(1)}, u32[]{:S(2)}, u32[]{:S(2)}) collective-permute-start(bf16[8,8,384]{2,1,0:T(8,128)(2,1)S(1)} %fusion.9), channel_id=1, source_target_pairs={{0,8},{4,12},{8,0},{12,4},{1,9},{5,13},{9,1},{13,5},{2,10},{6,14},... | collective-permute-start | bytes 147464 | tf_op jit(solution)/shard_map/ppermute | solution.py:16
  21.1 5.4 %collective-permute-start.3 = (bf16[8,8,384]{2,1,0:T(8,128)(2,1)S(1)}, bf16[8,8,384]{2,1,0:T(8,128)(2,1)S(1)}, u32[]{:S(2)}, u32[]{:S(2)}) collective-permute-start(bf16[8,8,384]{2,1,0:T(8,128)(2,1)S(1)} %fusion.9), channel_id=1, source_target_pairs={{0,4},{4,0},{8,12},{12,8},{1,5},{5,1},{9,13},{13,9},{2,6},{6,2},{1... | collective-permute-start | bytes 147464 | tf_op jit(solution)/shard_map/ppermute | solution.py:16
  31.0 17.8 %collective-permute-start.6 = (bf16[1024,384]{1,0:T(8,128)(2,1)S(1)}, bf16[1024,384]{1,0:T(8,128)(2,1)S(1)}, u32[]{:S(2)}, u32[]{:S(2)}) collective-permute-start(bf16[1024,384]{1,0:T(8,128)(2,1)S(1)} %fusion.7.refs_0_), channel_id=1, source_target_pairs={{0,2},{1,3},{2,0},{3,1},{4,6},{5,7},{6,4},{7,5},{8,10},{9,11},{10,... | collective-permute-start | bytes 2359304 | tf_op jit(solution)/shard_map/ppermute | solution.py:16
  32.6 17.7 %collective-permute-start.11 = (bf16[1024,384]{1,0:T(8,128)(2,1)}, bf16[1024,384]{1,0:T(8,128)(2,1)}, u32[]{:S(2)}, u32[]{:S(2)}) collective-permute-start(bf16[1024,384]{1,0:T(8,128)(2,1)} %refs_0_.1), channel_id=1, source_target_pairs={{0,4},{4,8},{8,12},{1,5},{5,9},{9,13},{2,6},{6,10},{10,14},{3,7},{... | collective-permute-start | bytes 2359304 | tf_op jit(solution)/shard_map/ppermute | solution.py:25
  36.3 18.9 %collective-permute-start.12 = (bf16[1024,384]{1,0:T(8,128)(2,1)}, bf16[1024,384]{1,0:T(8,128)(2,1)}, u32[]{:S(2)}, u32[]{:S(2)}) collective-permute-start(bf16[1024,384]{1,0:T(8,128)(2,1)} %refs_0_.1), channel_id=1, source_target_pairs={{4,0},{8,4},{12,8},{5,1},{9,5},{13,9},{6,2},{10,6},{14,10},{7,3},{... | collective-permute-start | bytes 2359304 | tf_op jit(solution)/shard_map/ppermute | solution.py:25
  37.6 19.0 %collective-permute-start.7 = (bf16[1024,384]{1,0:T(8,128)(2,1)S(1)}, bf16[1024,384]{1,0:T(8,128)(2,1)S(1)}, u32[]{:S(2)}, u32[]{:S(2)}) collective-permute-start(bf16[1024,384]{1,0:T(8,128)(2,1)S(1)} %fusion.7.refs_0_), channel_id=1, source_target_pairs={{0,1},{1,0},{2,3},{3,2},{4,5},{5,4},{6,7},{7,6},{8,9},{9,8},{10,11... | collective-permute-start | bytes 2359304 | tf_op jit(solution)/shard_map/ppermute | solution.py:16
  48.8 7.8 %collective-permute-start.8 = (bf16[1024,384]{1,0:T(8,128)(2,1)S(1)}, bf16[1024,384]{1,0:T(8,128)(2,1)S(1)}, u32[]{:S(2)}, u32[]{:S(2)}) collective-permute-start(bf16[1024,384]{1,0:T(8,128)(2,1)S(1)} %collective-permute-done.6.refs_1_), channel_id=1, source_target_pairs={{0,1},{1,0},{2,3},{3,2},{4,5},{5,4},{6,7},{7,6},{8,9},{9,8},{10,11... | collective-permute-start | bytes 2359304 | tf_op jit(solution)/shard_map/ppermute | solution.py:16
  50.2 13.4 %collective-permute-start.13 = (bf16[1024,384]{1,0:T(8,128)(2,1)}, bf16[1024,384]{1,0:T(8,128)(2,1)S(1)}, u32[]{:S(2)}, u32[]{:S(2)}) collective-permute-start(bf16[1024,384]{1,0:T(8,128)(2,1)} %collective-permute-done.11.refs_1_), channel_id=1, source_target_pairs={{4,8},{8,12},{5,9},{9,13},{6,10},{10,14},{7,11},{11,15},{20,24},{2... | collective-permute-start | bytes 2359304 | tf_op jit(solution)/shard_map/ppermute | solution.py:25
  55.3 29.0 %collective-permute-start.14 = (bf16[1024,384]{1,0:T(8,128)(2,1)}, bf16[1024,384]{1,0:T(8,128)(2,1)S(1)}, u32[]{:S(2)}, u32[]{:S(2)}) collective-permute-start(bf16[1024,384]{1,0:T(8,128)(2,1)} %collective-permute-done.12.refs_2_), channel_id=1, source_target_pairs={{4,0},{8,4},{5,1},{9,5},{6,2},{10,6},{7,3},{11,7},{20,16},{24,20},... | collective-permute-start | bytes 2359304 | tf_op jit(solution)/shard_map/ppermute | solution.py:25
  57.5 26.2 %collective-permute-start.17 = (bf16[256,384]{1,0:T(8,128)(2,1)S(1)}, bf16[256,384]{1,0:T(8,128)(2,1)S(1)}, u32[]{:S(2)}, u32[]{:S(2)}) collective-permute-start(bf16[256,384]{1,0:T(8,128)(2,1)S(1)} %get-tuple-element.6), channel_id=1, source_target_pairs={{0,4},{4,0},{8,12},{12,8},{1,5},{5,1},{9,13},{13,9},{2,6},{6,2},{1... | collective-permute-start | bytes 589832 | tf_op jit(solution)/shard_map/ppermute | solution.py:16
  60.1 27.7 %collective-permute-start.21 = (bf16[256,384]{1,0:T(8,128)(2,1)S(1)}, bf16[256,384]{1,0:T(8,128)(2,1)S(1)}, u32[]{:S(2)}, u32[]{:S(2)}) collective-permute-start(bf16[256,384]{1,0:T(8,128)(2,1)S(1)} %get-tuple-element.5), channel_id=1, source_target_pairs={{0,8},{4,12},{8,0},{12,4},{1,9},{5,13},{9,1},{13,5},{2,10},{6,14},... | collective-permute-start | bytes 589832 | tf_op jit(solution)/shard_map/ppermute | solution.py:16
  60.1 29.8 %collective-permute-start.9 = (bf16[16,1536]{1,0:T(8,128)(2,1)S(1)}, bf16[16,1536]{1,0:T(8,128)(2,1)S(1)}, u32[]{:S(2)}, u32[]{:S(2)}) collective-permute-start(bf16[16,1536]{1,0:T(8,128)(2,1)S(1)} %pad_maximum_fusion), channel_id=1, source_target_pairs={{0,4},{4,8},{8,12},{1,5},{5,9},{9,13},{2,6},{6,10},{10,14},{3,7},{... | collective-permute-start | bytes 147464 | tf_op jit(solution)/shard_map/ppermute | solution.py:25
  63.6 28.3 %copy-start.1 = (bf16[1024,384]{1,0:T(8,128)(2,1)}, bf16[1024,384]{1,0:T(8,128)(2,1)S(1)}, u32[]{:S(2)}) copy-start(bf16[1024,384]{1,0:T(8,128)(2,1)S(1)} %collective-permute-done.13.refs_3_) | copy-start | bytes 2359300
  63.6 34.0 %collective-permute-start.25 = (bf16[256,384]{1,0:T(8,128)(2,1)}, bf16[256,384]{1,0:T(8,128)(2,1)}, u32[]{:S(2)}, u32[]{:S(2)}) collective-permute-start(bf16[256,384]{1,0:T(8,128)(2,1)} %get-tuple-element.4), channel_id=1, source_target_pairs={{0,12},{4,8},{8,4},{12,0},{1,13},{5,9},{9,5},{13,1},{2,14},{6,10},... | collective-permute-start | bytes 589832 | tf_op jit(solution)/shard_map/ppermute | solution.py:16
  83.7 15.4 %collective-permute-start.18 = (bf16[256,384]{1,0:T(8,128)(2,1)S(1)}, bf16[256,384]{1,0:T(8,128)(2,1)}, u32[]{:S(2)}, u32[]{:S(2)}) collective-permute-start(bf16[256,384]{1,0:T(8,128)(2,1)S(1)} %collective-permute-done.17.refs_8_), channel_id=1, source_target_pairs={{0,2},{1,3},{2,0},{3,1},{4,6},{5,7},{6,4},{7,5},{8,10},{9,11},{10,... | collective-permute-start | bytes 589832 | tf_op jit(solution)/shard_map/ppermute | solution.py:16
  84.2 14.9 %collective-permute-start.19 = (bf16[256,384]{1,0:T(8,128)(2,1)S(1)}, bf16[256,384]{1,0:T(8,128)(2,1)}, u32[]{:S(2)}, u32[]{:S(2)}) collective-permute-start(bf16[256,384]{1,0:T(8,128)(2,1)S(1)} %collective-permute-done.17.refs_8_), channel_id=1, source_target_pairs={{0,1},{1,0},{2,3},{3,2},{4,5},{5,4},{6,7},{7,6},{8,9},{9,8},{10,11... | collective-permute-start | bytes 589832 | tf_op jit(solution)/shard_map/ppermute | solution.py:16
  87.9 11.9 %collective-permute-start.22 = (bf16[256,384]{1,0:T(8,128)(2,1)S(1)}, bf16[256,384]{1,0:T(8,128)(2,1)}, u32[]{:S(2)}, u32[]{:S(2)}) collective-permute-start(bf16[256,384]{1,0:T(8,128)(2,1)S(1)} %collective-permute-done.21.refs_12_), channel_id=1, source_target_pairs={{0,2},{1,3},{2,0},{3,1},{4,6},{5,7},{6,4},{7,5},{8,10},{9,11},{10,... | collective-permute-start | bytes 589832 | tf_op jit(solution)/shard_map/ppermute | solution.py:16
  90.6 6.3 %collective-permute-start.10 = (bf16[16,1536]{1,0:T(8,128)(2,1)}, bf16[16,1536]{1,0:T(8,128)(2,1)}, u32[]{:S(2)}, u32[]{:S(2)}) collective-permute-start(bf16[16,1536]{1,0:T(8,128)(2,1)} %pad_maximum_fusion.1), channel_id=1, source_target_pairs={{4,0},{8,4},{12,8},{5,1},{9,5},{13,9},{6,2},{10,6},{14,10},{7,3},{... | collective-permute-start | bytes 147464 | tf_op jit(solution)/shard_map/ppermute | solution.py:25
  92.1 15.1 %copy-start.6 = (bf16[16,1536]{1,0:T(8,128)(2,1)S(1)}, bf16[16,1536]{1,0:T(8,128)(2,1)}, u32[]{:S(2)}) copy-start(bf16[16,1536]{1,0:T(8,128)(2,1)} %copy-done.5) | copy-start | bytes 147460
  96.9 25.7 %collective-permute-start.15 = (bf16[1024,384]{1,0:T(8,128)(2,1)}, bf16[1024,384]{1,0:T(8,128)(2,1)S(1)}, u32[]{:S(2)}, u32[]{:S(2)}) collective-permute-start(bf16[1024,384]{1,0:T(8,128)(2,1)} %copy-done.1), channel_id=1, source_target_pairs={{8,12},{9,13},{10,14},{11,15},{24,28},{25,29},{26,30},{27,31}} | collective-permute-start | bytes 2359304 | tf_op jit(solution)/shard_map/ppermute | solution.py:25
  97.6 24.9 %collective-permute-start.16 = (bf16[1024,384]{1,0:T(8,128)(2,1)}, bf16[1024,384]{1,0:T(8,128)(2,1)S(1)}, u32[]{:S(2)}, u32[]{:S(2)}) collective-permute-start(bf16[1024,384]{1,0:T(8,128)(2,1)} %copy-done.3), channel_id=1, source_target_pairs={{4,0},{5,1},{6,2},{7,3},{20,16},{21,17},{22,18},{23,19}} | collective-permute-start | bytes 2359304 | tf_op jit(solution)/shard_map/ppermute | solution.py:25
  99.1 1.5 %collective-permute-start.23 = (bf16[256,384]{1,0:T(8,128)(2,1)S(1)}, bf16[256,384]{1,0:T(8,128)(2,1)S(1)}, u32[]{:S(2)}, u32[]{:S(2)}) collective-permute-start(bf16[256,384]{1,0:T(8,128)(2,1)S(1)} %collective-permute-done.21.refs_12_), channel_id=1, source_target_pairs={{0,1},{1,0},{2,3},{3,2},{4,5},{5,4},{6,7},{7,6},{8,9},{9,8},{10,11... | collective-permute-start | bytes 589832 | tf_op jit(solution)/shard_map/ppermute | solution.py:16
  99.2 7.5 %collective-permute-start.26 = (bf16[256,384]{1,0:T(8,128)(2,1)}, bf16[256,384]{1,0:T(8,128)(2,1)S(1)}, u32[]{:S(2)}, u32[]{:S(2)}) collective-permute-start(bf16[256,384]{1,0:T(8,128)(2,1)} %collective-permute-done.25.refs_16_), channel_id=1, source_target_pairs={{0,2},{1,3},{2,0},{3,1},{4,6},{5,7},{6,4},{7,5},{8,10},{9,11},{10,... | collective-permute-start | bytes 589832 | tf_op jit(solution)/shard_map/ppermute | solution.py:16
  99.8 6.9 %collective-permute-start.27 = (bf16[256,384]{1,0:T(8,128)(2,1)}, bf16[256,384]{1,0:T(8,128)(2,1)S(1)}, u32[]{:S(2)}, u32[]{:S(2)}) collective-permute-start(bf16[256,384]{1,0:T(8,128)(2,1)} %collective-permute-done.25.refs_16_), channel_id=1, source_target_pairs={{0,1},{1,0},{2,3},{3,2},{4,5},{5,4},{6,7},{7,6},{8,9},{9,8},{10,11... | collective-permute-start | bytes 589832 | tf_op jit(solution)/shard_map/ppermute | solution.py:16
  100.6 21.9 %collective-permute-start.20 = (bf16[256,384]{1,0:T(8,128)(2,1)}, bf16[256,384]{1,0:T(8,128)(2,1)S(1)}, u32[]{:S(2)}, u32[]{:S(2)}) collective-permute-start(bf16[256,384]{1,0:T(8,128)(2,1)} %collective-permute-done.18.refs_9_), channel_id=1, source_target_pairs={{0,1},{1,0},{2,3},{3,2},{4,5},{5,4},{6,7},{7,6},{8,9},{9,8},{10,11... | collective-permute-start | bytes 589832 | tf_op jit(solution)/shard_map/ppermute | solution.py:16
  106.7 15.8 %collective-permute-start.24 = (bf16[256,384]{1,0:T(8,128)(2,1)}, bf16[256,384]{1,0:T(8,128)(2,1)S(1)}, u32[]{:S(2)}, u32[]{:S(2)}) collective-permute-start(bf16[256,384]{1,0:T(8,128)(2,1)} %collective-permute-done.22.refs_13_), channel_id=1, source_target_pairs={{0,1},{1,0},{2,3},{3,2},{4,5},{5,4},{6,7},{7,6},{8,9},{9,8},{10,11... | collective-permute-start | bytes 589832 | tf_op jit(solution)/shard_map/ppermute | solution.py:16
  106.7 15.8 %collective-permute-start.28 = (bf16[256,384]{1,0:T(8,128)(2,1)S(1)}, bf16[256,384]{1,0:T(8,128)(2,1)S(1)}, u32[]{:S(2)}, u32[]{:S(2)}) collective-permute-start(bf16[256,384]{1,0:T(8,128)(2,1)S(1)} %collective-permute-done.26.refs_17_), channel_id=1, source_target_pairs={{0,1},{1,0},{2,3},{3,2},{4,5},{5,4},{6,7},{7,6},{8,9},{9,8},{10,11... | collective-permute-start | bytes 589832 | tf_op jit(solution)/shard_map/ppermute | solution.py:16
  109.9 12.7 %copy-start.4 = (bf16[1024,384]{1,0:T(8,128)(2,1)S(1)}, bf16[1024,384]{1,0:T(8,128)(2,1)}, u32[]{:S(2)}) copy-start(bf16[1024,384]{1,0:T(8,128)(2,1)} %copy-done.3) | copy-start | bytes 2359300
  (6 other events, 35.5 us)

commit v2 on v0

v2 whole, which is shorter than its diff:
```python
import functools

import jax
import jax.numpy as jnp
from jax import lax
from jax.experimental import pallas as pl
from jax.experimental.pallas import tpu as pltpu
from jax.sharding import PartitionSpec as P

PAD = 16
MIB = 1024 * 1024
VMEM = pl.BlockSpec(memory_space=pltpu.VMEM)
SMEM = pl.BlockSpec(memory_space=pltpu.SMEM)
SOME = pl.BlockSpec(memory_space=pl.ANY)
HALF_ROOT = 0.7071067811865476
DENSITY = 0.3989422804014327
LANES = 128


def swap(block, axis, flip):
    count = lax.axis_size(axis)
    return lax.ppermute(block, axis, [(i, i ^ flip) for i in range(count)])


def shift(block, axis, step, first=0):
    count = lax.axis_size(axis)
    if step > 0:
        pairs = [(i, i + 1) for i in range(first, count - 1)]
    else:
        pairs = [(i + 1, i) for i in range(count - 1 - first)]
    return lax.ppermute(block, axis, pairs)


def after(values, others=()):
    return lax.optimization_barrier(tuple(values) + tuple(others))[: len(values)]


def input_kernel(*refs, taps, tile, pieces, origins):
    parts, (low, high, weights, out, wide, wbuf, sems) = refs[:pieces], refs[pieces:]
    rows = parts[0].shape[0]
    half = taps // 2
    copies = []
    base = 0
    for e, origin in enumerate(origins()):
        span = parts[e].shape[1]
        src = weights.at[:, pl.ds(pl.multiple_of(origin, 16), span), :]
        copy = pltpu.make_async_copy(src, wbuf.at[:, pl.ds(base, span), :], sems.at[e])
        copy.start()
        copies.append(copy)
        base += span
    base = 0
    for e in range(pieces):
        span = parts[e].shape[1]
        wide[pl.ds(0, PAD), pl.ds(base, span)] = low[:, pl.ds(base, span)]
        wide[pl.ds(PAD, rows), pl.ds(base, span)] = parts[e][...]
        wide[pl.ds(PAD + rows, PAD), pl.ds(base, span)] = high[:, pl.ds(base, span)]
        base += span
    for copy in copies:
        copy.wait()

    def body(step, carry):
        start = pl.multiple_of(step * tile, tile)
        block = wide[pl.ds(start, tile + 2 * PAD), :]
        total = None
        for tap in range(taps):
            term = jnp.dot(block, wbuf[tap], preferred_element_type=jnp.float32)
            first = PAD + half - tap
            term = term[first : first + tile]
            total = term if total is None else total + term
        out[pl.ds(start, tile), :] = total.astype(out.dtype)
        return carry

    lax.fori_loop(0, rows // tile, body, 0)


def input_gradient(parts, low, high, weights, origins):
    taps, chans, width = weights.shape
    rows = parts[0].shape[0]
    return pl.pallas_call(
        functools.partial(
            input_kernel, taps=taps, tile=min(256, rows), pieces=len(parts), origins=origins
        ),
        out_shape=jax.ShapeDtypeStruct((rows, width), jnp.bfloat16),
        in_specs=[VMEM] * (len(parts) + 2) + [SOME],
        out_specs=VMEM,
        scratch_shapes=[
            pltpu.VMEM((rows + 2 * PAD, chans), jnp.bfloat16),
            pltpu.VMEM((taps, chans, width), jnp.bfloat16),
            pltpu.SemaphoreType.DMA((len(parts),)),
        ],
        cost_estimate=pl.CostEstimate(
            flops=2 * rows * chans * width * taps,
            bytes_accessed=2 * (rows * chans + taps * chans * width + rows * width),
            transcendentals=0,
        ),
        compiler_params=pltpu.CompilerParams(vmem_limit_bytes=32 * MIB),
    )(*parts, low, high, weights)


def weight_kernel(*refs, taps, tile, rows, size, nx, ng, layout, first):
    xs, gs, rest = refs[:nx], refs[nx : nx + ng], refs[nx + ng :]
    if first:
        out, xbuf, gbuf, acc, sems = rest
    else:
        before, out, xbuf, gbuf, acc, sems = rest
    half = taps // 2
    x_rows, g_rows, starts = layout()
    zeros = jnp.zeros((PAD, xbuf.shape[1]), xbuf.dtype)
    xbuf[pl.ds(0, PAD), :] = zeros
    xbuf[pl.ds(PAD + rows, PAD), :] = zeros
    pieces = [(src, xbuf, row) for src, row in zip(xs, x_rows)]
    pieces += [(src, gbuf, row) for src, row in zip(gs, g_rows)]

    def copy(at):
        src, dst, row = pieces[at]
        row = row if isinstance(row, int) else pl.multiple_of(row, 16)
        return pltpu.make_async_copy(src, dst.at[pl.ds(row, src.shape[0]), :], sems.at[at])

    def each(act):
        for at in range(nx + ng):
            row = pieces[at][2]
            if isinstance(row, int):
                act(at)
            else:
                pl.when(row >= 0)(functools.partial(act, at))

    each(lambda at: copy(at).start())
    acc[...] = jnp.zeros_like(acc) if first else before[...]
    each(lambda at: copy(at).wait())

    for begin in starts:

        def body(step, carry):
            start = begin + step * tile
            start = pl.multiple_of(start, 16)
            grad = gbuf[pl.ds(start, tile), :].T
            block = xbuf[pl.ds(start, tile + 2 * PAD), :].astype(jnp.float32)
            for tap in range(taps):
                at = PAD - half + tap
                moved = block[at : at + tile].astype(jnp.bfloat16)
                acc[tap] += jnp.dot(grad, moved, preferred_element_type=jnp.float32)
            return carry

        lax.fori_loop(0, size // tile, body, 0)
    out[...] = acc[...].astype(out.dtype)


def weight_gradient(xs, gs, layout, size, work, taps, rows, before=None, last=True):
    width, chunk = xs[0].shape[1], gs[0].shape[1]
    return pl.pallas_call(
        functools.partial(
            weight_kernel,
            taps=taps,
            tile=min(512, size),
            rows=rows,
            size=size,
            nx=len(xs),
            ng=len(gs),
            layout=layout,
            first=before is None,
        ),
        out_shape=jax.ShapeDtypeStruct(
            (taps, chunk, width), jnp.bfloat16 if last else jnp.float32
        ),
        in_specs=[SOME] * (len(xs) + len(gs)) + [VMEM] * (before is not None),
        out_specs=VMEM,
        scratch_shapes=[
            pltpu.VMEM((rows + 2 * PAD, width), jnp.bfloat16),
            pltpu.VMEM((rows, chunk), jnp.bfloat16),
            pltpu.VMEM((taps, chunk, width), jnp.float32),
            pltpu.SemaphoreType.DMA((len(xs) + len(gs),)),
        ],
        cost_estimate=pl.CostEstimate(
            flops=2 * work * chunk * width * taps,
            bytes_accessed=2 * work * (chunk + width),
            transcendentals=0,
        ),
        compiler_params=pltpu.CompilerParams(vmem_limit_bytes=40 * MIB),
    )(*xs, *gs, *([] if before is None else [before]))


def merge_pairs(value, scratch):
    size = value.shape[0] // 2
    sums = []
    for at in range(value.shape[1] // LANES):
        scratch[at] = value[:, at * LANES : (at + 1) * LANES]
        even = scratch[at, pl.ds(0, size, stride=2), :]
        sums.append(even + scratch[at, pl.ds(1, size, stride=2), :])
    return jnp.concatenate(sums, axis=1)


def make_pairs(value, scratch):
    size = value.shape[0]
    rows = []
    for at in range(value.shape[1] // LANES):
        part = value[:, at * LANES : (at + 1) * LANES]
        scratch[at, pl.ds(0, size, stride=2), :] = part
        scratch[at, pl.ds(1, size, stride=2), :] = part
        rows.append(scratch[at])
    return jnp.concatenate(rows, axis=1)


def pair_scratch(rows, width):
    return pltpu.VMEM((width // LANES, rows, LANES), jnp.float32)


def each_exon(owners, exons, seen, nblocks, most, act):
    mine = lax.axis_index("seq")
    span, count = exons.shape
    for i in range(seen.shape[0]):
        seen[i] = 0

    def body(t, carry):
        owner = owners[t]
        slot = (owner ^ mine) * most + seen[owner]
        seen[owner] += 1
        for e in range(span):
            where = exons[e, t]

            @pl.when(where // nblocks == mine)
            def _():
                act(slot, where % nblocks)

        return carry

    lax.fori_loop(0, count, body, 0)


def front_kernel(owners, exons, pre_act, *refs, nblocks, most, size):
    outs, (slots, pair, seen) = refs[:-3], refs[-3:]
    slots[...] = jnp.zeros_like(slots)

    def act(slot, block):
        at = pl.ds(pl.multiple_of(block * (2 * size), 2 * size), 2 * size)
        value = pre_act[at, :].astype(jnp.float32)
        value = value * (0.5 * (1.0 + lax.erf(value * HALF_ROOT)))
        mean = 0.5 * merge_pairs(value, pair)
        slots[pl.ds(pl.multiple_of(slot * size, size), size), :] = mean

    each_exon(owners, exons, seen, nblocks, most, act)
    group = most * size
    for d, out in enumerate(outs):
        out[...] = slots[pl.ds(d * group, group), :].astype(out.dtype)


def front(owners, exons, pre_act, most, size, groups):
    rows, width = pre_act.shape
    return pl.pallas_call(
        functools.partial(
            front_kernel, nblocks=rows // 2 // size, most=most, size=size
        ),
        out_shape=[jax.ShapeDtypeStruct((most * size, width), jnp.bfloat16)] * groups,
        in_specs=[SMEM] * 2 + [VMEM],
        out_specs=[VMEM] * groups,
        scratch_shapes=[
            pltpu.VMEM((groups * most * size, width), jnp.float32),
            pair_scratch(2 * size, width),
            pltpu.SMEM((groups,), jnp.int32),
        ],
        cost_estimate=pl.CostEstimate(flops=10**10, bytes_accessed=40 * MIB, transcendentals=0),
        compiler_params=pltpu.CompilerParams(vmem_limit_bytes=32 * MIB),
    )(owners, exons, pre_act)


def plain_kernel(pre_act, out_grad, slope, plain, both):
    value = pre_act[...].astype(jnp.float32)
    normal = 0.5 * (1.0 + lax.erf(value * HALF_ROOT))
    slope[...] = normal + value * (jnp.exp(-0.5 * value * value) * DENSITY)
    pooled = make_pairs(out_grad[...].astype(jnp.float32) * 0.5, both)
    plain[...] = (pooled * slope[...]).astype(plain.dtype)


def plain_gradient(pre_act, out_grad):
    rows, width = pre_act.shape
    return pl.pallas_call(
        plain_kernel,
        out_shape=[
            jax.ShapeDtypeStruct((rows, width), jnp.float32),
            jax.ShapeDtypeStruct((rows, width), jnp.bfloat16),
        ],
        in_specs=[VMEM] * 2,
        out_specs=[VMEM] * 2,
        scratch_shapes=[pair_scratch(rows, width)],
        compiler_params=pltpu.CompilerParams(vmem_limit_bytes=32 * MIB),
    )(pre_act, out_grad)


def gain_kernel(owners, exons, out_grad, slope, plain, *refs, nblocks, most, size):
    splices, (grad, gain, held, both, seen) = refs[:-5], refs[-5:]
    gain[...] = out_grad[...].astype(jnp.float32)
    grad[...] = plain[...]
    base = 0
    for splice in splices:
        held[pl.ds(base, splice.shape[0]), :] = splice[...].astype(jnp.float32)
        base += splice.shape[0]

    def add(slot, block):
        at = pl.ds(pl.multiple_of(block * size, size), size)
        gain[at, :] += held[pl.ds(pl.multiple_of(slot * size, size), size), :]

    def renew(slot, block):
        pooled = 0.5 * gain[pl.ds(pl.multiple_of(block * size, size), size), :]
        pooled = make_pairs(pooled, both)
        at = pl.ds(pl.multiple_of(block * (2 * size), 2 * size), 2 * size)
        grad[at, :] = (pooled * slope[at, :]).astype(grad.dtype)

    each_exon(owners, exons, seen, nblocks, most, add)
    each_exon(owners, exons, seen, nblocks, most, renew)


def gained_gradient(owners, exons, out_grad, slope, plain, splices, most, size, groups):
    rows, width = slope.shape
    return pl.pallas_call(
        functools.partial(
            gain_kernel, nblocks=rows // 2 // size, most=most, size=size
        ),
        out_shape=jax.ShapeDtypeStruct((rows, width), jnp.bfloat16),
        in_specs=[SMEM] * 2 + [VMEM] * (3 + len(splices)),
        out_specs=VMEM,
        scratch_shapes=[
            pltpu.VMEM((rows // 2, width), jnp.float32),
            pltpu.VMEM((groups * most * size, width), jnp.float32),
            pair_scratch(2 * size, width),
            pltpu.SMEM((groups,), jnp.int32),
        ],
        compiler_params=pltpu.CompilerParams(vmem_limit_bytes=32 * MIB),
    )(owners, exons, out_grad, slope, plain, *splices)


def gathered_gradient(pre_act, out_grad, coverage_obs, owners, exon_blocks):
    rows, width = pre_act.shape
    nseq = lax.axis_size("seq")
    mine = lax.axis_index("seq")
    most, block = coverage_obs.shape[1:3]
    nblocks = rows // 2 // block
    counts = owners.shape[0]
    value = pre_act.astype(jnp.float32)
    normal = 0.5 * (1.0 + jax.scipy.special.erf(value * HALF_ROOT))
    slope = normal + value * jnp.exp(-0.5 * value * value) * DENSITY
    act = value * normal
    pooled = (0.5 * jnp.sum(act.reshape(rows // 2, 2, width), axis=1)).astype(jnp.bfloat16)
    order = jnp.arange(counts, dtype=jnp.int32)
    same = owners[:, None] == owners[None, :]
    rank = jnp.sum((same & (order[:, None] < order[None, :])).astype(jnp.int32), axis=0)
    dest = jnp.arange(nseq, dtype=jnp.int32)
    slots = jnp.arange(most, dtype=jnp.int32)
    route = (owners[None, None, :] == dest[:, None, None]) & (
        rank[None, None, :] == slots[None, :, None]
    )
    route = route.astype(jnp.float32).reshape(nseq * most, counts)
    on_mine = exon_blocks // nblocks == mine
    holds = jnp.any(on_mine, axis=1)
    local_block = jnp.sum(jnp.where(on_mine, exon_blocks % nblocks, 0), axis=1)
    select = (
        holds[:, None] & (local_block[:, None] == jnp.arange(nblocks, dtype=jnp.int32)[None, :])
    ).astype(jnp.float32)
    picker = jnp.dot(route, select, precision=lax.Precision.HIGHEST).astype(jnp.bfloat16)
    pieces = pooled.reshape(nblocks, block * width)
    outgoing = jnp.dot(picker, pieces, preferred_element_type=jnp.float32).astype(jnp.bfloat16)
    outgoing = outgoing.reshape(nseq, most, block, width)
    arrived = lax.all_to_all(outgoing, "seq", split_axis=0, concat_axis=0, tiled=True)
    coverage = jnp.sum(arrived.astype(jnp.float32), axis=0)
    splice = jnp.tanh(coverage - coverage_obs[0]).astype(jnp.bfloat16)
    returned = lax.all_gather(splice, "seq", axis=0).reshape(nseq * most, block * width)
    gained = jnp.dot(picker.T, returned, preferred_element_type=jnp.float32)
    pooled_grad = out_grad.astype(jnp.float32) + gained.reshape(rows // 2, width)
    return (jnp.repeat(pooled_grad, 2, axis=0) * 0.5 * slope).astype(jnp.bfloat16)


def local(x_saved, pre_act, out_grad, conv_w, coverage_obs, owners, exon_blocks):
    rows, width = x_saved.shape
    taps = conv_w.shape[1]
    nseq = lax.axis_size("seq")
    nch = lax.axis_size("ch")
    chunk = conv_w.shape[0] // nseq
    most = coverage_obs.shape[1]
    size = coverage_obs.shape[2]
    direct = nseq == nch == 4 and chunk == width and width % 128 == 0
    exons = exon_blocks.T
    weights = conv_w.transpose(1, 0, 2)
    target = coverage_obs[0].reshape(most * size, width)

    if not direct:
        pre_grad = gathered_gradient(pre_act, out_grad, coverage_obs, owners, exon_blocks)
        x_all = lax.all_gather(x_saved, "seq", axis=0, tiled=True)
        whole = lax.all_gather(pre_grad, "ch", axis=1, tiled=True)
        blocks = whole.reshape(rows, nseq, chunk).transpose(1, 0, 2)
        g_all = lax.all_to_all(blocks, "seq", 0, 0, tiled=True).reshape(nseq * rows, chunk)
        low = shift(whole[rows - PAD :], "seq", 1)
        high = shift(whole[:PAD], "seq", -1)
        in_grad = input_gradient([whole], low, high, weights, lambda: [0])
        total = nseq * rows
        w_grad = weight_gradient(
            [x_all], [g_all], lambda: ([PAD], [0], [0]), total, total, taps, total
        )
        return (in_grad, w_grad.transpose(1, 0, 2))

    outgoing = front(owners, exons, pre_act, most, size, nseq)
    arrived = [outgoing[0]] + [swap(outgoing[d], "seq", d) for d in range(1, nseq)]
    coverage = functools.reduce(jnp.add, [a.astype(jnp.float32) for a in arrived])
    slope, plain = plain_gradient(pre_act, out_grad)
    splice = jnp.tanh(coverage - target).astype(jnp.bfloat16)
    splices = [splice] + [swap(splice, "seq", d) for d in range(1, nseq)]
    pre_grad = gained_gradient(owners, exons, out_grad, slope, plain, splices, most, size, nseq)

    mine = lax.axis_index("seq")
    place = lax.axis_index("ch")
    up1, down1 = shift(x_saved, "seq", 1), shift(x_saved, "seq", -1)
    pre_grad, up1, down1 = after([pre_grad, up1, down1])

    far = swap(pre_grad, "ch", 2)
    near = swap(pre_grad, "ch", 1)
    up2, down2 = shift(up1, "seq", 1, 1), shift(down1, "seq", -1, 1)
    far, near, up2, down2 = after([far, near, up2, down2])
    parts = [pre_grad, near, far, swap(far, "ch", 1)]

    quarter = rows // nch

    def chosen(flipped, options):
        want = mine ^ flipped ^ place
        picked = options[0]
        for t in range(1, nch):
            picked = jnp.where(want == t, options[t], picked)
        return picked

    slices = [lax.dynamic_slice_in_dim(p, place * quarter, quarter, axis=0) for p in parts]
    got = [swap(chosen(d, slices), "seq", d) for d in range(1, nseq)]
    low = shift(jnp.concatenate([p[rows - PAD :] for p in parts], axis=1), "seq", 1)
    high = shift(jnp.concatenate([p[:PAD] for p in parts], axis=1), "seq", -1)

    def origins():
        return [(lax.axis_index("ch") ^ t) * width for t in range(nch)]

    in_grad = input_gradient(parts, low, high, weights, origins)
    crossing = after([jnp.concatenate(got), up2, down2], [in_grad])
    crossing, up2, down2 = crossing

    across = swap(crossing, "ch", 2)
    up3, down3 = shift(up2, "seq", 1, 2), shift(down2, "seq", -1, 2)
    partial = weight_gradient(
        [up1[rows - PAD :], x_saved, down1[:PAD]],
        [chosen(0, parts)],
        lambda: ([0, PAD, PAD + rows], [0], [0]),
        rows,
        rows,
        taps,
        rows,
        last=False,
    )
    across, partial = after([across, partial])
    beside = swap(crossing, "ch", 1)
    beyond = swap(across, "ch", 1)

    def layout():
        mine = lax.axis_index("seq")
        place = lax.axis_index("ch")
        x_rows = [PAD + mine * rows]
        for hop in range(1, nseq):
            low_at, high_at = mine - hop, mine + hop
            x_rows += [
                jnp.where(low_at >= 0, PAD + low_at * rows, -1),
                jnp.where(high_at < nseq, PAD + high_at * rows, -1),
            ]
        g_rows = []
        for tag in range(nch):
            g_rows += [(mine ^ d) * rows + (place ^ tag) * quarter for d in range(1, nseq)]
        return x_rows, g_rows, [(mine ^ d) * rows for d in range(1, nseq)]

    g_pieces = []
    for piece in (crossing, beside, across, beyond):
        g_pieces += [piece[d * quarter : (d + 1) * quarter] for d in range(nseq - 1)]
    w_grad = weight_gradient(
        [x_saved, up1, down1, up2, down2, up3, down3],
        g_pieces,
        layout,
        rows,
        (nseq - 1) * rows,
        taps,
        nseq * rows,
        before=partial,
    )
    return (in_grad, w_grad.transpose(1, 0, 2))


def solution(mesh):
    in_specs = (
        P(("grp", "seq"), "ch"),
        P(("grp", "seq"), "ch"),
        P(("grp", "seq"), "ch"),
        P(None, None, "ch"),
        P(("grp", "seq"), None, None, "ch"),
        P("grp"),
        P("grp", None),
    )
    out_specs = (P(("grp", "seq"), "ch"), P(("grp", "seq"), None, "ch"))
    return jax.shard_map(local, mesh=mesh, in_specs=in_specs, out_specs=out_specs, check_vma=False)
```

time: 217 us -> 137 us (0.63)
  waiting for transfers between devices: 118 us -> 54.4 us
  matrix products: 33.7 us -> 0 us
  Pallas kernels: 0 us -> 32.4 us
  starting transfers between devices: 7.41 us -> 36.8 us
  blocking collectives: 23.6 us -> 0 us
  between operations: 14.3 us -> 1.2 us
  other arithmetic: 8.31 us -> 1.3 us
    reduce_scatter x1 -> x0, waiting for transfers between devices: 91.5 us -> none  [local(): lax.psum_scatter(jnp.stack(terms, axis=1).astype(jnp.bfloat16), 'seq', sc...]
    ppermute x4 -> x23, waiting for transfers between devices: 7.18 us -> 54.4 us  [the longest x8 29.3 us: shift(): return lax.ppermute(block, axis, pairs)]
    dot_general x13 -> x0, matrix products: 33.7 us -> none  [the longest x5 20.1 us: local(): jnp.dot(inner.T, x_rim[tap:tap + rows], preferred_element_type=jnp.float32)]
    pallas_call x0 -> x6, Pallas kernels: none -> 32.4 us  [the longest x2 16.1 us: weight_gradient(): pl.pallas_call(functools.partial(weight_kernel, taps=taps, tile=min(512,...]
    ppermute x4 -> x23, starting transfers between devices: 7.33 us -> 36.8 us  [the longest x8 18.5 us: shift(): return lax.ppermute(block, axis, pairs)]
    all_to_all x2 -> x0, blocking collectives: 23.6 us -> none  [the longest x1 13.7 us: local(): lax.all_to_all(outgoing, 'seq', split_axis=0, concat_axis=0, tiled=True)]
    all_gather x1 -> x0, waiting for transfers between devices: 19.5 us -> none  [local(): grad_rim = lax.all_gather(rimmed, 'ch', axis=1, tiled=True)]
    concatenate x2 -> x0, local copies, waits for them, and re-layouts: 6.68 us -> none  [with_halo(): block = jnp.concatenate([low, block, high], axis=dim)]
  transfers between devices with their start and end apart: 6 -> 23, of which waited for: 4 -> 10; matrix products, arithmetic and copies ran while one was open for 7% -> 3% of each run, Pallas kernels for 0% -> 14%
where the time goes in v2:
time: 137 us; the launch traced here: 136 us
  waiting for transfers between devices  54.4 us (40%)
  starting transfers between devices  36.8 us (27%)
  Pallas kernels  32.4 us (24%)
  local copies, waits for them, and re-layouts  9.97 us (7%)
    ppermute x8, waiting for transfers between devices, shift(): return lax.ppermute(block, axis, pairs)  29.3 us
    ppermute x15, waiting for transfers between devices, swap(): return lax.ppermute(block, axis, [(i, i ^ flip) for i in range(count)])  25.2 us
    ppermute x8, starting transfers between devices, shift(): return lax.ppermute(block, axis, pairs)  18.5 us
    ppermute x15, starting transfers between devices, swap(): return lax.ppermute(block, axis, [(i, i ^ flip) for i in range(count)])  18.3 us
    pallas_call x2, Pallas kernels, weight_gradient(): pl.pallas_call(functools.partial(weight_kernel, taps=taps, tile=min(512,...  16.1 us
    pallas_call x1, Pallas kernels, input_gradient(): pl.pallas_call(functools.partial(input_kernel, taps=taps, tile=min(256, r...  11.6 us
    unnamed x34, local copies, waits for them, and re-layouts  6.06 us
  transfers between devices with their start and end apart: 23, of which 10 were waited for; matrix products, arithmetic and copies ran while one was open for 3% of the time, Pallas kernels for 14%

profile of v2, /device:TPU:0, one launch (start us, length us, event | category | flops | bytes accessed | tf_op | source)
XLA Modules:
  0.0 136.1 jit_solution(15961129183840369206)
XLA Ops:
  0.6 1.3 collective-permute-start.7
  1.9 5.6 %collective-permute-start.6 = (bf16[1024,384]{1,0:T(8,128)(2,1)}, bf16[1024,384]{1,0:T(8,128)(2,1)S(1)}, u32[]{:S(2)}, u32[]{:S(2)}) collective-permute-start(bf16[1024,384]{1,0:T(8,128)(2,1)} %refs_0_.1), channel_id=1, source_target_pairs={{0,4},{4,8},{8,12},{1,5},{5,9},{9,13},{2,6},{6,10},{10,14},{3,7},{... | collective-permute-start | bytes 2359304 | tf_op jit(solution)/shard_map/ppermute | solution.py:31
  10.0 1.3 shard_map.87
  11.3 2.1 %collective-permute-start = (bf16[64,384]{1,0:T(8,128)(2,1)S(1)}, bf16[64,384]{1,0:T(8,128)(2,1)S(1)}, u32[]{:S(2)}, u32[]{:S(2)}) collective-permute-start(bf16[64,384]{1,0:T(8,128)(2,1)S(1)} %get-tuple-element.23), channel_id=1, source_target_pairs={{0,4},{4,0},{8,12},{12,8},{1,5},{5,1},{9,13},{13,9},{2,6},{6,2},{1... | collective-permute-start | bytes 147464 | tf_op jit(solution)/shard_map/ppermute | solution.py:22
  13.4 1.3 collective-permute-start.1
  14.7 1.4 %collective-permute-start.2 = (bf16[64,384]{1,0:T(8,128)(2,1)S(1)}, bf16[64,384]{1,0:T(8,128)(2,1)S(1)}, u32[]{:S(2)}, u32[]{:S(2)}) collective-permute-start(bf16[64,384]{1,0:T(8,128)(2,1)S(1)} %get-tuple-element.25), channel_id=1, source_target_pairs={{0,12},{4,8},{8,4},{12,0},{1,13},{5,9},{9,5},{13,1},{2,14},{6,10},... | collective-permute-start | bytes 147464 | tf_op jit(solution)/shard_map/ppermute | solution.py:22
  16.0 10.6 %collective-permute-done = bf16[64,384]{1,0:T(8,128)(2,1)S(1)} collective-permute-done((bf16[64,384]{1,0:T(8,128)(2,1)S(1)}, bf16[64,384]{1,0:T(8,128)(2,1)S(1)}, u32[]{:S(2)}, u32[]{:S(2)}) %collective-permute-start) | collective-permute-done | bytes 49184 | tf_op jit(solution)/shard_map/ppermute | solution.py:22
  27.1 1.6 %collective-permute-done.2 = bf16[64,384]{1,0:T(8,128)(2,1)S(1)} collective-permute-done((bf16[64,384]{1,0:T(8,128)(2,1)S(1)}, bf16[64,384]{1,0:T(8,128)(2,1)S(1)}, u32[]{:S(2)}, u32[]{:S(2)}) %collective-permute-start.2) | collective-permute-done | bytes 49184 | tf_op jit(solution)/shard_map/ppermute | solution.py:22
  28.7 4.1 %collective-permute-start.5 = (bf16[64,384]{1,0:T(8,128)(2,1)S(1)}, bf16[64,384]{1,0:T(8,128)(2,1)S(1)}, u32[]{:S(2)}, u32[]{:S(2)}) collective-permute-start(bf16[64,384]{1,0:T(8,128)(2,1)S(1)} %fusion.1.refs_0_), channel_id=1, source_target_pairs={{0,12},{4,8},{8,4},{12,0},{1,13},{5,9},{9,5},{13,1},{2,14},{6,10},... | collective-permute-start | bytes 147464 | tf_op jit(solution)/shard_map/ppermute | solution.py:22
  33.5 1.4 %shard_map.86 = (f32[1024,384]{1,0:T(8,128)S(1)}, bf16[1024,384]{1,0:T(8,128)(2,1)S(1)}) custom-call(bf16[1024,384]{1,0:T(8,128)(2,1)S(1)} %copy-done.1, bf16[512,384]{1,0:T(8,128)(2,1)S(1)} %copy-done), custom_call_target="tpu_custom_call" | custom-call | tf_op jit(solution)/shard_map/pallas_call | solution.py:275
  35.0 3.0 %collective-permute-done.4.refs_2_ = bf16[64,384]{1,0:T(8,128)(2,1)S(1)} collective-permute-done((bf16[64,384]{1,0:T(8,128)(2,1)S(1)}, bf16[64,384]{1,0:T(8,128)(2,1)S(1)}, u32[]{:S(2)}, u32[]{:S(2)}) %collective-permute-start.4) | collective-permute-done | bytes 49184 | tf_op jit(solution)/shard_map/ppermute | solution.py:22
  38.0 1.9 %shard_map.88.refs_0_ = bf16[1024,384]{1,0:T(8,128)(2,1)S(1)} custom-call(s32[16]{0:T(128)S(1)} %copy-done.5, s32[2,16]{1,0:T(2,128)S(1)} %bitcast.10, bf16[512,384]{1,0:T(8,128)(2,1)S(1)} %copy-done, f32[1024,384]{1,0:T(8,128)S(1)} %get-tuple-element.20.slope, bf16[1024,384]{1,0:T(8,128)(2,1)S(1)} %get-tuple-element.21.plain, ...), custom_call_target="tpu_custom_call" | custom-call | tf_op jit(solution)/shard_map/pallas_call | solution.py:313
  40.7 1.3 collective-permute-start.11
  42.1 1.6 %collective-permute-start.8 = (bf16[1024,384]{1,0:T(8,128)(2,1)S(1)}, bf16[1024,384]{1,0:T(8,128)(2,1)S(1)}, u32[]{:S(2)}, u32[]{:S(2)}) collective-permute-start(bf16[1024,384]{1,0:T(8,128)(2,1)S(1)} %shard_map.88.refs_0_), channel_id=1, source_target_pairs={{0,2},{1,3},{2,0},{3,1},{4,6},{5,7},{6,4},{7,5},{8,10},{9,11},{10,... | collective-permute-start | bytes 2359304 | tf_op jit(solution)/shard_map/ppermute | solution.py:22
  43.6 16.6 %collective-permute-done.11.refs_4_ = bf16[1024,384]{1,0:T(8,128)(2,1)S(1)} collective-permute-done((bf16[1024,384]{1,0:T(8,128)(2,1)S(1)}, bf16[1024,384]{1,0:T(8,128)(2,1)S(1)}, u32[]{:S(2)}, u32[]{:S(2)}) %collective-permute-start.11) | collective-permute-done | bytes 786464 | tf_op jit(solution)/shard_map/ppermute | solution.py:31
  60.3 1.8 %collective-permute-done.8.refs_2_ = bf16[1024,384]{1,0:T(8,128)(2,1)S(1)} collective-permute-done((bf16[1024,384]{1,0:T(8,128)(2,1)S(1)}, bf16[1024,384]{1,0:T(8,128)(2,1)S(1)}, u32[]{:S(2)}, u32[]{:S(2)}) %collective-permute-start.8) | collective-permute-done | bytes 786464 | tf_op jit(solution)/shard_map/ppermute | solution.py:22
  62.1 2.2 %collective-permute-done.12.refs_3_ = bf16[1024,384]{1,0:T(8,128)(2,1)S(1)} collective-permute-done((bf16[1024,384]{1,0:T(8,128)(2,1)S(1)}, bf16[1024,384]{1,0:T(8,128)(2,1)S(1)}, u32[]{:S(2)}, u32[]{:S(2)}) %collective-permute-start.12) | collective-permute-done | bytes 786464 | tf_op jit(solution)/shard_map/ppermute | solution.py:22
  64.3 6.3 %collective-permute-start.13 = (bf16[16,1536]{1,0:T(8,128)(2,1)S(1)}, bf16[16,1536]{1,0:T(8,128)(2,1)S(1)}, u32[]{:S(2)}, u32[]{:S(2)}) collective-permute-start(bf16[16,1536]{1,0:T(8,128)(2,1)S(1)} %pad_maximum_fusion.1), channel_id=1, source_target_pairs={{0,4},{4,8},{8,12},{1,5},{5,9},{9,13},{2,6},{6,10},{10,14},{3,7},{... | collective-permute-start | bytes 147464 | tf_op jit(solution)/shard_map/ppermute | solution.py:31
  70.7 1.3 collective-permute-start.14
  72.2 2.8 %collective-permute-start.15 = (bf16[256,384]{1,0:T(8,128)(2,1)S(1)}, bf16[256,384]{1,0:T(8,128)(2,1)S(1)}, u32[]{:S(2)}, u32[]{:S(2)}) collective-permute-start(bf16[256,384]{1,0:T(8,128)(2,1)S(1)} %get-tuple-element.38), channel_id=1, source_target_pairs={{0,4},{4,0},{8,12},{12,8},{1,5},{5,1},{9,13},{13,9},{2,6},{6,2},{1... | collective-permute-start | bytes 589832 | tf_op jit(solution)/shard_map/ppermute | solution.py:22
  75.0 1.5 %collective-permute-start.16 = (bf16[256,384]{1,0:T(8,128)(2,1)S(1)}, bf16[256,384]{1,0:T(8,128)(2,1)S(1)}, u32[]{:S(2)}, u32[]{:S(2)}) collective-permute-start(bf16[256,384]{1,0:T(8,128)(2,1)S(1)} %get-tuple-element.39), channel_id=1, source_target_pairs={{0,8},{4,12},{8,0},{12,4},{1,9},{5,13},{9,1},{13,5},{2,10},{6,14},... | collective-permute-start | bytes 589832 | tf_op jit(solution)/shard_map/ppermute | solution.py:22
  76.5 1.4 %collective-permute-start.17 = (bf16[256,384]{1,0:T(8,128)(2,1)S(1)}, bf16[256,384]{1,0:T(8,128)(2,1)S(1)}, u32[]{:S(2)}, u32[]{:S(2)}) collective-permute-start(bf16[256,384]{1,0:T(8,128)(2,1)S(1)} %get-tuple-element.40), channel_id=1, source_target_pairs={{0,12},{4,8},{8,4},{12,0},{1,13},{5,9},{9,5},{13,1},{2,14},{6,10},... | collective-permute-start | bytes 589832 | tf_op jit(solution)/shard_map/ppermute | solution.py:22
  77.9 2.7 %copy-done.10 = bf16[1536,5,384]{2,0,1:T(8,128)(2,1)S(1)} copy-done((bf16[1536,5,384]{2,0,1:T(8,128)(2,1)S(1)}, bf16[1536,5,384]{2,0,1:T(8,128)(2,1)}, u32[]{:S(2)}) %copy-start.10) | copy-done | bytes 5898264
  80.5 11.6 %shard_map.89 = bf16[1024,384]{1,0:T(8,128)(2,1)} custom-call(bf16[1024,384]{1,0:T(8,128)(2,1)S(1)} %shard_map.88.refs_0_, bf16[1024,384]{1,0:T(8,128)(2,1)S(1)} %collective-permute-done.9.refs_1_, bf16[1024,384]{1,0:T(8,128)(2,1)S(1)} %collective-permute-done.8.refs_2_, bf16[1024,384]{1,0:T(8,128)(2,1)S(1)} %collective-permute-done.12.refs_3_, ...), custom_call_target="tpu_custom_call" | custom-call | flops 6039797760 | bytes 9830400 | tf_op jit(solution)/shard_map/pallas_call | solution.py:79
  93.1 1.5 %collective-permute-start.21 = (bf16[768,384]{1,0:T(8,128)(2,1)}, bf16[768,384]{1,0:T(8,128)(2,1)}, u32[]{:S(2)}, u32[]{:S(2)}) collective-permute-start(bf16[768,384]{1,0:T(8,128)(2,1)} %pad_maximum_fusion), channel_id=1, source_target_pairs={{0,2},{1,3},{2,0},{3,1},{4,6},{5,7},{6,4},{7,5},{8,10},{9,11},{10,... | collective-permute-start | bytes 1769480 | tf_op jit(solution)/shard_map/ppermute | solution.py:22
  97.2 3.0 %shard_map.90.refs_19_ = f32[5,384,384]{2,1,0:T(8,128)S(1)} custom-call(bf16[16,384]{1,0:T(8,128)(2,1)S(1)} %slice.80.refs_0_, bf16[1024,384]{1,0:T(8,128)(2,1)S(1)} %copy-done.11, bf16[16,384]{1,0:T(8,128)(2,1)S(1)} %slice.81.refs_2_, bf16[1024,384]{1,0:T(8,128)(2,1)S(1)} %select_select_fusion.refs_3_), custom_call_target="tpu_custom_call" | custom-call | flops 1509949440 | bytes 1572864 | tf_op jit(solution)/shard_map/pallas_call | solution.py:150
  100.9 1.3 collective-permute-start.19
  102.2 5.5 %collective-permute-done.21 = bf16[768,384]{1,0:T(8,128)(2,1)} collective-permute-done((bf16[768,384]{1,0:T(8,128)(2,1)}, bf16[768,384]{1,0:T(8,128)(2,1)}, u32[]{:S(2)}, u32[]{:S(2)}) %collective-permute-start.21) | collective-permute-done | bytes 589856 | tf_op jit(solution)/shard_map/ppermute | solution.py:22
  107.7 1.2 fusion.9
  108.9 1.2 fusion.7
  110.2 12.6 %collective-permute-done.19.refs_6_ = bf16[1024,384]{1,0:T(8,128)(2,1)S(1)} collective-permute-done((bf16[1024,384]{1,0:T(8,128)(2,1)S(1)}, bf16[1024,384]{1,0:T(8,128)(2,1)S(1)}, u32[]{:S(2)}, u32[]{:S(2)}) %collective-permute-start.19) | collective-permute-done | bytes 786464 | tf_op jit(solution)/shard_map/ppermute | solution.py:31
  122.9 13.1 %shard_map.91 = bf16[5,384,384]{2,1,0:T(8,128)(2,1)} custom-call(bf16[1024,384]{1,0:T(8,128)(2,1)S(1)} %copy-done.11, bf16[1024,384]{1,0:T(8,128)(2,1)S(1)} %copy-done.9, bf16[1024,384]{1,0:T(8,128)(2,1)S(1)} %copy-done.7, bf16[1024,384]{1,0:T(8,128)(2,1)S(1)} %copy-done.13, bf16[1024,384]{1,0:T(8,128)(2,1)S(1)} %copy-done.15, ...), custom_call_target="tpu_custom_call" | custom-call | flops 4529848320 | bytes 4718592 | tf_op jit(solution)/shard_map/pallas_call | solution.py:150
  (69 shorter events, 9.1 us)
Async XLA Ops:
  0.6 39.3 %collective-permute-start.7 = (bf16[1024,384]{1,0:T(8,128)(2,1)}, bf16[1024,384]{1,0:T(8,128)(2,1)S(1)}, u32[]{:S(2)}, u32[]{:S(2)}) collective-permute-start(bf16[1024,384]{1,0:T(8,128)(2,1)} %refs_0_.1), channel_id=1, source_target_pairs={{4,0},{8,4},{12,8},{5,1},{9,5},{13,9},{6,2},{10,6},{14,10},{7,3},{... | collective-permute-start | bytes 2359304 | tf_op jit(solution)/shard_map/ppermute | solution.py:31
  1.9 38.0 %collective-permute-start.6 = (bf16[1024,384]{1,0:T(8,128)(2,1)}, bf16[1024,384]{1,0:T(8,128)(2,1)S(1)}, u32[]{:S(2)}, u32[]{:S(2)}) collective-permute-start(bf16[1024,384]{1,0:T(8,128)(2,1)} %refs_0_.1), channel_id=1, source_target_pairs={{0,4},{4,8},{8,12},{1,5},{5,9},{9,13},{2,6},{6,10},{10,14},{3,7},{... | collective-permute-start | bytes 2359304 | tf_op jit(solution)/shard_map/ppermute | solution.py:31
  10.0 18.7 %copy-start.16 = (f32[1,8,8,384]{3,2,1,0:T(8,128)S(1)}, f32[1,8,8,384]{3,2,1,0:T(8,128)}, u32[]{:S(2)}) copy-start(f32[1,8,8,384]{3,2,1,0:T(8,128)} %param.11) | copy-start | bytes 294916
  10.0 23.5 %copy-start = (bf16[512,384]{1,0:T(8,128)(2,1)S(1)}, bf16[512,384]{1,0:T(8,128)(2,1)}, u32[]{:S(2)}) copy-start(bf16[512,384]{1,0:T(8,128)(2,1)} %out_grad.3) | copy-start | bytes 1179652
  11.3 26.7 %copy-start.3 = (s32[16,2]{0,1:T(2,128)S(1)}, s32[16,2]{0,1:T(2,128)}, u32[]{:S(2)}) copy-start(s32[16,2]{0,1:T(2,128)} %param.13) | copy-start | bytes 388
  11.3 26.7 %copy-start.5 = (s32[16]{0:T(128)S(1)}, s32[16]{0:T(128)}, u32[]{:S(2)}) copy-start(s32[16]{0:T(128)} %owners.3) | copy-start | bytes 196
  11.3 15.3 %collective-permute-start = (bf16[64,384]{1,0:T(8,128)(2,1)S(1)}, bf16[64,384]{1,0:T(8,128)(2,1)S(1)}, u32[]{:S(2)}, u32[]{:S(2)}) collective-permute-start(bf16[64,384]{1,0:T(8,128)(2,1)S(1)} %get-tuple-element.23), channel_id=1, source_target_pairs={{0,4},{4,0},{8,12},{12,8},{1,5},{5,1},{9,13},{13,9},{2,6},{6,2},{1... | collective-permute-start | bytes 147464 | tf_op jit(solution)/shard_map/ppermute | solution.py:22
  13.4 13.7 %collective-permute-start.1 = (bf16[64,384]{1,0:T(8,128)(2,1)S(1)}, bf16[64,384]{1,0:T(8,128)(2,1)S(1)}, u32[]{:S(2)}, u32[]{:S(2)}) collective-permute-start(bf16[64,384]{1,0:T(8,128)(2,1)S(1)} %get-tuple-element.24), channel_id=1, source_target_pairs={{0,8},{4,12},{8,0},{12,4},{1,9},{5,13},{9,1},{13,5},{2,10},{6,14},... | collective-permute-start | bytes 147464 | tf_op jit(solution)/shard_map/ppermute | solution.py:22
  14.7 14.0 %collective-permute-start.2 = (bf16[64,384]{1,0:T(8,128)(2,1)S(1)}, bf16[64,384]{1,0:T(8,128)(2,1)S(1)}, u32[]{:S(2)}, u32[]{:S(2)}) collective-permute-start(bf16[64,384]{1,0:T(8,128)(2,1)S(1)} %get-tuple-element.25), channel_id=1, source_target_pairs={{0,12},{4,8},{8,4},{12,0},{1,13},{5,9},{9,5},{13,1},{2,14},{6,10},... | collective-permute-start | bytes 147464 | tf_op jit(solution)/shard_map/ppermute | solution.py:22
  28.7 6.3 %collective-permute-start.5 = (bf16[64,384]{1,0:T(8,128)(2,1)S(1)}, bf16[64,384]{1,0:T(8,128)(2,1)S(1)}, u32[]{:S(2)}, u32[]{:S(2)}) collective-permute-start(bf16[64,384]{1,0:T(8,128)(2,1)S(1)} %fusion.1.refs_0_), channel_id=1, source_target_pairs={{0,12},{4,8},{8,4},{12,0},{1,13},{5,9},{9,5},{13,1},{2,14},{6,10},... | collective-permute-start | bytes 147464 | tf_op jit(solution)/shard_map/ppermute | solution.py:22
  32.8 5.1 %collective-permute-start.4 = (bf16[64,384]{1,0:T(8,128)(2,1)S(1)}, bf16[64,384]{1,0:T(8,128)(2,1)S(1)}, u32[]{:S(2)}, u32[]{:S(2)}) collective-permute-start(bf16[64,384]{1,0:T(8,128)(2,1)S(1)} %fusion.1.refs_0_), channel_id=1, source_target_pairs={{0,8},{4,12},{8,0},{12,4},{1,9},{5,13},{9,1},{13,5},{2,10},{6,14},... | collective-permute-start | bytes 147464 | tf_op jit(solution)/shard_map/ppermute | solution.py:22
  32.9 5.1 %collective-permute-start.3 = (bf16[64,384]{1,0:T(8,128)(2,1)S(1)}, bf16[64,384]{1,0:T(8,128)(2,1)S(1)}, u32[]{:S(2)}, u32[]{:S(2)}) collective-permute-start(bf16[64,384]{1,0:T(8,128)(2,1)S(1)} %fusion.1.refs_0_), channel_id=1, source_target_pairs={{0,4},{4,0},{8,12},{12,8},{1,5},{5,1},{9,13},{13,9},{2,6},{6,2},{1... | collective-permute-start | bytes 147464 | tf_op jit(solution)/shard_map/ppermute | solution.py:22
  40.0 22.1 %copy-start.6 = (bf16[1024,384]{1,0:T(8,128)(2,1)}, bf16[1024,384]{1,0:T(8,128)(2,1)S(1)}, u32[]{:S(2)}) copy-start(bf16[1024,384]{1,0:T(8,128)(2,1)S(1)} %collective-permute-done.7.refs_2_) | copy-start | bytes 2359300
  40.0 22.1 %copy-start.8 = (bf16[1024,384]{1,0:T(8,128)(2,1)}, bf16[1024,384]{1,0:T(8,128)(2,1)S(1)}, u32[]{:S(2)}) copy-start(bf16[1024,384]{1,0:T(8,128)(2,1)S(1)} %collective-permute-done.6.refs_1_) | copy-start | bytes 2359300
  40.0 3.7 %collective-permute-start.10 = (bf16[1024,384]{1,0:T(8,128)(2,1)S(1)}, bf16[1024,384]{1,0:T(8,128)(2,1)S(1)}, u32[]{:S(2)}, u32[]{:S(2)}) collective-permute-start(bf16[1024,384]{1,0:T(8,128)(2,1)S(1)} %collective-permute-done.6.refs_1_), channel_id=1, source_target_pairs={{4,8},{8,12},{5,9},{9,13},{6,10},{10,14},{7,11},{11,15},{20,24},{2... | collective-permute-start | bytes 2359304 | tf_op jit(solution)/shard_map/ppermute | solution.py:31
  40.7 19.6 %collective-permute-start.11 = (bf16[1024,384]{1,0:T(8,128)(2,1)S(1)}, bf16[1024,384]{1,0:T(8,128)(2,1)S(1)}, u32[]{:S(2)}, u32[]{:S(2)}) collective-permute-start(bf16[1024,384]{1,0:T(8,128)(2,1)S(1)} %collective-permute-done.7.refs_2_), channel_id=1, source_target_pairs={{4,0},{8,4},{5,1},{9,5},{6,2},{10,6},{7,3},{11,7},{20,16},{24,20},... | collective-permute-start | bytes 2359304 | tf_op jit(solution)/shard_map/ppermute | solution.py:31
  42.0 18.3 %collective-permute-start.9 = (bf16[1024,384]{1,0:T(8,128)(2,1)S(1)}, bf16[1024,384]{1,0:T(8,128)(2,1)S(1)}, u32[]{:S(2)}, u32[]{:S(2)}) collective-permute-start(bf16[1024,384]{1,0:T(8,128)(2,1)S(1)} %shard_map.88.refs_0_), channel_id=1, source_target_pairs={{0,1},{1,0},{2,3},{3,2},{4,5},{5,4},{6,7},{7,6},{8,9},{9,8},{10,11... | collective-permute-start | bytes 2359304 | tf_op jit(solution)/shard_map/ppermute | solution.py:22
  42.1 20.0 %collective-permute-start.8 = (bf16[1024,384]{1,0:T(8,128)(2,1)S(1)}, bf16[1024,384]{1,0:T(8,128)(2,1)S(1)}, u32[]{:S(2)}, u32[]{:S(2)}) collective-permute-start(bf16[1024,384]{1,0:T(8,128)(2,1)S(1)} %shard_map.88.refs_0_), channel_id=1, source_target_pairs={{0,2},{1,3},{2,0},{3,1},{4,6},{5,7},{6,4},{7,5},{8,10},{9,11},{10,... | collective-permute-start | bytes 2359304 | tf_op jit(solution)/shard_map/ppermute | solution.py:22
  43.6 18.4 %copy-start.12 = (bf16[1024,384]{1,0:T(8,128)(2,1)}, bf16[1024,384]{1,0:T(8,128)(2,1)S(1)}, u32[]{:S(2)}) copy-start(bf16[1024,384]{1,0:T(8,128)(2,1)S(1)} %collective-permute-done.10.refs_3_) | copy-start | bytes 2359300
  62.0 2.3 %collective-permute-start.12 = (bf16[1024,384]{1,0:T(8,128)(2,1)S(1)}, bf16[1024,384]{1,0:T(8,128)(2,1)S(1)}, u32[]{:S(2)}, u32[]{:S(2)}) collective-permute-start(bf16[1024,384]{1,0:T(8,128)(2,1)S(1)} %collective-permute-done.8.refs_2_), channel_id=1, source_target_pairs={{0,1},{1,0},{2,3},{3,2},{4,5},{5,4},{6,7},{7,6},{8,9},{9,8},{10,11... | collective-permute-start | bytes 2359304 | tf_op jit(solution)/shard_map/ppermute | solution.py:22
  64.3 13.5 %collective-permute-start.13 = (bf16[16,1536]{1,0:T(8,128)(2,1)S(1)}, bf16[16,1536]{1,0:T(8,128)(2,1)S(1)}, u32[]{:S(2)}, u32[]{:S(2)}) collective-permute-start(bf16[16,1536]{1,0:T(8,128)(2,1)S(1)} %pad_maximum_fusion.1), channel_id=1, source_target_pairs={{0,4},{4,8},{8,12},{1,5},{5,9},{9,13},{2,6},{6,10},{10,14},{3,7},{... | collective-permute-start | bytes 147464 | tf_op jit(solution)/shard_map/ppermute | solution.py:31
  70.7 7.2 %collective-permute-start.14 = (bf16[16,1536]{1,0:T(8,128)(2,1)S(1)}, bf16[16,1536]{1,0:T(8,128)(2,1)S(1)}, u32[]{:S(2)}, u32[]{:S(2)}) collective-permute-start(bf16[16,1536]{1,0:T(8,128)(2,1)S(1)} %pad_maximum_fusion.2), channel_id=1, source_target_pairs={{4,0},{8,4},{12,8},{5,1},{9,5},{13,9},{6,2},{10,6},{14,10},{7,3},{... | collective-permute-start | bytes 147464 | tf_op jit(solution)/shard_map/ppermute | solution.py:31
  72.2 20.0 %collective-permute-start.15 = (bf16[256,384]{1,0:T(8,128)(2,1)S(1)}, bf16[256,384]{1,0:T(8,128)(2,1)S(1)}, u32[]{:S(2)}, u32[]{:S(2)}) collective-permute-start(bf16[256,384]{1,0:T(8,128)(2,1)S(1)} %get-tuple-element.38), channel_id=1, source_target_pairs={{0,4},{4,0},{8,12},{12,8},{1,5},{5,1},{9,13},{13,9},{2,6},{6,2},{1... | collective-permute-start | bytes 589832 | tf_op jit(solution)/shard_map/ppermute | solution.py:22
  75.0 17.3 %collective-permute-start.16 = (bf16[256,384]{1,0:T(8,128)(2,1)S(1)}, bf16[256,384]{1,0:T(8,128)(2,1)S(1)}, u32[]{:S(2)}, u32[]{:S(2)}) collective-permute-start(bf16[256,384]{1,0:T(8,128)(2,1)S(1)} %get-tuple-element.39), channel_id=1, source_target_pairs={{0,8},{4,12},{8,0},{12,4},{1,9},{5,13},{9,1},{13,5},{2,10},{6,14},... | collective-permute-start | bytes 589832 | tf_op jit(solution)/shard_map/ppermute | solution.py:22
  76.5 15.7 %collective-permute-start.17 = (bf16[256,384]{1,0:T(8,128)(2,1)S(1)}, bf16[256,384]{1,0:T(8,128)(2,1)S(1)}, u32[]{:S(2)}, u32[]{:S(2)}) collective-permute-start(bf16[256,384]{1,0:T(8,128)(2,1)S(1)} %get-tuple-element.40), channel_id=1, source_target_pairs={{0,12},{4,8},{8,4},{12,0},{1,13},{5,9},{9,5},{13,1},{2,14},{6,10},... | collective-permute-start | bytes 589832 | tf_op jit(solution)/shard_map/ppermute | solution.py:22
  93.1 14.6 %collective-permute-start.21 = (bf16[768,384]{1,0:T(8,128)(2,1)}, bf16[768,384]{1,0:T(8,128)(2,1)}, u32[]{:S(2)}, u32[]{:S(2)}) collective-permute-start(bf16[768,384]{1,0:T(8,128)(2,1)} %pad_maximum_fusion), channel_id=1, source_target_pairs={{0,2},{1,3},{2,0},{3,1},{4,6},{5,7},{6,4},{7,5},{8,10},{9,11},{10,... | collective-permute-start | bytes 1769480 | tf_op jit(solution)/shard_map/ppermute | solution.py:22
  96.2 13.9 %collective-permute-start.20 = (bf16[768,384]{1,0:T(8,128)(2,1)}, bf16[768,384]{1,0:T(8,128)(2,1)S(1)}, u32[]{:S(2)}, u32[]{:S(2)}) collective-permute-start(bf16[768,384]{1,0:T(8,128)(2,1)} %pad_maximum_fusion), channel_id=1, source_target_pairs={{0,1},{1,0},{2,3},{3,2},{4,5},{5,4},{6,7},{7,6},{8,9},{9,8},{10,11... | collective-permute-start | bytes 1769480 | tf_op jit(solution)/shard_map/ppermute | solution.py:22
  100.2 10.0 %collective-permute-start.18 = (bf16[1024,384]{1,0:T(8,128)(2,1)S(1)}, bf16[1024,384]{1,0:T(8,128)(2,1)S(1)}, u32[]{:S(2)}, u32[]{:S(2)}) collective-permute-start(bf16[1024,384]{1,0:T(8,128)(2,1)S(1)} %copy-done.13), channel_id=1, source_target_pairs={{8,12},{9,13},{10,14},{11,15},{24,28},{25,29},{26,30},{27,31}} | collective-permute-start | bytes 2359304 | tf_op jit(solution)/shard_map/ppermute | solution.py:31
  100.9 21.9 %collective-permute-start.19 = (bf16[1024,384]{1,0:T(8,128)(2,1)S(1)}, bf16[1024,384]{1,0:T(8,128)(2,1)S(1)}, u32[]{:S(2)}, u32[]{:S(2)}) collective-permute-start(bf16[1024,384]{1,0:T(8,128)(2,1)S(1)} %copy-done.15), channel_id=1, source_target_pairs={{4,0},{5,1},{6,2},{7,3},{20,16},{21,17},{22,18},{23,19}} | collective-permute-start | bytes 2359304 | tf_op jit(solution)/shard_map/ppermute | solution.py:31
  107.7 2.5 %collective-permute-start.22 = (bf16[768,384]{1,0:T(8,128)(2,1)}, bf16[768,384]{1,0:T(8,128)(2,1)S(1)}, u32[]{:S(2)}, u32[]{:S(2)}) collective-permute-start(bf16[768,384]{1,0:T(8,128)(2,1)} %collective-permute-done.21), channel_id=1, source_target_pairs={{0,1},{1,0},{2,3},{3,2},{4,5},{5,4},{6,7},{7,6},{8,9},{9,8},{10,11... | collective-permute-start | bytes 1769480 | tf_op jit(solution)/shard_map/ppermute | solution.py:22
  110.0 12.8 %copy-start.7 = (bf16[1024,384]{1,0:T(8,128)(2,1)S(1)}, bf16[1024,384]{1,0:T(8,128)(2,1)}, u32[]{:S(2)}) copy-start(bf16[1024,384]{1,0:T(8,128)(2,1)} %copy-done.6) | copy-start | bytes 2359300
  110.1 12.8 %copy-start.9 = (bf16[1024,384]{1,0:T(8,128)(2,1)S(1)}, bf16[1024,384]{1,0:T(8,128)(2,1)}, u32[]{:S(2)}) copy-start(bf16[1024,384]{1,0:T(8,128)(2,1)} %copy-done.8) | copy-start | bytes 2359300
  (8 other events, 16.8 us)

commit v3 on v2

--- a/solution.py
+++ b/solution.py
@@ -15,6 +15,7 @@
 HALF_ROOT = 0.7071067811865476
 DENSITY = 0.3989422804014327
 LANES = 128
+LITTLE = pl.CostEstimate(flops=1000, bytes_accessed=1000, transcendentals=0)
 
 
 def swap(block, axis, flip):
@@ -88,12 +89,8 @@
             pltpu.VMEM((taps, chans, width), jnp.bfloat16),
             pltpu.SemaphoreType.DMA((len(parts),)),
         ],
-        cost_estimate=pl.CostEstimate(
-            flops=2 * rows * chans * width * taps,
-            bytes_accessed=2 * (rows * chans + taps * chans * width + rows * width),
-            transcendentals=0,
-        ),
-        compiler_params=pltpu.CompilerParams(vmem_limit_bytes=32 * MIB),
+        cost_estimate=LITTLE,
+        compiler_params=pltpu.CompilerParams(vmem_limit_bytes=(20 if len(parts) > 1 else 32) * MIB),
     )(*parts, low, high, weights)
 
 
@@ -145,7 +142,7 @@
     out[...] = acc[...].astype(out.dtype)
 
 
-def weight_gradient(xs, gs, layout, size, work, taps, rows, before=None, last=True):
+def weight_gradient(xs, gs, layout, size, taps, rows, before=None, last=True, vmem=40):
     width, chunk = xs[0].shape[1], gs[0].shape[1]
     return pl.pallas_call(
         functools.partial(
@@ -170,12 +167,8 @@
             pltpu.VMEM((taps, chunk, width), jnp.float32),
             pltpu.SemaphoreType.DMA((len(xs) + len(gs),)),
         ],
-        cost_estimate=pl.CostEstimate(
-            flops=2 * work * chunk * width * taps,
-            bytes_accessed=2 * work * (chunk + width),
-            transcendentals=0,
-        ),
-        compiler_params=pltpu.CompilerParams(vmem_limit_bytes=40 * MIB),
+        cost_estimate=LITTLE,
+        compiler_params=pltpu.CompilerParams(vmem_limit_bytes=vmem * MIB),
     )(*xs, *gs, *([] if before is None else [before]))
 
 
@@ -257,8 +250,8 @@
             pair_scratch(2 * size, width),
             pltpu.SMEM((groups,), jnp.int32),
         ],
-        cost_estimate=pl.CostEstimate(flops=10**10, bytes_accessed=40 * MIB, transcendentals=0),
-        compiler_params=pltpu.CompilerParams(vmem_limit_bytes=32 * MIB),
+        cost_estimate=LITTLE,
+        compiler_params=pltpu.CompilerParams(vmem_limit_bytes=16 * MIB),
     )(owners, exons, pre_act)
 
 
@@ -281,7 +274,8 @@
         in_specs=[VMEM] * 2,
         out_specs=[VMEM] * 2,
         scratch_shapes=[pair_scratch(rows, width)],
-        compiler_params=pltpu.CompilerParams(vmem_limit_bytes=32 * MIB),
+        cost_estimate=LITTLE,
+        compiler_params=pltpu.CompilerParams(vmem_limit_bytes=16 * MIB),
     )(pre_act, out_grad)
 
 
@@ -323,7 +317,7 @@
             pair_scratch(2 * size, width),
             pltpu.SMEM((groups,), jnp.int32),
         ],
-        compiler_params=pltpu.CompilerParams(vmem_limit_bytes=32 * MIB),
+        compiler_params=pltpu.CompilerParams(vmem_limit_bytes=16 * MIB),
     )(owners, exons, out_grad, slope, plain, *splices)
 
 
@@ -391,30 +385,31 @@
         in_grad = input_gradient([whole], low, high, weights, lambda: [0])
         total = nseq * rows
         w_grad = weight_gradient(
-            [x_all], [g_all], lambda: ([PAD], [0], [0]), total, total, taps, total
+            [x_all], [g_all], lambda: ([PAD], [0], [0]), total, taps, total
         )
         return (in_grad, w_grad.transpose(1, 0, 2))
 
+    mine = lax.axis_index("seq")
+    place = lax.axis_index("ch")
     outgoing = front(owners, exons, pre_act, most, size, nseq)
+    slope, plain = plain_gradient(*after([pre_act, out_grad], outgoing))
+    (source,) = after([x_saved], [plain])
+    up1, down1 = shift(source, "seq", 1), shift(source, "seq", -1)
     arrived = [outgoing[0]] + [swap(outgoing[d], "seq", d) for d in range(1, nseq)]
     coverage = functools.reduce(jnp.add, [a.astype(jnp.float32) for a in arrived])
-    slope, plain = plain_gradient(pre_act, out_grad)
     splice = jnp.tanh(coverage - target).astype(jnp.bfloat16)
     splices = [splice] + [swap(splice, "seq", d) for d in range(1, nseq)]
     pre_grad = gained_gradient(owners, exons, out_grad, slope, plain, splices, most, size, nseq)
-
-    mine = lax.axis_index("seq")
-    place = lax.axis_index("ch")
-    up1, down1 = shift(x_saved, "seq", 1), shift(x_saved, "seq", -1)
     pre_grad, up1, down1 = after([pre_grad, up1, down1])
 
     far = swap(pre_grad, "ch", 2)
     near = swap(pre_grad, "ch", 1)
     up2, down2 = shift(up1, "seq", 1, 1), shift(down1, "seq", -1, 1)
     far, near, up2, down2 = after([far, near, up2, down2])
-    parts = [pre_grad, near, far, swap(far, "ch", 1)]
+    parts = after([pre_grad, near, far, swap(far, "ch", 1)])
 
     quarter = rows // nch
+    half = taps // 2
 
     def chosen(flipped, options):
         want = mine ^ flipped ^ place
@@ -424,31 +419,45 @@
         return picked
 
     slices = [lax.dynamic_slice_in_dim(p, place * quarter, quarter, axis=0) for p in parts]
-    got = [swap(chosen(d, slices), "seq", d) for d in range(1, nseq)]
-    low = shift(jnp.concatenate([p[rows - PAD :] for p in parts], axis=1), "seq", 1)
-    high = shift(jnp.concatenate([p[:PAD] for p in parts], axis=1), "seq", -1)
-
-    def origins():
-        return [(lax.axis_index("ch") ^ t) * width for t in range(nch)]
-
-    in_grad = input_gradient(parts, low, high, weights, origins)
-    crossing = after([jnp.concatenate(got), up2, down2], [in_grad])
-    crossing, up2, down2 = crossing
-
-    across = swap(crossing, "ch", 2)
+    heads = jnp.concatenate([p[:half] for p in parts])
+    tails = jnp.concatenate([p[rows - half :] for p in parts])
+    spare = jnp.zeros((-len(heads) % PAD, width), jnp.bfloat16)
+    sent = [chosen(d, slices) for d in range(1, nseq)]
+    for d in (1, 3):
+        edge = jnp.where((mine ^ d) > mine, tails, heads)
+        sent[d - 1] = jnp.concatenate([sent[d - 1], edge, spare])
+    *sent, up2, down2 = after([*sent, up2, down2])
+    got = [swap(block, "seq", d) for d, block in zip(range(1, nseq), sent)]
     up3, down3 = shift(up2, "seq", 1, 2), shift(down2, "seq", -1, 2)
+
     partial = weight_gradient(
         [up1[rows - PAD :], x_saved, down1[:PAD]],
         [chosen(0, parts)],
         lambda: ([0, PAD, PAD + rows], [0], [0]),
         rows,
-        rows,
         taps,
         rows,
         last=False,
+        vmem=20,
     )
-    across, partial = after([across, partial])
+    *got, partial = after([*got, partial])
+
+    crossing = jnp.concatenate([block[:quarter] for block in got])
+    across = swap(crossing, "ch", 2)
     beside = swap(crossing, "ch", 1)
+    edges = [got[d - 1][quarter : quarter + len(heads)] for d in (1, 3)]
+    edges = [jnp.concatenate(jnp.split(e, nch), axis=1) for e in edges]
+    nothing = jnp.zeros_like(edges[0])
+    low = jnp.where(mine % 2 == 1, edges[0], jnp.where(mine == 2, edges[1], nothing))
+    high = jnp.where(mine % 2 == 0, edges[0], jnp.where(mine == 1, edges[1], nothing))
+    low = jnp.pad(low, ((PAD - half, 0), (0, 0)))
+    high = jnp.pad(high, ((0, PAD - half), (0, 0)))
+
+    def origins():
+        return [(lax.axis_index("ch") ^ t) * width for t in range(nch)]
+
+    in_grad = input_gradient(parts, low, high, weights, origins)
+    across, in_grad, up3, down3 = after([across, in_grad, up3, down3])
     beyond = swap(across, "ch", 1)
 
     def layout():
@@ -474,10 +483,10 @@
         g_pieces,
         layout,
         rows,
-        (nseq - 1) * rows,
         taps,
         nseq * rows,
         before=partial,
+        vmem=24,
     )
     return (in_grad, w_grad.transpose(1, 0, 2))
 

time: 137 us -> 125 us (0.912)
  starting transfers between devices: 36.8 us -> 27.1 us
    ppermute x8 -> x6, waiting for transfers between devices: 29.3 us -> 5.69 us  [shift(): return lax.ppermute(block, axis, pairs)]
    ppermute x15, waiting for transfers between devices: 25.2 us -> 48.1 us  [swap(): return lax.ppermute(block, axis, [(i, i ^ flip) for i in range(count)])]
    ppermute x8 -> x6, starting transfers between devices: 18.5 us -> 10.9 us  [shift(): return lax.ppermute(block, axis, pairs)]
    slice x4 -> x3, local copies, waits for them, and re-layouts: 2.48 us -> 0.18 us  [local(): g_pieces += [piece[d * quarter:(d + 1) * quarter] for d in range(nseq - 1)]]
    ppermute x15, starting transfers between devices: 18.3 us -> 16.2 us  [swap(): return lax.ppermute(block, axis, [(i, i ^ flip) for i in range(count)])]
    unnamed x34 -> x36, local copies, waits for them, and re-layouts: 6.06 us -> 7.08 us
  transfers between devices with their start and end apart: 23 -> 21, of which waited for: 10 -> 11; matrix products, arithmetic and copies ran while one was open for 3% -> 2% of each run, Pallas kernels for 14% -> 13%
where the time goes in v3:
time: 125 us; the launch traced here: 124 us
  waiting for transfers between devices  53.8 us (43%)
  Pallas kernels  32.3 us (26%)
  starting transfers between devices  27.1 us (22%)
  local copies, waits for them, and re-layouts  8.92 us (7%)
    ppermute x15, waiting for transfers between devices, swap(): return lax.ppermute(block, axis, [(i, i ^ flip) for i in range(count)])  48.1 us
    ppermute x15, starting transfers between devices, swap(): return lax.ppermute(block, axis, [(i, i ^ flip) for i in range(count)])  16.2 us
    pallas_call x2, Pallas kernels, weight_gradient(): pl.pallas_call(functools.partial(weight_kernel, taps=taps, tile=min(512,...  16.1 us
    pallas_call x1, Pallas kernels, input_gradient(): pl.pallas_call(functools.partial(input_kernel, taps=taps, tile=min(256, r...  11.6 us
    ppermute x6, starting transfers between devices, shift(): return lax.ppermute(block, axis, pairs)  10.9 us
    unnamed x36, local copies, waits for them, and re-layouts  7.08 us
    ppermute x6, waiting for transfers between devices, shift(): return lax.ppermute(block, axis, pairs)  5.69 us
  transfers between devices with their start and end apart: 21, of which 11 were waited for; matrix products, arithmetic and copies ran while one was open for 2% of the time, Pallas kernels for 13%

profile of v3, /device:TPU:0, one launch (start us, length us, event | category | flops | bytes accessed | tf_op | source)
XLA Modules:
  0.0 124.0 jit_solution(15343792146462898127)
XLA Ops:
  0.7 1.1 copy-done.1
  3.1 1.2 shard_map.86
  4.3 1.0 copy-done.4
  5.3 1.4 %shard_map.87 = (f32[1024,384]{1,0:T(8,128)S(1)}, bf16[1024,384]{1,0:T(8,128)(2,1)S(1)}) custom-call(bf16[1024,384]{1,0:T(8,128)(2,1)S(1)} %copy-done.1, bf16[512,384]{1,0:T(8,128)(2,1)S(1)} %copy-done.4), custom_call_target="tpu_custom_call" | custom-call | flops 1000 | bytes 1000 | tf_op jit(solution)/shard_map/pallas_call | solution.py:268
  6.8 1.3 %collective-permute-start.7 = (bf16[1024,384]{1,0:T(8,128)(2,1)S(1)}, bf16[1024,384]{1,0:T(8,128)(2,1)S(1)}, u32[]{:S(2)}, u32[]{:S(2)}) collective-permute-start(bf16[1024,384]{1,0:T(8,128)(2,1)S(1)} %copy-done.2), channel_id=1, source_target_pairs={{4,0},{8,4},{12,8},{5,1},{9,5},{13,9},{6,2},{10,6},{14,10},{7,3},{... | collective-permute-start | bytes 2359304 | tf_op jit(solution)/shard_map/ppermute | solution.py:32
  8.1 5.6 %collective-permute-start.6 = (bf16[1024,384]{1,0:T(8,128)(2,1)S(1)}, bf16[1024,384]{1,0:T(8,128)(2,1)S(1)}, u32[]{:S(2)}, u32[]{:S(2)}) collective-permute-start(bf16[1024,384]{1,0:T(8,128)(2,1)S(1)} %copy-done.2), channel_id=1, source_target_pairs={{0,4},{4,8},{8,12},{1,5},{5,9},{9,13},{2,6},{6,10},{10,14},{3,7},{... | collective-permute-start | bytes 2359304 | tf_op jit(solution)/shard_map/ppermute | solution.py:32
  13.7 2.0 %collective-permute-start = (bf16[64,384]{1,0:T(8,128)(2,1)S(1)}, bf16[64,384]{1,0:T(8,128)(2,1)S(1)}, u32[]{:S(2)}, u32[]{:S(2)}) collective-permute-start(bf16[64,384]{1,0:T(8,128)(2,1)S(1)} %get-tuple-element.36), channel_id=1, source_target_pairs={{0,4},{4,0},{8,12},{12,8},{1,5},{5,1},{9,13},{13,9},{2,6},{6,2},{1... | collective-permute-start | bytes 147464 | tf_op jit(solution)/shard_map/ppermute | solution.py:23
  15.7 1.4 %collective-permute-start.1 = (bf16[64,384]{1,0:T(8,128)(2,1)S(1)}, bf16[64,384]{1,0:T(8,128)(2,1)S(1)}, u32[]{:S(2)}, u32[]{:S(2)}) collective-permute-start(bf16[64,384]{1,0:T(8,128)(2,1)S(1)} %get-tuple-element.37), channel_id=1, source_target_pairs={{0,8},{4,12},{8,0},{12,4},{1,9},{5,13},{9,1},{13,5},{2,10},{6,14},... | collective-permute-start | bytes 147464 | tf_op jit(solution)/shard_map/ppermute | solution.py:23
  17.2 1.4 %collective-permute-start.2 = (bf16[64,384]{1,0:T(8,128)(2,1)S(1)}, bf16[64,384]{1,0:T(8,128)(2,1)S(1)}, u32[]{:S(2)}, u32[]{:S(2)}) collective-permute-start(bf16[64,384]{1,0:T(8,128)(2,1)S(1)} %get-tuple-element.38), channel_id=1, source_target_pairs={{0,12},{4,8},{8,4},{12,0},{1,13},{5,9},{9,5},{13,1},{2,14},{6,10},... | collective-permute-start | bytes 147464 | tf_op jit(solution)/shard_map/ppermute | solution.py:23
  18.5 14.0 %collective-permute-done = bf16[64,384]{1,0:T(8,128)(2,1)S(1)} collective-permute-done((bf16[64,384]{1,0:T(8,128)(2,1)S(1)}, bf16[64,384]{1,0:T(8,128)(2,1)S(1)}, u32[]{:S(2)}, u32[]{:S(2)}) %collective-permute-start) | collective-permute-done | bytes 49184 | tf_op jit(solution)/shard_map/ppermute | solution.py:23
  33.1 1.8 %collective-permute-done.2 = bf16[64,384]{1,0:T(8,128)(2,1)S(1)} collective-permute-done((bf16[64,384]{1,0:T(8,128)(2,1)S(1)}, bf16[64,384]{1,0:T(8,128)(2,1)S(1)}, u32[]{:S(2)}, u32[]{:S(2)}) %collective-permute-start.2) | collective-permute-done | bytes 49184 | tf_op jit(solution)/shard_map/ppermute | solution.py:23
  34.9 4.0 %collective-permute-start.5 = (bf16[64,384]{1,0:T(8,128)(2,1)S(1)}, bf16[64,384]{1,0:T(8,128)(2,1)S(1)}, u32[]{:S(2)}, u32[]{:S(2)}) collective-permute-start(bf16[64,384]{1,0:T(8,128)(2,1)S(1)} %fusion.1.refs_0_), channel_id=1, source_target_pairs={{0,12},{4,8},{8,4},{12,0},{1,13},{5,9},{9,5},{13,1},{2,14},{6,10},... | collective-permute-start | bytes 147464 | tf_op jit(solution)/shard_map/ppermute | solution.py:23
  39.6 1.4 %collective-permute-done.5.refs_3_ = bf16[64,384]{1,0:T(8,128)(2,1)S(1)} collective-permute-done((bf16[64,384]{1,0:T(8,128)(2,1)S(1)}, bf16[64,384]{1,0:T(8,128)(2,1)S(1)}, u32[]{:S(2)}, u32[]{:S(2)}) %collective-permute-start.5) | collective-permute-done | bytes 49184 | tf_op jit(solution)/shard_map/ppermute | solution.py:23
  41.0 3.1 %collective-permute-done.4.refs_2_ = bf16[64,384]{1,0:T(8,128)(2,1)S(1)} collective-permute-done((bf16[64,384]{1,0:T(8,128)(2,1)S(1)}, bf16[64,384]{1,0:T(8,128)(2,1)S(1)}, u32[]{:S(2)}, u32[]{:S(2)}) %collective-permute-start.4) | collective-permute-done | bytes 49184 | tf_op jit(solution)/shard_map/ppermute | solution.py:23
  44.1 1.9 %shard_map.88.refs_0_ = bf16[1024,384]{1,0:T(8,128)(2,1)S(1)} custom-call(s32[16]{0:T(128)S(1)} %copy-done.16, s32[2,16]{1,0:T(2,128)S(1)} %bitcast.11, bf16[512,384]{1,0:T(8,128)(2,1)S(1)} %copy-done.4, f32[1024,384]{1,0:T(8,128)S(1)} %get-tuple-element.41.slope, bf16[1024,384]{1,0:T(8,128)(2,1)S(1)} %get-tuple-element.42.plain, ...), custom_call_target="tpu_custom_call" | custom-call | tf_op jit(solution)/shard_map/pallas_call | solution.py:307
  46.1 1.6 %collective-permute-start.8 = (bf16[1024,384]{1,0:T(8,128)(2,1)S(1)}, bf16[1024,384]{1,0:T(8,128)(2,1)S(1)}, u32[]{:S(2)}, u32[]{:S(2)}) collective-permute-start(bf16[1024,384]{1,0:T(8,128)(2,1)S(1)} %shard_map.88.refs_0_), channel_id=1, source_target_pairs={{0,2},{1,3},{2,0},{3,1},{4,6},{5,7},{6,4},{7,5},{8,10},{9,11},{10,... | collective-permute-start | bytes 2359304 | tf_op jit(solution)/shard_map/ppermute | solution.py:23
  48.3 1.3 %collective-permute-start.11 = (bf16[1024,384]{1,0:T(8,128)(2,1)S(1)}, bf16[1024,384]{1,0:T(8,128)(2,1)S(1)}, u32[]{:S(2)}, u32[]{:S(2)}) collective-permute-start(bf16[1024,384]{1,0:T(8,128)(2,1)S(1)} %collective-permute-done.7.refs_2_), channel_id=1, source_target_pairs={{4,0},{8,4},{5,1},{9,5},{6,2},{10,6},{7,3},{11,7},{20,16},{24,20},... | collective-permute-start | bytes 2359304 | tf_op jit(solution)/shard_map/ppermute | solution.py:32
  49.7 16.4 %collective-permute-done.8.refs_2_ = bf16[1024,384]{1,0:T(8,128)(2,1)S(1)} collective-permute-done((bf16[1024,384]{1,0:T(8,128)(2,1)S(1)}, bf16[1024,384]{1,0:T(8,128)(2,1)S(1)}, u32[]{:S(2)}, u32[]{:S(2)}) %collective-permute-start.8) | collective-permute-done | bytes 786464 | tf_op jit(solution)/shard_map/ppermute | solution.py:23
  66.1 5.7 %collective-permute-done.11.refs_4_ = bf16[1024,384]{1,0:T(8,128)(2,1)S(1)} collective-permute-done((bf16[1024,384]{1,0:T(8,128)(2,1)S(1)}, bf16[1024,384]{1,0:T(8,128)(2,1)S(1)}, u32[]{:S(2)}, u32[]{:S(2)}) %collective-permute-start.11) | collective-permute-done | bytes 786464 | tf_op jit(solution)/shard_map/ppermute | solution.py:32
  71.7 0.9 copy-done.11
  72.7 0.8 slice.81.refs_0_
  74.6 0.8 collective-permute-start.14
  75.4 1.1 collective-permute-start.13
  76.5 2.6 %collective-permute-start.15 = (bf16[272,384]{1,0:T(8,128)(2,1)S(1)}, bf16[272,384]{1,0:T(8,128)(2,1)S(1)}, u32[]{:S(2)}, u32[]{:S(2)}) collective-permute-start(bf16[272,384]{1,0:T(8,128)(2,1)S(1)} %get-tuple-element.57), channel_id=1, source_target_pairs={{0,12},{4,8},{8,4},{12,0},{1,13},{5,9},{9,5},{13,1},{2,14},{6,10},... | collective-permute-start | bytes 626696 | tf_op jit(solution)/shard_map/ppermute | solution.py:23
  80.0 1.3 %collective-permute-start.18 = (bf16[1024,384]{1,0:T(8,128)(2,1)S(1)}, bf16[1024,384]{1,0:T(8,128)(2,1)S(1)}, u32[]{:S(2)}, u32[]{:S(2)}) collective-permute-start(bf16[1024,384]{1,0:T(8,128)(2,1)S(1)} %copy-done.12), channel_id=1, source_target_pairs={{4,0},{5,1},{6,2},{7,3},{20,16},{21,17},{22,18},{23,19}} | collective-permute-start | bytes 2359304 | tf_op jit(solution)/shard_map/ppermute | solution.py:32
  81.3 3.0 %shard_map.89.refs_19_ = f32[5,384,384]{2,1,0:T(8,128)S(1)} custom-call(bf16[16,384]{1,0:T(8,128)(2,1)S(1)} %slice.81.refs_0_, bf16[1024,384]{1,0:T(8,128)(2,1)S(1)} %copy-done.3, bf16[16,384]{1,0:T(8,128)(2,1)S(1)} %slice.82.refs_2_, bf16[1024,384]{1,0:T(8,128)(2,1)S(1)} %select_select_fusion.refs_3_), custom_call_target="tpu_custom_call" | custom-call | flops 1000 | bytes 1000 | tf_op jit(solution)/shard_map/pallas_call | solution.py:147
  84.3 3.9 %collective-permute-done.14.refs_8_ = bf16[256,384]{1,0:T(8,128)(2,1)S(1)} collective-permute-done((bf16[256,384]{1,0:T(8,128)(2,1)S(1)}, bf16[256,384]{1,0:T(8,128)(2,1)S(1)}, u32[]{:S(2)}, u32[]{:S(2)}) %collective-permute-start.14) | collective-permute-done | bytes 196640 | tf_op jit(solution)/shard_map/ppermute | solution.py:23
  88.2 4.5 %collective-permute-done.15 = bf16[272,384]{1,0:T(8,128)(2,1)S(1)} collective-permute-done((bf16[272,384]{1,0:T(8,128)(2,1)S(1)}, bf16[272,384]{1,0:T(8,128)(2,1)S(1)}, u32[]{:S(2)}, u32[]{:S(2)}) %collective-permute-start.15) | collective-permute-done | bytes 208928 | tf_op jit(solution)/shard_map/ppermute | solution.py:23
  93.6 2.7 %copy-done = bf16[1536,5,384]{2,0,1:T(8,128)(2,1)S(1)} copy-done((bf16[1536,5,384]{2,0,1:T(8,128)(2,1)S(1)}, bf16[1536,5,384]{2,0,1:T(8,128)(2,1)}, u32[]{:S(2)}) %copy-start) | copy-done | bytes 5898264
  96.3 11.6 %shard_map.90 = bf16[1024,384]{1,0:T(8,128)(2,1)} custom-call(bf16[1024,384]{1,0:T(8,128)(2,1)S(1)} %shard_map.88.refs_0_, bf16[1024,384]{1,0:T(8,128)(2,1)S(1)} %collective-permute-done.9.refs_1_, bf16[1024,384]{1,0:T(8,128)(2,1)S(1)} %collective-permute-done.8.refs_2_, bf16[1024,384]{1,0:T(8,128)(2,1)S(1)} %collective-permute-done.12.refs_3_, ...), custom_call_target="tpu_custom_call" | custom-call | flops 1000 | bytes 1000 | tf_op jit(solution)/shard_map/pallas_call | solution.py:80
  108.8 1.8 %collective-permute-done.20 = bf16[768,384]{1,0:T(8,128)(2,1)S(1)} collective-permute-done((bf16[768,384]{1,0:T(8,128)(2,1)S(1)}, bf16[768,384]{1,0:T(8,128)(2,1)S(1)}, u32[]{:S(2)}, u32[]{:S(2)}) %collective-permute-start.20) | collective-permute-done | bytes 589856 | tf_op jit(solution)/shard_map/ppermute | solution.py:23
  110.8 13.1 %shard_map.91 = bf16[5,384,384]{2,1,0:T(8,128)(2,1)} custom-call(bf16[1024,384]{1,0:T(8,128)(2,1)S(1)} %copy-done.3, bf16[1024,384]{1,0:T(8,128)(2,1)S(1)} %copy-done.8, bf16[1024,384]{1,0:T(8,128)(2,1)S(1)} %copy-done.6, bf16[1024,384]{1,0:T(8,128)(2,1)S(1)} %copy-done.10, bf16[1024,384]{1,0:T(8,128)(2,1)S(1)} %copy-done.12, ...), custom_call_target="tpu_custom_call" | custom-call | flops 1000 | bytes 1000 | tf_op jit(solution)/shard_map/pallas_call | solution.py:147
  (75 shorter events, 7.2 us)
Async XLA Ops:
  0.6 43.4 %copy-start.16 = (s32[16]{0:T(128)S(1)}, s32[16]{0:T(128)}, u32[]{:S(2)}) copy-start(s32[16]{0:T(128)} %owners.3) | copy-start | bytes 196
  0.6 43.4 %copy-start.14 = (s32[16,2]{0,1:T(2,128)S(1)}, s32[16,2]{0,1:T(2,128)}, u32[]{:S(2)}) copy-start(s32[16,2]{0,1:T(2,128)} %param.13) | copy-start | bytes 388
  3.1 3.6 %copy-start.2 = (bf16[1024,384]{1,0:T(8,128)(2,1)S(1)}, bf16[1024,384]{1,0:T(8,128)(2,1)}, u32[]{:S(2)}) copy-start(bf16[1024,384]{1,0:T(8,128)(2,1)} %refs_0_.1) | copy-start | bytes 2359300
  5.3 29.5 %copy-start.17 = (f32[1,8,8,384]{3,2,1,0:T(8,128)S(1)}, f32[1,8,8,384]{3,2,1,0:T(8,128)}, u32[]{:S(2)}) copy-start(f32[1,8,8,384]{3,2,1,0:T(8,128)} %param.11) | copy-start | bytes 294916
  6.8 39.2 %collective-permute-start.7 = (bf16[1024,384]{1,0:T(8,128)(2,1)S(1)}, bf16[1024,384]{1,0:T(8,128)(2,1)S(1)}, u32[]{:S(2)}, u32[]{:S(2)}) collective-permute-start(bf16[1024,384]{1,0:T(8,128)(2,1)S(1)} %copy-done.2), channel_id=1, source_target_pairs={{4,0},{8,4},{12,8},{5,1},{9,5},{13,9},{6,2},{10,6},{14,10},{7,3},{... | collective-permute-start | bytes 2359304 | tf_op jit(solution)/shard_map/ppermute | solution.py:32
  8.1 37.9 %collective-permute-start.6 = (bf16[1024,384]{1,0:T(8,128)(2,1)S(1)}, bf16[1024,384]{1,0:T(8,128)(2,1)S(1)}, u32[]{:S(2)}, u32[]{:S(2)}) collective-permute-start(bf16[1024,384]{1,0:T(8,128)(2,1)S(1)} %copy-done.2), channel_id=1, source_target_pairs={{0,4},{4,8},{8,12},{1,5},{5,9},{9,13},{2,6},{6,10},{10,14},{3,7},{... | collective-permute-start | bytes 2359304 | tf_op jit(solution)/shard_map/ppermute | solution.py:32
  13.7 18.8 %collective-permute-start = (bf16[64,384]{1,0:T(8,128)(2,1)S(1)}, bf16[64,384]{1,0:T(8,128)(2,1)S(1)}, u32[]{:S(2)}, u32[]{:S(2)}) collective-permute-start(bf16[64,384]{1,0:T(8,128)(2,1)S(1)} %get-tuple-element.36), channel_id=1, source_target_pairs={{0,4},{4,0},{8,12},{12,8},{1,5},{5,1},{9,13},{13,9},{2,6},{6,2},{1... | collective-permute-start | bytes 147464 | tf_op jit(solution)/shard_map/ppermute | solution.py:23
  15.7 17.3 %collective-permute-start.1 = (bf16[64,384]{1,0:T(8,128)(2,1)S(1)}, bf16[64,384]{1,0:T(8,128)(2,1)S(1)}, u32[]{:S(2)}, u32[]{:S(2)}) collective-permute-start(bf16[64,384]{1,0:T(8,128)(2,1)S(1)} %get-tuple-element.37), channel_id=1, source_target_pairs={{0,8},{4,12},{8,0},{12,4},{1,9},{5,13},{9,1},{13,5},{2,10},{6,14},... | collective-permute-start | bytes 147464 | tf_op jit(solution)/shard_map/ppermute | solution.py:23
  17.2 17.7 %collective-permute-start.2 = (bf16[64,384]{1,0:T(8,128)(2,1)S(1)}, bf16[64,384]{1,0:T(8,128)(2,1)S(1)}, u32[]{:S(2)}, u32[]{:S(2)}) collective-permute-start(bf16[64,384]{1,0:T(8,128)(2,1)S(1)} %get-tuple-element.38), channel_id=1, source_target_pairs={{0,12},{4,8},{8,4},{12,0},{1,13},{5,9},{9,5},{13,1},{2,14},{6,10},... | collective-permute-start | bytes 147464 | tf_op jit(solution)/shard_map/ppermute | solution.py:23
  34.9 6.1 %collective-permute-start.5 = (bf16[64,384]{1,0:T(8,128)(2,1)S(1)}, bf16[64,384]{1,0:T(8,128)(2,1)S(1)}, u32[]{:S(2)}, u32[]{:S(2)}) collective-permute-start(bf16[64,384]{1,0:T(8,128)(2,1)S(1)} %fusion.1.refs_0_), channel_id=1, source_target_pairs={{0,12},{4,8},{8,4},{12,0},{1,13},{5,9},{9,5},{13,1},{2,14},{6,10},... | collective-permute-start | bytes 147464 | tf_op jit(solution)/shard_map/ppermute | solution.py:23
  38.9 5.1 %collective-permute-start.4 = (bf16[64,384]{1,0:T(8,128)(2,1)S(1)}, bf16[64,384]{1,0:T(8,128)(2,1)S(1)}, u32[]{:S(2)}, u32[]{:S(2)}) collective-permute-start(bf16[64,384]{1,0:T(8,128)(2,1)S(1)} %fusion.1.refs_0_), channel_id=1, source_target_pairs={{0,8},{4,12},{8,0},{12,4},{1,9},{5,13},{9,1},{13,5},{2,10},{6,14},... | collective-permute-start | bytes 147464 | tf_op jit(solution)/shard_map/ppermute | solution.py:23
  38.9 5.1 %collective-permute-start.3 = (bf16[64,384]{1,0:T(8,128)(2,1)S(1)}, bf16[64,384]{1,0:T(8,128)(2,1)S(1)}, u32[]{:S(2)}, u32[]{:S(2)}) collective-permute-start(bf16[64,384]{1,0:T(8,128)(2,1)S(1)} %fusion.1.refs_0_), channel_id=1, source_target_pairs={{0,4},{4,0},{8,12},{12,8},{1,5},{5,1},{9,13},{13,9},{2,6},{6,2},{1... | collective-permute-start | bytes 147464 | tf_op jit(solution)/shard_map/ppermute | solution.py:23
  46.0 20.1 %copy-start.5 = (bf16[1024,384]{1,0:T(8,128)(2,1)}, bf16[1024,384]{1,0:T(8,128)(2,1)S(1)}, u32[]{:S(2)}) copy-start(bf16[1024,384]{1,0:T(8,128)(2,1)S(1)} %collective-permute-done.7.refs_2_) | copy-start | bytes 2359300
  46.0 25.7 %copy-start.7 = (bf16[1024,384]{1,0:T(8,128)(2,1)}, bf16[1024,384]{1,0:T(8,128)(2,1)S(1)}, u32[]{:S(2)}) copy-start(bf16[1024,384]{1,0:T(8,128)(2,1)S(1)} %collective-permute-done.6.refs_1_) | copy-start | bytes 2359300
  46.0 3.6 %collective-permute-start.9 = (bf16[1024,384]{1,0:T(8,128)(2,1)S(1)}, bf16[1024,384]{1,0:T(8,128)(2,1)S(1)}, u32[]{:S(2)}, u32[]{:S(2)}) collective-permute-start(bf16[1024,384]{1,0:T(8,128)(2,1)S(1)} %shard_map.88.refs_0_), channel_id=1, source_target_pairs={{0,1},{1,0},{2,3},{3,2},{4,5},{5,4},{6,7},{7,6},{8,9},{9,8},{10,11... | collective-permute-start | bytes 2359304 | tf_op jit(solution)/shard_map/ppermute | solution.py:23
  46.1 20.0 %collective-permute-start.8 = (bf16[1024,384]{1,0:T(8,128)(2,1)S(1)}, bf16[1024,384]{1,0:T(8,128)(2,1)S(1)}, u32[]{:S(2)}, u32[]{:S(2)}) collective-permute-start(bf16[1024,384]{1,0:T(8,128)(2,1)S(1)} %shard_map.88.refs_0_), channel_id=1, source_target_pairs={{0,2},{1,3},{2,0},{3,1},{4,6},{5,7},{6,4},{7,5},{8,10},{9,11},{10,... | collective-permute-start | bytes 2359304 | tf_op jit(solution)/shard_map/ppermute | solution.py:23
  47.6 18.4 %collective-permute-start.10 = (bf16[1024,384]{1,0:T(8,128)(2,1)S(1)}, bf16[1024,384]{1,0:T(8,128)(2,1)S(1)}, u32[]{:S(2)}, u32[]{:S(2)}) collective-permute-start(bf16[1024,384]{1,0:T(8,128)(2,1)S(1)} %collective-permute-done.6.refs_1_), channel_id=1, source_target_pairs={{4,8},{8,12},{5,9},{9,13},{6,10},{10,14},{7,11},{11,15},{20,24},{2... | collective-permute-start | bytes 2359304 | tf_op jit(solution)/shard_map/ppermute | solution.py:32
  48.3 23.4 %collective-permute-start.11 = (bf16[1024,384]{1,0:T(8,128)(2,1)S(1)}, bf16[1024,384]{1,0:T(8,128)(2,1)S(1)}, u32[]{:S(2)}, u32[]{:S(2)}) collective-permute-start(bf16[1024,384]{1,0:T(8,128)(2,1)S(1)} %collective-permute-done.7.refs_2_), channel_id=1, source_target_pairs={{4,0},{8,4},{5,1},{9,5},{6,2},{10,6},{7,3},{11,7},{20,16},{24,20},... | collective-permute-start | bytes 2359304 | tf_op jit(solution)/shard_map/ppermute | solution.py:32
  66.0 5.7 %copy-start.9 = (bf16[1024,384]{1,0:T(8,128)(2,1)}, bf16[1024,384]{1,0:T(8,128)(2,1)S(1)}, u32[]{:S(2)}) copy-start(bf16[1024,384]{1,0:T(8,128)(2,1)S(1)} %collective-permute-done.10.refs_3_) | copy-start | bytes 2359300
  71.7 2.5 %collective-permute-start.12 = (bf16[1024,384]{1,0:T(8,128)(2,1)S(1)}, bf16[1024,384]{1,0:T(8,128)(2,1)S(1)}, u32[]{:S(2)}, u32[]{:S(2)}) collective-permute-start(bf16[1024,384]{1,0:T(8,128)(2,1)S(1)} %collective-permute-done.8.refs_2_), channel_id=1, source_target_pairs={{0,1},{1,0},{2,3},{3,2},{4,5},{5,4},{6,7},{7,6},{8,9},{9,8},{10,11... | collective-permute-start | bytes 2359304 | tf_op jit(solution)/shard_map/ppermute | solution.py:23
  72.6 6.5 %copy-start.10 = (bf16[1024,384]{1,0:T(8,128)(2,1)S(1)}, bf16[1024,384]{1,0:T(8,128)(2,1)}, u32[]{:S(2)}) copy-start(bf16[1024,384]{1,0:T(8,128)(2,1)} %copy-done.9) | copy-start | bytes 2359300
  74.6 5.4 %copy-start.12 = (bf16[1024,384]{1,0:T(8,128)(2,1)S(1)}, bf16[1024,384]{1,0:T(8,128)(2,1)}, u32[]{:S(2)}) copy-start(bf16[1024,384]{1,0:T(8,128)(2,1)} %copy-done.11) | copy-start | bytes 2359300
  74.6 6.7 %copy-start.3 = (bf16[1024,384]{1,0:T(8,128)(2,1)S(1)}, bf16[1024,384]{1,0:T(8,128)(2,1)}, u32[]{:S(2)}) copy-start(bf16[1024,384]{1,0:T(8,128)(2,1)} %refs_0_.1) | copy-start | bytes 2359300
  74.6 13.5 %collective-permute-start.14 = (bf16[256,384]{1,0:T(8,128)(2,1)S(1)}, bf16[256,384]{1,0:T(8,128)(2,1)S(1)}, u32[]{:S(2)}, u32[]{:S(2)}) collective-permute-start(bf16[256,384]{1,0:T(8,128)(2,1)S(1)} %get-tuple-element.56), channel_id=1, source_target_pairs={{0,8},{4,12},{8,0},{12,4},{1,9},{5,13},{9,1},{13,5},{2,10},{6,14},... | collective-permute-start | bytes 589832 | tf_op jit(solution)/shard_map/ppermute | solution.py:23
  75.4 12.8 %collective-permute-start.13 = (bf16[272,384]{1,0:T(8,128)(2,1)S(1)}, bf16[272,384]{1,0:T(8,128)(2,1)S(1)}, u32[]{:S(2)}, u32[]{:S(2)}) collective-permute-start(bf16[272,384]{1,0:T(8,128)(2,1)S(1)} %get-tuple-element.55), channel_id=1, source_target_pairs={{0,4},{4,0},{8,12},{12,8},{1,5},{5,1},{9,13},{13,9},{2,6},{6,2},{1... | collective-permute-start | bytes 626696 | tf_op jit(solution)/shard_map/ppermute | solution.py:23
  76.5 16.2 %collective-permute-start.15 = (bf16[272,384]{1,0:T(8,128)(2,1)S(1)}, bf16[272,384]{1,0:T(8,128)(2,1)S(1)}, u32[]{:S(2)}, u32[]{:S(2)}) collective-permute-start(bf16[272,384]{1,0:T(8,128)(2,1)S(1)} %get-tuple-element.57), channel_id=1, source_target_pairs={{0,12},{4,8},{8,4},{12,0},{1,13},{5,9},{9,5},{13,1},{2,14},{6,10},... | collective-permute-start | bytes 626696 | tf_op jit(solution)/shard_map/ppermute | solution.py:23
  79.1 28.9 %collective-permute-start.17 = (bf16[1024,384]{1,0:T(8,128)(2,1)S(1)}, bf16[1024,384]{1,0:T(8,128)(2,1)S(1)}, u32[]{:S(2)}, u32[]{:S(2)}) collective-permute-start(bf16[1024,384]{1,0:T(8,128)(2,1)S(1)} %copy-done.10), channel_id=1, source_target_pairs={{8,12},{9,13},{10,14},{11,15},{24,28},{25,29},{26,30},{27,31}} | collective-permute-start | bytes 2359304 | tf_op jit(solution)/shard_map/ppermute | solution.py:32
  80.0 28.0 %collective-permute-start.18 = (bf16[1024,384]{1,0:T(8,128)(2,1)S(1)}, bf16[1024,384]{1,0:T(8,128)(2,1)S(1)}, u32[]{:S(2)}, u32[]{:S(2)}) collective-permute-start(bf16[1024,384]{1,0:T(8,128)(2,1)S(1)} %copy-done.12), channel_id=1, source_target_pairs={{4,0},{5,1},{6,2},{7,3},{20,16},{21,17},{22,18},{23,19}} | collective-permute-start | bytes 2359304 | tf_op jit(solution)/shard_map/ppermute | solution.py:32
  92.9 15.9 %collective-permute-start.19 = (bf16[768,384]{1,0:T(8,128)(2,1)S(1)}, bf16[768,384]{1,0:T(8,128)(2,1)S(1)}, u32[]{:S(2)}, u32[]{:S(2)}) collective-permute-start(bf16[768,384]{1,0:T(8,128)(2,1)S(1)} %pad_maximum_fusion), channel_id=1, source_target_pairs={{0,1},{1,0},{2,3},{3,2},{4,5},{5,4},{6,7},{7,6},{8,9},{9,8},{10,11... | collective-permute-start | bytes 1769480 | tf_op jit(solution)/shard_map/ppermute | solution.py:23
  92.9 15.7 %collective-permute-start.16 = (bf16[768,384]{1,0:T(8,128)(2,1)S(1)}, bf16[768,384]{1,0:T(8,128)(2,1)S(1)}, u32[]{:S(2)}, u32[]{:S(2)}) collective-permute-start(bf16[768,384]{1,0:T(8,128)(2,1)S(1)} %pad_maximum_fusion), channel_id=1, source_target_pairs={{0,2},{1,3},{2,0},{3,1},{4,6},{5,7},{6,4},{7,5},{8,10},{9,11},{10,... | collective-permute-start | bytes 1769480 | tf_op jit(solution)/shard_map/ppermute | solution.py:23
  93.6 2.7 %copy-start = (bf16[1536,5,384]{2,0,1:T(8,128)(2,1)S(1)}, bf16[1536,5,384]{2,0,1:T(8,128)(2,1)}, u32[]{:S(2)}) copy-start(bf16[1536,5,384]{2,0,1:T(8,128)(2,1)} %param.10) | copy-start | bytes 17694724
  108.7 2.0 %collective-permute-start.20 = (bf16[768,384]{1,0:T(8,128)(2,1)S(1)}, bf16[768,384]{1,0:T(8,128)(2,1)S(1)}, u32[]{:S(2)}, u32[]{:S(2)}) collective-permute-start(bf16[768,384]{1,0:T(8,128)(2,1)S(1)} %collective-permute-done.16), channel_id=1, source_target_pairs={{0,1},{1,0},{2,3},{3,2},{4,5},{5,4},{6,7},{7,6},{8,9},{9,8},{10,11... | collective-permute-start | bytes 1769480 | tf_op jit(solution)/shard_map/ppermute | solution.py:23
  (7 other events, 8.4 us)

commit v4 on v3

--- a/solution.py
+++ b/solution.py
@@ -36,35 +36,21 @@
     return lax.optimization_barrier(tuple(values) + tuple(others))[: len(values)]
 
 
-def input_kernel(*refs, taps, tile, pieces, origins):
-    parts, (low, high, weights, out, wide, wbuf, sems) = refs[:pieces], refs[pieces:]
-    rows = parts[0].shape[0]
+def input_kernel(part, low, high, weights, out, block):
+    taps = weights.shape[0]
+    rows = part.shape[0]
     half = taps // 2
-    copies = []
-    base = 0
-    for e, origin in enumerate(origins()):
-        span = parts[e].shape[1]
-        src = weights.at[:, pl.ds(pl.multiple_of(origin, 16), span), :]
-        copy = pltpu.make_async_copy(src, wbuf.at[:, pl.ds(base, span), :], sems.at[e])
-        copy.start()
-        copies.append(copy)
-        base += span
-    base = 0
-    for e in range(pieces):
-        span = parts[e].shape[1]
-        wide[pl.ds(0, PAD), pl.ds(base, span)] = low[:, pl.ds(base, span)]
-        wide[pl.ds(PAD, rows), pl.ds(base, span)] = parts[e][...]
-        wide[pl.ds(PAD + rows, PAD), pl.ds(base, span)] = high[:, pl.ds(base, span)]
-        base += span
-    for copy in copies:
-        copy.wait()
+    block[pl.ds(0, PAD), :] = low[...]
+    block[pl.ds(PAD, rows), :] = part[...]
+    block[pl.ds(PAD + rows, PAD), :] = high[...]
+    tile = min(256, rows)
 
     def body(step, carry):
         start = pl.multiple_of(step * tile, tile)
-        block = wide[pl.ds(start, tile + 2 * PAD), :]
+        rows_in = block[pl.ds(start, tile + 2 * PAD), :]
         total = None
         for tap in range(taps):
-            term = jnp.dot(block, wbuf[tap], preferred_element_type=jnp.float32)
+            term = jnp.dot(rows_in, weights[tap], preferred_element_type=jnp.float32)
             first = PAD + half - tap
             term = term[first : first + tile]
             total = term if total is None else total + term
@@ -74,35 +60,76 @@
     lax.fori_loop(0, rows // tile, body, 0)
 
 
-def input_gradient(parts, low, high, weights, origins):
+def input_gradient(part, low, high, weights):
     taps, chans, width = weights.shape
+    rows = part.shape[0]
+    return pl.pallas_call(
+        input_kernel,
+        out_shape=jax.ShapeDtypeStruct((rows, width), jnp.bfloat16),
+        in_specs=[VMEM] * 4,
+        out_specs=VMEM,
+        scratch_shapes=[pltpu.VMEM((rows + 2 * PAD, chans), jnp.bfloat16)],
+        compiler_params=pltpu.CompilerParams(vmem_limit_bytes=32 * MIB),
+    )(part, low, high, weights)
+
+
+def pieces_kernel(*refs, taps, tile, pieces):
+    parts, (low, high, weights, out, block) = refs[:pieces], refs[pieces:]
+    rows = parts[0].shape[0]
+    width = out.shape[1]
+    half = taps // 2
+    base = 0
+    for part in parts:
+        span = pl.ds(base, part.shape[1])
+        block[pl.ds(0, PAD), span] = low[:, span]
+        block[pl.ds(PAD, rows), span] = part[...]
+        block[pl.ds(PAD + rows, PAD), span] = high[:, span]
+        base += part.shape[1]
+
+    def body(step, carry):
+        start = pl.multiple_of(step * tile, tile)
+        terms = jnp.dot(
+            block[pl.ds(start, tile + 2 * PAD), :],
+            weights[...],
+            preferred_element_type=jnp.float32,
+        )
+        total = None
+        for tap in range(taps):
+            first = PAD + half - tap
+            term = terms[first : first + tile, tap * width : (tap + 1) * width]
+            total = term if total is None else total + term
+        out[pl.ds(start, tile), :] = total.astype(out.dtype)
+        return carry
+
+    lax.fori_loop(0, rows // tile, body, 0)
+
+
+def pieces_gradient(parts, low, high, weights, taps):
+    chans = weights.shape[0]
+    width = weights.shape[1] // taps
     rows = parts[0].shape[0]
     return pl.pallas_call(
-        functools.partial(
-            input_kernel, taps=taps, tile=min(256, rows), pieces=len(parts), origins=origins
-        ),
+        functools.partial(pieces_kernel, taps=taps, tile=min(512, rows), pieces=len(parts)),
         out_shape=jax.ShapeDtypeStruct((rows, width), jnp.bfloat16),
-        in_specs=[VMEM] * (len(parts) + 2) + [SOME],
+        in_specs=[VMEM] * (len(parts) + 3),
         out_specs=VMEM,
-        scratch_shapes=[
-            pltpu.VMEM((rows + 2 * PAD, chans), jnp.bfloat16),
-            pltpu.VMEM((taps, chans, width), jnp.bfloat16),
-            pltpu.SemaphoreType.DMA((len(parts),)),
-        ],
+        scratch_shapes=[pltpu.VMEM((rows + 2 * PAD, chans), jnp.bfloat16)],
         cost_estimate=LITTLE,
-        compiler_params=pltpu.CompilerParams(vmem_limit_bytes=(20 if len(parts) > 1 else 32) * MIB),
+        compiler_params=pltpu.CompilerParams(vmem_limit_bytes=24 * MIB),
     )(*parts, low, high, weights)
 
 
-def weight_kernel(*refs, taps, tile, rows, size, nx, ng, layout, first):
-    xs, gs, rest = refs[:nx], refs[nx : nx + ng], refs[nx + ng :]
-    if first:
-        out, xbuf, gbuf, acc, sems = rest
-    else:
-        before, out, xbuf, gbuf, acc, sems = rest
+def weight_kernel(*refs, taps, tile, rows, size, nx, ng, layout, first, last, origins):
+    xs, gs, rest = refs[:nx], refs[nx : nx + ng], list(refs[nx + ng :])
+    before = None if first else rest.pop(0)
+    weights = rest.pop(0) if origins else None
+    out = rest.pop(0)
+    laid = rest.pop(0) if origins else None
+    xbuf, gbuf, acc, sems = rest
+    width = xbuf.shape[1]
     half = taps // 2
     x_rows, g_rows, starts = layout()
-    zeros = jnp.zeros((PAD, xbuf.shape[1]), xbuf.dtype)
+    zeros = jnp.zeros((PAD, width), xbuf.dtype)
     xbuf[pl.ds(0, PAD), :] = zeros
     xbuf[pl.ds(PAD + rows, PAD), :] = zeros
     pieces = [(src, xbuf, row) for src, row in zip(xs, x_rows)]
@@ -122,54 +149,102 @@
                 pl.when(row >= 0)(functools.partial(act, at))
 
     each(lambda at: copy(at).start())
+    moves = []
+    if origins:
+        where = origins()
+        span = weights.shape[1] // len(where)
+        for e, origin in enumerate(where):
+            for tap in range(taps):
+                moves.append(
+                    pltpu.make_async_copy(
+                        weights.at[tap, pl.ds(pl.multiple_of(origin, 16), span), :],
+                        laid.at[pl.ds(e * span, span), pl.ds(tap * width, width)],
+                        sems.at[nx + ng + len(moves)],
+                    )
+                )
+        for move in moves:
+            move.start()
     acc[...] = jnp.zeros_like(acc) if first else before[...]
     each(lambda at: copy(at).wait())
 
     for begin in starts:
 
         def body(step, carry):
-            start = begin + step * tile
-            start = pl.multiple_of(start, 16)
+            start = pl.multiple_of(begin + step * tile, 16)
             grad = gbuf[pl.ds(start, tile), :].T
             block = xbuf[pl.ds(start, tile + 2 * PAD), :].astype(jnp.float32)
+            moved = []
             for tap in range(taps):
                 at = PAD - half + tap
-                moved = block[at : at + tile].astype(jnp.bfloat16)
-                acc[tap] += jnp.dot(grad, moved, preferred_element_type=jnp.float32)
+                moved.append(block[at : at + tile].astype(jnp.bfloat16))
+            if width % LANES:
+                for tap in range(taps):
+                    acc[tap] += jnp.dot(grad, moved[tap], preferred_element_type=jnp.float32)
+            else:
+                moved = jnp.concatenate(moved, axis=1)
+                acc[...] += jnp.dot(grad, moved, preferred_element_type=jnp.float32)
             return carry
 
         lax.fori_loop(0, size // tile, body, 0)
-    out[...] = acc[...].astype(out.dtype)
-
-
-def weight_gradient(xs, gs, layout, size, taps, rows, before=None, last=True, vmem=40):
+    if last and width % LANES == 0:
+        for tap in range(taps):
+            out[tap] = acc[:, tap * width : (tap + 1) * width].astype(out.dtype)
+    else:
+        out[...] = acc[...].astype(out.dtype)
+    for move in moves:
+        move.wait()
+
+
+def weight_gradient(
+    xs, gs, layout, size, taps, rows, before=None, last=True, vmem=40, weights=None, origins=None
+):
     width, chunk = xs[0].shape[1], gs[0].shape[1]
+    split = (taps, chunk, width)
+    joined = split if width % LANES else (chunk, taps * width)
+    out_shape = [
+        jax.ShapeDtypeStruct(split, jnp.bfloat16)
+        if last
+        else jax.ShapeDtypeStruct(joined, jnp.float32)
+    ]
+    moves = 0
+    if origins:
+        moves = taps * 4
+        out_shape.append(
+            jax.ShapeDtypeStruct((weights.shape[1], taps * width), weights.dtype)
+        )
     return pl.pallas_call(
         functools.partial(
             weight_kernel,
             taps=taps,
-            tile=min(512, size),
+            tile=min(1024, size) if width % LANES == 0 else min(512, size),
             rows=rows,
             size=size,
             nx=len(xs),
             ng=len(gs),
             layout=layout,
             first=before is None,
+            last=last,
+            origins=origins,
         ),
-        out_shape=jax.ShapeDtypeStruct(
-            (taps, chunk, width), jnp.bfloat16 if last else jnp.float32
-        ),
-        in_specs=[SOME] * (len(xs) + len(gs)) + [VMEM] * (before is not None),
-        out_specs=VMEM,
+        out_shape=out_shape,
+        in_specs=[SOME] * (len(xs) + len(gs))
+        + [VMEM] * (before is not None)
+        + [SOME] * (weights is not None),
+        out_specs=[VMEM] * len(out_shape),
         scratch_shapes=[
             pltpu.VMEM((rows + 2 * PAD, width), jnp.bfloat16),
             pltpu.VMEM((rows, chunk), jnp.bfloat16),
-            pltpu.VMEM((taps, chunk, width), jnp.float32),
-            pltpu.SemaphoreType.DMA((len(xs) + len(gs),)),
+            pltpu.VMEM(joined, jnp.float32),
+            pltpu.SemaphoreType.DMA((len(xs) + len(gs) + moves,)),
         ],
         cost_estimate=LITTLE,
         compiler_params=pltpu.CompilerParams(vmem_limit_bytes=vmem * MIB),
-    )(*xs, *gs, *([] if before is None else [before]))
+    )(
+        *xs,
+        *gs,
+        *([] if before is None else [before]),
+        *([] if weights is None else [weights]),
+    )
 
 
 def merge_pairs(value, scratch):
@@ -382,9 +457,9 @@
         g_all = lax.all_to_all(blocks, "seq", 0, 0, tiled=True).reshape(nseq * rows, chunk)
         low = shift(whole[rows - PAD :], "seq", 1)
         high = shift(whole[:PAD], "seq", -1)
-        in_grad = input_gradient([whole], low, high, weights, lambda: [0])
+        in_grad = input_gradient(whole, low, high, weights)
         total = nseq * rows
-        w_grad = weight_gradient(
+        (w_grad,) = weight_gradient(
             [x_all], [g_all], lambda: ([PAD], [0], [0]), total, taps, total
         )
         return (in_grad, w_grad.transpose(1, 0, 2))
@@ -393,14 +468,13 @@
     place = lax.axis_index("ch")
     outgoing = front(owners, exons, pre_act, most, size, nseq)
     slope, plain = plain_gradient(*after([pre_act, out_grad], outgoing))
-    (source,) = after([x_saved], [plain])
-    up1, down1 = shift(source, "seq", 1), shift(source, "seq", -1)
     arrived = [outgoing[0]] + [swap(outgoing[d], "seq", d) for d in range(1, nseq)]
     coverage = functools.reduce(jnp.add, [a.astype(jnp.float32) for a in arrived])
     splice = jnp.tanh(coverage - target).astype(jnp.bfloat16)
     splices = [splice] + [swap(splice, "seq", d) for d in range(1, nseq)]
     pre_grad = gained_gradient(owners, exons, out_grad, slope, plain, splices, most, size, nseq)
-    pre_grad, up1, down1 = after([pre_grad, up1, down1])
+    (source,) = after([x_saved], splices[1:])
+    up1, down1 = shift(source, "seq", 1), shift(source, "seq", -1)
 
     far = swap(pre_grad, "ch", 2)
     near = swap(pre_grad, "ch", 1)
@@ -430,7 +504,10 @@
     got = [swap(block, "seq", d) for d, block in zip(range(1, nseq), sent)]
     up3, down3 = shift(up2, "seq", 1, 2), shift(down2, "seq", -1, 2)
 
-    partial = weight_gradient(
+    def origins():
+        return [(lax.axis_index("ch") ^ t) * width for t in range(nch)]
+
+    partial, laid = weight_gradient(
         [up1[rows - PAD :], x_saved, down1[:PAD]],
         [chosen(0, parts)],
         lambda: ([0, PAD, PAD + rows], [0], [0]),
@@ -438,7 +515,9 @@
         taps,
         rows,
         last=False,
-        vmem=20,
+        vmem=24,
+        weights=weights,
+        origins=origins,
     )
     *got, partial = after([*got, partial])
 
@@ -453,10 +532,7 @@
     low = jnp.pad(low, ((PAD - half, 0), (0, 0)))
     high = jnp.pad(high, ((0, PAD - half), (0, 0)))
 
-    def origins():
-        return [(lax.axis_index("ch") ^ t) * width for t in range(nch)]
-
-    in_grad = input_gradient(parts, low, high, weights, origins)
+    in_grad = pieces_gradient(parts, low, high, laid, taps)
     across, in_grad, up3, down3 = after([across, in_grad, up3, down3])
     beyond = swap(across, "ch", 1)
 
@@ -478,7 +554,7 @@
     g_pieces = []
     for piece in (crossing, beside, across, beyond):
         g_pieces += [piece[d * quarter : (d + 1) * quarter] for d in range(nseq - 1)]
-    w_grad = weight_gradient(
+    (w_grad,) = weight_gradient(
         [x_saved, up1, down1, up2, down2, up3, down3],
         g_pieces,
         layout,
@@ -486,7 +562,7 @@
         taps,
         nseq * rows,
         before=partial,
-        vmem=24,
+        vmem=32,
     )
     return (in_grad, w_grad.transpose(1, 0, 2))
 

time: 125 us -> 114 us (0.912)
  Pallas kernels: 32.3 us -> 26.6 us
  waiting for transfers between devices: 53.8 us -> 48.7 us
  local copies, waits for them, and re-layouts: 8.92 us -> 7.47 us
    ppermute x15, waiting for transfers between devices: 48.1 us -> 30.1 us  [swap(): return lax.ppermute(block, axis, [(i, i ^ flip) for i in range(count)])]
    ppermute x6, waiting for transfers between devices: 5.69 us -> 18.6 us  [shift(): return lax.ppermute(block, axis, pairs)]
    pallas_call x3, Pallas kernels: 27.8 us -> 22.1 us  [the longest x2 13.6 us: weight_gradient(): pl.pallas_call(functools.partial(weight_kernel, taps=taps, tile=min(1024,...]
    ppermute x15, starting transfers between devices: 16.2 us -> 18.2 us  [swap(): return lax.ppermute(block, axis, [(i, i ^ flip) for i in range(count)])]
    unnamed x36 -> x34, local copies, waits for them, and re-layouts: 7.08 us -> 5.69 us
  transfers between devices with their start and end apart: 21 -> 21, of which waited for: 11 -> 12; matrix products, arithmetic and copies ran while one was open for 2% -> 2% of each run, Pallas kernels for 13% -> 13%
where the time goes in v4:
time: 114 us
  waiting for transfers between devices  48.7 us (43%)
  starting transfers between devices  28.1 us (25%)
  Pallas kernels  26.6 us (23%)
  local copies, waits for them, and re-layouts  7.47 us (7%)
  other arithmetic  1.57 us (1%)
  between operations  1.21 us (1%)
    ppermute x15, waiting for transfers between devices, swap(): return lax.ppermute(block, axis, [(i, i ^ flip) for i in range(count)])  30.1 us
    ppermute x6, waiting for transfers between devices, shift(): return lax.ppermute(block, axis, pairs)  18.6 us
    ppermute x15, starting transfers between devices, swap(): return lax.ppermute(block, axis, [(i, i ^ flip) for i in range(count)])  18.2 us
    pallas_call x2, Pallas kernels, weight_gradient(): pl.pallas_call(functools.partial(weight_kernel, taps=taps, tile=min(1024,...  13.6 us
    ppermute x6, starting transfers between devices, shift(): return lax.ppermute(block, axis, pairs)  9.86 us
    pallas_call x1, Pallas kernels, pieces_gradient(): pl.pallas_call(functools.partial(pieces_kernel, taps=taps, tile=min(512,...  8.5 us
    unnamed x34, local copies, waits for them, and re-layouts  5.69 us
  transfers between devices with their start and end apart: 21, of which 12 were waited for; matrix products, arithmetic and copies ran while one was open for 2% of the time, Pallas kernels for 13%

profile of v4, /device:TPU:0, one launch (start us, length us, event | category | flops | bytes accessed | tf_op | source)
XLA Modules:
  0.0 113.6 jit_solution(10704035185056506861)
XLA Ops:
  0.7 1.1 copy-done.1
  3.1 1.2 %shard_map.86 = (bf16[64,384]{1,0:T(8,128)(2,1)S(1)}, bf16[64,384]{1,0:T(8,128)(2,1)S(1)}, bf16[64,384]{1,0:T(8,128)(2,1)S(1)}, bf16[64,384]{1,0:T(8,128)(2,1)S(1)}) custom-call(s32[16]{0:T(128)S(1)} %copy-done.15, s32[2,16]{1,0:T(2,128)S(1)} %bitcast.10, bf16[1024,384]{1,0:T(8,128)(2,1)S(1)} %copy-done.1), custom_call_target="tpu_custom_call" | custom-call | flops 1000 | bytes 1000 | tf_op jit(solution)/shard_map/pallas_call | solution.py:316
  4.4 3.1 %collective-permute-start = (bf16[64,384]{1,0:T(8,128)(2,1)S(1)}, bf16[64,384]{1,0:T(8,128)(2,1)S(1)}, u32[]{:S(2)}, u32[]{:S(2)}) collective-permute-start(bf16[64,384]{1,0:T(8,128)(2,1)S(1)} %get-tuple-element.35), channel_id=1, source_target_pairs={{0,4},{4,0},{8,12},{12,8},{1,5},{5,1},{9,13},{13,9},{2,6},{6,2},{1... | collective-permute-start | bytes 147464 | tf_op jit(solution)/shard_map/ppermute | solution.py:23
  7.5 2.7 %collective-permute-start.1 = (bf16[64,384]{1,0:T(8,128)(2,1)S(1)}, bf16[64,384]{1,0:T(8,128)(2,1)S(1)}, u32[]{:S(2)}, u32[]{:S(2)}) collective-permute-start(bf16[64,384]{1,0:T(8,128)(2,1)S(1)} %get-tuple-element.36), channel_id=1, source_target_pairs={{0,8},{4,12},{8,0},{12,4},{1,9},{5,13},{9,1},{13,5},{2,10},{6,14},... | collective-permute-start | bytes 147464 | tf_op jit(solution)/shard_map/ppermute | solution.py:23
  10.3 3.2 %collective-permute-done.1 = bf16[64,384]{1,0:T(8,128)(2,1)S(1)} collective-permute-done((bf16[64,384]{1,0:T(8,128)(2,1)S(1)}, bf16[64,384]{1,0:T(8,128)(2,1)S(1)}, u32[]{:S(2)}, u32[]{:S(2)}) %collective-permute-start.1) | collective-permute-done | bytes 49184 | tf_op jit(solution)/shard_map/ppermute | solution.py:23
  13.4 2.7 %collective-permute-done.2 = bf16[64,384]{1,0:T(8,128)(2,1)S(1)} collective-permute-done((bf16[64,384]{1,0:T(8,128)(2,1)S(1)}, bf16[64,384]{1,0:T(8,128)(2,1)S(1)}, u32[]{:S(2)}, u32[]{:S(2)}) %collective-permute-start.2) | collective-permute-done | bytes 49184 | tf_op jit(solution)/shard_map/ppermute | solution.py:23
  16.1 0.9 fusion.1.refs_0_
  17.2 1.3 %collective-permute-start.4 = (bf16[64,384]{1,0:T(8,128)(2,1)S(1)}, bf16[64,384]{1,0:T(8,128)(2,1)S(1)}, u32[]{:S(2)}, u32[]{:S(2)}) collective-permute-start(bf16[64,384]{1,0:T(8,128)(2,1)S(1)} %fusion.1.refs_0_), channel_id=1, source_target_pairs={{0,8},{4,12},{8,0},{12,4},{1,9},{5,13},{9,1},{13,5},{2,10},{6,14},... | collective-permute-start | bytes 147464 | tf_op jit(solution)/shard_map/ppermute | solution.py:23
  18.5 3.0 %collective-permute-start.5 = (bf16[64,384]{1,0:T(8,128)(2,1)S(1)}, bf16[64,384]{1,0:T(8,128)(2,1)S(1)}, u32[]{:S(2)}, u32[]{:S(2)}) collective-permute-start(bf16[64,384]{1,0:T(8,128)(2,1)S(1)} %fusion.1.refs_0_), channel_id=1, source_target_pairs={{0,12},{4,8},{8,4},{12,0},{1,13},{5,9},{9,5},{13,1},{2,14},{6,10},... | collective-permute-start | bytes 147464 | tf_op jit(solution)/shard_map/ppermute | solution.py:23
  22.3 2.1 %collective-permute-done.5.refs_3_ = bf16[64,384]{1,0:T(8,128)(2,1)S(1)} collective-permute-done((bf16[64,384]{1,0:T(8,128)(2,1)S(1)}, bf16[64,384]{1,0:T(8,128)(2,1)S(1)}, u32[]{:S(2)}, u32[]{:S(2)}) %collective-permute-start.5) | collective-permute-done | bytes 49184 | tf_op jit(solution)/shard_map/ppermute | solution.py:23
  24.4 1.3 %collective-permute-start.10 = (bf16[1024,384]{1,0:T(8,128)(2,1)}, bf16[1024,384]{1,0:T(8,128)(2,1)S(1)}, u32[]{:S(2)}, u32[]{:S(2)}) collective-permute-start(bf16[1024,384]{1,0:T(8,128)(2,1)} %refs_0_.1), channel_id=1, source_target_pairs={{4,0},{8,4},{12,8},{5,1},{9,5},{13,9},{6,2},{10,6},{14,10},{7,3},{... | collective-permute-start | bytes 2359304 | tf_op jit(solution)/shard_map/ppermute | solution.py:32
  25.7 4.6 %collective-permute-start.8 = (bf16[1024,384]{1,0:T(8,128)(2,1)}, bf16[1024,384]{1,0:T(8,128)(2,1)S(1)}, u32[]{:S(2)}, u32[]{:S(2)}) collective-permute-start(bf16[1024,384]{1,0:T(8,128)(2,1)} %refs_0_.1), channel_id=1, source_target_pairs={{0,4},{4,8},{8,12},{1,5},{5,9},{9,13},{2,6},{6,10},{10,14},{3,7},{... | collective-permute-start | bytes 2359304 | tf_op jit(solution)/shard_map/ppermute | solution.py:32
  30.3 1.0 copy-done.4
  31.3 1.4 %shard_map.87 = (f32[1024,384]{1,0:T(8,128)S(1)}, bf16[1024,384]{1,0:T(8,128)(2,1)S(1)}) custom-call(bf16[1024,384]{1,0:T(8,128)(2,1)S(1)} %copy-done.1, bf16[512,384]{1,0:T(8,128)(2,1)S(1)} %copy-done.4), custom_call_target="tpu_custom_call" | custom-call | flops 1000 | bytes 1000 | tf_op jit(solution)/shard_map/pallas_call | solution.py:343
  32.7 1.9 %shard_map.88.refs_0_ = bf16[1024,384]{1,0:T(8,128)(2,1)S(1)} custom-call(s32[16]{0:T(128)S(1)} %copy-done.16, s32[2,16]{1,0:T(2,128)S(1)} %bitcast.11, bf16[512,384]{1,0:T(8,128)(2,1)S(1)} %copy-done.4, f32[1024,384]{1,0:T(8,128)S(1)} %get-tuple-element.40.slope, bf16[1024,384]{1,0:T(8,128)(2,1)S(1)} %get-tuple-element.41.plain, ...), custom_call_target="tpu_custom_call" | custom-call | tf_op jit(solution)/shard_map/pallas_call | solution.py:382
  34.6 1.6 %collective-permute-start.6 = (bf16[1024,384]{1,0:T(8,128)(2,1)S(1)}, bf16[1024,384]{1,0:T(8,128)(2,1)S(1)}, u32[]{:S(2)}, u32[]{:S(2)}) collective-permute-start(bf16[1024,384]{1,0:T(8,128)(2,1)S(1)} %shard_map.88.refs_0_), channel_id=1, source_target_pairs={{0,2},{1,3},{2,0},{3,1},{4,6},{5,7},{6,4},{7,5},{8,10},{9,11},{10,... | collective-permute-start | bytes 2359304 | tf_op jit(solution)/shard_map/ppermute | solution.py:23
  36.2 6.9 %collective-permute-done.10.refs_2_ = bf16[1024,384]{1,0:T(8,128)(2,1)S(1)} collective-permute-done((bf16[1024,384]{1,0:T(8,128)(2,1)}, bf16[1024,384]{1,0:T(8,128)(2,1)S(1)}, u32[]{:S(2)}, u32[]{:S(2)}) %collective-permute-start.10) | collective-permute-done | bytes 786464 | tf_op jit(solution)/shard_map/ppermute | solution.py:32
  43.1 1.3 %collective-permute-start.11 = (bf16[1024,384]{1,0:T(8,128)(2,1)S(1)}, bf16[1024,384]{1,0:T(8,128)(2,1)S(1)}, u32[]{:S(2)}, u32[]{:S(2)}) collective-permute-start(bf16[1024,384]{1,0:T(8,128)(2,1)S(1)} %collective-permute-done.10.refs_2_), channel_id=1, source_target_pairs={{4,0},{8,4},{5,1},{9,5},{6,2},{10,6},{7,3},{11,7},{20,16},{24,20},... | collective-permute-start | bytes 2359304 | tf_op jit(solution)/shard_map/ppermute | solution.py:32
  45.1 5.6 %collective-permute-done.6.refs_2_ = bf16[1024,384]{1,0:T(8,128)(2,1)S(1)} collective-permute-done((bf16[1024,384]{1,0:T(8,128)(2,1)S(1)}, bf16[1024,384]{1,0:T(8,128)(2,1)S(1)}, u32[]{:S(2)}, u32[]{:S(2)}) %collective-permute-start.6) | collective-permute-done | bytes 786464 | tf_op jit(solution)/shard_map/ppermute | solution.py:23
  50.7 9.9 %collective-permute-done.11.refs_4_ = bf16[1024,384]{1,0:T(8,128)(2,1)S(1)} collective-permute-done((bf16[1024,384]{1,0:T(8,128)(2,1)S(1)}, bf16[1024,384]{1,0:T(8,128)(2,1)S(1)}, u32[]{:S(2)}, u32[]{:S(2)}) %collective-permute-start.11) | collective-permute-done | bytes 786464 | tf_op jit(solution)/shard_map/ppermute | solution.py:32
  63.8 1.3 %collective-permute-start.13 = (bf16[272,384]{1,0:T(8,128)(2,1)S(1)}, bf16[272,384]{1,0:T(8,128)(2,1)S(1)}, u32[]{:S(2)}, u32[]{:S(2)}) collective-permute-start(bf16[272,384]{1,0:T(8,128)(2,1)S(1)} %get-tuple-element.51), channel_id=1, source_target_pairs={{0,4},{4,0},{8,12},{12,8},{1,5},{5,1},{9,13},{13,9},{2,6},{6,2},{1... | collective-permute-start | bytes 626696 | tf_op jit(solution)/shard_map/ppermute | solution.py:23
  65.0 3.4 %collective-permute-start.15 = (bf16[272,384]{1,0:T(8,128)(2,1)S(1)}, bf16[272,384]{1,0:T(8,128)(2,1)S(1)}, u32[]{:S(2)}, u32[]{:S(2)}) collective-permute-start(bf16[272,384]{1,0:T(8,128)(2,1)S(1)} %get-tuple-element.53), channel_id=1, source_target_pairs={{0,12},{4,8},{8,4},{12,0},{1,13},{5,9},{9,5},{13,1},{2,14},{6,10},... | collective-permute-start | bytes 626696 | tf_op jit(solution)/shard_map/ppermute | solution.py:23
  69.1 1.3 %collective-permute-start.18 = (bf16[1024,384]{1,0:T(8,128)(2,1)}, bf16[1024,384]{1,0:T(8,128)(2,1)S(1)}, u32[]{:S(2)}, u32[]{:S(2)}) collective-permute-start(bf16[1024,384]{1,0:T(8,128)(2,1)} %copy-done.9), channel_id=1, source_target_pairs={{4,0},{5,1},{6,2},{7,3},{20,16},{21,17},{22,18},{23,19}} | collective-permute-start | bytes 2359304 | tf_op jit(solution)/shard_map/ppermute | solution.py:32
  70.6 1.1 copy-done.2
  71.7 2.8 %shard_map.89 = (f32[384,1920]{1,0:T(8,128)S(1)}, bf16[1536,1920]{1,0:T(8,128)(2,1)S(1)}) custom-call(bf16[16,384]{1,0:T(8,128)(2,1)S(1)} %slice.94.refs_0_, bf16[1024,384]{1,0:T(8,128)(2,1)S(1)} %copy-done.2, bf16[16,384]{1,0:T(8,128)(2,1)S(1)} %slice.95.refs_2_, bf16[1024,384]{1,0:T(8,128)(2,1)S(1)} %select_select_fusion.refs_3_, ...), custom_call_target="tpu_custom_call" | custom-call | flops 1000 | bytes 1000 | tf_op jit(solution)/shard_map/pallas_call | solution.py:215
  74.6 11.4 %collective-permute-done.14.refs_8_ = bf16[256,384]{1,0:T(8,128)(2,1)S(1)} collective-permute-done((bf16[256,384]{1,0:T(8,128)(2,1)S(1)}, bf16[256,384]{1,0:T(8,128)(2,1)S(1)}, u32[]{:S(2)}, u32[]{:S(2)}) %collective-permute-start.14) | collective-permute-done | bytes 196640 | tf_op jit(solution)/shard_map/ppermute | solution.py:23
  86.2 1.6 %collective-permute-start.16 = (bf16[768,384]{1,0:T(8,128)(2,1)S(1)}, bf16[768,384]{1,0:T(8,128)(2,1)S(1)}, u32[]{:S(2)}, u32[]{:S(2)}) collective-permute-start(bf16[768,384]{1,0:T(8,128)(2,1)S(1)} %pad_maximum_fusion), channel_id=1, source_target_pairs={{0,2},{1,3},{2,0},{3,1},{4,6},{5,7},{6,4},{7,5},{8,10},{9,11},{10,... | collective-permute-start | bytes 1769480 | tf_op jit(solution)/shard_map/ppermute | solution.py:23
  87.8 8.5 %shard_map.90 = bf16[1024,384]{1,0:T(8,128)(2,1)} custom-call(bf16[1024,384]{1,0:T(8,128)(2,1)S(1)} %shard_map.88.refs_0_, bf16[1024,384]{1,0:T(8,128)(2,1)S(1)} %collective-permute-done.7.refs_1_, bf16[1024,384]{1,0:T(8,128)(2,1)S(1)} %collective-permute-done.6.refs_2_, bf16[1024,384]{1,0:T(8,128)(2,1)S(1)} %collective-permute-done.12.refs_3_, ...), custom_call_target="tpu_custom_call" | custom-call | flops 1000 | bytes 1000 | tf_op jit(solution)/shard_map/pallas_call | solution.py:111
  96.3 1.7 %collective-permute-done.18.refs_6_ = bf16[1024,384]{1,0:T(8,128)(2,1)S(1)} collective-permute-done((bf16[1024,384]{1,0:T(8,128)(2,1)}, bf16[1024,384]{1,0:T(8,128)(2,1)S(1)}, u32[]{:S(2)}, u32[]{:S(2)}) %collective-permute-start.18) | collective-permute-done | bytes 786464 | tf_op jit(solution)/shard_map/ppermute | solution.py:32
  98.0 2.5 %collective-permute-done.16 = bf16[768,384]{1,0:T(8,128)(2,1)S(1)} collective-permute-done((bf16[768,384]{1,0:T(8,128)(2,1)S(1)}, bf16[768,384]{1,0:T(8,128)(2,1)S(1)}, u32[]{:S(2)}, u32[]{:S(2)}) %collective-permute-start.16) | collective-permute-done | bytes 589856 | tf_op jit(solution)/shard_map/ppermute | solution.py:23
  100.8 1.8 %collective-permute-done.20 = bf16[768,384]{1,0:T(8,128)(2,1)S(1)} collective-permute-done((bf16[768,384]{1,0:T(8,128)(2,1)S(1)}, bf16[768,384]{1,0:T(8,128)(2,1)S(1)}, u32[]{:S(2)}, u32[]{:S(2)}) %collective-permute-start.20) | collective-permute-done | bytes 589856 | tf_op jit(solution)/shard_map/ppermute | solution.py:23
  102.7 10.8 %shard_map.91 = bf16[5,384,384]{2,1,0:T(8,128)(2,1)} custom-call(bf16[1024,384]{1,0:T(8,128)(2,1)S(1)} %copy-done.3, bf16[1024,384]{1,0:T(8,128)(2,1)S(1)} %copy-done.8, bf16[1024,384]{1,0:T(8,128)(2,1)S(1)} %copy-done.6, bf16[1024,384]{1,0:T(8,128)(2,1)S(1)} %copy-done.12, bf16[1024,384]{1,0:T(8,128)(2,1)S(1)} %copy-done.10, ...), custom_call_target="tpu_custom_call" | custom-call | flops 1000 | bytes 1000 | tf_op jit(solution)/shard_map/pallas_call | solution.py:215
  (73 shorter events, 7.2 us)
Async XLA Ops:
  0.6 32.1 %copy-start.14 = (s32[16,2]{0,1:T(2,128)S(1)}, s32[16,2]{0,1:T(2,128)}, u32[]{:S(2)}) copy-start(s32[16,2]{0,1:T(2,128)} %param.13) | copy-start | bytes 388
  0.6 32.1 %copy-start.16 = (s32[16]{0:T(128)S(1)}, s32[16]{0:T(128)}, u32[]{:S(2)}) copy-start(s32[16]{0:T(128)} %owners.3) | copy-start | bytes 196
  0.7 1.1 %copy-start.1 = (bf16[1024,384]{1,0:T(8,128)(2,1)S(1)}, bf16[1024,384]{1,0:T(8,128)(2,1)}, u32[]{:S(2)}) copy-start(bf16[1024,384]{1,0:T(8,128)(2,1)} %pre_act.2) | copy-start | bytes 2359300
  4.4 5.9 %collective-permute-start = (bf16[64,384]{1,0:T(8,128)(2,1)S(1)}, bf16[64,384]{1,0:T(8,128)(2,1)S(1)}, u32[]{:S(2)}, u32[]{:S(2)}) collective-permute-start(bf16[64,384]{1,0:T(8,128)(2,1)S(1)} %get-tuple-element.35), channel_id=1, source_target_pairs={{0,4},{4,0},{8,12},{12,8},{1,5},{5,1},{9,13},{13,9},{2,6},{6,2},{1... | collective-permute-start | bytes 147464 | tf_op jit(solution)/shard_map/ppermute | solution.py:23
  7.5 5.9 %collective-permute-start.1 = (bf16[64,384]{1,0:T(8,128)(2,1)S(1)}, bf16[64,384]{1,0:T(8,128)(2,1)S(1)}, u32[]{:S(2)}, u32[]{:S(2)}) collective-permute-start(bf16[64,384]{1,0:T(8,128)(2,1)S(1)} %get-tuple-element.36), channel_id=1, source_target_pairs={{0,8},{4,12},{8,0},{12,4},{1,9},{5,13},{9,1},{13,5},{2,10},{6,14},... | collective-permute-start | bytes 147464 | tf_op jit(solution)/shard_map/ppermute | solution.py:23
  10.2 5.9 %collective-permute-start.2 = (bf16[64,384]{1,0:T(8,128)(2,1)S(1)}, bf16[64,384]{1,0:T(8,128)(2,1)S(1)}, u32[]{:S(2)}, u32[]{:S(2)}) collective-permute-start(bf16[64,384]{1,0:T(8,128)(2,1)S(1)} %get-tuple-element.37), channel_id=1, source_target_pairs={{0,12},{4,8},{8,4},{12,0},{1,13},{5,9},{9,5},{13,1},{2,14},{6,10},... | collective-permute-start | bytes 147464 | tf_op jit(solution)/shard_map/ppermute | solution.py:23
  17.1 4.7 %collective-permute-start.3 = (bf16[64,384]{1,0:T(8,128)(2,1)S(1)}, bf16[64,384]{1,0:T(8,128)(2,1)S(1)}, u32[]{:S(2)}, u32[]{:S(2)}) collective-permute-start(bf16[64,384]{1,0:T(8,128)(2,1)S(1)} %fusion.1.refs_0_), channel_id=1, source_target_pairs={{0,4},{4,0},{8,12},{12,8},{1,5},{5,1},{9,13},{13,9},{2,6},{6,2},{1... | collective-permute-start | bytes 147464 | tf_op jit(solution)/shard_map/ppermute | solution.py:23
  17.2 5.1 %collective-permute-start.4 = (bf16[64,384]{1,0:T(8,128)(2,1)S(1)}, bf16[64,384]{1,0:T(8,128)(2,1)S(1)}, u32[]{:S(2)}, u32[]{:S(2)}) collective-permute-start(bf16[64,384]{1,0:T(8,128)(2,1)S(1)} %fusion.1.refs_0_), channel_id=1, source_target_pairs={{0,8},{4,12},{8,0},{12,4},{1,9},{5,13},{9,1},{13,5},{2,10},{6,14},... | collective-permute-start | bytes 147464 | tf_op jit(solution)/shard_map/ppermute | solution.py:23
  18.5 5.9 %collective-permute-start.5 = (bf16[64,384]{1,0:T(8,128)(2,1)S(1)}, bf16[64,384]{1,0:T(8,128)(2,1)S(1)}, u32[]{:S(2)}, u32[]{:S(2)}) collective-permute-start(bf16[64,384]{1,0:T(8,128)(2,1)S(1)} %fusion.1.refs_0_), channel_id=1, source_target_pairs={{0,12},{4,8},{8,4},{12,0},{1,13},{5,9},{9,5},{13,1},{2,14},{6,10},... | collective-permute-start | bytes 147464 | tf_op jit(solution)/shard_map/ppermute | solution.py:23
  24.4 18.7 %collective-permute-start.10 = (bf16[1024,384]{1,0:T(8,128)(2,1)}, bf16[1024,384]{1,0:T(8,128)(2,1)S(1)}, u32[]{:S(2)}, u32[]{:S(2)}) collective-permute-start(bf16[1024,384]{1,0:T(8,128)(2,1)} %refs_0_.1), channel_id=1, source_target_pairs={{4,0},{8,4},{12,8},{5,1},{9,5},{13,9},{6,2},{10,6},{14,10},{7,3},{... | collective-permute-start | bytes 2359304 | tf_op jit(solution)/shard_map/ppermute | solution.py:32
  25.7 18.7 %collective-permute-start.8 = (bf16[1024,384]{1,0:T(8,128)(2,1)}, bf16[1024,384]{1,0:T(8,128)(2,1)S(1)}, u32[]{:S(2)}, u32[]{:S(2)}) collective-permute-start(bf16[1024,384]{1,0:T(8,128)(2,1)} %refs_0_.1), channel_id=1, source_target_pairs={{0,4},{4,8},{8,12},{1,5},{5,9},{9,13},{2,6},{6,10},{10,14},{3,7},{... | collective-permute-start | bytes 2359304 | tf_op jit(solution)/shard_map/ppermute | solution.py:32
  34.6 16.1 %collective-permute-start.6 = (bf16[1024,384]{1,0:T(8,128)(2,1)S(1)}, bf16[1024,384]{1,0:T(8,128)(2,1)S(1)}, u32[]{:S(2)}, u32[]{:S(2)}) collective-permute-start(bf16[1024,384]{1,0:T(8,128)(2,1)S(1)} %shard_map.88.refs_0_), channel_id=1, source_target_pairs={{0,2},{1,3},{2,0},{3,1},{4,6},{5,7},{6,4},{7,5},{8,10},{9,11},{10,... | collective-permute-start | bytes 2359304 | tf_op jit(solution)/shard_map/ppermute | solution.py:23
  36.2 14.6 %collective-permute-start.7 = (bf16[1024,384]{1,0:T(8,128)(2,1)S(1)}, bf16[1024,384]{1,0:T(8,128)(2,1)S(1)}, u32[]{:S(2)}, u32[]{:S(2)}) collective-permute-start(bf16[1024,384]{1,0:T(8,128)(2,1)S(1)} %shard_map.88.refs_0_), channel_id=1, source_target_pairs={{0,1},{1,0},{2,3},{3,2},{4,5},{5,4},{6,7},{7,6},{8,9},{9,8},{10,11... | collective-permute-start | bytes 2359304 | tf_op jit(solution)/shard_map/ppermute | solution.py:23
  43.1 17.6 %copy-start.5 = (bf16[1024,384]{1,0:T(8,128)(2,1)}, bf16[1024,384]{1,0:T(8,128)(2,1)S(1)}, u32[]{:S(2)}) copy-start(bf16[1024,384]{1,0:T(8,128)(2,1)S(1)} %collective-permute-done.10.refs_2_) | copy-start | bytes 2359300
  43.1 17.6 %collective-permute-start.11 = (bf16[1024,384]{1,0:T(8,128)(2,1)S(1)}, bf16[1024,384]{1,0:T(8,128)(2,1)S(1)}, u32[]{:S(2)}, u32[]{:S(2)}) collective-permute-start(bf16[1024,384]{1,0:T(8,128)(2,1)S(1)} %collective-permute-done.10.refs_2_), channel_id=1, source_target_pairs={{4,0},{8,4},{5,1},{9,5},{6,2},{10,6},{7,3},{11,7},{20,16},{24,20},... | collective-permute-start | bytes 2359304 | tf_op jit(solution)/shard_map/ppermute | solution.py:32
  44.4 16.3 %copy-start.7 = (bf16[1024,384]{1,0:T(8,128)(2,1)}, bf16[1024,384]{1,0:T(8,128)(2,1)S(1)}, u32[]{:S(2)}) copy-start(bf16[1024,384]{1,0:T(8,128)(2,1)S(1)} %collective-permute-done.8.refs_1_) | copy-start | bytes 2359300
  44.4 16.3 %collective-permute-start.9 = (bf16[1024,384]{1,0:T(8,128)(2,1)S(1)}, bf16[1024,384]{1,0:T(8,128)(2,1)S(1)}, u32[]{:S(2)}, u32[]{:S(2)}) collective-permute-start(bf16[1024,384]{1,0:T(8,128)(2,1)S(1)} %collective-permute-done.8.refs_1_), channel_id=1, source_target_pairs={{4,8},{8,12},{5,9},{9,13},{6,10},{10,14},{7,11},{11,15},{20,24},{2... | collective-permute-start | bytes 2359304 | tf_op jit(solution)/shard_map/ppermute | solution.py:32
  60.7 2.6 %collective-permute-start.12 = (bf16[1024,384]{1,0:T(8,128)(2,1)S(1)}, bf16[1024,384]{1,0:T(8,128)(2,1)S(1)}, u32[]{:S(2)}, u32[]{:S(2)}) collective-permute-start(bf16[1024,384]{1,0:T(8,128)(2,1)S(1)} %collective-permute-done.6.refs_2_), channel_id=1, source_target_pairs={{0,1},{1,0},{2,3},{3,2},{4,5},{5,4},{6,7},{7,6},{8,9},{9,8},{10,11... | collective-permute-start | bytes 2359304 | tf_op jit(solution)/shard_map/ppermute | solution.py:23
  63.4 7.2 %copy-start = (bf16[1536,5,384]{2,0,1:T(8,128)(2,1)S(1)}, bf16[1536,5,384]{2,0,1:T(8,128)(2,1)}, u32[]{:S(2)}) copy-start(bf16[1536,5,384]{2,0,1:T(8,128)(2,1)} %param.10) | copy-start | bytes 17694724
  63.8 22.3 %collective-permute-start.13 = (bf16[272,384]{1,0:T(8,128)(2,1)S(1)}, bf16[272,384]{1,0:T(8,128)(2,1)S(1)}, u32[]{:S(2)}, u32[]{:S(2)}) collective-permute-start(bf16[272,384]{1,0:T(8,128)(2,1)S(1)} %get-tuple-element.51), channel_id=1, source_target_pairs={{0,4},{4,0},{8,12},{12,8},{1,5},{5,1},{9,13},{13,9},{2,6},{6,2},{1... | collective-permute-start | bytes 626696 | tf_op jit(solution)/shard_map/ppermute | solution.py:23
  65.0 21.0 %collective-permute-start.15 = (bf16[272,384]{1,0:T(8,128)(2,1)S(1)}, bf16[272,384]{1,0:T(8,128)(2,1)S(1)}, u32[]{:S(2)}, u32[]{:S(2)}) collective-permute-start(bf16[272,384]{1,0:T(8,128)(2,1)S(1)} %get-tuple-element.53), channel_id=1, source_target_pairs={{0,12},{4,8},{8,4},{12,0},{1,13},{5,9},{9,5},{13,1},{2,14},{6,10},... | collective-permute-start | bytes 626696 | tf_op jit(solution)/shard_map/ppermute | solution.py:23
  68.4 17.6 %collective-permute-start.14 = (bf16[256,384]{1,0:T(8,128)(2,1)S(1)}, bf16[256,384]{1,0:T(8,128)(2,1)S(1)}, u32[]{:S(2)}, u32[]{:S(2)}) collective-permute-start(bf16[256,384]{1,0:T(8,128)(2,1)S(1)} %get-tuple-element.52), channel_id=1, source_target_pairs={{0,8},{4,12},{8,0},{12,4},{1,9},{5,13},{9,1},{13,5},{2,10},{6,14},... | collective-permute-start | bytes 589832 | tf_op jit(solution)/shard_map/ppermute | solution.py:23
  68.4 27.9 %collective-permute-start.17 = (bf16[1024,384]{1,0:T(8,128)(2,1)}, bf16[1024,384]{1,0:T(8,128)(2,1)S(1)}, u32[]{:S(2)}, u32[]{:S(2)}) collective-permute-start(bf16[1024,384]{1,0:T(8,128)(2,1)} %copy-done.11), channel_id=1, source_target_pairs={{8,12},{9,13},{10,14},{11,15},{24,28},{25,29},{26,30},{27,31}} | collective-permute-start | bytes 2359304 | tf_op jit(solution)/shard_map/ppermute | solution.py:32
  69.1 28.9 %collective-permute-start.18 = (bf16[1024,384]{1,0:T(8,128)(2,1)}, bf16[1024,384]{1,0:T(8,128)(2,1)S(1)}, u32[]{:S(2)}, u32[]{:S(2)}) collective-permute-start(bf16[1024,384]{1,0:T(8,128)(2,1)} %copy-done.9), channel_id=1, source_target_pairs={{4,0},{5,1},{6,2},{7,3},{20,16},{21,17},{22,18},{23,19}} | collective-permute-start | bytes 2359304 | tf_op jit(solution)/shard_map/ppermute | solution.py:32
  86.2 14.4 %collective-permute-start.16 = (bf16[768,384]{1,0:T(8,128)(2,1)S(1)}, bf16[768,384]{1,0:T(8,128)(2,1)S(1)}, u32[]{:S(2)}, u32[]{:S(2)}) collective-permute-start(bf16[768,384]{1,0:T(8,128)(2,1)S(1)} %pad_maximum_fusion), channel_id=1, source_target_pairs={{0,2},{1,3},{2,0},{3,1},{4,6},{5,7},{6,4},{7,5},{8,10},{9,11},{10,... | collective-permute-start | bytes 1769480 | tf_op jit(solution)/shard_map/ppermute | solution.py:23
  87.7 13.0 %collective-permute-start.19 = (bf16[768,384]{1,0:T(8,128)(2,1)S(1)}, bf16[768,384]{1,0:T(8,128)(2,1)S(1)}, u32[]{:S(2)}, u32[]{:S(2)}) collective-permute-start(bf16[768,384]{1,0:T(8,128)(2,1)S(1)} %pad_maximum_fusion), channel_id=1, source_target_pairs={{0,1},{1,0},{2,3},{3,2},{4,5},{5,4},{6,7},{7,6},{8,9},{9,8},{10,11... | collective-permute-start | bytes 1769480 | tf_op jit(solution)/shard_map/ppermute | solution.py:23
  87.8 14.8 %copy-start.12 = (bf16[1024,384]{1,0:T(8,128)(2,1)S(1)}, bf16[1024,384]{1,0:T(8,128)(2,1)}, u32[]{:S(2)}) copy-start(bf16[1024,384]{1,0:T(8,128)(2,1)} %copy-done.11) | copy-start | bytes 2359300
  100.6 2.0 %collective-permute-start.20 = (bf16[768,384]{1,0:T(8,128)(2,1)S(1)}, bf16[768,384]{1,0:T(8,128)(2,1)S(1)}, u32[]{:S(2)}, u32[]{:S(2)}) collective-permute-start(bf16[768,384]{1,0:T(8,128)(2,1)S(1)} %collective-permute-done.16), channel_id=1, source_target_pairs={{0,1},{1,0},{2,3},{3,2},{4,5},{5,4},{6,7},{7,6},{8,9},{9,8},{10,11... | collective-permute-start | bytes 1769480 | tf_op jit(solution)/shard_map/ppermute | solution.py:23
  100.6 2.1 %copy-start.10 = (bf16[1024,384]{1,0:T(8,128)(2,1)S(1)}, bf16[1024,384]{1,0:T(8,128)(2,1)}, u32[]{:S(2)}) copy-start(bf16[1024,384]{1,0:T(8,128)(2,1)} %copy-done.9) | copy-start | bytes 2359300
  100.7 2.0 %copy-start.3 = (bf16[1024,384]{1,0:T(8,128)(2,1)S(1)}, bf16[1024,384]{1,0:T(8,128)(2,1)}, u32[]{:S(2)}) copy-start(bf16[1024,384]{1,0:T(8,128)(2,1)} %refs_0_.1) | copy-start | bytes 2359300
  100.7 2.0 %copy-start.6 = (bf16[1024,384]{1,0:T(8,128)(2,1)S(1)}, bf16[1024,384]{1,0:T(8,128)(2,1)}, u32[]{:S(2)}) copy-start(bf16[1024,384]{1,0:T(8,128)(2,1)} %copy-done.5) | copy-start | bytes 2359300
  100.7 2.0 %copy-start.8 = (bf16[1024,384]{1,0:T(8,128)(2,1)S(1)}, bf16[1024,384]{1,0:T(8,128)(2,1)}, u32[]{:S(2)}) copy-start(bf16[1024,384]{1,0:T(8,128)(2,1)} %copy-done.7) | copy-start | bytes 2359300
  (6 other events, 5.5 us)

commit v5 on v4

--- a/solution.py
+++ b/solution.py
@@ -73,53 +73,65 @@
     )(part, low, high, weights)
 
 
-def pieces_kernel(*refs, taps, tile, pieces):
-    parts, (low, high, weights, out, block) = refs[:pieces], refs[pieces:]
+def pieces_kernel(*refs, taps, pieces, middle):
+    parts, rest = refs[:pieces], refs[pieces:]
+    if middle:
+        weights, out, block = rest
+    else:
+        low, high, center, weights, out, block = rest
     rows = parts[0].shape[0]
-    width = out.shape[1]
+    width = weights.shape[1] // taps
     half = taps // 2
+    quarter = rows // 4
+    kept = [(0, rows)] if middle else [(0, quarter + PAD), (rows - quarter - PAD, quarter + PAD)]
     base = 0
     for part in parts:
         span = pl.ds(base, part.shape[1])
-        block[pl.ds(0, PAD), span] = low[:, span]
-        block[pl.ds(PAD, rows), span] = part[...]
-        block[pl.ds(PAD + rows, PAD), span] = high[:, span]
+        for begin, count in kept:
+            block[pl.ds(PAD + begin, count), span] = part[pl.ds(begin, count), :]
+        if not middle:
+            block[pl.ds(0, PAD), span] = low[:, span]
+            block[pl.ds(PAD + rows, PAD), span] = high[:, span]
         base += part.shape[1]
 
-    def body(step, carry):
-        start = pl.multiple_of(step * tile, tile)
+    def tile(start, count):
         terms = jnp.dot(
-            block[pl.ds(start, tile + 2 * PAD), :],
+            block[pl.ds(start, count + 2 * PAD), :],
             weights[...],
             preferred_element_type=jnp.float32,
         )
         total = None
         for tap in range(taps):
             first = PAD + half - tap
-            term = terms[first : first + tile, tap * width : (tap + 1) * width]
+            term = terms[first : first + count, tap * width : (tap + 1) * width]
             total = term if total is None else total + term
-        out[pl.ds(start, tile), :] = total.astype(out.dtype)
-        return carry
-
-    lax.fori_loop(0, rows // tile, body, 0)
-
-
-def pieces_gradient(parts, low, high, weights, taps):
+        return total.astype(out.dtype)
+
+    if middle:
+        out[...] = tile(quarter, 2 * quarter)
+    else:
+        out[pl.ds(0, quarter), :] = tile(0, quarter)
+        out[pl.ds(quarter, 2 * quarter), :] = center[...]
+        out[pl.ds(3 * quarter, quarter), :] = tile(3 * quarter, quarter)
+
+
+def pieces_gradient(parts, weights, taps, rest=()):
     chans = weights.shape[0]
     width = weights.shape[1] // taps
     rows = parts[0].shape[0]
+    middle = not rest
     return pl.pallas_call(
-        functools.partial(pieces_kernel, taps=taps, tile=min(512, rows), pieces=len(parts)),
-        out_shape=jax.ShapeDtypeStruct((rows, width), jnp.bfloat16),
-        in_specs=[VMEM] * (len(parts) + 3),
+        functools.partial(pieces_kernel, taps=taps, pieces=len(parts), middle=middle),
+        out_shape=jax.ShapeDtypeStruct((rows // 2 if middle else rows, width), jnp.bfloat16),
+        in_specs=[VMEM] * (len(parts) + len(rest) + 1),
         out_specs=VMEM,
         scratch_shapes=[pltpu.VMEM((rows + 2 * PAD, chans), jnp.bfloat16)],
         cost_estimate=LITTLE,
         compiler_params=pltpu.CompilerParams(vmem_limit_bytes=24 * MIB),
-    )(*parts, low, high, weights)
-
-
-def weight_kernel(*refs, taps, tile, rows, size, nx, ng, layout, first, last, origins):
+    )(*parts, *rest, weights)
+
+
+def weight_kernel(*refs, taps, tile, rows, size, nx, ng, layout, first, last, origins, span):
     xs, gs, rest = refs[:nx], refs[nx : nx + ng], list(refs[nx + ng :])
     before = None if first else rest.pop(0)
     weights = rest.pop(0) if origins else None
@@ -128,17 +140,25 @@
     xbuf, gbuf, acc, sems = rest
     width = xbuf.shape[1]
     half = taps // 2
-    x_rows, g_rows, starts = layout()
+    x_rows, g_rows, starts, blanks, seams = layout()
     zeros = jnp.zeros((PAD, width), xbuf.dtype)
     xbuf[pl.ds(0, PAD), :] = zeros
     xbuf[pl.ds(PAD + rows, PAD), :] = zeros
-    pieces = [(src, xbuf, row) for src, row in zip(xs, x_rows)]
-    pieces += [(src, gbuf, row) for src, row in zip(gs, g_rows)]
+    for wanted, row in blanks:
+
+        @pl.when(wanted)
+        def _():
+            xbuf[pl.ds(row, PAD), :] = zeros
+
+    pieces = [(src, xbuf, row, src.shape[0]) for src, row in zip(xs, x_rows)]
+    pieces += [(src, gbuf, row, span or src.shape[0]) for src, row in zip(gs, g_rows)]
 
     def copy(at):
-        src, dst, row = pieces[at]
+        src, dst, row, count = pieces[at]
         row = row if isinstance(row, int) else pl.multiple_of(row, 16)
-        return pltpu.make_async_copy(src, dst.at[pl.ds(row, src.shape[0]), :], sems.at[at])
+        return pltpu.make_async_copy(
+            src.at[pl.ds(0, count), :], dst.at[pl.ds(row, count), :], sems.at[at]
+        )
 
     def each(act):
         for at in range(nx + ng):
@@ -152,13 +172,13 @@
     moves = []
     if origins:
         where = origins()
-        span = weights.shape[1] // len(where)
+        depth = weights.shape[1] // len(where)
         for e, origin in enumerate(where):
             for tap in range(taps):
                 moves.append(
                     pltpu.make_async_copy(
-                        weights.at[tap, pl.ds(pl.multiple_of(origin, 16), span), :],
-                        laid.at[pl.ds(e * span, span), pl.ds(tap * width, width)],
+                        weights.at[tap, pl.ds(pl.multiple_of(origin, 16), depth), :],
+                        laid.at[pl.ds(e * depth, depth), pl.ds(tap * width, width)],
                         sems.at[nx + ng + len(moves)],
                     )
                 )
@@ -167,25 +187,32 @@
     acc[...] = jnp.zeros_like(acc) if first else before[...]
     each(lambda at: copy(at).wait())
 
+    def add(start, count, side=None):
+        grad = gbuf[pl.ds(start, count), :].T
+        block = xbuf[pl.ds(start, count + 2 * PAD), :].astype(jnp.float32)
+        if side is not None:
+            row = lax.broadcasted_iota(jnp.int32, block.shape, 0)
+            block = jnp.where(row >= count + PAD if side > 0 else row < PAD, block, 0.0)
+        moved = []
+        for tap in range(taps):
+            at = PAD - half + tap
+            moved.append(block[at : at + count].astype(jnp.bfloat16))
+        if width % LANES:
+            for tap in range(taps):
+                acc[tap] += jnp.dot(grad, moved[tap], preferred_element_type=jnp.float32)
+        else:
+            moved = jnp.concatenate(moved, axis=1)
+            acc[...] += jnp.dot(grad, moved, preferred_element_type=jnp.float32)
+
     for begin in starts:
 
         def body(step, carry):
-            start = pl.multiple_of(begin + step * tile, 16)
-            grad = gbuf[pl.ds(start, tile), :].T
-            block = xbuf[pl.ds(start, tile + 2 * PAD), :].astype(jnp.float32)
-            moved = []
-            for tap in range(taps):
-                at = PAD - half + tap
-                moved.append(block[at : at + tile].astype(jnp.bfloat16))
-            if width % LANES:
-                for tap in range(taps):
-                    acc[tap] += jnp.dot(grad, moved[tap], preferred_element_type=jnp.float32)
-            else:
-                moved = jnp.concatenate(moved, axis=1)
-                acc[...] += jnp.dot(grad, moved, preferred_element_type=jnp.float32)
+            add(pl.multiple_of(begin + step * tile, 16), tile)
             return carry
 
         lax.fori_loop(0, size // tile, body, 0)
+    for wanted, row, side in seams:
+        pl.when(wanted)(functools.partial(add, row, PAD, side))
     if last and width % LANES == 0:
         for tap in range(taps):
             out[tap] = acc[:, tap * width : (tap + 1) * width].astype(out.dtype)
@@ -196,7 +223,7 @@
 
 
 def weight_gradient(
-    xs, gs, layout, size, taps, rows, before=None, last=True, vmem=40, weights=None, origins=None
+    xs, gs, layout, size, taps, rows, before=None, last=True, vmem=40, weights=None, origins=None, span=None
 ):
     width, chunk = xs[0].shape[1], gs[0].shape[1]
     split = (taps, chunk, width)
@@ -225,6 +252,7 @@
             first=before is None,
             last=last,
             origins=origins,
+            span=span,
         ),
         out_shape=out_shape,
         in_specs=[SOME] * (len(xs) + len(gs))
@@ -460,21 +488,27 @@
         in_grad = input_gradient(whole, low, high, weights)
         total = nseq * rows
         (w_grad,) = weight_gradient(
-            [x_all], [g_all], lambda: ([PAD], [0], [0]), total, taps, total
+            [x_all], [g_all], lambda: ([PAD], [0], [0], [], []), total, taps, total
         )
         return (in_grad, w_grad.transpose(1, 0, 2))
 
     mine = lax.axis_index("seq")
     place = lax.axis_index("ch")
+    early = x_saved[: rows // 2]
+    up_early, down_early = shift(early, "seq", 1), shift(early, "seq", -1)
     outgoing = front(owners, exons, pre_act, most, size, nseq)
-    slope, plain = plain_gradient(*after([pre_act, out_grad], outgoing))
+    slope, plain = plain_gradient(pre_act, out_grad)
     arrived = [outgoing[0]] + [swap(outgoing[d], "seq", d) for d in range(1, nseq)]
+    *arrived, up_early, down_early, slope, plain = after(
+        [*arrived, up_early, down_early, slope, plain]
+    )
     coverage = functools.reduce(jnp.add, [a.astype(jnp.float32) for a in arrived])
     splice = jnp.tanh(coverage - target).astype(jnp.bfloat16)
     splices = [splice] + [swap(splice, "seq", d) for d in range(1, nseq)]
     pre_grad = gained_gradient(owners, exons, out_grad, slope, plain, splices, most, size, nseq)
-    (source,) = after([x_saved], splices[1:])
-    up1, down1 = shift(source, "seq", 1), shift(source, "seq", -1)
+    (late,) = after([x_saved[rows // 2 :]], splices[1:])
+    up1 = jnp.concatenate([up_early, shift(late, "seq", 1)])
+    down1 = jnp.concatenate([down_early, shift(late, "seq", -1)])
 
     far = swap(pre_grad, "ch", 2)
     near = swap(pre_grad, "ch", 1)
@@ -510,7 +544,7 @@
     partial, laid = weight_gradient(
         [up1[rows - PAD :], x_saved, down1[:PAD]],
         [chosen(0, parts)],
-        lambda: ([0, PAD, PAD + rows], [0], [0]),
+        lambda: ([0, PAD, PAD + rows], [0], [0], [], []),
         rows,
         taps,
         rows,
@@ -519,11 +553,12 @@
         weights=weights,
         origins=origins,
     )
-    *got, partial = after([*got, partial])
-
-    crossing = jnp.concatenate([block[:quarter] for block in got])
-    across = swap(crossing, "ch", 2)
-    beside = swap(crossing, "ch", 1)
+    center = pieces_gradient(parts, laid, taps)
+    first, partial, center = after([got[0], partial, center])
+    got[0] = first
+
+    across = [swap(block, "ch", 2) for block in got]
+    beside = [swap(block, "ch", 1) for block in got]
     edges = [got[d - 1][quarter : quarter + len(heads)] for d in (1, 3)]
     edges = [jnp.concatenate(jnp.split(e, nch), axis=1) for e in edges]
     nothing = jnp.zeros_like(edges[0])
@@ -531,38 +566,59 @@
     high = jnp.where(mine % 2 == 0, edges[0], jnp.where(mine == 1, edges[1], nothing))
     low = jnp.pad(low, ((PAD - half, 0), (0, 0)))
     high = jnp.pad(high, ((0, PAD - half), (0, 0)))
-
-    in_grad = pieces_gradient(parts, low, high, laid, taps)
-    across, in_grad, up3, down3 = after([across, in_grad, up3, down3])
-    beyond = swap(across, "ch", 1)
-
-    def layout():
+    in_grad = pieces_gradient(parts, laid, taps, [low, high, center])
+    *across, in_grad = after([*across, in_grad])
+    beyond = [swap(block, "ch", 1) for block in across]
+
+    seam = (nseq - 1) * rows
+
+    def layout(hops, blocks, closing):
         mine = lax.axis_index("seq")
         place = lax.axis_index("ch")
         x_rows = [PAD + mine * rows]
-        for hop in range(1, nseq):
+        for hop in range(1, hops):
             low_at, high_at = mine - hop, mine + hop
             x_rows += [
                 jnp.where(low_at >= 0, PAD + low_at * rows, -1),
                 jnp.where(high_at < nseq, PAD + high_at * rows, -1),
             ]
-        g_rows = []
-        for tag in range(nch):
-            g_rows += [(mine ^ d) * rows + (place ^ tag) * quarter for d in range(1, nseq)]
-        return x_rows, g_rows, [(mine ^ d) * rows for d in range(1, nseq)]
-
-    g_pieces = []
-    for piece in (crossing, beside, across, beyond):
-        g_pieces += [piece[d * quarter : (d + 1) * quarter] for d in range(nseq - 1)]
-    (w_grad,) = weight_gradient(
-        [x_saved, up1, down1, up2, down2, up3, down3],
-        g_pieces,
-        layout,
+        used = (2, 3) if closing else blocks
+        g_rows = [
+            (mine ^ d) * rows + (place ^ tag) * quarter for d in used for tag in range(nch)
+        ]
+        starts = [(mine ^ d) * rows for d in blocks]
+        if closing:
+            seams = [(mine == 0, seam - PAD, 1), (mine == nseq - 1, rows, -1)]
+            return x_rows, g_rows, starts, [], seams
+        return x_rows, g_rows, starts, [(mine == 0, PAD + seam), (mine == nseq - 1, rows)], []
+
+    def sources(blocks):
+        return [
+            kind[d - 1] for d in blocks for kind in (got, beside, across, beyond)
+        ]
+
+    (partial,) = weight_gradient(
+        [x_saved, up1, down1, up2, down2],
+        sources((1, 2)),
+        functools.partial(layout, 3, (1, 2), False),
         rows,
         taps,
         nseq * rows,
         before=partial,
+        last=False,
         vmem=32,
+        span=quarter,
+    )
+    (w_grad,) = weight_gradient(
+        [x_saved, up1, down1, up2, down2, up3, down3],
+        sources((2, 3)),
+        functools.partial(layout, 4, (3,), True),
+        rows,
+        taps,
+        nseq * rows,
+        before=after([partial], [in_grad])[0],
+        vmem=32,
+        span=quarter,
     )
     return (in_grad, w_grad.transpose(1, 0, 2))
 

time: 114 us -> 116 us (1.018)
  waiting for transfers between devices: 48.7 us -> 37.3 us
  starting transfers between devices: 28.1 us -> 36.6 us
  local copies, waits for them, and re-layouts: 7.47 us -> 10.4 us
  Pallas kernels: 26.6 us -> 29.1 us
    ppermute x6 -> x8, waiting for transfers between devices: 18.6 us -> 8.37 us  [shift(): return lax.ppermute(block, axis, pairs)]
    ppermute x6 -> x8, starting transfers between devices: 9.86 us -> 16.3 us  [shift(): return lax.ppermute(block, axis, pairs)]
    unnamed x34 -> x36, local copies, waits for them, and re-layouts: 5.69 us -> 8.16 us
    pallas_call x2 -> x3, Pallas kernels: 13.6 us -> 15.9 us  [weight_gradient(): pl.pallas_call(functools.partial(weight_kernel, taps=taps, tile=min(1024,...]
    ppermute x15 -> x21, starting transfers between devices: 18.2 us -> 20.3 us  [swap(): return lax.ppermute(block, axis, [(i, i ^ flip) for i in range(count)])]
    ppermute x15 -> x21, waiting for transfers between devices: 30.1 us -> 28.9 us  [swap(): return lax.ppermute(block, axis, [(i, i ^ flip) for i in range(count)])]
    pallas_call x1 -> x2, Pallas kernels: 8.5 us -> 8.44 us  [pieces_gradient(): pl.pallas_call(functools.partial(pieces_kernel, taps=taps, pieces=len(par...]
  transfers between devices with their start and end apart: 21 -> 29, of which waited for: 12 -> 14; matrix products, arithmetic and copies ran while one was open for 2% -> 1% of each run, Pallas kernels for 13% -> 19%
where the time goes in v5:
time: 116 us; the launch traced here: 115 us
  waiting for transfers between devices  37.3 us (32%)
  starting transfers between devices  36.6 us (32%)
  Pallas kernels  29.1 us (25%)
  local copies, waits for them, and re-layouts  10.4 us (9%)
  between operations  1.21 us (1%)
    ppermute x21, waiting for transfers between devices, swap(): return lax.ppermute(block, axis, [(i, i ^ flip) for i in range(count)])  28.9 us
    ppermute x21, starting transfers between devices, swap(): return lax.ppermute(block, axis, [(i, i ^ flip) for i in range(count)])  20.3 us
    ppermute x8, starting transfers between devices, shift(): return lax.ppermute(block, axis, pairs)  16.3 us
    pallas_call x3, Pallas kernels, weight_gradient(): pl.pallas_call(functools.partial(weight_kernel, taps=taps, tile=min(1024,...  15.9 us
    pallas_call x2, Pallas kernels, pieces_gradient(): pl.pallas_call(functools.partial(pieces_kernel, taps=taps, pieces=len(par...  8.44 us
    ppermute x8, waiting for transfers between devices, shift(): return lax.ppermute(block, axis, pairs)  8.37 us
    unnamed x36, local copies, waits for them, and re-layouts  8.16 us
  transfers between devices with their start and end apart: 29, of which 14 were waited for; matrix products, arithmetic and copies ran while one was open for 1% of the time, Pallas kernels for 19%

profile of v5, /device:TPU:0, one launch (start us, length us, event | category | flops | bytes accessed | tf_op | source)
XLA Modules:
  0.0 115.1 jit_solution(1487316482954029858)
XLA Ops:
  0.7 1.3 %fusion.6 = (bf16[512,384]{1,0:T(8,128)(2,1)S(1)}, bf16[512,384]{1,0:T(8,128)(2,1)S(1)}) fusion(bf16[1024,384]{1,0:T(8,128)(2,1)} %refs_0_.3), kind=kLoop, calls=%fused_computation.27 | loop fusion | bytes 1572864 | tf_op jit(solution)/shard_map/slice | solution.py:509
  1.9 5.0 %collective-permute-start.3 = (bf16[512,384]{1,0:T(8,128)(2,1)S(1)}, bf16[512,384]{1,0:T(8,128)(2,1)S(1)}, u32[]{:S(2)}, u32[]{:S(2)}) collective-permute-start(bf16[512,384]{1,0:T(8,128)(2,1)S(1)} %get-tuple-element.93), channel_id=1, source_target_pairs={{0,4},{4,8},{8,12},{1,5},{5,9},{9,13},{2,6},{6,10},{10,14},{3,7},{... | collective-permute-start | bytes 1179656 | tf_op jit(solution)/shard_map/ppermute | solution.py:32
  6.9 1.3 %collective-permute-start.4 = (bf16[512,384]{1,0:T(8,128)(2,1)S(1)}, bf16[512,384]{1,0:T(8,128)(2,1)S(1)}, u32[]{:S(2)}, u32[]{:S(2)}) collective-permute-start(bf16[512,384]{1,0:T(8,128)(2,1)S(1)} %get-tuple-element.93), channel_id=1, source_target_pairs={{4,0},{8,4},{12,8},{5,1},{9,5},{13,9},{6,2},{10,6},{14,10},{7,3},{... | collective-permute-start | bytes 1179656 | tf_op jit(solution)/shard_map/ppermute | solution.py:32
  10.7 1.3 %shard_map.86 = (bf16[64,384]{1,0:T(8,128)(2,1)S(1)}, bf16[64,384]{1,0:T(8,128)(2,1)S(1)}, bf16[64,384]{1,0:T(8,128)(2,1)S(1)}, bf16[64,384]{1,0:T(8,128)(2,1)S(1)}) custom-call(s32[16]{0:T(128)S(1)} %copy-done.14, s32[2,16]{1,0:T(2,128)S(1)} %bitcast.10, bf16[1024,384]{1,0:T(8,128)(2,1)S(1)} %copy-done.10), custom_call_target="tpu_custom_call" | custom-call | flops 1000 | bytes 1000 | tf_op jit(solution)/shard_map/pallas_call | solution.py:344
  12.0 2.7 %collective-permute-start = (bf16[64,384]{1,0:T(8,128)(2,1)S(1)}, bf16[64,384]{1,0:T(8,128)(2,1)S(1)}, u32[]{:S(2)}, u32[]{:S(2)}) collective-permute-start(bf16[64,384]{1,0:T(8,128)(2,1)S(1)} %get-tuple-element.41), channel_id=1, source_target_pairs={{0,4},{4,0},{8,12},{12,8},{1,5},{5,1},{9,13},{13,9},{2,6},{6,2},{1... | collective-permute-start | bytes 147464 | tf_op jit(solution)/shard_map/ppermute | solution.py:23
  14.7 2.7 %collective-permute-start.1 = (bf16[64,384]{1,0:T(8,128)(2,1)S(1)}, bf16[64,384]{1,0:T(8,128)(2,1)S(1)}, u32[]{:S(2)}, u32[]{:S(2)}) collective-permute-start(bf16[64,384]{1,0:T(8,128)(2,1)S(1)} %get-tuple-element.42), channel_id=1, source_target_pairs={{0,8},{4,12},{8,0},{12,4},{1,9},{5,13},{9,1},{13,5},{2,10},{6,14},... | collective-permute-start | bytes 147464 | tf_op jit(solution)/shard_map/ppermute | solution.py:23
  18.3 1.5 %shard_map.87 = (f32[1024,384]{1,0:T(8,128)S(1)}, bf16[1024,384]{1,0:T(8,128)(2,1)S(1)}) custom-call(bf16[1024,384]{1,0:T(8,128)(2,1)S(1)} %copy-done.10, bf16[512,384]{1,0:T(8,128)(2,1)S(1)} %copy-done.11), custom_call_target="tpu_custom_call" | custom-call | flops 1000 | bytes 1000 | tf_op jit(solution)/shard_map/pallas_call | solution.py:371
  20.9 2.0 %collective-permute-done.1 = bf16[64,384]{1,0:T(8,128)(2,1)S(1)} collective-permute-done((bf16[64,384]{1,0:T(8,128)(2,1)S(1)}, bf16[64,384]{1,0:T(8,128)(2,1)S(1)}, u32[]{:S(2)}, u32[]{:S(2)}) %collective-permute-start.1) | collective-permute-done | bytes 49184 | tf_op jit(solution)/shard_map/ppermute | solution.py:23
  22.9 2.1 %collective-permute-done.2 = bf16[64,384]{1,0:T(8,128)(2,1)S(1)} collective-permute-done((bf16[64,384]{1,0:T(8,128)(2,1)S(1)}, bf16[64,384]{1,0:T(8,128)(2,1)S(1)}, u32[]{:S(2)}, u32[]{:S(2)}) %collective-permute-start.2) | collective-permute-done | bytes 49184 | tf_op jit(solution)/shard_map/ppermute | solution.py:23
  25.3 4.3 %collective-permute-start.7 = (bf16[64,384]{1,0:T(8,128)(2,1)S(1)}, bf16[64,384]{1,0:T(8,128)(2,1)S(1)}, u32[]{:S(2)}, u32[]{:S(2)}) collective-permute-start(bf16[64,384]{1,0:T(8,128)(2,1)S(1)} %fusion.1.refs_0_), channel_id=1, source_target_pairs={{0,12},{4,8},{8,4},{12,0},{1,13},{5,9},{9,5},{13,1},{2,14},{6,10},... | collective-permute-start | bytes 147464 | tf_op jit(solution)/shard_map/ppermute | solution.py:23
  30.2 1.9 %collective-permute-done.7.refs_3_ = bf16[64,384]{1,0:T(8,128)(2,1)S(1)} collective-permute-done((bf16[64,384]{1,0:T(8,128)(2,1)S(1)}, bf16[64,384]{1,0:T(8,128)(2,1)S(1)}, u32[]{:S(2)}, u32[]{:S(2)}) %collective-permute-start.7) | collective-permute-done | bytes 49184 | tf_op jit(solution)/shard_map/ppermute | solution.py:23
  32.1 1.3 %collective-permute-start.12 = (bf16[512,384]{1,0:T(8,128)(2,1)S(1)}, bf16[512,384]{1,0:T(8,128)(2,1)S(1)}, u32[]{:S(2)}, u32[]{:S(2)}) collective-permute-start(bf16[512,384]{1,0:T(8,128)(2,1)S(1)} %get-tuple-element.53), channel_id=1, source_target_pairs={{4,0},{8,4},{12,8},{5,1},{9,5},{13,9},{6,2},{10,6},{14,10},{7,3},{... | collective-permute-start | bytes 1179656 | tf_op jit(solution)/shard_map/ppermute | solution.py:32
  33.4 4.6 %collective-permute-start.10 = (bf16[512,384]{1,0:T(8,128)(2,1)S(1)}, bf16[512,384]{1,0:T(8,128)(2,1)S(1)}, u32[]{:S(2)}, u32[]{:S(2)}) collective-permute-start(bf16[512,384]{1,0:T(8,128)(2,1)S(1)} %get-tuple-element.53), channel_id=1, source_target_pairs={{0,4},{4,8},{8,12},{1,5},{5,9},{9,13},{2,6},{6,10},{10,14},{3,7},{... | collective-permute-start | bytes 1179656 | tf_op jit(solution)/shard_map/ppermute | solution.py:32
  38.1 1.9 %shard_map.88.refs_0_ = bf16[1024,384]{1,0:T(8,128)(2,1)S(1)} custom-call(s32[16]{0:T(128)S(1)} %copy-done.14, s32[2,16]{1,0:T(2,128)S(1)} %bitcast.11, bf16[512,384]{1,0:T(8,128)(2,1)S(1)} %copy-done.12, f32[1024,384]{1,0:T(8,128)S(1)} %get-tuple-element.46.slope, bf16[1024,384]{1,0:T(8,128)(2,1)S(1)} %get-tuple-element.47.plain, ...), custom_call_target="tpu_custom_call" | custom-call | tf_op jit(solution)/shard_map/pallas_call | solution.py:410
  40.1 1.6 %collective-permute-start.8 = (bf16[1024,384]{1,0:T(8,128)(2,1)S(1)}, bf16[1024,384]{1,0:T(8,128)(2,1)S(1)}, u32[]{:S(2)}, u32[]{:S(2)}) collective-permute-start(bf16[1024,384]{1,0:T(8,128)(2,1)S(1)} %shard_map.88.refs_0_), channel_id=1, source_target_pairs={{0,2},{1,3},{2,0},{3,1},{4,6},{5,7},{6,4},{7,5},{8,10},{9,11},{10,... | collective-permute-start | bytes 2359304 | tf_op jit(solution)/shard_map/ppermute | solution.py:23
  41.9 1.3 %collective-permute-start.13 = (bf16[1024,384]{1,0:T(8,128)(2,1)S(1)}, bf16[1024,384]{1,0:T(8,128)(2,1)S(1)}, u32[]{:S(2)}, u32[]{:S(2)}) collective-permute-start(bf16[1024,384]{1,0:T(8,128)(2,1)S(1)} %constant_dynamic-update-slice_fusion.2.refs_2_), channel_id=1, source_target_pairs={{4,0},{8,4},{5,1},{9,5},{6,2},{10,6},{7,3},{11,7},{20,16},{24,20},... | collective-permute-start | bytes 2359304 | tf_op jit(solution)/shard_map/ppermute | solution.py:32
  44.9 10.5 %collective-permute-done.8.refs_2_ = bf16[1024,384]{1,0:T(8,128)(2,1)S(1)} collective-permute-done((bf16[1024,384]{1,0:T(8,128)(2,1)S(1)}, bf16[1024,384]{1,0:T(8,128)(2,1)S(1)}, u32[]{:S(2)}, u32[]{:S(2)}) %collective-permute-start.8) | collective-permute-done | bytes 786464 | tf_op jit(solution)/shard_map/ppermute | solution.py:23
  55.5 8.1 %collective-permute-done.13.refs_4_ = bf16[1024,384]{1,0:T(8,128)(2,1)S(1)} collective-permute-done((bf16[1024,384]{1,0:T(8,128)(2,1)S(1)}, bf16[1024,384]{1,0:T(8,128)(2,1)S(1)}, u32[]{:S(2)}, u32[]{:S(2)}) %collective-permute-start.13) | collective-permute-done | bytes 786464 | tf_op jit(solution)/shard_map/ppermute | solution.py:32
  66.4 1.3 %collective-permute-start.15 = (bf16[272,384]{1,0:T(8,128)(2,1)S(1)}, bf16[272,384]{1,0:T(8,128)(2,1)S(1)}, u32[]{:S(2)}, u32[]{:S(2)}) collective-permute-start(bf16[272,384]{1,0:T(8,128)(2,1)S(1)} %get-tuple-element.63), channel_id=1, source_target_pairs={{0,4},{4,0},{8,12},{12,8},{1,5},{5,1},{9,13},{13,9},{2,6},{6,2},{1... | collective-permute-start | bytes 626696 | tf_op jit(solution)/shard_map/ppermute | solution.py:23
  67.7 2.2 %collective-permute-start.17 = (bf16[256,384]{1,0:T(8,128)(2,1)S(1)}, bf16[256,384]{1,0:T(8,128)(2,1)S(1)}, u32[]{:S(2)}, u32[]{:S(2)}) collective-permute-start(bf16[256,384]{1,0:T(8,128)(2,1)S(1)} %get-tuple-element.67), channel_id=1, source_target_pairs={{0,8},{4,12},{8,0},{12,4},{1,9},{5,13},{9,1},{13,5},{2,10},{6,14},... | collective-permute-start | bytes 589832 | tf_op jit(solution)/shard_map/ppermute | solution.py:23
  70.1 2.7 %copy-done.1 = bf16[1536,5,384]{2,0,1:T(8,128)(2,1)S(1)} copy-done((bf16[1536,5,384]{2,0,1:T(8,128)(2,1)S(1)}, bf16[1536,5,384]{2,0,1:T(8,128)(2,1)}, u32[]{:S(2)}) %copy-start.1) | copy-done | bytes 5898264
  72.8 2.8 %shard_map.89 = (f32[384,1920]{1,0:T(8,128)S(1)}, bf16[1536,1920]{1,0:T(8,128)(2,1)S(1)}) custom-call(bf16[16,384]{1,0:T(8,128)(2,1)S(1)} %slice.58.refs_0_, bf16[1024,384]{1,0:T(8,128)(2,1)S(1)} %copy-done, bf16[16,384]{1,0:T(8,128)(2,1)S(1)} %slice.57.refs_2_, bf16[1024,384]{1,0:T(8,128)(2,1)S(1)} %select_select_fusion.refs_3_, ...), custom_call_target="tpu_custom_call" | custom-call | flops 1000 | bytes 1000 | tf_op jit(solution)/shard_map/pallas_call | solution.py:242
  75.6 3.7 %shard_map.90.refs_6_ = bf16[512,384]{1,0:T(8,128)(2,1)S(1)} custom-call(bf16[1024,384]{1,0:T(8,128)(2,1)S(1)} %shard_map.88.refs_0_, bf16[1024,384]{1,0:T(8,128)(2,1)S(1)} %collective-permute-done.9.refs_1_, bf16[1024,384]{1,0:T(8,128)(2,1)S(1)} %collective-permute-done.8.refs_2_, bf16[1024,384]{1,0:T(8,128)(2,1)S(1)} %collective-permute-done.14.refs_3_, ...), custom_call_target="tpu_custom_call" | custom-call | flops 1000 | bytes 1000 | tf_op jit(solution)/shard_map/pallas_call | solution.py:123
  79.3 1.2 %collective-permute-start.19 = (bf16[272,384]{1,0:T(8,128)(2,1)S(1)}, bf16[272,384]{1,0:T(8,128)(2,1)S(1)}, u32[]{:S(2)}, u32[]{:S(2)}) collective-permute-start(bf16[272,384]{1,0:T(8,128)(2,1)S(1)} %get-tuple-element.68), channel_id=1, source_target_pairs={{0,12},{4,8},{8,4},{12,0},{1,13},{5,9},{9,5},{13,1},{2,14},{6,10},... | collective-permute-start | bytes 626696 | tf_op jit(solution)/shard_map/ppermute | solution.py:23
  81.3 1.5 %collective-permute-start.22 = (bf16[1024,384]{1,0:T(8,128)(2,1)S(1)}, bf16[1024,384]{1,0:T(8,128)(2,1)S(1)}, u32[]{:S(2)}, u32[]{:S(2)}) collective-permute-start(bf16[1024,384]{1,0:T(8,128)(2,1)S(1)} %copy-done.7), channel_id=1, source_target_pairs={{4,0},{5,1},{6,2},{7,3},{20,16},{21,17},{22,18},{23,19}} | collective-permute-start | bytes 2359304 | tf_op jit(solution)/shard_map/ppermute | solution.py:32
  83.4 1.5 %collective-permute-start.16 = (bf16[272,384]{1,0:T(8,128)(2,1)S(1)}, bf16[272,384]{1,0:T(8,128)(2,1)S(1)}, u32[]{:S(2)}, u32[]{:S(2)}) collective-permute-start(bf16[272,384]{1,0:T(8,128)(2,1)S(1)} %collective-permute-done.15.refs_5_), channel_id=1, source_target_pairs={{0,2},{1,3},{2,0},{3,1},{4,6},{5,7},{6,4},{7,5},{8,10},{9,11},{10,... | collective-permute-start | bytes 626696 | tf_op jit(solution)/shard_map/ppermute | solution.py:23
  84.9 3.2 %collective-permute-done.19.refs_11_ = bf16[272,384]{1,0:T(8,128)(2,1)S(1)} collective-permute-done((bf16[272,384]{1,0:T(8,128)(2,1)S(1)}, bf16[272,384]{1,0:T(8,128)(2,1)S(1)}, u32[]{:S(2)}, u32[]{:S(2)}) %collective-permute-start.19) | collective-permute-done | bytes 208928 | tf_op jit(solution)/shard_map/ppermute | solution.py:23
  88.1 2.5 %collective-permute-done.18.refs_11_.refs_9_ = bf16[256,384]{1,0:T(8,128)(2,1)S(1)} collective-permute-done((bf16[256,384]{1,0:T(8,128)(2,1)S(1)}, bf16[256,384]{1,0:T(8,128)(2,1)S(1)}, u32[]{:S(2)}, u32[]{:S(2)}) %collective-permute-start.18) | collective-permute-done | bytes 196640 | tf_op jit(solution)/shard_map/ppermute | solution.py:23
  91.3 3.8 %collective-permute-done.16.refs_7_ = bf16[272,384]{1,0:T(8,128)(2,1)S(1)} collective-permute-done((bf16[272,384]{1,0:T(8,128)(2,1)S(1)}, bf16[272,384]{1,0:T(8,128)(2,1)S(1)}, u32[]{:S(2)}, u32[]{:S(2)}) %collective-permute-start.16) | collective-permute-done | bytes 208928 | tf_op jit(solution)/shard_map/ppermute | solution.py:23
  95.1 4.8 %shard_map.91 = bf16[1024,384]{1,0:T(8,128)(2,1)} custom-call(bf16[1024,384]{1,0:T(8,128)(2,1)S(1)} %shard_map.88.refs_0_, bf16[1024,384]{1,0:T(8,128)(2,1)S(1)} %collective-permute-done.9.refs_1_, bf16[1024,384]{1,0:T(8,128)(2,1)S(1)} %collective-permute-done.8.refs_2_, bf16[1024,384]{1,0:T(8,128)(2,1)S(1)} %collective-permute-done.14.refs_3_, ...), custom_call_target="tpu_custom_call" | custom-call | flops 1000 | bytes 1000 | tf_op jit(solution)/shard_map/pallas_call | solution.py:123
  101.9 6.4 %shard_map.92.refs_15_ = f32[384,1920]{1,0:T(8,128)S(1)} custom-call(bf16[1024,384]{1,0:T(8,128)(2,1)S(1)} %copy-done, bf16[1024,384]{1,0:T(8,128)(2,1)S(1)} %copy-done.3, bf16[1024,384]{1,0:T(8,128)(2,1)S(1)} %copy-done.5, bf16[1024,384]{1,0:T(8,128)(2,1)S(1)} %copy-done.9, bf16[1024,384]{1,0:T(8,128)(2,1)S(1)} %copy-done.7, ...), custom_call_target="tpu_custom_call" | custom-call | flops 1000 | bytes 1000 | tf_op jit(solution)/shard_map/pallas_call | solution.py:242
  108.3 6.7 %shard_map.93 = bf16[5,384,384]{2,1,0:T(8,128)(2,1)} custom-call(bf16[1024,384]{1,0:T(8,128)(2,1)S(1)} %copy-done, bf16[1024,384]{1,0:T(8,128)(2,1)S(1)} %copy-done.3, bf16[1024,384]{1,0:T(8,128)(2,1)S(1)} %copy-done.5, bf16[1024,384]{1,0:T(8,128)(2,1)S(1)} %copy-done.9, bf16[1024,384]{1,0:T(8,128)(2,1)S(1)} %copy-done.7, ...), custom_call_target="tpu_custom_call" | custom-call | flops 1000 | bytes 1000 | tf_op jit(solution)/shard_map/pallas_call | solution.py:242
  (90 shorter events, 14.4 us)
Async XLA Ops:
  0.6 37.5 %copy-start.12 = (bf16[512,384]{1,0:T(8,128)(2,1)S(1)}, bf16[512,384]{1,0:T(8,128)(2,1)}, u32[]{:S(2)}) copy-start(bf16[512,384]{1,0:T(8,128)(2,1)} %out_grad.3) | copy-start | bytes 1179652
  0.6 24.4 %copy-start.16 = (f32[1,8,8,384]{3,2,1,0:T(8,128)S(1)}, f32[1,8,8,384]{3,2,1,0:T(8,128)}, u32[]{:S(2)}) copy-start(f32[1,8,8,384]{3,2,1,0:T(8,128)} %param.11) | copy-start | bytes 294916
  1.9 23.1 %collective-permute-start.3 = (bf16[512,384]{1,0:T(8,128)(2,1)S(1)}, bf16[512,384]{1,0:T(8,128)(2,1)S(1)}, u32[]{:S(2)}, u32[]{:S(2)}) collective-permute-start(bf16[512,384]{1,0:T(8,128)(2,1)S(1)} %get-tuple-element.93), channel_id=1, source_target_pairs={{0,4},{4,8},{8,12},{1,5},{5,9},{9,13},{2,6},{6,10},{10,14},{3,7},{... | collective-permute-start | bytes 1179656 | tf_op jit(solution)/shard_map/ppermute | solution.py:32
  6.9 18.2 %collective-permute-start.4 = (bf16[512,384]{1,0:T(8,128)(2,1)S(1)}, bf16[512,384]{1,0:T(8,128)(2,1)S(1)}, u32[]{:S(2)}, u32[]{:S(2)}) collective-permute-start(bf16[512,384]{1,0:T(8,128)(2,1)S(1)} %get-tuple-element.93), channel_id=1, source_target_pairs={{4,0},{8,4},{12,8},{5,1},{9,5},{13,9},{6,2},{10,6},{14,10},{7,3},{... | collective-permute-start | bytes 1179656 | tf_op jit(solution)/shard_map/ppermute | solution.py:32
  12.0 9.0 %collective-permute-start = (bf16[64,384]{1,0:T(8,128)(2,1)S(1)}, bf16[64,384]{1,0:T(8,128)(2,1)S(1)}, u32[]{:S(2)}, u32[]{:S(2)}) collective-permute-start(bf16[64,384]{1,0:T(8,128)(2,1)S(1)} %get-tuple-element.41), channel_id=1, source_target_pairs={{0,4},{4,0},{8,12},{12,8},{1,5},{5,1},{9,13},{13,9},{2,6},{6,2},{1... | collective-permute-start | bytes 147464 | tf_op jit(solution)/shard_map/ppermute | solution.py:23
  14.7 8.2 %collective-permute-start.1 = (bf16[64,384]{1,0:T(8,128)(2,1)S(1)}, bf16[64,384]{1,0:T(8,128)(2,1)S(1)}, u32[]{:S(2)}, u32[]{:S(2)}) collective-permute-start(bf16[64,384]{1,0:T(8,128)(2,1)S(1)} %get-tuple-element.42), channel_id=1, source_target_pairs={{0,8},{4,12},{8,0},{12,4},{1,9},{5,13},{9,1},{13,5},{2,10},{6,14},... | collective-permute-start | bytes 147464 | tf_op jit(solution)/shard_map/ppermute | solution.py:23
  17.3 7.7 %collective-permute-start.2 = (bf16[64,384]{1,0:T(8,128)(2,1)S(1)}, bf16[64,384]{1,0:T(8,128)(2,1)S(1)}, u32[]{:S(2)}, u32[]{:S(2)}) collective-permute-start(bf16[64,384]{1,0:T(8,128)(2,1)S(1)} %get-tuple-element.43), channel_id=1, source_target_pairs={{0,12},{4,8},{8,4},{12,0},{1,13},{5,9},{9,5},{13,1},{2,14},{6,10},... | collective-permute-start | bytes 147464 | tf_op jit(solution)/shard_map/ppermute | solution.py:23
  25.1 4.5 %collective-permute-start.5 = (bf16[64,384]{1,0:T(8,128)(2,1)S(1)}, bf16[64,384]{1,0:T(8,128)(2,1)S(1)}, u32[]{:S(2)}, u32[]{:S(2)}) collective-permute-start(bf16[64,384]{1,0:T(8,128)(2,1)S(1)} %fusion.1.refs_0_), channel_id=1, source_target_pairs={{0,4},{4,0},{8,12},{12,8},{1,5},{5,1},{9,13},{13,9},{2,6},{6,2},{1... | collective-permute-start | bytes 147464 | tf_op jit(solution)/shard_map/ppermute | solution.py:23
  25.2 5.1 %collective-permute-start.6 = (bf16[64,384]{1,0:T(8,128)(2,1)S(1)}, bf16[64,384]{1,0:T(8,128)(2,1)S(1)}, u32[]{:S(2)}, u32[]{:S(2)}) collective-permute-start(bf16[64,384]{1,0:T(8,128)(2,1)S(1)} %fusion.1.refs_0_), channel_id=1, source_target_pairs={{0,8},{4,12},{8,0},{12,4},{1,9},{5,13},{9,1},{13,5},{2,10},{6,14},... | collective-permute-start | bytes 147464 | tf_op jit(solution)/shard_map/ppermute | solution.py:23
  25.3 6.9 %collective-permute-start.7 = (bf16[64,384]{1,0:T(8,128)(2,1)S(1)}, bf16[64,384]{1,0:T(8,128)(2,1)S(1)}, u32[]{:S(2)}, u32[]{:S(2)}) collective-permute-start(bf16[64,384]{1,0:T(8,128)(2,1)S(1)} %fusion.1.refs_0_), channel_id=1, source_target_pairs={{0,12},{4,8},{8,4},{12,0},{1,13},{5,9},{9,5},{13,1},{2,14},{6,10},... | collective-permute-start | bytes 147464 | tf_op jit(solution)/shard_map/ppermute | solution.py:23
  32.1 9.7 %collective-permute-start.12 = (bf16[512,384]{1,0:T(8,128)(2,1)S(1)}, bf16[512,384]{1,0:T(8,128)(2,1)S(1)}, u32[]{:S(2)}, u32[]{:S(2)}) collective-permute-start(bf16[512,384]{1,0:T(8,128)(2,1)S(1)} %get-tuple-element.53), channel_id=1, source_target_pairs={{4,0},{8,4},{12,8},{5,1},{9,5},{13,9},{6,2},{10,6},{14,10},{7,3},{... | collective-permute-start | bytes 1179656 | tf_op jit(solution)/shard_map/ppermute | solution.py:32
  33.4 9.8 %collective-permute-start.10 = (bf16[512,384]{1,0:T(8,128)(2,1)S(1)}, bf16[512,384]{1,0:T(8,128)(2,1)S(1)}, u32[]{:S(2)}, u32[]{:S(2)}) collective-permute-start(bf16[512,384]{1,0:T(8,128)(2,1)S(1)} %get-tuple-element.53), channel_id=1, source_target_pairs={{0,4},{4,8},{8,12},{1,5},{5,9},{9,13},{2,6},{6,10},{10,14},{3,7},{... | collective-permute-start | bytes 1179656 | tf_op jit(solution)/shard_map/ppermute | solution.py:32
  40.1 15.4 %collective-permute-start.8 = (bf16[1024,384]{1,0:T(8,128)(2,1)S(1)}, bf16[1024,384]{1,0:T(8,128)(2,1)S(1)}, u32[]{:S(2)}, u32[]{:S(2)}) collective-permute-start(bf16[1024,384]{1,0:T(8,128)(2,1)S(1)} %shard_map.88.refs_0_), channel_id=1, source_target_pairs={{0,2},{1,3},{2,0},{3,1},{4,6},{5,7},{6,4},{7,5},{8,10},{9,11},{10,... | collective-permute-start | bytes 2359304 | tf_op jit(solution)/shard_map/ppermute | solution.py:23
  41.6 13.8 %collective-permute-start.9 = (bf16[1024,384]{1,0:T(8,128)(2,1)S(1)}, bf16[1024,384]{1,0:T(8,128)(2,1)S(1)}, u32[]{:S(2)}, u32[]{:S(2)}) collective-permute-start(bf16[1024,384]{1,0:T(8,128)(2,1)S(1)} %shard_map.88.refs_0_), channel_id=1, source_target_pairs={{0,1},{1,0},{2,3},{3,2},{4,5},{5,4},{6,7},{7,6},{8,9},{9,8},{10,11... | collective-permute-start | bytes 2359304 | tf_op jit(solution)/shard_map/ppermute | solution.py:23
  41.9 21.7 %copy-start.4 = (bf16[1024,384]{1,0:T(8,128)(2,1)}, bf16[1024,384]{1,0:T(8,128)(2,1)S(1)}, u32[]{:S(2)}) copy-start(bf16[1024,384]{1,0:T(8,128)(2,1)S(1)} %constant_dynamic-update-slice_fusion.2.refs_2_) | copy-start | bytes 2359300
  41.9 21.7 %collective-permute-start.13 = (bf16[1024,384]{1,0:T(8,128)(2,1)S(1)}, bf16[1024,384]{1,0:T(8,128)(2,1)S(1)}, u32[]{:S(2)}, u32[]{:S(2)}) collective-permute-start(bf16[1024,384]{1,0:T(8,128)(2,1)S(1)} %constant_dynamic-update-slice_fusion.2.refs_2_), channel_id=1, source_target_pairs={{4,0},{8,4},{5,1},{9,5},{6,2},{10,6},{7,3},{11,7},{20,16},{24,20},... | collective-permute-start | bytes 2359304 | tf_op jit(solution)/shard_map/ppermute | solution.py:32
  43.3 20.2 %collective-permute-start.11 = (bf16[1024,384]{1,0:T(8,128)(2,1)S(1)}, bf16[1024,384]{1,0:T(8,128)(2,1)S(1)}, u32[]{:S(2)}, u32[]{:S(2)}) collective-permute-start(bf16[1024,384]{1,0:T(8,128)(2,1)S(1)} %constant_dynamic-update-slice_fusion.refs_1_), channel_id=1, source_target_pairs={{4,8},{8,12},{5,9},{9,13},{6,10},{10,14},{7,11},{11,15},{20,24},{2... | collective-permute-start | bytes 2359304 | tf_op jit(solution)/shard_map/ppermute | solution.py:32
  63.6 2.4 %collective-permute-start.14 = (bf16[1024,384]{1,0:T(8,128)(2,1)S(1)}, bf16[1024,384]{1,0:T(8,128)(2,1)S(1)}, u32[]{:S(2)}, u32[]{:S(2)}) collective-permute-start(bf16[1024,384]{1,0:T(8,128)(2,1)S(1)} %collective-permute-done.8.refs_2_), channel_id=1, source_target_pairs={{0,1},{1,0},{2,3},{3,2},{4,5},{5,4},{6,7},{7,6},{8,9},{9,8},{10,11... | collective-permute-start | bytes 2359304 | tf_op jit(solution)/shard_map/ppermute | solution.py:23
  66.4 17.0 %collective-permute-start.15 = (bf16[272,384]{1,0:T(8,128)(2,1)S(1)}, bf16[272,384]{1,0:T(8,128)(2,1)S(1)}, u32[]{:S(2)}, u32[]{:S(2)}) collective-permute-start(bf16[272,384]{1,0:T(8,128)(2,1)S(1)} %get-tuple-element.63), channel_id=1, source_target_pairs={{0,4},{4,0},{8,12},{12,8},{1,5},{5,1},{9,13},{13,9},{2,6},{6,2},{1... | collective-permute-start | bytes 626696 | tf_op jit(solution)/shard_map/ppermute | solution.py:23
  67.7 15.0 %collective-permute-start.17 = (bf16[256,384]{1,0:T(8,128)(2,1)S(1)}, bf16[256,384]{1,0:T(8,128)(2,1)S(1)}, u32[]{:S(2)}, u32[]{:S(2)}) collective-permute-start(bf16[256,384]{1,0:T(8,128)(2,1)S(1)} %get-tuple-element.67), channel_id=1, source_target_pairs={{0,8},{4,12},{8,0},{12,4},{1,9},{5,13},{9,1},{13,5},{2,10},{6,14},... | collective-permute-start | bytes 589832 | tf_op jit(solution)/shard_map/ppermute | solution.py:23
  79.3 8.8 %collective-permute-start.19 = (bf16[272,384]{1,0:T(8,128)(2,1)S(1)}, bf16[272,384]{1,0:T(8,128)(2,1)S(1)}, u32[]{:S(2)}, u32[]{:S(2)}) collective-permute-start(bf16[272,384]{1,0:T(8,128)(2,1)S(1)} %get-tuple-element.68), channel_id=1, source_target_pairs={{0,12},{4,8},{8,4},{12,0},{1,13},{5,9},{9,5},{13,1},{2,14},{6,10},... | collective-permute-start | bytes 626696 | tf_op jit(solution)/shard_map/ppermute | solution.py:23
  80.5 27.7 %collective-permute-start.21 = (bf16[1024,384]{1,0:T(8,128)(2,1)S(1)}, bf16[1024,384]{1,0:T(8,128)(2,1)S(1)}, u32[]{:S(2)}, u32[]{:S(2)}) collective-permute-start(bf16[1024,384]{1,0:T(8,128)(2,1)S(1)} %copy-done.9), channel_id=1, source_target_pairs={{8,12},{9,13},{10,14},{11,15},{24,28},{25,29},{26,30},{27,31}} | collective-permute-start | bytes 2359304 | tf_op jit(solution)/shard_map/ppermute | solution.py:32
  81.3 27.0 %collective-permute-start.22 = (bf16[1024,384]{1,0:T(8,128)(2,1)S(1)}, bf16[1024,384]{1,0:T(8,128)(2,1)S(1)}, u32[]{:S(2)}, u32[]{:S(2)}) collective-permute-start(bf16[1024,384]{1,0:T(8,128)(2,1)S(1)} %copy-done.7), channel_id=1, source_target_pairs={{4,0},{5,1},{6,2},{7,3},{20,16},{21,17},{22,18},{23,19}} | collective-permute-start | bytes 2359304 | tf_op jit(solution)/shard_map/ppermute | solution.py:32
  82.8 7.9 %collective-permute-start.18 = (bf16[256,384]{1,0:T(8,128)(2,1)S(1)}, bf16[256,384]{1,0:T(8,128)(2,1)S(1)}, u32[]{:S(2)}, u32[]{:S(2)}) collective-permute-start(bf16[256,384]{1,0:T(8,128)(2,1)S(1)} %collective-permute-done.17.refs_9_.refs_7_), channel_id=1, source_target_pairs={{0,2},{1,3},{2,0},{3,1},{4,6},{5,7},{6,4},{7,5},{8,10},{9,11},{10,... | collective-permute-start | bytes 589832 | tf_op jit(solution)/shard_map/ppermute | solution.py:23
  83.4 11.8 %collective-permute-start.16 = (bf16[272,384]{1,0:T(8,128)(2,1)S(1)}, bf16[272,384]{1,0:T(8,128)(2,1)S(1)}, u32[]{:S(2)}, u32[]{:S(2)}) collective-permute-start(bf16[272,384]{1,0:T(8,128)(2,1)S(1)} %collective-permute-done.15.refs_5_), channel_id=1, source_target_pairs={{0,2},{1,3},{2,0},{3,1},{4,6},{5,7},{6,4},{7,5},{8,10},{9,11},{10,... | collective-permute-start | bytes 626696 | tf_op jit(solution)/shard_map/ppermute | solution.py:23
  88.1 12.4 %collective-permute-start.27 = (bf16[272,384]{1,0:T(8,128)(2,1)S(1)}, bf16[272,384]{1,0:T(8,128)(2,1)S(1)}, u32[]{:S(2)}, u32[]{:S(2)}) collective-permute-start(bf16[272,384]{1,0:T(8,128)(2,1)S(1)} %collective-permute-done.15.refs_5_), channel_id=1, source_target_pairs={{0,1},{1,0},{2,3},{3,2},{4,5},{5,4},{6,7},{7,6},{8,9},{9,8},{10,11... | collective-permute-start | bytes 626696 | tf_op jit(solution)/shard_map/ppermute | solution.py:23
  90.6 9.3 %collective-permute-start.20 = (bf16[272,384]{1,0:T(8,128)(2,1)S(1)}, bf16[272,384]{1,0:T(8,128)(2,1)S(1)}, u32[]{:S(2)}, u32[]{:S(2)}) collective-permute-start(bf16[272,384]{1,0:T(8,128)(2,1)S(1)} %collective-permute-done.19.refs_11_), channel_id=1, source_target_pairs={{0,2},{1,3},{2,0},{3,1},{4,6},{5,7},{6,4},{7,5},{8,10},{9,11},{10,... | collective-permute-start | bytes 626696 | tf_op jit(solution)/shard_map/ppermute | solution.py:23
  95.1 5.3 %collective-permute-start.23 = (bf16[256,384]{1,0:T(8,128)(2,1)S(1)}, bf16[256,384]{1,0:T(8,128)(2,1)S(1)}, u32[]{:S(2)}, u32[]{:S(2)}) collective-permute-start(bf16[256,384]{1,0:T(8,128)(2,1)S(1)} %collective-permute-done.17.refs_9_.refs_7_), channel_id=1, source_target_pairs={{0,1},{1,0},{2,3},{3,2},{4,5},{5,4},{6,7},{7,6},{8,9},{9,8},{10,11... | collective-permute-start | bytes 589832 | tf_op jit(solution)/shard_map/ppermute | solution.py:23
  99.9 1.6 %collective-permute-start.24 = (bf16[256,384]{1,0:T(8,128)(2,1)S(1)}, bf16[256,384]{1,0:T(8,128)(2,1)S(1)}, u32[]{:S(2)}, u32[]{:S(2)}) collective-permute-start(bf16[256,384]{1,0:T(8,128)(2,1)S(1)} %collective-permute-done.18.refs_11_.refs_9_), channel_id=1, source_target_pairs={{0,1},{1,0},{2,3},{3,2},{4,5},{5,4},{6,7},{7,6},{8,9},{9,8},{10,11... | collective-permute-start | bytes 589832 | tf_op jit(solution)/shard_map/ppermute | solution.py:23
  100.4 1.5 %collective-permute-start.28 = (bf16[272,384]{1,0:T(8,128)(2,1)S(1)}, bf16[272,384]{1,0:T(8,128)(2,1)S(1)}, u32[]{:S(2)}, u32[]{:S(2)}) collective-permute-start(bf16[272,384]{1,0:T(8,128)(2,1)S(1)} %collective-permute-done.16.refs_7_), channel_id=1, source_target_pairs={{0,1},{1,0},{2,3},{3,2},{4,5},{5,4},{6,7},{7,6},{8,9},{9,8},{10,11... | collective-permute-start | bytes 626696 | tf_op jit(solution)/shard_map/ppermute | solution.py:23
  100.5 7.8 %collective-permute-start.25 = (bf16[272,384]{1,0:T(8,128)(2,1)S(1)}, bf16[272,384]{1,0:T(8,128)(2,1)S(1)}, u32[]{:S(2)}, u32[]{:S(2)}) collective-permute-start(bf16[272,384]{1,0:T(8,128)(2,1)S(1)} %collective-permute-done.19.refs_11_), channel_id=1, source_target_pairs={{0,1},{1,0},{2,3},{3,2},{4,5},{5,4},{6,7},{7,6},{8,9},{9,8},{10,11... | collective-permute-start | bytes 626696 | tf_op jit(solution)/shard_map/ppermute | solution.py:23
  101.5 6.8 %collective-permute-start.26 = (bf16[272,384]{1,0:T(8,128)(2,1)S(1)}, bf16[272,384]{1,0:T(8,128)(2,1)S(1)}, u32[]{:S(2)}, u32[]{:S(2)}) collective-permute-start(bf16[272,384]{1,0:T(8,128)(2,1)S(1)} %collective-permute-done.20.refs_13_), channel_id=1, source_target_pairs={{0,1},{1,0},{2,3},{3,2},{4,5},{5,4},{6,7},{7,6},{8,9},{9,8},{10,11... | collective-permute-start | bytes 626696 | tf_op jit(solution)/shard_map/ppermute | solution.py:23
  (14 other events, 65.3 us)

commit v6 on v5

--- a/solution.py
+++ b/solution.py
@@ -15,6 +15,7 @@
 HALF_ROOT = 0.7071067811865476
 DENSITY = 0.3989422804014327
 LANES = 128
+GAINF = 1000
 LITTLE = pl.CostEstimate(flops=1000, bytes_accessed=1000, transcendentals=0)
 
 
@@ -78,7 +79,7 @@
     if middle:
         weights, out, block = rest
     else:
-        low, high, center, weights, out, block = rest
+        near_edge, far_edge, center, weights, out, block = rest
     rows = parts[0].shape[0]
     width = weights.shape[1] // taps
     half = taps // 2
@@ -89,10 +90,19 @@
         span = pl.ds(base, part.shape[1])
         for begin, count in kept:
             block[pl.ds(PAD + begin, count), span] = part[pl.ds(begin, count), :]
-        if not middle:
-            block[pl.ds(0, PAD), span] = low[:, span]
-            block[pl.ds(PAD + rows, PAD), span] = high[:, span]
         base += part.shape[1]
+    if not middle:
+        mine = lax.axis_index("seq")
+        one = near_edge[pl.ds(quarter, PAD), :].astype(jnp.float32)
+        other = far_edge[pl.ds(quarter, PAD), :].astype(jnp.float32)
+        low = jnp.where(mine % 2 == 1, one, jnp.where(mine == 2, other, 0.0))
+        high = jnp.where(mine % 2 == 0, one, jnp.where(mine == 1, other, 0.0))
+        for at in range(pieces):
+            span = pl.ds(at * part.shape[1], part.shape[1])
+            lower = pltpu.roll(low, PAD - half - half * at, 0)
+            upper = pltpu.roll(high, (PAD - half * at) % PAD, 0)
+            block[pl.ds(0, PAD), span] = lower.astype(block.dtype)
+            block[pl.ds(PAD + rows, PAD), span] = upper.astype(block.dtype)
 
     def tile(start, count):
         terms = jnp.dot(
@@ -315,7 +325,7 @@
 
             @pl.when(where // nblocks == mine)
             def _():
-                act(slot, where % nblocks)
+                act(t, slot, where % nblocks)
 
         return carry
 
@@ -326,7 +336,7 @@
     outs, (slots, pair, seen) = refs[:-3], refs[-3:]
     slots[...] = jnp.zeros_like(slots)
 
-    def act(slot, block):
+    def act(t, slot, block):
         at = pl.ds(pl.multiple_of(block * (2 * size), 2 * size), 2 * size)
         value = pre_act[at, :].astype(jnp.float32)
         value = value * (0.5 * (1.0 + lax.erf(value * HALF_ROOT)))
@@ -382,37 +392,43 @@
     )(pre_act, out_grad)
 
 
-def gain_kernel(owners, exons, out_grad, slope, plain, *refs, nblocks, most, size):
+def gain_kernel(owners, exons, out_grad, slope, *refs, nblocks, most, size):
     splices, (grad, gain, held, both, seen) = refs[:-5], refs[-5:]
     gain[...] = out_grad[...].astype(jnp.float32)
-    grad[...] = plain[...]
     base = 0
     for splice in splices:
         held[pl.ds(base, splice.shape[0]), :] = splice[...].astype(jnp.float32)
         base += splice.shape[0]
 
-    def add(slot, block):
+    def add(t, slot, block):
         at = pl.ds(pl.multiple_of(block * size, size), size)
         gain[at, :] += held[pl.ds(pl.multiple_of(slot * size, size), size), :]
 
-    def renew(slot, block):
+    def final(block):
         pooled = 0.5 * gain[pl.ds(pl.multiple_of(block * size, size), size), :]
-        pooled = make_pairs(pooled, both)
         at = pl.ds(pl.multiple_of(block * (2 * size), 2 * size), 2 * size)
-        grad[at, :] = (pooled * slope[at, :]).astype(grad.dtype)
+        return make_pairs(pooled, both) * slope[at, :]
+
+    def renew(t, slot, block):
+        at = pl.ds(pl.multiple_of(t * (2 * size), 2 * size), 2 * size)
+        grad[at, :] = final(block).astype(grad.dtype)
 
     each_exon(owners, exons, seen, nblocks, most, add)
     each_exon(owners, exons, seen, nblocks, most, renew)
-
-
-def gained_gradient(owners, exons, out_grad, slope, plain, splices, most, size, groups):
+    count = exons.shape[1]
+    row = lax.broadcasted_iota(jnp.int32, (2 * size, grad.shape[1]), 0)
+    for at, block, first in ((count, 0, 0), (count + 1, nblocks - 1, 2 * size - 2)):
+        rows = final(block)
+        rows = jnp.where(row % 2 == 0, rows[first : first + 1], rows[first + 1 : first + 2])
+        grad[pl.ds(at * 2 * size, 2 * size), :] = rows.astype(grad.dtype)
+
+
+def gained_rows(owners, exons, out_grad, slope, splices, most, size, groups):
     rows, width = slope.shape
     return pl.pallas_call(
-        functools.partial(
-            gain_kernel, nblocks=rows // 2 // size, most=most, size=size
-        ),
-        out_shape=jax.ShapeDtypeStruct((rows, width), jnp.bfloat16),
-        in_specs=[SMEM] * 2 + [VMEM] * (3 + len(splices)),
+        functools.partial(gain_kernel, nblocks=rows // 2 // size, most=most, size=size),
+        out_shape=jax.ShapeDtypeStruct(((exons.shape[1] + 2) * 2 * size, width), jnp.bfloat16),
+        in_specs=[SMEM] * 2 + [VMEM] * (2 + len(splices)),
         out_specs=VMEM,
         scratch_shapes=[
             pltpu.VMEM((rows // 2, width), jnp.float32),
@@ -420,8 +436,81 @@
             pair_scratch(2 * size, width),
             pltpu.SMEM((groups,), jnp.int32),
         ],
+        cost_estimate=pl.CostEstimate(flops=GAINF, bytes_accessed=1000, transcendentals=0),
         compiler_params=pltpu.CompilerParams(vmem_limit_bytes=16 * MIB),
-    )(owners, exons, out_grad, slope, plain, *splices)
+    )(owners, exons, out_grad, slope, *splices)
+
+
+def mend_kernel(exons, *refs, pieces, nblocks, size):
+    gained, parts, sent, own = (
+        refs[pieces : 2 * pieces],
+        refs[2 * pieces : 3 * pieces],
+        refs[3 * pieces : -1],
+        refs[-1],
+    )
+    mine = lax.axis_index("seq")
+    place = lax.axis_index("ch")
+    span, count = exons.shape
+    rows = parts[0].shape[0]
+    quarter = rows // pieces
+
+    def body(t, carry):
+        for e in range(span):
+            where = exons[e, t]
+
+            @pl.when(where // nblocks == mine)
+            def _():
+                to = pl.ds(pl.multiple_of(where % nblocks * (2 * size), 2 * size), 2 * size)
+                at = pl.ds(pl.multiple_of(t * (2 * size), 2 * size), 2 * size)
+                for part, new in zip(parts, gained):
+                    part[to, :] = new[at, :]
+
+        return carry
+
+    lax.fori_loop(0, count, body, 0)
+    row = lax.broadcasted_iota(jnp.int32, (PAD, own.shape[1]), 0)
+    for d, out in enumerate(sent, 1):
+        for tag, part in enumerate(parts):
+
+            @pl.when(mine ^ d ^ place == tag)
+            def _():
+                at = pl.ds(pl.multiple_of(place * quarter, quarter), quarter)
+                out[pl.ds(0, quarter), :] = part[at, :]
+
+        if out.shape[0] > quarter:
+            after_me = (mine ^ d) > mine
+            edge = jnp.zeros(row.shape, jnp.float32)
+            for tag, new in enumerate(gained):
+                head = new[pl.ds(count * 2 * size, PAD), :].astype(jnp.float32)
+                tail = new[pl.ds((count + 1) * 2 * size, PAD), :].astype(jnp.float32)
+                edge = jnp.where(row // 2 == tag, jnp.where(after_me, tail, head), edge)
+            out[pl.ds(quarter, PAD), :] = edge.astype(out.dtype)
+    for tag, part in enumerate(parts):
+
+        @pl.when(mine ^ place == tag)
+        def _():
+            own[...] = part[...]
+
+
+def mend(exons, parts, gained, size):
+    rows, width = parts[0].shape
+    pieces = len(parts)
+    whole = jax.ShapeDtypeStruct((rows, width), jnp.bfloat16)
+    quarter = rows // pieces
+    sent = [
+        jax.ShapeDtypeStruct((quarter + (PAD if d in (1, 3) else 0), width), jnp.bfloat16)
+        for d in range(1, pieces)
+    ]
+    outs = pl.pallas_call(
+        functools.partial(mend_kernel, pieces=pieces, nblocks=rows // 2 // size, size=size),
+        out_shape=[whole] * pieces + sent + [whole],
+        in_specs=[SMEM] + [VMEM] * (2 * pieces),
+        out_specs=[VMEM] * (pieces + len(sent) + 1),
+        input_output_aliases={1 + at: at for at in range(pieces)},
+        cost_estimate=LITTLE,
+        compiler_params=pltpu.CompilerParams(vmem_limit_bytes=24 * MIB),
+    )(exons, *parts, *gained)
+    return outs[:pieces], outs[pieces:-1], outs[-1]
 
 
 def gathered_gradient(pre_act, out_grad, coverage_obs, owners, exon_blocks):
@@ -492,48 +581,27 @@
         )
         return (in_grad, w_grad.transpose(1, 0, 2))
 
-    mine = lax.axis_index("seq")
-    place = lax.axis_index("ch")
-    early = x_saved[: rows // 2]
-    up_early, down_early = shift(early, "seq", 1), shift(early, "seq", -1)
     outgoing = front(owners, exons, pre_act, most, size, nseq)
     slope, plain = plain_gradient(pre_act, out_grad)
     arrived = [outgoing[0]] + [swap(outgoing[d], "seq", d) for d in range(1, nseq)]
-    *arrived, up_early, down_early, slope, plain = after(
-        [*arrived, up_early, down_early, slope, plain]
-    )
+    (source,) = after([x_saved], outgoing)
+    up1, down1 = shift(source, "seq", 1), shift(source, "seq", -1)
+    *arrived, plain, slope = after([*arrived, plain, slope])
+    far, near = swap(plain, "ch", 2), swap(plain, "ch", 1)
     coverage = functools.reduce(jnp.add, [a.astype(jnp.float32) for a in arrived])
     splice = jnp.tanh(coverage - target).astype(jnp.bfloat16)
     splices = [splice] + [swap(splice, "seq", d) for d in range(1, nseq)]
-    pre_grad = gained_gradient(owners, exons, out_grad, slope, plain, splices, most, size, nseq)
-    (late,) = after([x_saved[rows // 2 :]], splices[1:])
-    up1 = jnp.concatenate([up_early, shift(late, "seq", 1)])
-    down1 = jnp.concatenate([down_early, shift(late, "seq", -1)])
-
-    far = swap(pre_grad, "ch", 2)
-    near = swap(pre_grad, "ch", 1)
+    gained = gained_rows(owners, exons, out_grad, slope, splices, most, size, nseq)
+    gained, up1, down1 = after([gained, up1, down1])
+
+    far_gained, near_gained = swap(gained, "ch", 2), swap(gained, "ch", 1)
     up2, down2 = shift(up1, "seq", 1, 1), shift(down1, "seq", -1, 1)
-    far, near, up2, down2 = after([far, near, up2, down2])
-    parts = after([pre_grad, near, far, swap(far, "ch", 1)])
+    beyond = swap(far, "ch", 1)
+    gained = [gained, near_gained, far_gained, swap(far_gained, "ch", 1)]
+    *gained, beyond, up2, down2 = after([*gained, beyond, up2, down2])
 
     quarter = rows // nch
-    half = taps // 2
-
-    def chosen(flipped, options):
-        want = mine ^ flipped ^ place
-        picked = options[0]
-        for t in range(1, nch):
-            picked = jnp.where(want == t, options[t], picked)
-        return picked
-
-    slices = [lax.dynamic_slice_in_dim(p, place * quarter, quarter, axis=0) for p in parts]
-    heads = jnp.concatenate([p[:half] for p in parts])
-    tails = jnp.concatenate([p[rows - half :] for p in parts])
-    spare = jnp.zeros((-len(heads) % PAD, width), jnp.bfloat16)
-    sent = [chosen(d, slices) for d in range(1, nseq)]
-    for d in (1, 3):
-        edge = jnp.where((mine ^ d) > mine, tails, heads)
-        sent[d - 1] = jnp.concatenate([sent[d - 1], edge, spare])
+    parts, sent, own = mend(exons, [plain, near, far, beyond], gained, size)
     *sent, up2, down2 = after([*sent, up2, down2])
     got = [swap(block, "seq", d) for d, block in zip(range(1, nseq), sent)]
     up3, down3 = shift(up2, "seq", 1, 2), shift(down2, "seq", -1, 2)
@@ -543,7 +611,7 @@
 
     partial, laid = weight_gradient(
         [up1[rows - PAD :], x_saved, down1[:PAD]],
-        [chosen(0, parts)],
+        [own],
         lambda: ([0, PAD, PAD + rows], [0], [0], [], []),
         rows,
         taps,
@@ -554,71 +622,44 @@
         origins=origins,
     )
     center = pieces_gradient(parts, laid, taps)
-    first, partial, center = after([got[0], partial, center])
-    got[0] = first
-
-    across = [swap(block, "ch", 2) for block in got]
-    beside = [swap(block, "ch", 1) for block in got]
-    edges = [got[d - 1][quarter : quarter + len(heads)] for d in (1, 3)]
-    edges = [jnp.concatenate(jnp.split(e, nch), axis=1) for e in edges]
-    nothing = jnp.zeros_like(edges[0])
-    low = jnp.where(mine % 2 == 1, edges[0], jnp.where(mine == 2, edges[1], nothing))
-    high = jnp.where(mine % 2 == 0, edges[0], jnp.where(mine == 1, edges[1], nothing))
-    low = jnp.pad(low, ((PAD - half, 0), (0, 0)))
-    high = jnp.pad(high, ((0, PAD - half), (0, 0)))
-    in_grad = pieces_gradient(parts, laid, taps, [low, high, center])
-    *across, in_grad = after([*across, in_grad])
-    beyond = [swap(block, "ch", 1) for block in across]
-
-    seam = (nseq - 1) * rows
-
-    def layout(hops, blocks, closing):
+    *got, partial, center = after([*got, partial, center])
+
+    crossing = jnp.concatenate([block[:quarter] for block in got])
+    across = swap(crossing, "ch", 2)
+    beside = swap(crossing, "ch", 1)
+    in_grad = pieces_gradient(parts, laid, taps, [got[0], got[2], center])
+    across, in_grad, up3, down3 = after([across, in_grad, up3, down3])
+    beyond = swap(across, "ch", 1)
+
+    def layout():
         mine = lax.axis_index("seq")
         place = lax.axis_index("ch")
         x_rows = [PAD + mine * rows]
-        for hop in range(1, hops):
+        for hop in range(1, nseq):
             low_at, high_at = mine - hop, mine + hop
             x_rows += [
                 jnp.where(low_at >= 0, PAD + low_at * rows, -1),
                 jnp.where(high_at < nseq, PAD + high_at * rows, -1),
             ]
-        used = (2, 3) if closing else blocks
         g_rows = [
-            (mine ^ d) * rows + (place ^ tag) * quarter for d in used for tag in range(nch)
+            (mine ^ d) * rows + (place ^ tag) * quarter
+            for tag in range(nch)
+            for d in range(1, nseq)
         ]
-        starts = [(mine ^ d) * rows for d in blocks]
-        if closing:
-            seams = [(mine == 0, seam - PAD, 1), (mine == nseq - 1, rows, -1)]
-            return x_rows, g_rows, starts, [], seams
-        return x_rows, g_rows, starts, [(mine == 0, PAD + seam), (mine == nseq - 1, rows)], []
-
-    def sources(blocks):
-        return [
-            kind[d - 1] for d in blocks for kind in (got, beside, across, beyond)
-        ]
-
-    (partial,) = weight_gradient(
-        [x_saved, up1, down1, up2, down2],
-        sources((1, 2)),
-        functools.partial(layout, 3, (1, 2), False),
+        return x_rows, g_rows, [(mine ^ d) * rows for d in range(1, nseq)], [], []
+
+    g_pieces = []
+    for piece in (crossing, beside, across, beyond):
+        g_pieces += [piece[d * quarter : (d + 1) * quarter] for d in range(nseq - 1)]
+    (w_grad,) = weight_gradient(
+        [x_saved, up1, down1, up2, down2, up3, down3],
+        g_pieces,
+        layout,
         rows,
         taps,
         nseq * rows,
         before=partial,
-        last=False,
         vmem=32,
-        span=quarter,
-    )
-    (w_grad,) = weight_gradient(
-        [x_saved, up1, down1, up2, down2, up3, down3],
-        sources((2, 3)),
-        functools.partial(layout, 4, (3,), True),
-        rows,
-        taps,
-        nseq * rows,
-        before=after([partial], [in_grad])[0],
-        vmem=32,
-        span=quarter,
     )
     return (in_grad, w_grad.transpose(1, 0, 2))
 

time: 116 us -> 109 us (0.940)
  waiting for transfers between devices: 37.3 us -> 44 us
  local copies, waits for them, and re-layouts: 10.4 us -> 3.7 us
  starting transfers between devices: 36.6 us -> 31.7 us
    ppermute x8 -> x6, starting transfers between devices: 16.3 us -> 8.46 us  [shift(): return lax.ppermute(block, axis, pairs)]
    unnamed x36 -> x18, local copies, waits for them, and re-layouts: 8.16 us -> 3.47 us
    ppermute x8 -> x6, waiting for transfers between devices: 8.37 us -> 13 us  [shift(): return lax.ppermute(block, axis, pairs)]
    ppermute x21 -> x18, starting transfers between devices: 20.3 us -> 23.3 us  [swap(): return lax.ppermute(block, axis, [(i, i ^ flip) for i in range(count)])]
    pallas_call x3 -> x2, Pallas kernels: 15.9 us -> 13.7 us  [weight_gradient(): pl.pallas_call(functools.partial(weight_kernel, taps=taps, tile=min(1024,...]
    ppermute x21 -> x18, waiting for transfers between devices: 28.9 us -> 31 us  [swap(): return lax.ppermute(block, axis, [(i, i ^ flip) for i in range(count)])]
    pallas_call x1 -> x2, Pallas kernels: 1.95 us -> 3.27 us  [the longest x1 1.89 us: gained_rows(): pl.pallas_call(functools.partial(gain_kernel, nblocks=rows // 2 // size,...]
  transfers between devices with their start and end apart: 29 -> 24, of which waited for: 14 -> 9; matrix products, arithmetic and copies ran while one was open for 1% -> 0% of each run, Pallas kernels for 19% -> 14%
where the time goes in v6:
time: 109 us
  waiting for transfers between devices  44 us (40%)
  starting transfers between devices  31.7 us (29%)
  Pallas kernels  28.2 us (26%)
  local copies, waits for them, and re-layouts  3.7 us (3%)
  between operations  1.09 us (1%)
    ppermute x18, waiting for transfers between devices, swap(): return lax.ppermute(block, axis, [(i, i ^ flip) for i in range(count)])  31 us
    ppermute x18, starting transfers between devices, swap(): return lax.ppermute(block, axis, [(i, i ^ flip) for i in range(count)])  23.3 us
    pallas_call x2, Pallas kernels, weight_gradient(): pl.pallas_call(functools.partial(weight_kernel, taps=taps, tile=min(1024,...  13.7 us
    ppermute x6, waiting for transfers between devices, shift(): return lax.ppermute(block, axis, pairs)  13 us
    pallas_call x2, Pallas kernels, pieces_gradient(): pl.pallas_call(functools.partial(pieces_kernel, taps=taps, pieces=len(par...  8.51 us
    ppermute x6, starting transfers between devices, shift(): return lax.ppermute(block, axis, pairs)  8.46 us
    unnamed x18, local copies, waits for them, and re-layouts  3.47 us
  transfers between devices with their start and end apart: 24, of which 9 were waited for; matrix products, arithmetic and copies ran while one was open for 0% of the time, Pallas kernels for 14%

profile of v6, /device:TPU:0, one launch (start us, length us, event | category | flops | bytes accessed | tf_op | source)
XLA Modules:
  0.0 108.9 jit_solution(16646463779728938829)
XLA Ops:
  0.6 1.1 %copy-done.1 = bf16[1024,384]{1,0:T(8,128)(2,1)S(1)} copy-done((bf16[1024,384]{1,0:T(8,128)(2,1)S(1)}, bf16[1024,384]{1,0:T(8,128)(2,1)}, u32[]{:S(2)}) %copy-start.1) | copy-done | bytes 786456
  3.1 1.3 %shard_map.86 = (bf16[64,384]{1,0:T(8,128)(2,1)S(1)}, bf16[64,384]{1,0:T(8,128)(2,1)S(1)}, bf16[64,384]{1,0:T(8,128)(2,1)S(1)}, bf16[64,384]{1,0:T(8,128)(2,1)S(1)}) custom-call(s32[16]{0:T(128)S(1)} %copy-done.7, s32[2,16]{1,0:T(2,128)S(1)} %bitcast.10, bf16[1024,384]{1,0:T(8,128)(2,1)S(1)} %copy-done.1), custom_call_target="tpu_custom_call" | custom-call | flops 1000 | bytes 1000 | tf_op jit(solution)/shard_map/pallas_call | solution.py:354
  4.4 3.3 %collective-permute-start = (bf16[64,384]{1,0:T(8,128)(2,1)S(1)}, bf16[64,384]{1,0:T(8,128)(2,1)S(1)}, u32[]{:S(2)}, u32[]{:S(2)}) collective-permute-start(bf16[64,384]{1,0:T(8,128)(2,1)S(1)} %get-tuple-element.50), channel_id=1, source_target_pairs={{0,4},{4,0},{8,12},{12,8},{1,5},{5,1},{9,13},{13,9},{2,6},{6,2},{1... | collective-permute-start | bytes 147464 | tf_op jit(solution)/shard_map/ppermute | solution.py:24
  7.7 2.4 %collective-permute-start.1 = (bf16[64,384]{1,0:T(8,128)(2,1)S(1)}, bf16[64,384]{1,0:T(8,128)(2,1)S(1)}, u32[]{:S(2)}, u32[]{:S(2)}) collective-permute-start(bf16[64,384]{1,0:T(8,128)(2,1)S(1)} %get-tuple-element.51), channel_id=1, source_target_pairs={{0,8},{4,12},{8,0},{12,4},{1,9},{5,13},{9,1},{13,5},{2,10},{6,14},... | collective-permute-start | bytes 147464 | tf_op jit(solution)/shard_map/ppermute | solution.py:24
  10.1 3.0 %collective-permute-start.8 = (bf16[1024,384]{1,0:T(8,128)(2,1)}, bf16[1024,384]{1,0:T(8,128)(2,1)S(1)}, u32[]{:S(2)}, u32[]{:S(2)}) collective-permute-start(bf16[1024,384]{1,0:T(8,128)(2,1)} %refs_0_.1), channel_id=1, source_target_pairs={{0,4},{4,8},{8,12},{1,5},{5,9},{9,13},{2,6},{6,10},{10,14},{3,7},{... | collective-permute-start | bytes 2359304 | tf_op jit(solution)/shard_map/ppermute | solution.py:33
  13.1 1.3 %collective-permute-start.9 = (bf16[1024,384]{1,0:T(8,128)(2,1)}, bf16[1024,384]{1,0:T(8,128)(2,1)S(1)}, u32[]{:S(2)}, u32[]{:S(2)}) collective-permute-start(bf16[1024,384]{1,0:T(8,128)(2,1)} %refs_0_.1), channel_id=1, source_target_pairs={{4,0},{8,4},{12,8},{5,1},{9,5},{13,9},{6,2},{10,6},{14,10},{7,3},{... | collective-permute-start | bytes 2359304 | tf_op jit(solution)/shard_map/ppermute | solution.py:33
  15.4 1.5 %shard_map.87 = (f32[1024,384]{1,0:T(8,128)S(1)}, bf16[1024,384]{1,0:T(8,128)(2,1)S(1)}) custom-call(bf16[1024,384]{1,0:T(8,128)(2,1)S(1)} %copy-done.1, bf16[512,384]{1,0:T(8,128)(2,1)S(1)} %copy-done.3), custom_call_target="tpu_custom_call" | custom-call | flops 1000 | bytes 1000 | tf_op jit(solution)/shard_map/pallas_call | solution.py:381
  17.0 1.6 %collective-permute-start.4 = (bf16[1024,384]{1,0:T(8,128)(2,1)S(1)}, bf16[1024,384]{1,0:T(8,128)(2,1)S(1)}, u32[]{:S(2)}, u32[]{:S(2)}) collective-permute-start(bf16[1024,384]{1,0:T(8,128)(2,1)S(1)} %get-tuple-element.55.refs_0_), channel_id=1, source_target_pairs={{0,2},{1,3},{2,0},{3,1},{4,6},{5,7},{6,4},{7,5},{8,10},{9,11},{10,... | collective-permute-start | bytes 2359304 | tf_op jit(solution)/shard_map/ppermute | solution.py:24
  18.6 2.7 %collective-permute-start.5 = (bf16[64,384]{1,0:T(8,128)(2,1)S(1)}, bf16[64,384]{1,0:T(8,128)(2,1)S(1)}, u32[]{:S(2)}, u32[]{:S(2)}) collective-permute-start(bf16[64,384]{1,0:T(8,128)(2,1)S(1)} %fusion.1.refs_0_), channel_id=1, source_target_pairs={{0,4},{4,0},{8,12},{12,8},{1,5},{5,1},{9,13},{13,9},{2,6},{6,2},{1... | collective-permute-start | bytes 147464 | tf_op jit(solution)/shard_map/ppermute | solution.py:24
  21.3 3.3 %collective-permute-start.6 = (bf16[64,384]{1,0:T(8,128)(2,1)S(1)}, bf16[64,384]{1,0:T(8,128)(2,1)S(1)}, u32[]{:S(2)}, u32[]{:S(2)}) collective-permute-start(bf16[64,384]{1,0:T(8,128)(2,1)S(1)} %fusion.1.refs_0_), channel_id=1, source_target_pairs={{0,8},{4,12},{8,0},{12,4},{1,9},{5,13},{9,1},{13,5},{2,10},{6,14},... | collective-permute-start | bytes 147464 | tf_op jit(solution)/shard_map/ppermute | solution.py:24
  24.5 10.4 %collective-permute-done.5.refs_1_ = bf16[64,384]{1,0:T(8,128)(2,1)S(1)} collective-permute-done((bf16[64,384]{1,0:T(8,128)(2,1)S(1)}, bf16[64,384]{1,0:T(8,128)(2,1)S(1)}, u32[]{:S(2)}, u32[]{:S(2)}) %collective-permute-start.5) | collective-permute-done | bytes 49184 | tf_op jit(solution)/shard_map/ppermute | solution.py:24
  35.0 2.7 %collective-permute-start.7 = (bf16[64,384]{1,0:T(8,128)(2,1)S(1)}, bf16[64,384]{1,0:T(8,128)(2,1)S(1)}, u32[]{:S(2)}, u32[]{:S(2)}) collective-permute-start(bf16[64,384]{1,0:T(8,128)(2,1)S(1)} %fusion.1.refs_0_), channel_id=1, source_target_pairs={{0,12},{4,8},{8,4},{12,0},{1,13},{5,9},{9,5},{13,1},{2,14},{6,10},... | collective-permute-start | bytes 147464 | tf_op jit(solution)/shard_map/ppermute | solution.py:24
  37.7 3.3 %collective-permute-done.7.refs_3_ = bf16[64,384]{1,0:T(8,128)(2,1)S(1)} collective-permute-done((bf16[64,384]{1,0:T(8,128)(2,1)S(1)}, bf16[64,384]{1,0:T(8,128)(2,1)S(1)}, u32[]{:S(2)}, u32[]{:S(2)}) %collective-permute-start.7) | collective-permute-done | bytes 49184 | tf_op jit(solution)/shard_map/ppermute | solution.py:24
  41.0 1.9 %shard_map.88.refs_4_ = bf16[288,384]{1,0:T(8,128)(2,1)S(1)} custom-call(s32[16]{0:T(128)S(1)} %copy-done.7, s32[2,16]{1,0:T(2,128)S(1)} %bitcast.11, bf16[512,384]{1,0:T(8,128)(2,1)S(1)} %copy-done.4, f32[1024,384]{1,0:T(8,128)S(1)} %get-tuple-element.56.slope, bf16[64,384]{1,0:T(8,128)(2,1)S(1)} %fusion.1.refs_0_, ...), custom_call_target="tpu_custom_call" | custom-call | flops 1000 | bytes 1000 | tf_op jit(solution)/shard_map/pallas_call | solution.py:428
  43.6 1.3 %collective-permute-start.15 = (bf16[1024,384]{1,0:T(8,128)(2,1)S(1)}, bf16[1024,384]{1,0:T(8,128)(2,1)S(1)}, u32[]{:S(2)}, u32[]{:S(2)}) collective-permute-start(bf16[1024,384]{1,0:T(8,128)(2,1)S(1)} %collective-permute-done.9.refs_2_), channel_id=1, source_target_pairs={{4,0},{8,4},{5,1},{9,5},{6,2},{10,6},{7,3},{11,7},{20,16},{24,20},... | collective-permute-start | bytes 2359304 | tf_op jit(solution)/shard_map/ppermute | solution.py:33
  45.5 1.5 %collective-permute-start.11 = (bf16[288,384]{1,0:T(8,128)(2,1)S(1)}, bf16[288,384]{1,0:T(8,128)(2,1)S(1)}, u32[]{:S(2)}, u32[]{:S(2)}) collective-permute-start(bf16[288,384]{1,0:T(8,128)(2,1)S(1)} %shard_map.88.refs_4_), channel_id=1, source_target_pairs={{0,2},{1,3},{2,0},{3,1},{4,6},{5,7},{6,4},{7,5},{8,10},{9,11},{10,... | collective-permute-start | bytes 663560 | tf_op jit(solution)/shard_map/ppermute | solution.py:24
  47.0 5.9 %collective-permute-done.11.refs_6_ = bf16[288,384]{1,0:T(8,128)(2,1)S(1)} collective-permute-done((bf16[288,384]{1,0:T(8,128)(2,1)S(1)}, bf16[288,384]{1,0:T(8,128)(2,1)S(1)}, u32[]{:S(2)}, u32[]{:S(2)}) %collective-permute-start.11) | collective-permute-done | bytes 221216 | tf_op jit(solution)/shard_map/ppermute | solution.py:24
  52.9 1.5 %collective-permute-done.10.refs_5_ = bf16[288,384]{1,0:T(8,128)(2,1)S(1)} collective-permute-done((bf16[288,384]{1,0:T(8,128)(2,1)S(1)}, bf16[288,384]{1,0:T(8,128)(2,1)S(1)}, u32[]{:S(2)}, u32[]{:S(2)}) %collective-permute-start.10) | collective-permute-done | bytes 221216 | tf_op jit(solution)/shard_map/ppermute | solution.py:24
  54.5 1.3 %collective-permute-done.12.refs_7_ = bf16[288,384]{1,0:T(8,128)(2,1)S(1)} collective-permute-done((bf16[288,384]{1,0:T(8,128)(2,1)S(1)}, bf16[288,384]{1,0:T(8,128)(2,1)S(1)}, u32[]{:S(2)}, u32[]{:S(2)}) %collective-permute-start.12) | collective-permute-done | bytes 221216 | tf_op jit(solution)/shard_map/ppermute | solution.py:24
  55.8 7.1 %collective-permute-done.15.refs_4_ = bf16[1024,384]{1,0:T(8,128)(2,1)S(1)} collective-permute-done((bf16[1024,384]{1,0:T(8,128)(2,1)S(1)}, bf16[1024,384]{1,0:T(8,128)(2,1)S(1)}, u32[]{:S(2)}, u32[]{:S(2)}) %collective-permute-start.15) | collective-permute-done | bytes 786464 | tf_op jit(solution)/shard_map/ppermute | solution.py:33
  63.0 1.4 %shard_map.89 = (bf16[1024,384]{1,0:T(8,128)(2,1)S(1)}, bf16[1024,384]{1,0:T(8,128)(2,1)S(1)}, bf16[1024,384]{1,0:T(8,128)(2,1)S(1)}, bf16[1024,384]{1,0:T(8,128...) custom-call(s32[2,16]{1,0:T(2,128)S(1)} %bitcast.12, ...), custom_call_target="tpu_custom_call", output_to_operand_aliasing={{0}: (1, {}), {1}: (2, {}), {2}: (3, {}), {3}: (4, {})} | custom-call | flops 1000 | bytes 1000 | tf_op jit(solution)/shard_map/pallas_call | solution.py:504
  64.4 1.9 %collective-permute-start.16 = (bf16[272,384]{1,0:T(8,128)(2,1)S(1)}, bf16[272,384]{1,0:T(8,128)(2,1)S(1)}, u32[]{:S(2)}, u32[]{:S(2)}) collective-permute-start(bf16[272,384]{1,0:T(8,128)(2,1)S(1)} %get-tuple-element.75), channel_id=1, source_target_pairs={{0,4},{4,0},{8,12},{12,8},{1,5},{5,1},{9,13},{13,9},{2,6},{6,2},{1... | collective-permute-start | bytes 626696 | tf_op jit(solution)/shard_map/ppermute | solution.py:24
  66.7 1.3 %collective-permute-start.17 = (bf16[256,384]{1,0:T(8,128)(2,1)S(1)}, bf16[256,384]{1,0:T(8,128)(2,1)S(1)}, u32[]{:S(2)}, u32[]{:S(2)}) collective-permute-start(bf16[256,384]{1,0:T(8,128)(2,1)S(1)} %get-tuple-element.76), channel_id=1, source_target_pairs={{0,8},{4,12},{8,0},{12,4},{1,9},{5,13},{9,1},{13,5},{2,10},{6,14},... | collective-permute-start | bytes 589832 | tf_op jit(solution)/shard_map/ppermute | solution.py:24
  68.6 1.5 %collective-permute-start.21 = (bf16[1024,384]{1,0:T(8,128)(2,1)S(1)}, bf16[1024,384]{1,0:T(8,128)(2,1)S(1)}, u32[]{:S(2)}, u32[]{:S(2)}) collective-permute-start(bf16[1024,384]{1,0:T(8,128)(2,1)S(1)} %collective-permute-done.15.refs_4_), channel_id=1, source_target_pairs={{4,0},{5,1},{6,2},{7,3},{20,16},{21,17},{22,18},{23,19}} | collective-permute-start | bytes 2359304 | tf_op jit(solution)/shard_map/ppermute | solution.py:33
  70.1 2.9 %shard_map.90 = (f32[384,1920]{1,0:T(8,128)S(1)}, bf16[1536,1920]{1,0:T(8,128)(2,1)S(1)}) custom-call(bf16[16,384]{1,0:T(8,128)(2,1)S(1)} %slice.39.refs_0_, bf16[1024,384]{1,0:T(8,128)(2,1)S(1)} %copy-done.2, bf16[16,384]{1,0:T(8,128)(2,1)S(1)} %slice.40.refs_2_, bf16[1024,384]{1,0:T(8,128)(2,1)S(1)} %get-tuple-element.78.refs_3_, ...), custom_call_target="tpu_custom_call" | custom-call | flops 1000 | bytes 1000 | tf_op jit(solution)/shard_map/pallas_call | solution.py:252
  73.0 3.7 %shard_map.91.refs_6_ = bf16[512,384]{1,0:T(8,128)(2,1)S(1)} custom-call(bf16[1024,384]{1,0:T(8,128)(2,1)S(1)} %get-tuple-element.80.refs_0_, bf16[1024,384]{1,0:T(8,128)(2,1)S(1)} %get-tuple-element.81.refs_1_, bf16[1024,384]{1,0:T(8,128)(2,1)S(1)} %get-tuple-element.82.refs_2_, bf16[1024,384]{1,0:T(8,128)(2,1)S(1)} %get-tuple-element.83.refs_3_, ...), custom_call_target="tpu_custom_call" | custom-call | flops 1000 | bytes 1000 | tf_op jit(solution)/shard_map/pallas_call | solution.py:133
  76.7 6.7 %collective-permute-done.17.refs_8_ = bf16[256,384]{1,0:T(8,128)(2,1)S(1)} collective-permute-done((bf16[256,384]{1,0:T(8,128)(2,1)S(1)}, bf16[256,384]{1,0:T(8,128)(2,1)S(1)}, u32[]{:S(2)}, u32[]{:S(2)}) %collective-permute-start.17) | collective-permute-done | bytes 196640 | tf_op jit(solution)/shard_map/ppermute | solution.py:24
  83.5 1.6 %collective-permute-start.19 = (bf16[768,384]{1,0:T(8,128)(2,1)S(1)}, bf16[768,384]{1,0:T(8,128)(2,1)S(1)}, u32[]{:S(2)}, u32[]{:S(2)}) collective-permute-start(bf16[768,384]{1,0:T(8,128)(2,1)S(1)} %pad_maximum_fusion), channel_id=1, source_target_pairs={{0,2},{1,3},{2,0},{3,1},{4,6},{5,7},{6,4},{7,5},{8,10},{9,11},{10,... | collective-permute-start | bytes 1769480 | tf_op jit(solution)/shard_map/ppermute | solution.py:24
  85.1 4.8 %shard_map.92 = bf16[1024,384]{1,0:T(8,128)(2,1)} custom-call(bf16[1024,384]{1,0:T(8,128)(2,1)S(1)} %get-tuple-element.80.refs_0_, bf16[1024,384]{1,0:T(8,128)(2,1)S(1)} %get-tuple-element.81.refs_1_, bf16[1024,384]{1,0:T(8,128)(2,1)S(1)} %get-tuple-element.82.refs_2_, bf16[1024,384]{1,0:T(8,128)(2,1)S(1)} %get-tuple-element.83.refs_3_, ...), custom_call_target="tpu_custom_call" | custom-call | flops 1000 | bytes 1000 | tf_op jit(solution)/shard_map/pallas_call | solution.py:133
  89.9 5.9 %collective-permute-done.21.refs_6_ = bf16[1024,384]{1,0:T(8,128)(2,1)S(1)} collective-permute-done((bf16[1024,384]{1,0:T(8,128)(2,1)S(1)}, bf16[1024,384]{1,0:T(8,128)(2,1)S(1)}, u32[]{:S(2)}, u32[]{:S(2)}) %collective-permute-start.21) | collective-permute-done | bytes 786464 | tf_op jit(solution)/shard_map/ppermute | solution.py:33
  95.9 1.9 %collective-permute-done.23 = bf16[768,384]{1,0:T(8,128)(2,1)S(1)} collective-permute-done((bf16[768,384]{1,0:T(8,128)(2,1)S(1)}, bf16[768,384]{1,0:T(8,128)(2,1)S(1)}, u32[]{:S(2)}, u32[]{:S(2)}) %collective-permute-start.23) | collective-permute-done | bytes 589856 | tf_op jit(solution)/shard_map/ppermute | solution.py:24
  97.8 10.8 %shard_map.93 = bf16[5,384,384]{2,1,0:T(8,128)(2,1)} custom-call(bf16[1024,384]{1,0:T(8,128)(2,1)S(1)} %copy-done.2, bf16[1024,384]{1,0:T(8,128)(2,1)S(1)} %collective-permute-done.8.refs_1_, bf16[1024,384]{1,0:T(8,128)(2,1)S(1)} %collective-permute-done.9.refs_2_, bf16[1024,384]{1,0:T(8,128)(2,1)S(1)} %collective-permute-done.14.refs_3_, ...), custom_call_target="tpu_custom_call" | custom-call | flops 1000 | bytes 1000 | tf_op jit(solution)/shard_map/pallas_call | solution.py:252
  (51 shorter events, 5.4 us)
Async XLA Ops:
  0.6 1.1 %copy-start.1 = (bf16[1024,384]{1,0:T(8,128)(2,1)S(1)}, bf16[1024,384]{1,0:T(8,128)(2,1)}, u32[]{:S(2)}) copy-start(bf16[1024,384]{1,0:T(8,128)(2,1)} %pre_act.3) | copy-start | bytes 2359300
  1.8 0.7 copy-start.5
  3.1 15.4 %copy-start.8 = (f32[1,8,8,384]{3,2,1,0:T(8,128)S(1)}, f32[1,8,8,384]{3,2,1,0:T(8,128)}, u32[]{:S(2)}) copy-start(f32[1,8,8,384]{3,2,1,0:T(8,128)} %param.11) | copy-start | bytes 294916
  3.1 37.9 %copy-start.4 = (bf16[512,384]{1,0:T(8,128)(2,1)S(1)}, bf16[512,384]{1,0:T(8,128)(2,1)}, u32[]{:S(2)}) copy-start(bf16[512,384]{1,0:T(8,128)(2,1)} %out_grad.3) | copy-start | bytes 1179652
  4.4 12.5 %collective-permute-start = (bf16[64,384]{1,0:T(8,128)(2,1)S(1)}, bf16[64,384]{1,0:T(8,128)(2,1)S(1)}, u32[]{:S(2)}, u32[]{:S(2)}) collective-permute-start(bf16[64,384]{1,0:T(8,128)(2,1)S(1)} %get-tuple-element.50), channel_id=1, source_target_pairs={{0,4},{4,0},{8,12},{12,8},{1,5},{5,1},{9,13},{13,9},{2,6},{6,2},{1... | collective-permute-start | bytes 147464 | tf_op jit(solution)/shard_map/ppermute | solution.py:24
  7.7 9.3 %collective-permute-start.1 = (bf16[64,384]{1,0:T(8,128)(2,1)S(1)}, bf16[64,384]{1,0:T(8,128)(2,1)S(1)}, u32[]{:S(2)}, u32[]{:S(2)}) collective-permute-start(bf16[64,384]{1,0:T(8,128)(2,1)S(1)} %get-tuple-element.51), channel_id=1, source_target_pairs={{0,8},{4,12},{8,0},{12,4},{1,9},{5,13},{9,1},{13,5},{2,10},{6,14},... | collective-permute-start | bytes 147464 | tf_op jit(solution)/shard_map/ppermute | solution.py:24
  10.0 6.9 %collective-permute-start.2 = (bf16[64,384]{1,0:T(8,128)(2,1)S(1)}, bf16[64,384]{1,0:T(8,128)(2,1)S(1)}, u32[]{:S(2)}, u32[]{:S(2)}) collective-permute-start(bf16[64,384]{1,0:T(8,128)(2,1)S(1)} %get-tuple-element.52), channel_id=1, source_target_pairs={{0,12},{4,8},{8,4},{12,0},{1,13},{5,9},{9,5},{13,1},{2,14},{6,10},... | collective-permute-start | bytes 147464 | tf_op jit(solution)/shard_map/ppermute | solution.py:24
  10.1 32.7 %collective-permute-start.8 = (bf16[1024,384]{1,0:T(8,128)(2,1)}, bf16[1024,384]{1,0:T(8,128)(2,1)S(1)}, u32[]{:S(2)}, u32[]{:S(2)}) collective-permute-start(bf16[1024,384]{1,0:T(8,128)(2,1)} %refs_0_.1), channel_id=1, source_target_pairs={{0,4},{4,8},{8,12},{1,5},{5,9},{9,13},{2,6},{6,10},{10,14},{3,7},{... | collective-permute-start | bytes 2359304 | tf_op jit(solution)/shard_map/ppermute | solution.py:33
  13.1 29.8 %collective-permute-start.9 = (bf16[1024,384]{1,0:T(8,128)(2,1)}, bf16[1024,384]{1,0:T(8,128)(2,1)S(1)}, u32[]{:S(2)}, u32[]{:S(2)}) collective-permute-start(bf16[1024,384]{1,0:T(8,128)(2,1)} %refs_0_.1), channel_id=1, source_target_pairs={{4,0},{8,4},{12,8},{5,1},{9,5},{13,9},{6,2},{10,6},{14,10},{7,3},{... | collective-permute-start | bytes 2359304 | tf_op jit(solution)/shard_map/ppermute | solution.py:33
  14.4 1.0 copy-start.3
  16.9 46.1 %copy-start.6 = (s32[16,2]{0,1:T(2,128)S(1)}, s32[16,2]{0,1:T(2,128)}, u32[]{:S(2)}) copy-start(s32[16,2]{0,1:T(2,128)} %param.13) | copy-start | bytes 388
  17.0 27.9 %collective-permute-start.4 = (bf16[1024,384]{1,0:T(8,128)(2,1)S(1)}, bf16[1024,384]{1,0:T(8,128)(2,1)S(1)}, u32[]{:S(2)}, u32[]{:S(2)}) collective-permute-start(bf16[1024,384]{1,0:T(8,128)(2,1)S(1)} %get-tuple-element.55.refs_0_), channel_id=1, source_target_pairs={{0,2},{1,3},{2,0},{3,1},{4,6},{5,7},{6,4},{7,5},{8,10},{9,11},{10,... | collective-permute-start | bytes 2359304 | tf_op jit(solution)/shard_map/ppermute | solution.py:24
  18.5 51.6 %copy-start.2 = (bf16[1024,384]{1,0:T(8,128)(2,1)S(1)}, bf16[1024,384]{1,0:T(8,128)(2,1)}, u32[]{:S(2)}) copy-start(bf16[1024,384]{1,0:T(8,128)(2,1)} %refs_0_.1) | copy-start | bytes 2359300
  18.6 16.4 %collective-permute-start.5 = (bf16[64,384]{1,0:T(8,128)(2,1)S(1)}, bf16[64,384]{1,0:T(8,128)(2,1)S(1)}, u32[]{:S(2)}, u32[]{:S(2)}) collective-permute-start(bf16[64,384]{1,0:T(8,128)(2,1)S(1)} %fusion.1.refs_0_), channel_id=1, source_target_pairs={{0,4},{4,0},{8,12},{12,8},{1,5},{5,1},{9,13},{13,9},{2,6},{6,2},{1... | collective-permute-start | bytes 147464 | tf_op jit(solution)/shard_map/ppermute | solution.py:24
  21.3 16.4 %collective-permute-start.6 = (bf16[64,384]{1,0:T(8,128)(2,1)S(1)}, bf16[64,384]{1,0:T(8,128)(2,1)S(1)}, u32[]{:S(2)}, u32[]{:S(2)}) collective-permute-start(bf16[64,384]{1,0:T(8,128)(2,1)S(1)} %fusion.1.refs_0_), channel_id=1, source_target_pairs={{0,8},{4,12},{8,0},{12,4},{1,9},{5,13},{9,1},{13,5},{2,10},{6,14},... | collective-permute-start | bytes 147464 | tf_op jit(solution)/shard_map/ppermute | solution.py:24
  35.0 6.0 %collective-permute-start.7 = (bf16[64,384]{1,0:T(8,128)(2,1)S(1)}, bf16[64,384]{1,0:T(8,128)(2,1)S(1)}, u32[]{:S(2)}, u32[]{:S(2)}) collective-permute-start(bf16[64,384]{1,0:T(8,128)(2,1)S(1)} %fusion.1.refs_0_), channel_id=1, source_target_pairs={{0,12},{4,8},{8,4},{12,0},{1,13},{5,9},{9,5},{13,1},{2,14},{6,10},... | collective-permute-start | bytes 147464 | tf_op jit(solution)/shard_map/ppermute | solution.py:24
  41.0 29.2 %copy-start = (bf16[1536,5,384]{2,0,1:T(8,128)(2,1)S(1)}, bf16[1536,5,384]{2,0,1:T(8,128)(2,1)}, u32[]{:S(2)}) copy-start(bf16[1536,5,384]{2,0,1:T(8,128)(2,1)} %param.10) | copy-start | bytes 17694724
  42.9 13.0 %collective-permute-start.14 = (bf16[1024,384]{1,0:T(8,128)(2,1)S(1)}, bf16[1024,384]{1,0:T(8,128)(2,1)S(1)}, u32[]{:S(2)}, u32[]{:S(2)}) collective-permute-start(bf16[1024,384]{1,0:T(8,128)(2,1)S(1)} %collective-permute-done.8.refs_1_), channel_id=1, source_target_pairs={{4,8},{8,12},{5,9},{9,13},{6,10},{10,14},{7,11},{11,15},{20,24},{2... | collective-permute-start | bytes 2359304 | tf_op jit(solution)/shard_map/ppermute | solution.py:33
  43.6 19.4 %collective-permute-start.15 = (bf16[1024,384]{1,0:T(8,128)(2,1)S(1)}, bf16[1024,384]{1,0:T(8,128)(2,1)S(1)}, u32[]{:S(2)}, u32[]{:S(2)}) collective-permute-start(bf16[1024,384]{1,0:T(8,128)(2,1)S(1)} %collective-permute-done.9.refs_2_), channel_id=1, source_target_pairs={{4,0},{8,4},{5,1},{9,5},{6,2},{10,6},{7,3},{11,7},{20,16},{24,20},... | collective-permute-start | bytes 2359304 | tf_op jit(solution)/shard_map/ppermute | solution.py:33
  44.9 18.1 %collective-permute-start.13 = (bf16[1024,384]{1,0:T(8,128)(2,1)S(1)}, bf16[1024,384]{1,0:T(8,128)(2,1)S(1)}, u32[]{:S(2)}, u32[]{:S(2)}) collective-permute-start(bf16[1024,384]{1,0:T(8,128)(2,1)S(1)} %collective-permute-done.4.refs_2_), channel_id=1, source_target_pairs={{0,1},{1,0},{2,3},{3,2},{4,5},{5,4},{6,7},{7,6},{8,9},{9,8},{10,11... | collective-permute-start | bytes 2359304 | tf_op jit(solution)/shard_map/ppermute | solution.py:24
  45.0 18.0 %collective-permute-start.3 = (bf16[1024,384]{1,0:T(8,128)(2,1)S(1)}, bf16[1024,384]{1,0:T(8,128)(2,1)S(1)}, u32[]{:S(2)}, u32[]{:S(2)}) collective-permute-start(bf16[1024,384]{1,0:T(8,128)(2,1)S(1)} %get-tuple-element.55.refs_0_), channel_id=1, source_target_pairs={{0,1},{1,0},{2,3},{3,2},{4,5},{5,4},{6,7},{7,6},{8,9},{9,8},{10,11... | collective-permute-start | bytes 2359304 | tf_op jit(solution)/shard_map/ppermute | solution.py:24
  45.5 7.4 %collective-permute-start.11 = (bf16[288,384]{1,0:T(8,128)(2,1)S(1)}, bf16[288,384]{1,0:T(8,128)(2,1)S(1)}, u32[]{:S(2)}, u32[]{:S(2)}) collective-permute-start(bf16[288,384]{1,0:T(8,128)(2,1)S(1)} %shard_map.88.refs_4_), channel_id=1, source_target_pairs={{0,2},{1,3},{2,0},{3,1},{4,6},{5,7},{6,4},{7,5},{8,10},{9,11},{10,... | collective-permute-start | bytes 663560 | tf_op jit(solution)/shard_map/ppermute | solution.py:24
  52.9 1.5 %collective-permute-start.10 = (bf16[288,384]{1,0:T(8,128)(2,1)S(1)}, bf16[288,384]{1,0:T(8,128)(2,1)S(1)}, u32[]{:S(2)}, u32[]{:S(2)}) collective-permute-start(bf16[288,384]{1,0:T(8,128)(2,1)S(1)} %shard_map.88.refs_4_), channel_id=1, source_target_pairs={{0,1},{1,0},{2,3},{3,2},{4,5},{5,4},{6,7},{7,6},{8,9},{9,8},{10,11... | collective-permute-start | bytes 663560 | tf_op jit(solution)/shard_map/ppermute | solution.py:24
  54.4 1.5 %collective-permute-start.12 = (bf16[288,384]{1,0:T(8,128)(2,1)S(1)}, bf16[288,384]{1,0:T(8,128)(2,1)S(1)}, u32[]{:S(2)}, u32[]{:S(2)}) collective-permute-start(bf16[288,384]{1,0:T(8,128)(2,1)S(1)} %collective-permute-done.11.refs_6_), channel_id=1, source_target_pairs={{0,1},{1,0},{2,3},{3,2},{4,5},{5,4},{6,7},{7,6},{8,9},{9,8},{10,11... | collective-permute-start | bytes 663560 | tf_op jit(solution)/shard_map/ppermute | solution.py:24
  64.4 19.0 %collective-permute-start.16 = (bf16[272,384]{1,0:T(8,128)(2,1)S(1)}, bf16[272,384]{1,0:T(8,128)(2,1)S(1)}, u32[]{:S(2)}, u32[]{:S(2)}) collective-permute-start(bf16[272,384]{1,0:T(8,128)(2,1)S(1)} %get-tuple-element.75), channel_id=1, source_target_pairs={{0,4},{4,0},{8,12},{12,8},{1,5},{5,1},{9,13},{13,9},{2,6},{6,2},{1... | collective-permute-start | bytes 626696 | tf_op jit(solution)/shard_map/ppermute | solution.py:24
  66.2 17.1 %collective-permute-start.18 = (bf16[272,384]{1,0:T(8,128)(2,1)S(1)}, bf16[272,384]{1,0:T(8,128)(2,1)S(1)}, u32[]{:S(2)}, u32[]{:S(2)}) collective-permute-start(bf16[272,384]{1,0:T(8,128)(2,1)S(1)} %get-tuple-element.77), channel_id=1, source_target_pairs={{0,12},{4,8},{8,4},{12,0},{1,13},{5,9},{9,5},{13,1},{2,14},{6,10},... | collective-permute-start | bytes 626696 | tf_op jit(solution)/shard_map/ppermute | solution.py:24
  66.7 16.7 %collective-permute-start.17 = (bf16[256,384]{1,0:T(8,128)(2,1)S(1)}, bf16[256,384]{1,0:T(8,128)(2,1)S(1)}, u32[]{:S(2)}, u32[]{:S(2)}) collective-permute-start(bf16[256,384]{1,0:T(8,128)(2,1)S(1)} %get-tuple-element.76), channel_id=1, source_target_pairs={{0,8},{4,12},{8,0},{12,4},{1,9},{5,13},{9,1},{13,5},{2,10},{6,14},... | collective-permute-start | bytes 589832 | tf_op jit(solution)/shard_map/ppermute | solution.py:24
  67.9 22.0 %collective-permute-start.20 = (bf16[1024,384]{1,0:T(8,128)(2,1)S(1)}, bf16[1024,384]{1,0:T(8,128)(2,1)S(1)}, u32[]{:S(2)}, u32[]{:S(2)}) collective-permute-start(bf16[1024,384]{1,0:T(8,128)(2,1)S(1)} %collective-permute-done.14.refs_3_), channel_id=1, source_target_pairs={{8,12},{9,13},{10,14},{11,15},{24,28},{25,29},{26,30},{27,31}} | collective-permute-start | bytes 2359304 | tf_op jit(solution)/shard_map/ppermute | solution.py:33
  68.6 27.1 %collective-permute-start.21 = (bf16[1024,384]{1,0:T(8,128)(2,1)S(1)}, bf16[1024,384]{1,0:T(8,128)(2,1)S(1)}, u32[]{:S(2)}, u32[]{:S(2)}) collective-permute-start(bf16[1024,384]{1,0:T(8,128)(2,1)S(1)} %collective-permute-done.15.refs_4_), channel_id=1, source_target_pairs={{4,0},{5,1},{6,2},{7,3},{20,16},{21,17},{22,18},{23,19}} | collective-permute-start | bytes 2359304 | tf_op jit(solution)/shard_map/ppermute | solution.py:33
  83.5 12.3 %collective-permute-start.19 = (bf16[768,384]{1,0:T(8,128)(2,1)S(1)}, bf16[768,384]{1,0:T(8,128)(2,1)S(1)}, u32[]{:S(2)}, u32[]{:S(2)}) collective-permute-start(bf16[768,384]{1,0:T(8,128)(2,1)S(1)} %pad_maximum_fusion), channel_id=1, source_target_pairs={{0,2},{1,3},{2,0},{3,1},{4,6},{5,7},{6,4},{7,5},{8,10},{9,11},{10,... | collective-permute-start | bytes 1769480 | tf_op jit(solution)/shard_map/ppermute | solution.py:24
  85.1 10.8 %collective-permute-start.22 = (bf16[768,384]{1,0:T(8,128)(2,1)S(1)}, bf16[768,384]{1,0:T(8,128)(2,1)S(1)}, u32[]{:S(2)}, u32[]{:S(2)}) collective-permute-start(bf16[768,384]{1,0:T(8,128)(2,1)S(1)} %pad_maximum_fusion), channel_id=1, source_target_pairs={{0,1},{1,0},{2,3},{3,2},{4,5},{5,4},{6,7},{7,6},{8,9},{9,8},{10,11... | collective-permute-start | bytes 1769480 | tf_op jit(solution)/shard_map/ppermute | solution.py:24
  95.8 2.0 %collective-permute-start.23 = (bf16[768,384]{1,0:T(8,128)(2,1)S(1)}, bf16[768,384]{1,0:T(8,128)(2,1)S(1)}, u32[]{:S(2)}, u32[]{:S(2)}) collective-permute-start(bf16[768,384]{1,0:T(8,128)(2,1)S(1)} %collective-permute-done.19), channel_id=1, source_target_pairs={{0,1},{1,0},{2,3},{3,2},{4,5},{5,4},{6,7},{7,6},{8,9},{9,8},{10,11... | collective-permute-start | bytes 1769480 | tf_op jit(solution)/shard_map/ppermute | solution.py:24
  (1 other events, 0.7 us)

commit v7 on v6

--- a/solution.py
+++ b/solution.py
@@ -15,7 +15,7 @@
 HALF_ROOT = 0.7071067811865476
 DENSITY = 0.3989422804014327
 LANES = 128
-GAINF = 1000
+LONG = pl.CostEstimate(flops=10**10, bytes_accessed=1000, transcendentals=0)
 LITTLE = pl.CostEstimate(flops=1000, bytes_accessed=1000, transcendentals=0)
 
 
@@ -141,7 +141,7 @@
     )(*parts, *rest, weights)
 
 
-def weight_kernel(*refs, taps, tile, rows, size, nx, ng, layout, first, last, origins, span):
+def weight_kernel(*refs, taps, tile, rows, size, nx, ng, layout, first, last, origins, span, stages):
     xs, gs, rest = refs[:nx], refs[nx : nx + ng], list(refs[nx + ng :])
     before = None if first else rest.pop(0)
     weights = rest.pop(0) if origins else None
@@ -170,8 +170,10 @@
             src.at[pl.ds(0, count), :], dst.at[pl.ds(row, count), :], sems.at[at]
         )
 
-    def each(act):
+    def each(act, stage=None):
         for at in range(nx + ng):
+            if stages and stage is not None and stages[at] != stage:
+                continue
             row = pieces[at][2]
             if isinstance(row, int):
                 act(at)
@@ -195,7 +197,8 @@
         for move in moves:
             move.start()
     acc[...] = jnp.zeros_like(acc) if first else before[...]
-    each(lambda at: copy(at).wait())
+    if not stages:
+        each(lambda at: copy(at).wait())
 
     def add(start, count, side=None):
         grad = gbuf[pl.ds(start, count), :].T
@@ -214,7 +217,9 @@
             moved = jnp.concatenate(moved, axis=1)
             acc[...] += jnp.dot(grad, moved, preferred_element_type=jnp.float32)
 
-    for begin in starts:
+    for stage, begin in enumerate(starts):
+        if stages:
+            each(lambda at: copy(at).wait(), stage)
 
         def body(step, carry):
             add(pl.multiple_of(begin + step * tile, 16), tile)
@@ -233,7 +238,8 @@
 
 
 def weight_gradient(
-    xs, gs, layout, size, taps, rows, before=None, last=True, vmem=40, weights=None, origins=None, span=None
+    xs, gs, layout, size, taps, rows, before=None, last=True, vmem=40, weights=None, origins=None, span=None,
+    stages=None
 ):
     width, chunk = xs[0].shape[1], gs[0].shape[1]
     split = (taps, chunk, width)
@@ -263,6 +269,7 @@
             last=last,
             origins=origins,
             span=span,
+            stages=stages,
         ),
         out_shape=out_shape,
         in_specs=[SOME] * (len(xs) + len(gs))
@@ -436,7 +443,7 @@
             pair_scratch(2 * size, width),
             pltpu.SMEM((groups,), jnp.int32),
         ],
-        cost_estimate=pl.CostEstimate(flops=GAINF, bytes_accessed=1000, transcendentals=0),
+        cost_estimate=LONG,
         compiler_params=pltpu.CompilerParams(vmem_limit_bytes=16 * MIB),
     )(owners, exons, out_grad, slope, *splices)
 
@@ -590,9 +597,11 @@
     far, near = swap(plain, "ch", 2), swap(plain, "ch", 1)
     coverage = functools.reduce(jnp.add, [a.astype(jnp.float32) for a in arrived])
     splice = jnp.tanh(coverage - target).astype(jnp.bfloat16)
-    splices = [splice] + [swap(splice, "seq", d) for d in range(1, nseq)]
+    beside = swap(splice, "seq", 1)
+    both = swap(jnp.concatenate([splice, beside]), "seq", 2)
+    both, up1, down1 = after([both, up1, down1])
+    splices = [splice, beside, both]
     gained = gained_rows(owners, exons, out_grad, slope, splices, most, size, nseq)
-    gained, up1, down1 = after([gained, up1, down1])
 
     far_gained, near_gained = swap(gained, "ch", 2), swap(gained, "ch", 1)
     up2, down2 = shift(up1, "seq", 1, 1), shift(down1, "seq", -1, 1)
@@ -643,14 +652,16 @@
             ]
         g_rows = [
             (mine ^ d) * rows + (place ^ tag) * quarter
+            for d in range(1, nseq)
             for tag in range(nch)
-            for d in range(1, nseq)
         ]
         return x_rows, g_rows, [(mine ^ d) * rows for d in range(1, nseq)], [], []
 
-    g_pieces = []
-    for piece in (crossing, beside, across, beyond):
-        g_pieces += [piece[d * quarter : (d + 1) * quarter] for d in range(nseq - 1)]
+    g_pieces, stages = [], [0] * 5 + [1] * 2
+    for d in range(nseq - 1):
+        for piece in (crossing, beside, across, beyond):
+            g_pieces.append(piece[d * quarter : (d + 1) * quarter])
+            stages.append(d)
     (w_grad,) = weight_gradient(
         [x_saved, up1, down1, up2, down2, up3, down3],
         g_pieces,
@@ -660,6 +671,7 @@
         nseq * rows,
         before=partial,
         vmem=32,
+        stages=stages,
     )
     return (in_grad, w_grad.transpose(1, 0, 2))
 

time: 109 us -> 111 us (1.018)
  waiting for transfers between devices: 44 us -> 47.6 us
  starting transfers between devices: 31.7 us -> 29.5 us
    ppermute x18 -> x17, waiting for transfers between devices: 31 us -> 37 us  [swap(): return lax.ppermute(block, axis, [(i, i ^ flip) for i in range(count)])]
    ppermute x6, waiting for transfers between devices: 13 us -> 10.6 us  [shift(): return lax.ppermute(block, axis, pairs)]
    ppermute x18 -> x17, starting transfers between devices: 23.3 us -> 21 us  [swap(): return lax.ppermute(block, axis, [(i, i ^ flip) for i in range(count)])]
    unnamed x18 -> x22, local copies, waits for them, and re-layouts: 3.47 us -> 3.5 us
  transfers between devices with their start and end apart: 24 -> 23, of which waited for: 9 -> 10; matrix products, arithmetic and copies ran while one was open for 0% -> 0% of each run, Pallas kernels for 14% -> 13%
where the time goes in v7:
time: 111 us
  waiting for transfers between devices  47.6 us (43%)
  starting transfers between devices  29.5 us (27%)
  Pallas kernels  28.7 us (26%)
  local copies, waits for them, and re-layouts  3.73 us (3%)
  between operations  1.13 us (1%)
    ppermute x17, waiting for transfers between devices, swap(): return lax.ppermute(block, axis, [(i, i ^ flip) for i in range(count)])  37 us
    ppermute x17, starting transfers between devices, swap(): return lax.ppermute(block, axis, [(i, i ^ flip) for i in range(count)])  21 us
    pallas_call x2, Pallas kernels, weight_gradient(): pl.pallas_call(functools.partial(weight_kernel, taps=taps, tile=min(1024,...  13.8 us
    ppermute x6, waiting for transfers between devices, shift(): return lax.ppermute(block, axis, pairs)  10.6 us
    pallas_call x2, Pallas kernels, pieces_gradient(): pl.pallas_call(functools.partial(pieces_kernel, taps=taps, pieces=len(par...  8.51 us
    ppermute x6, starting transfers between devices, shift(): return lax.ppermute(block, axis, pairs)  8.45 us
    unnamed x22, local copies, waits for them, and re-layouts  3.5 us
  transfers between devices with their start and end apart: 23, of which 10 were waited for; matrix products, arithmetic and copies ran while one was open for 0% of the time, Pallas kernels for 13%

profile of v7, /device:TPU:0, one launch (start us, length us, event | category | flops | bytes accessed | tf_op | source)
XLA Modules:
  0.0 110.8 jit_solution(6933222873079875003)
XLA Ops:
  0.7 1.1 %copy-done = bf16[1024,384]{1,0:T(8,128)(2,1)S(1)} copy-done((bf16[1024,384]{1,0:T(8,128)(2,1)S(1)}, bf16[1024,384]{1,0:T(8,128)(2,1)}, u32[]{:S(2)}) %copy-start) | copy-done | bytes 786456
  3.1 1.4 %shard_map.86 = (bf16[64,384]{1,0:T(8,128)(2,1)S(1)}, bf16[64,384]{1,0:T(8,128)(2,1)S(1)}, bf16[64,384]{1,0:T(8,128)(2,1)S(1)}, bf16[64,384]{1,0:T(8,128)(2,1)S(1)}) custom-call(s32[16]{0:T(128)S(1)} %copy-done.6, s32[2,16]{1,0:T(2,128)S(1)} %bitcast.12, bf16[1024,384]{1,0:T(8,128)(2,1)S(1)} %copy-done), custom_call_target="tpu_custom_call" | custom-call | flops 1000 | bytes 1000 | tf_op jit(solution)/shard_map/pallas_call | solution.py:361
  4.6 3.1 %collective-permute-start = (bf16[64,384]{1,0:T(8,128)(2,1)S(1)}, bf16[64,384]{1,0:T(8,128)(2,1)S(1)}, u32[]{:S(2)}, u32[]{:S(2)}) collective-permute-start(bf16[64,384]{1,0:T(8,128)(2,1)S(1)} %get-tuple-element.50), channel_id=1, source_target_pairs={{0,4},{4,0},{8,12},{12,8},{1,5},{5,1},{9,13},{13,9},{2,6},{6,2},{1... | collective-permute-start | bytes 147464 | tf_op jit(solution)/shard_map/ppermute | solution.py:24
  7.7 2.3 %collective-permute-start.1 = (bf16[64,384]{1,0:T(8,128)(2,1)S(1)}, bf16[64,384]{1,0:T(8,128)(2,1)S(1)}, u32[]{:S(2)}, u32[]{:S(2)}) collective-permute-start(bf16[64,384]{1,0:T(8,128)(2,1)S(1)} %get-tuple-element.51), channel_id=1, source_target_pairs={{0,8},{4,12},{8,0},{12,4},{1,9},{5,13},{9,1},{13,5},{2,10},{6,14},... | collective-permute-start | bytes 147464 | tf_op jit(solution)/shard_map/ppermute | solution.py:24
  10.2 3.0 %collective-permute-start.7 = (bf16[1024,384]{1,0:T(8,128)(2,1)}, bf16[1024,384]{1,0:T(8,128)(2,1)S(1)}, u32[]{:S(2)}, u32[]{:S(2)}) collective-permute-start(bf16[1024,384]{1,0:T(8,128)(2,1)} %refs_0_.1), channel_id=1, source_target_pairs={{0,4},{4,8},{8,12},{1,5},{5,9},{9,13},{2,6},{6,10},{10,14},{3,7},{... | collective-permute-start | bytes 2359304 | tf_op jit(solution)/shard_map/ppermute | solution.py:33
  13.2 1.3 %collective-permute-start.8 = (bf16[1024,384]{1,0:T(8,128)(2,1)}, bf16[1024,384]{1,0:T(8,128)(2,1)S(1)}, u32[]{:S(2)}, u32[]{:S(2)}) collective-permute-start(bf16[1024,384]{1,0:T(8,128)(2,1)} %refs_0_.1), channel_id=1, source_target_pairs={{4,0},{8,4},{12,8},{5,1},{9,5},{13,9},{6,2},{10,6},{14,10},{7,3},{... | collective-permute-start | bytes 2359304 | tf_op jit(solution)/shard_map/ppermute | solution.py:33
  15.5 1.5 %shard_map.87 = (f32[1024,384]{1,0:T(8,128)S(1)}, bf16[1024,384]{1,0:T(8,128)(2,1)S(1)}) custom-call(bf16[1024,384]{1,0:T(8,128)(2,1)S(1)} %copy-done, bf16[512,384]{1,0:T(8,128)(2,1)S(1)} %copy-done.2), custom_call_target="tpu_custom_call" | custom-call | flops 1000 | bytes 1000 | tf_op jit(solution)/shard_map/pallas_call | solution.py:388
  17.0 1.6 %collective-permute-start.4 = (bf16[1024,384]{1,0:T(8,128)(2,1)S(1)}, bf16[1024,384]{1,0:T(8,128)(2,1)S(1)}, u32[]{:S(2)}, u32[]{:S(2)}) collective-permute-start(bf16[1024,384]{1,0:T(8,128)(2,1)S(1)} %get-tuple-element.55.refs_0_), channel_id=1, source_target_pairs={{0,2},{1,3},{2,0},{3,1},{4,6},{5,7},{6,4},{7,5},{8,10},{9,11},{10,... | collective-permute-start | bytes 2359304 | tf_op jit(solution)/shard_map/ppermute | solution.py:24
  18.6 2.7 %collective-permute-start.5 = (bf16[64,384]{1,0:T(8,128)(2,1)S(1)}, bf16[64,384]{1,0:T(8,128)(2,1)S(1)}, u32[]{:S(2)}, u32[]{:S(2)}) collective-permute-start(bf16[64,384]{1,0:T(8,128)(2,1)S(1)} %fusion.1.refs_0_), channel_id=1, source_target_pairs={{0,4},{4,0},{8,12},{12,8},{1,5},{5,1},{9,13},{13,9},{2,6},{6,2},{1... | collective-permute-start | bytes 147464 | tf_op jit(solution)/shard_map/ppermute | solution.py:24
  21.3 13.2 %collective-permute-done.5.refs_1_ = bf16[64,384]{1,0:T(8,128)(2,1)S(1)} collective-permute-done((bf16[64,384]{1,0:T(8,128)(2,1)S(1)}, bf16[64,384]{1,0:T(8,128)(2,1)S(1)}, u32[]{:S(2)}, u32[]{:S(2)}) %collective-permute-start.5) | collective-permute-done | bytes 49184 | tf_op jit(solution)/shard_map/ppermute | solution.py:24
  34.5 4.3 %collective-permute-start.6 = (bf16[128,384]{1,0:T(8,128)(2,1)S(1)}, bf16[128,384]{1,0:T(8,128)(2,1)S(1)}, u32[]{:S(2)}, u32[]{:S(2)}) collective-permute-start(bf16[128,384]{1,0:T(8,128)(2,1)S(1)} %pad_maximum_fusion.1), channel_id=1, source_target_pairs={{0,8},{4,12},{8,0},{12,4},{1,9},{5,13},{9,1},{13,5},{2,10},{6,14},... | collective-permute-start | bytes 294920 | tf_op jit(solution)/shard_map/ppermute | solution.py:24
  38.8 2.6 %collective-permute-done.6.refs_2_ = bf16[128,384]{1,0:T(8,128)(2,1)S(1)} collective-permute-done((bf16[128,384]{1,0:T(8,128)(2,1)S(1)}, bf16[128,384]{1,0:T(8,128)(2,1)S(1)}, u32[]{:S(2)}, u32[]{:S(2)}) %collective-permute-start.6) | collective-permute-done | bytes 98336 | tf_op jit(solution)/shard_map/ppermute | solution.py:24
  42.1 1.3 %collective-permute-start.14 = (bf16[1024,384]{1,0:T(8,128)(2,1)S(1)}, bf16[1024,384]{1,0:T(8,128)(2,1)S(1)}, u32[]{:S(2)}, u32[]{:S(2)}) collective-permute-start(bf16[1024,384]{1,0:T(8,128)(2,1)S(1)} %collective-permute-done.8.refs_2_), channel_id=1, source_target_pairs={{4,0},{8,4},{5,1},{9,5},{6,2},{10,6},{7,3},{11,7},{20,16},{24,20},... | collective-permute-start | bytes 2359304 | tf_op jit(solution)/shard_map/ppermute | solution.py:33
  43.6 2.0 %shard_map.88.refs_4_ = bf16[288,384]{1,0:T(8,128)(2,1)S(1)} custom-call(s32[16]{0:T(128)S(1)} %copy-done.7, s32[2,16]{1,0:T(2,128)S(1)} %bitcast.13, bf16[512,384]{1,0:T(8,128)(2,1)S(1)} %copy-done.3, f32[1024,384]{1,0:T(8,128)S(1)} %get-tuple-element.56.slope, bf16[64,384]{1,0:T(8,128)(2,1)S(1)} %fusion.1.refs_0_, ...), custom_call_target="tpu_custom_call" | custom-call | flops 10000000000 | bytes 1000 | tf_op jit(solution)/shard_map/pallas_call | solution.py:435
  45.6 1.6 %collective-permute-start.10 = (bf16[288,384]{1,0:T(8,128)(2,1)S(1)}, bf16[288,384]{1,0:T(8,128)(2,1)S(1)}, u32[]{:S(2)}, u32[]{:S(2)}) collective-permute-start(bf16[288,384]{1,0:T(8,128)(2,1)S(1)} %shard_map.88.refs_4_), channel_id=1, source_target_pairs={{0,2},{1,3},{2,0},{3,1},{4,6},{5,7},{6,4},{7,5},{8,10},{9,11},{10,... | collective-permute-start | bytes 663560 | tf_op jit(solution)/shard_map/ppermute | solution.py:24
  47.2 6.3 %collective-permute-done.10.refs_6_ = bf16[288,384]{1,0:T(8,128)(2,1)S(1)} collective-permute-done((bf16[288,384]{1,0:T(8,128)(2,1)S(1)}, bf16[288,384]{1,0:T(8,128)(2,1)S(1)}, u32[]{:S(2)}, u32[]{:S(2)}) %collective-permute-start.10) | collective-permute-done | bytes 221216 | tf_op jit(solution)/shard_map/ppermute | solution.py:24
  53.5 1.5 %collective-permute-done.9.refs_5_ = bf16[288,384]{1,0:T(8,128)(2,1)S(1)} collective-permute-done((bf16[288,384]{1,0:T(8,128)(2,1)S(1)}, bf16[288,384]{1,0:T(8,128)(2,1)S(1)}, u32[]{:S(2)}, u32[]{:S(2)}) %collective-permute-start.9) | collective-permute-done | bytes 221216 | tf_op jit(solution)/shard_map/ppermute | solution.py:24
  55.1 1.3 %collective-permute-done.11.refs_7_ = bf16[288,384]{1,0:T(8,128)(2,1)S(1)} collective-permute-done((bf16[288,384]{1,0:T(8,128)(2,1)S(1)}, bf16[288,384]{1,0:T(8,128)(2,1)S(1)}, u32[]{:S(2)}, u32[]{:S(2)}) %collective-permute-start.11) | collective-permute-done | bytes 221216 | tf_op jit(solution)/shard_map/ppermute | solution.py:24
  56.4 5.3 %collective-permute-done.14.refs_4_ = bf16[1024,384]{1,0:T(8,128)(2,1)S(1)} collective-permute-done((bf16[1024,384]{1,0:T(8,128)(2,1)S(1)}, bf16[1024,384]{1,0:T(8,128)(2,1)S(1)}, u32[]{:S(2)}, u32[]{:S(2)}) %collective-permute-start.14) | collective-permute-done | bytes 786464 | tf_op jit(solution)/shard_map/ppermute | solution.py:33
  61.8 1.4 %shard_map.89 = (bf16[1024,384]{1,0:T(8,128)(2,1)S(1)}, bf16[1024,384]{1,0:T(8,128)(2,1)S(1)}, bf16[1024,384]{1,0:T(8,128)(2,1)S(1)}, bf16[1024,384]{1,0:T(8,128...) custom-call(s32[2,16]{1,0:T(2,128)S(1)} %bitcast.14, ...), custom_call_target="tpu_custom_call", output_to_operand_aliasing={{0}: (1, {}), {1}: (2, {}), {2}: (3, {}), {3}: (4, {})} | custom-call | flops 1000 | bytes 1000 | tf_op jit(solution)/shard_map/pallas_call | solution.py:511
  63.2 1.8 %collective-permute-start.15 = (bf16[272,384]{1,0:T(8,128)(2,1)S(1)}, bf16[272,384]{1,0:T(8,128)(2,1)S(1)}, u32[]{:S(2)}, u32[]{:S(2)}) collective-permute-start(bf16[272,384]{1,0:T(8,128)(2,1)S(1)} %get-tuple-element.75), channel_id=1, source_target_pairs={{0,4},{4,0},{8,12},{12,8},{1,5},{5,1},{9,13},{13,9},{2,6},{6,2},{1... | collective-permute-start | bytes 626696 | tf_op jit(solution)/shard_map/ppermute | solution.py:24
  65.0 1.0 collective-permute-start.17
  67.5 1.5 %collective-permute-start.20 = (bf16[1024,384]{1,0:T(8,128)(2,1)S(1)}, bf16[1024,384]{1,0:T(8,128)(2,1)S(1)}, u32[]{:S(2)}, u32[]{:S(2)}) collective-permute-start(bf16[1024,384]{1,0:T(8,128)(2,1)S(1)} %collective-permute-done.14.refs_4_), channel_id=1, source_target_pairs={{4,0},{5,1},{6,2},{7,3},{20,16},{21,17},{22,18},{23,19}} | collective-permute-start | bytes 2359304 | tf_op jit(solution)/shard_map/ppermute | solution.py:33
  69.0 2.8 %shard_map.90 = (f32[384,1920]{1,0:T(8,128)S(1)}, bf16[1536,1920]{1,0:T(8,128)(2,1)S(1)}) custom-call(bf16[16,384]{1,0:T(8,128)(2,1)S(1)} %slice.39.refs_0_, bf16[1024,384]{1,0:T(8,128)(2,1)S(1)} %copy-done.1, bf16[16,384]{1,0:T(8,128)(2,1)S(1)} %slice.40.refs_2_, bf16[1024,384]{1,0:T(8,128)(2,1)S(1)} %get-tuple-element.78.refs_3_, ...), custom_call_target="tpu_custom_call" | custom-call | flops 1000 | bytes 1000 | tf_op jit(solution)/shard_map/pallas_call | solution.py:258
  71.9 3.7 %shard_map.91.refs_6_ = bf16[512,384]{1,0:T(8,128)(2,1)S(1)} custom-call(bf16[1024,384]{1,0:T(8,128)(2,1)S(1)} %get-tuple-element.80.refs_0_, bf16[1024,384]{1,0:T(8,128)(2,1)S(1)} %get-tuple-element.81.refs_1_, bf16[1024,384]{1,0:T(8,128)(2,1)S(1)} %get-tuple-element.82.refs_2_, bf16[1024,384]{1,0:T(8,128)(2,1)S(1)} %get-tuple-element.83.refs_3_, ...), custom_call_target="tpu_custom_call" | custom-call | flops 1000 | bytes 1000 | tf_op jit(solution)/shard_map/pallas_call | solution.py:133
  75.6 8.0 %collective-permute-done.16.refs_11_ = bf16[256,384]{1,0:T(8,128)(2,1)S(1)} collective-permute-done((bf16[256,384]{1,0:T(8,128)(2,1)S(1)}, bf16[256,384]{1,0:T(8,128)(2,1)S(1)}, u32[]{:S(2)}, u32[]{:S(2)}) %collective-permute-start.16) | collective-permute-done | bytes 196640 | tf_op jit(solution)/shard_map/ppermute | solution.py:24
  83.7 1.6 %collective-permute-start.18 = (bf16[768,384]{1,0:T(8,128)(2,1)S(1)}, bf16[768,384]{1,0:T(8,128)(2,1)S(1)}, u32[]{:S(2)}, u32[]{:S(2)}) collective-permute-start(bf16[768,384]{1,0:T(8,128)(2,1)S(1)} %pad_maximum_fusion), channel_id=1, source_target_pairs={{0,2},{1,3},{2,0},{3,1},{4,6},{5,7},{6,4},{7,5},{8,10},{9,11},{10,... | collective-permute-start | bytes 1769480 | tf_op jit(solution)/shard_map/ppermute | solution.py:24
  85.2 4.8 %shard_map.92 = bf16[1024,384]{1,0:T(8,128)(2,1)} custom-call(bf16[1024,384]{1,0:T(8,128)(2,1)S(1)} %get-tuple-element.80.refs_0_, bf16[1024,384]{1,0:T(8,128)(2,1)S(1)} %get-tuple-element.81.refs_1_, bf16[1024,384]{1,0:T(8,128)(2,1)S(1)} %get-tuple-element.82.refs_2_, bf16[1024,384]{1,0:T(8,128)(2,1)S(1)} %get-tuple-element.83.refs_3_, ...), custom_call_target="tpu_custom_call" | custom-call | flops 1000 | bytes 1000 | tf_op jit(solution)/shard_map/pallas_call | solution.py:133
  90.1 5.3 %collective-permute-done.20.refs_6_ = bf16[1024,384]{1,0:T(8,128)(2,1)S(1)} collective-permute-done((bf16[1024,384]{1,0:T(8,128)(2,1)S(1)}, bf16[1024,384]{1,0:T(8,128)(2,1)S(1)}, u32[]{:S(2)}, u32[]{:S(2)}) %collective-permute-start.20) | collective-permute-done | bytes 786464 | tf_op jit(solution)/shard_map/ppermute | solution.py:33
  95.4 2.2 %collective-permute-done.18 = bf16[768,384]{1,0:T(8,128)(2,1)S(1)} collective-permute-done((bf16[768,384]{1,0:T(8,128)(2,1)S(1)}, bf16[768,384]{1,0:T(8,128)(2,1)S(1)}, u32[]{:S(2)}, u32[]{:S(2)}) %collective-permute-start.18) | collective-permute-done | bytes 589856 | tf_op jit(solution)/shard_map/ppermute | solution.py:24
  97.7 1.9 %collective-permute-done.22 = bf16[768,384]{1,0:T(8,128)(2,1)S(1)} collective-permute-done((bf16[768,384]{1,0:T(8,128)(2,1)S(1)}, bf16[768,384]{1,0:T(8,128)(2,1)S(1)}, u32[]{:S(2)}, u32[]{:S(2)}) %collective-permute-start.22) | collective-permute-done | bytes 589856 | tf_op jit(solution)/shard_map/ppermute | solution.py:24
  99.6 11.0 %shard_map.93 = bf16[5,384,384]{2,1,0:T(8,128)(2,1)} custom-call(bf16[1024,384]{1,0:T(8,128)(2,1)S(1)} %copy-done.1, bf16[1024,384]{1,0:T(8,128)(2,1)S(1)} %collective-permute-done.7.refs_1_, bf16[1024,384]{1,0:T(8,128)(2,1)S(1)} %collective-permute-done.8.refs_2_, bf16[1024,384]{1,0:T(8,128)(2,1)S(1)} %collective-permute-done.13.refs_3_, ...), custom_call_target="tpu_custom_call" | custom-call | flops 1000 | bytes 1000 | tf_op jit(solution)/shard_map/pallas_call | solution.py:258
  (55 shorter events, 5.2 us)
Async XLA Ops:
  0.6 42.9 %copy-start.5 = (s32[16,2]{0,1:T(2,128)S(1)}, s32[16,2]{0,1:T(2,128)}, u32[]{:S(2)}) copy-start(s32[16,2]{0,1:T(2,128)} %param.13) | copy-start | bytes 388
  0.6 42.9 %copy-start.7 = (s32[16]{0:T(128)S(1)}, s32[16]{0:T(128)}, u32[]{:S(2)}) copy-start(s32[16]{0:T(128)} %owners.3) | copy-start | bytes 196
  0.7 1.1 %copy-start = (bf16[1024,384]{1,0:T(8,128)(2,1)S(1)}, bf16[1024,384]{1,0:T(8,128)(2,1)}, u32[]{:S(2)}) copy-start(bf16[1024,384]{1,0:T(8,128)(2,1)} %pre_act.3) | copy-start | bytes 2359300
  3.1 15.4 %copy-start.8 = (f32[1,8,8,384]{3,2,1,0:T(8,128)S(1)}, f32[1,8,8,384]{3,2,1,0:T(8,128)}, u32[]{:S(2)}) copy-start(f32[1,8,8,384]{3,2,1,0:T(8,128)} %param.11) | copy-start | bytes 294916
  3.1 40.4 %copy-start.3 = (bf16[512,384]{1,0:T(8,128)(2,1)S(1)}, bf16[512,384]{1,0:T(8,128)(2,1)}, u32[]{:S(2)}) copy-start(bf16[512,384]{1,0:T(8,128)(2,1)} %out_grad.3) | copy-start | bytes 1179652
  4.6 12.4 %collective-permute-start = (bf16[64,384]{1,0:T(8,128)(2,1)S(1)}, bf16[64,384]{1,0:T(8,128)(2,1)S(1)}, u32[]{:S(2)}, u32[]{:S(2)}) collective-permute-start(bf16[64,384]{1,0:T(8,128)(2,1)S(1)} %get-tuple-element.50), channel_id=1, source_target_pairs={{0,4},{4,0},{8,12},{12,8},{1,5},{5,1},{9,13},{13,9},{2,6},{6,2},{1... | collective-permute-start | bytes 147464 | tf_op jit(solution)/shard_map/ppermute | solution.py:24
  7.7 9.3 %collective-permute-start.1 = (bf16[64,384]{1,0:T(8,128)(2,1)S(1)}, bf16[64,384]{1,0:T(8,128)(2,1)S(1)}, u32[]{:S(2)}, u32[]{:S(2)}) collective-permute-start(bf16[64,384]{1,0:T(8,128)(2,1)S(1)} %get-tuple-element.51), channel_id=1, source_target_pairs={{0,8},{4,12},{8,0},{12,4},{1,9},{5,13},{9,1},{13,5},{2,10},{6,14},... | collective-permute-start | bytes 147464 | tf_op jit(solution)/shard_map/ppermute | solution.py:24
  10.0 6.9 %collective-permute-start.2 = (bf16[64,384]{1,0:T(8,128)(2,1)S(1)}, bf16[64,384]{1,0:T(8,128)(2,1)S(1)}, u32[]{:S(2)}, u32[]{:S(2)}) collective-permute-start(bf16[64,384]{1,0:T(8,128)(2,1)S(1)} %get-tuple-element.52), channel_id=1, source_target_pairs={{0,12},{4,8},{8,4},{12,0},{1,13},{5,9},{9,5},{13,1},{2,14},{6,10},... | collective-permute-start | bytes 147464 | tf_op jit(solution)/shard_map/ppermute | solution.py:24
  10.2 31.3 %collective-permute-start.7 = (bf16[1024,384]{1,0:T(8,128)(2,1)}, bf16[1024,384]{1,0:T(8,128)(2,1)S(1)}, u32[]{:S(2)}, u32[]{:S(2)}) collective-permute-start(bf16[1024,384]{1,0:T(8,128)(2,1)} %refs_0_.1), channel_id=1, source_target_pairs={{0,4},{4,8},{8,12},{1,5},{5,9},{9,13},{2,6},{6,10},{10,14},{3,7},{... | collective-permute-start | bytes 2359304 | tf_op jit(solution)/shard_map/ppermute | solution.py:33
  13.2 28.3 %collective-permute-start.8 = (bf16[1024,384]{1,0:T(8,128)(2,1)}, bf16[1024,384]{1,0:T(8,128)(2,1)S(1)}, u32[]{:S(2)}, u32[]{:S(2)}) collective-permute-start(bf16[1024,384]{1,0:T(8,128)(2,1)} %refs_0_.1), channel_id=1, source_target_pairs={{4,0},{8,4},{12,8},{5,1},{9,5},{13,9},{6,2},{10,6},{14,10},{7,3},{... | collective-permute-start | bytes 2359304 | tf_op jit(solution)/shard_map/ppermute | solution.py:33
  14.5 1.0 copy-start.2
  17.0 26.5 %collective-permute-start.4 = (bf16[1024,384]{1,0:T(8,128)(2,1)S(1)}, bf16[1024,384]{1,0:T(8,128)(2,1)S(1)}, u32[]{:S(2)}, u32[]{:S(2)}) collective-permute-start(bf16[1024,384]{1,0:T(8,128)(2,1)S(1)} %get-tuple-element.55.refs_0_), channel_id=1, source_target_pairs={{0,2},{1,3},{2,0},{3,1},{4,6},{5,7},{6,4},{7,5},{8,10},{9,11},{10,... | collective-permute-start | bytes 2359304 | tf_op jit(solution)/shard_map/ppermute | solution.py:24
  18.6 15.9 %collective-permute-start.5 = (bf16[64,384]{1,0:T(8,128)(2,1)S(1)}, bf16[64,384]{1,0:T(8,128)(2,1)S(1)}, u32[]{:S(2)}, u32[]{:S(2)}) collective-permute-start(bf16[64,384]{1,0:T(8,128)(2,1)S(1)} %fusion.1.refs_0_), channel_id=1, source_target_pairs={{0,4},{4,0},{8,12},{12,8},{1,5},{5,1},{9,13},{13,9},{2,6},{6,2},{1... | collective-permute-start | bytes 147464 | tf_op jit(solution)/shard_map/ppermute | solution.py:24
  34.5 34.5 %slice-start = ((s8[5898240]{0:T(1024)(128)(4,1)}), s8[4194304]{0:T(1024)(128)(4,1)S(1)}, s32[]{:S(2)}) async-start(s8[5898240]{0:T(1024)(128)(4,1)} %bitcast.9), calls=%async_computation | async-start | bytes 8388608
  34.5 34.5 %slice-start.1 = ((s8[5898240]{0:T(1024)(128)(4,1)}), s8[1703936]{0:T(1024)(128)(4,1)S(1)}, s32[]{:S(2)}) async-start(s8[5898240]{0:T(1024)(128)(4,1)} %bitcast.9), calls=%async_computation.1 | async-start | bytes 3407872
  34.5 6.9 %collective-permute-start.6 = (bf16[128,384]{1,0:T(8,128)(2,1)S(1)}, bf16[128,384]{1,0:T(8,128)(2,1)S(1)}, u32[]{:S(2)}, u32[]{:S(2)}) collective-permute-start(bf16[128,384]{1,0:T(8,128)(2,1)S(1)} %pad_maximum_fusion.1), channel_id=1, source_target_pairs={{0,8},{4,12},{8,0},{12,4},{1,9},{5,13},{9,1},{13,5},{2,10},{6,14},... | collective-permute-start | bytes 294920 | tf_op jit(solution)/shard_map/ppermute | solution.py:24
  38.8 23.0 %collective-permute-start.3 = (bf16[1024,384]{1,0:T(8,128)(2,1)S(1)}, bf16[1024,384]{1,0:T(8,128)(2,1)S(1)}, u32[]{:S(2)}, u32[]{:S(2)}) collective-permute-start(bf16[1024,384]{1,0:T(8,128)(2,1)S(1)} %get-tuple-element.55.refs_0_), channel_id=1, source_target_pairs={{0,1},{1,0},{2,3},{3,2},{4,5},{5,4},{6,7},{7,6},{8,9},{9,8},{10,11... | collective-permute-start | bytes 2359304 | tf_op jit(solution)/shard_map/ppermute | solution.py:24
  41.4 15.0 %collective-permute-start.13 = (bf16[1024,384]{1,0:T(8,128)(2,1)S(1)}, bf16[1024,384]{1,0:T(8,128)(2,1)S(1)}, u32[]{:S(2)}, u32[]{:S(2)}) collective-permute-start(bf16[1024,384]{1,0:T(8,128)(2,1)S(1)} %collective-permute-done.7.refs_1_), channel_id=1, source_target_pairs={{4,8},{8,12},{5,9},{9,13},{6,10},{10,14},{7,11},{11,15},{20,24},{2... | collective-permute-start | bytes 2359304 | tf_op jit(solution)/shard_map/ppermute | solution.py:33
  42.1 19.6 %collective-permute-start.14 = (bf16[1024,384]{1,0:T(8,128)(2,1)S(1)}, bf16[1024,384]{1,0:T(8,128)(2,1)S(1)}, u32[]{:S(2)}, u32[]{:S(2)}) collective-permute-start(bf16[1024,384]{1,0:T(8,128)(2,1)S(1)} %collective-permute-done.8.refs_2_), channel_id=1, source_target_pairs={{4,0},{8,4},{5,1},{9,5},{6,2},{10,6},{7,3},{11,7},{20,16},{24,20},... | collective-permute-start | bytes 2359304 | tf_op jit(solution)/shard_map/ppermute | solution.py:33
  43.5 18.3 %collective-permute-start.12 = (bf16[1024,384]{1,0:T(8,128)(2,1)S(1)}, bf16[1024,384]{1,0:T(8,128)(2,1)S(1)}, u32[]{:S(2)}, u32[]{:S(2)}) collective-permute-start(bf16[1024,384]{1,0:T(8,128)(2,1)S(1)} %collective-permute-done.4.refs_2_), channel_id=1, source_target_pairs={{0,1},{1,0},{2,3},{3,2},{4,5},{5,4},{6,7},{7,6},{8,9},{9,8},{10,11... | collective-permute-start | bytes 2359304 | tf_op jit(solution)/shard_map/ppermute | solution.py:24
  45.6 23.4 %copy-start.1 = (bf16[1024,384]{1,0:T(8,128)(2,1)S(1)}, bf16[1024,384]{1,0:T(8,128)(2,1)}, u32[]{:S(2)}) copy-start(bf16[1024,384]{1,0:T(8,128)(2,1)} %refs_0_.1) | copy-start | bytes 2359300
  45.6 7.9 %collective-permute-start.10 = (bf16[288,384]{1,0:T(8,128)(2,1)S(1)}, bf16[288,384]{1,0:T(8,128)(2,1)S(1)}, u32[]{:S(2)}, u32[]{:S(2)}) collective-permute-start(bf16[288,384]{1,0:T(8,128)(2,1)S(1)} %shard_map.88.refs_4_), channel_id=1, source_target_pairs={{0,2},{1,3},{2,0},{3,1},{4,6},{5,7},{6,4},{7,5},{8,10},{9,11},{10,... | collective-permute-start | bytes 663560 | tf_op jit(solution)/shard_map/ppermute | solution.py:24
  53.5 1.5 %collective-permute-start.9 = (bf16[288,384]{1,0:T(8,128)(2,1)S(1)}, bf16[288,384]{1,0:T(8,128)(2,1)S(1)}, u32[]{:S(2)}, u32[]{:S(2)}) collective-permute-start(bf16[288,384]{1,0:T(8,128)(2,1)S(1)} %shard_map.88.refs_4_), channel_id=1, source_target_pairs={{0,1},{1,0},{2,3},{3,2},{4,5},{5,4},{6,7},{7,6},{8,9},{9,8},{10,11... | collective-permute-start | bytes 663560 | tf_op jit(solution)/shard_map/ppermute | solution.py:24
  55.0 1.5 %collective-permute-start.11 = (bf16[288,384]{1,0:T(8,128)(2,1)S(1)}, bf16[288,384]{1,0:T(8,128)(2,1)S(1)}, u32[]{:S(2)}, u32[]{:S(2)}) collective-permute-start(bf16[288,384]{1,0:T(8,128)(2,1)S(1)} %collective-permute-done.10.refs_6_), channel_id=1, source_target_pairs={{0,1},{1,0},{2,3},{3,2},{4,5},{5,4},{6,7},{7,6},{8,9},{9,8},{10,11... | collective-permute-start | bytes 663560 | tf_op jit(solution)/shard_map/ppermute | solution.py:24
  63.2 20.3 %collective-permute-start.15 = (bf16[272,384]{1,0:T(8,128)(2,1)S(1)}, bf16[272,384]{1,0:T(8,128)(2,1)S(1)}, u32[]{:S(2)}, u32[]{:S(2)}) collective-permute-start(bf16[272,384]{1,0:T(8,128)(2,1)S(1)} %get-tuple-element.75), channel_id=1, source_target_pairs={{0,4},{4,0},{8,12},{12,8},{1,5},{5,1},{9,13},{13,9},{2,6},{6,2},{1... | collective-permute-start | bytes 626696 | tf_op jit(solution)/shard_map/ppermute | solution.py:24
  65.0 18.5 %collective-permute-start.17 = (bf16[272,384]{1,0:T(8,128)(2,1)S(1)}, bf16[272,384]{1,0:T(8,128)(2,1)S(1)}, u32[]{:S(2)}, u32[]{:S(2)}) collective-permute-start(bf16[272,384]{1,0:T(8,128)(2,1)S(1)} %get-tuple-element.77), channel_id=1, source_target_pairs={{0,12},{4,8},{8,4},{12,0},{1,13},{5,9},{9,5},{13,1},{2,14},{6,10},... | collective-permute-start | bytes 626696 | tf_op jit(solution)/shard_map/ppermute | solution.py:24
  66.0 17.5 %collective-permute-start.16 = (bf16[256,384]{1,0:T(8,128)(2,1)S(1)}, bf16[256,384]{1,0:T(8,128)(2,1)S(1)}, u32[]{:S(2)}, u32[]{:S(2)}) collective-permute-start(bf16[256,384]{1,0:T(8,128)(2,1)S(1)} %get-tuple-element.76), channel_id=1, source_target_pairs={{0,8},{4,12},{8,0},{12,4},{1,9},{5,13},{9,1},{13,5},{2,10},{6,14},... | collective-permute-start | bytes 589832 | tf_op jit(solution)/shard_map/ppermute | solution.py:24
  66.8 23.3 %collective-permute-start.19 = (bf16[1024,384]{1,0:T(8,128)(2,1)S(1)}, bf16[1024,384]{1,0:T(8,128)(2,1)S(1)}, u32[]{:S(2)}, u32[]{:S(2)}) collective-permute-start(bf16[1024,384]{1,0:T(8,128)(2,1)S(1)} %collective-permute-done.13.refs_3_), channel_id=1, source_target_pairs={{8,12},{9,13},{10,14},{11,15},{24,28},{25,29},{26,30},{27,31}} | collective-permute-start | bytes 2359304 | tf_op jit(solution)/shard_map/ppermute | solution.py:33
  67.5 27.9 %collective-permute-start.20 = (bf16[1024,384]{1,0:T(8,128)(2,1)S(1)}, bf16[1024,384]{1,0:T(8,128)(2,1)S(1)}, u32[]{:S(2)}, u32[]{:S(2)}) collective-permute-start(bf16[1024,384]{1,0:T(8,128)(2,1)S(1)} %collective-permute-done.14.refs_4_), channel_id=1, source_target_pairs={{4,0},{5,1},{6,2},{7,3},{20,16},{21,17},{22,18},{23,19}} | collective-permute-start | bytes 2359304 | tf_op jit(solution)/shard_map/ppermute | solution.py:33
  83.7 13.9 %collective-permute-start.18 = (bf16[768,384]{1,0:T(8,128)(2,1)S(1)}, bf16[768,384]{1,0:T(8,128)(2,1)S(1)}, u32[]{:S(2)}, u32[]{:S(2)}) collective-permute-start(bf16[768,384]{1,0:T(8,128)(2,1)S(1)} %pad_maximum_fusion), channel_id=1, source_target_pairs={{0,2},{1,3},{2,0},{3,1},{4,6},{5,7},{6,4},{7,5},{8,10},{9,11},{10,... | collective-permute-start | bytes 1769480 | tf_op jit(solution)/shard_map/ppermute | solution.py:24
  85.2 12.4 %collective-permute-start.21 = (bf16[768,384]{1,0:T(8,128)(2,1)S(1)}, bf16[768,384]{1,0:T(8,128)(2,1)S(1)}, u32[]{:S(2)}, u32[]{:S(2)}) collective-permute-start(bf16[768,384]{1,0:T(8,128)(2,1)S(1)} %pad_maximum_fusion), channel_id=1, source_target_pairs={{0,1},{1,0},{2,3},{3,2},{4,5},{5,4},{6,7},{7,6},{8,9},{9,8},{10,11... | collective-permute-start | bytes 1769480 | tf_op jit(solution)/shard_map/ppermute | solution.py:24
  97.6 2.0 %collective-permute-start.22 = (bf16[768,384]{1,0:T(8,128)(2,1)S(1)}, bf16[768,384]{1,0:T(8,128)(2,1)S(1)}, u32[]{:S(2)}, u32[]{:S(2)}) collective-permute-start(bf16[768,384]{1,0:T(8,128)(2,1)S(1)} %collective-permute-done.18), channel_id=1, source_target_pairs={{0,1},{1,0},{2,3},{3,2},{4,5},{5,4},{6,7},{7,6},{8,9},{9,8},{10,11... | collective-permute-start | bytes 1769480 | tf_op jit(solution)/shard_map/ppermute | solution.py:24
  (2 other events, 1.3 us)

commit v8 on v7

--- a/solution.py
+++ b/solution.py
@@ -589,31 +589,28 @@
         return (in_grad, w_grad.transpose(1, 0, 2))
 
     outgoing = front(owners, exons, pre_act, most, size, nseq)
-    slope, plain = plain_gradient(pre_act, out_grad)
+    slope, plain = plain_gradient(*after([pre_act, out_grad], outgoing))
     arrived = [outgoing[0]] + [swap(outgoing[d], "seq", d) for d in range(1, nseq)]
-    (source,) = after([x_saved], outgoing)
-    up1, down1 = shift(source, "seq", 1), shift(source, "seq", -1)
+    far, near = swap(plain, "ch", 2), swap(plain, "ch", 1)
     *arrived, plain, slope = after([*arrived, plain, slope])
-    far, near = swap(plain, "ch", 2), swap(plain, "ch", 1)
     coverage = functools.reduce(jnp.add, [a.astype(jnp.float32) for a in arrived])
     splice = jnp.tanh(coverage - target).astype(jnp.bfloat16)
-    beside = swap(splice, "seq", 1)
-    both = swap(jnp.concatenate([splice, beside]), "seq", 2)
-    both, up1, down1 = after([both, up1, down1])
-    splices = [splice, beside, both]
+    splices = [splice] + [swap(splice, "seq", d) for d in range(1, nseq)]
+    (source,) = after([x_saved], [splice])
+    up1, down1 = shift(source, "seq", 1), shift(source, "seq", -1)
+    *splices, far, near = after([*splices, far, near])
     gained = gained_rows(owners, exons, out_grad, slope, splices, most, size, nseq)
 
     far_gained, near_gained = swap(gained, "ch", 2), swap(gained, "ch", 1)
-    up2, down2 = shift(up1, "seq", 1, 1), shift(down1, "seq", -1, 1)
     beyond = swap(far, "ch", 1)
     gained = [gained, near_gained, far_gained, swap(far_gained, "ch", 1)]
-    *gained, beyond, up2, down2 = after([*gained, beyond, up2, down2])
+    *gained, beyond, up1, down1 = after([*gained, beyond, up1, down1])
 
     quarter = rows // nch
     parts, sent, own = mend(exons, [plain, near, far, beyond], gained, size)
-    *sent, up2, down2 = after([*sent, up2, down2])
+    *sent, up1, down1 = after([*sent, up1, down1])
     got = [swap(block, "seq", d) for d, block in zip(range(1, nseq), sent)]
-    up3, down3 = shift(up2, "seq", 1, 2), shift(down2, "seq", -1, 2)
+    up2, down2 = shift(up1, "seq", 1, 1), shift(down1, "seq", -1, 1)
 
     def origins():
         return [(lax.axis_index("ch") ^ t) * width for t in range(nch)]
@@ -637,41 +634,60 @@
     across = swap(crossing, "ch", 2)
     beside = swap(crossing, "ch", 1)
     in_grad = pieces_gradient(parts, laid, taps, [got[0], got[2], center])
-    across, in_grad, up3, down3 = after([across, in_grad, up3, down3])
+    across, in_grad = after([across, in_grad])
     beyond = swap(across, "ch", 1)
-
-    def layout():
+    up3, down3 = shift(up2, "seq", 1, 2), shift(down2, "seq", -1, 2)
+
+    seam = (nseq - 1) * rows
+
+    def layout(hops, blocks, closing):
         mine = lax.axis_index("seq")
         place = lax.axis_index("ch")
         x_rows = [PAD + mine * rows]
-        for hop in range(1, nseq):
+        for hop in range(1, hops):
             low_at, high_at = mine - hop, mine + hop
             x_rows += [
                 jnp.where(low_at >= 0, PAD + low_at * rows, -1),
                 jnp.where(high_at < nseq, PAD + high_at * rows, -1),
             ]
+        used = (2, 3) if closing else blocks
         g_rows = [
-            (mine ^ d) * rows + (place ^ tag) * quarter
-            for d in range(1, nseq)
-            for tag in range(nch)
+            (mine ^ d) * rows + (place ^ tag) * quarter for d in used for tag in range(nch)
         ]
-        return x_rows, g_rows, [(mine ^ d) * rows for d in range(1, nseq)], [], []
-
-    g_pieces, stages = [], [0] * 5 + [1] * 2
-    for d in range(nseq - 1):
-        for piece in (crossing, beside, across, beyond):
-            g_pieces.append(piece[d * quarter : (d + 1) * quarter])
-            stages.append(d)
-    (w_grad,) = weight_gradient(
-        [x_saved, up1, down1, up2, down2, up3, down3],
-        g_pieces,
-        layout,
+        starts = [(mine ^ d) * rows for d in blocks]
+        if closing:
+            seams = [(mine == 0, seam - PAD, 1), (mine == nseq - 1, rows, -1)]
+            return x_rows, g_rows, starts, [], seams
+        return x_rows, g_rows, starts, [(mine == 0, PAD + seam), (mine == nseq - 1, rows)], []
+
+    def sources(blocks):
+        return [
+            kind[(d - 1) * quarter : d * quarter]
+            for d in blocks
+            for kind in (crossing, beside, across, beyond)
+        ]
+
+    (partial,) = weight_gradient(
+        [x_saved, up1, down1, up2, down2],
+        sources((1, 2)),
+        functools.partial(layout, 3, (1, 2), False),
         rows,
         taps,
         nseq * rows,
         before=partial,
+        last=False,
         vmem=32,
-        stages=stages,
+        stages=[0] * 9 + [1] * 4,
+    )
+    (w_grad,) = weight_gradient(
+        [x_saved, up1, down1, up2, down2, up3, down3],
+        sources((2, 3)),
+        functools.partial(layout, 4, (3,), True),
+        rows,
+        taps,
+        nseq * rows,
+        before=after([partial], [in_grad])[0],
+        vmem=32,
     )
     return (in_grad, w_grad.transpose(1, 0, 2))
 

time: 111 us -> 110 us (level)
  starting transfers between devices: 29.5 us -> 24 us
  Pallas kernels: 28.7 us -> 30.9 us
    ppermute x6, waiting for transfers between devices: 10.6 us -> 21.6 us  [shift(): return lax.ppermute(block, axis, pairs)]
    ppermute x17 -> x18, waiting for transfers between devices: 37 us -> 26.9 us  [swap(): return lax.ppermute(block, axis, [(i, i ^ flip) for i in range(count)])]
    ppermute x17 -> x18, starting transfers between devices: 21 us -> 16.8 us  [swap(): return lax.ppermute(block, axis, [(i, i ^ flip) for i in range(count)])]
    pallas_call x2 -> x3, Pallas kernels: 13.8 us -> 16.1 us  [weight_gradient(): pl.pallas_call(functools.partial(weight_kernel, taps=taps, tile=min(1024,...]
    ppermute x6, starting transfers between devices: 8.45 us -> 7.23 us  [shift(): return lax.ppermute(block, axis, pairs)]
    unnamed x22 -> x20, local copies, waits for them, and re-layouts: 3.5 us -> 3.55 us
  transfers between devices with their start and end apart: 23 -> 24, of which waited for: 10 -> 9; matrix products, arithmetic and copies ran while one was open for 0% -> 1% of each run, Pallas kernels for 13% -> 18%
where the time goes in v8:
time: 110 us; the launch traced here: 109 us
  waiting for transfers between devices  48.5 us (44%)
  Pallas kernels  30.9 us (28%)
  starting transfers between devices  24 us (22%)
  local copies, waits for them, and re-layouts  3.78 us (3%)
  other arithmetic  1.15 us (1%)
  between operations  1.13 us (1%)
    ppermute x18, waiting for transfers between devices, swap(): return lax.ppermute(block, axis, [(i, i ^ flip) for i in range(count)])  26.9 us
    ppermute x6, waiting for transfers between devices, shift(): return lax.ppermute(block, axis, pairs)  21.6 us
    ppermute x18, starting transfers between devices, swap(): return lax.ppermute(block, axis, [(i, i ^ flip) for i in range(count)])  16.8 us
    pallas_call x3, Pallas kernels, weight_gradient(): pl.pallas_call(functools.partial(weight_kernel, taps=taps, tile=min(1024,...  16.1 us
    pallas_call x2, Pallas kernels, pieces_gradient(): pl.pallas_call(functools.partial(pieces_kernel, taps=taps, pieces=len(par...  8.5 us
    ppermute x6, starting transfers between devices, shift(): return lax.ppermute(block, axis, pairs)  7.23 us
    unnamed x20, local copies, waits for them, and re-layouts  3.55 us
  transfers between devices with their start and end apart: 24, of which 9 were waited for; matrix products, arithmetic and copies ran while one was open for 1% of the time, Pallas kernels for 18%

profile of v8, /device:TPU:0, one launch (start us, length us, event | category | flops | bytes accessed | tf_op | source)
XLA Modules:
  0.0 109.5 jit_solution(12703380193152708556)
XLA Ops:
  0.7 1.2 %copy-done.1 = bf16[1024,384]{1,0:T(8,128)(2,1)S(1)} copy-done((bf16[1024,384]{1,0:T(8,128)(2,1)S(1)}, bf16[1024,384]{1,0:T(8,128)(2,1)}, u32[]{:S(2)}) %copy-start.1) | copy-done | bytes 786456
  3.2 1.4 %shard_map.86 = (bf16[64,384]{1,0:T(8,128)(2,1)S(1)}, bf16[64,384]{1,0:T(8,128)(2,1)S(1)}, bf16[64,384]{1,0:T(8,128)(2,1)S(1)}, bf16[64,384]{1,0:T(8,128)(2,1)S(1)}) custom-call(s32[16]{0:T(128)S(1)} %copy-done.6, s32[2,16]{1,0:T(2,128)S(1)} %bitcast.12, bf16[1024,384]{1,0:T(8,128)(2,1)S(1)} %copy-done.1), custom_call_target="tpu_custom_call" | custom-call | flops 1000 | bytes 1000 | tf_op jit(solution)/shard_map/pallas_call | solution.py:361
  4.6 1.0 copy-done.2
  5.6 1.5 %shard_map.87 = (f32[1024,384]{1,0:T(8,128)S(1)}, bf16[1024,384]{1,0:T(8,128)(2,1)S(1)}) custom-call(bf16[1024,384]{1,0:T(8,128)(2,1)S(1)} %copy-done.1, bf16[512,384]{1,0:T(8,128)(2,1)S(1)} %copy-done.2), custom_call_target="tpu_custom_call" | custom-call | flops 1000 | bytes 1000 | tf_op jit(solution)/shard_map/pallas_call | solution.py:388
  7.1 3.0 %collective-permute-start.6 = (bf16[1024,384]{1,0:T(8,128)(2,1)S(1)}, bf16[1024,384]{1,0:T(8,128)(2,1)S(1)}, u32[]{:S(2)}, u32[]{:S(2)}) collective-permute-start(bf16[1024,384]{1,0:T(8,128)(2,1)S(1)} %get-tuple-element.61.refs_0_), channel_id=1, source_target_pairs={{0,2},{1,3},{2,0},{3,1},{4,6},{5,7},{6,4},{7,5},{8,10},{9,11},{10,... | collective-permute-start | bytes 2359304 | tf_op jit(solution)/shard_map/ppermute | solution.py:24
  10.1 1.6 %collective-permute-start = (bf16[64,384]{1,0:T(8,128)(2,1)S(1)}, bf16[64,384]{1,0:T(8,128)(2,1)S(1)}, u32[]{:S(2)}, u32[]{:S(2)}) collective-permute-start(bf16[64,384]{1,0:T(8,128)(2,1)S(1)} %get-tuple-element.54), channel_id=1, source_target_pairs={{0,4},{4,0},{8,12},{12,8},{1,5},{5,1},{9,13},{13,9},{2,6},{6,2},{1... | collective-permute-start | bytes 147464 | tf_op jit(solution)/shard_map/ppermute | solution.py:24
  11.7 2.4 %collective-permute-start.1 = (bf16[64,384]{1,0:T(8,128)(2,1)S(1)}, bf16[64,384]{1,0:T(8,128)(2,1)S(1)}, u32[]{:S(2)}, u32[]{:S(2)}) collective-permute-start(bf16[64,384]{1,0:T(8,128)(2,1)S(1)} %get-tuple-element.55), channel_id=1, source_target_pairs={{0,8},{4,12},{8,0},{12,4},{1,9},{5,13},{9,1},{13,5},{2,10},{6,14},... | collective-permute-start | bytes 147464 | tf_op jit(solution)/shard_map/ppermute | solution.py:24
  14.5 3.4 %collective-permute-done.1 = bf16[64,384]{1,0:T(8,128)(2,1)S(1)} collective-permute-done((bf16[64,384]{1,0:T(8,128)(2,1)S(1)}, bf16[64,384]{1,0:T(8,128)(2,1)S(1)}, u32[]{:S(2)}, u32[]{:S(2)}) %collective-permute-start.1) | collective-permute-done | bytes 49184 | tf_op jit(solution)/shard_map/ppermute | solution.py:24
  17.9 2.1 %collective-permute-done.2 = bf16[64,384]{1,0:T(8,128)(2,1)S(1)} collective-permute-done((bf16[64,384]{1,0:T(8,128)(2,1)S(1)}, bf16[64,384]{1,0:T(8,128)(2,1)S(1)}, u32[]{:S(2)}, u32[]{:S(2)}) %collective-permute-start.2) | collective-permute-done | bytes 49184 | tf_op jit(solution)/shard_map/ppermute | solution.py:24
  20.0 1.1 fusion.1.refs_0_
  21.2 2.0 %collective-permute-start.4 = (bf16[64,384]{1,0:T(8,128)(2,1)S(1)}, bf16[64,384]{1,0:T(8,128)(2,1)S(1)}, u32[]{:S(2)}, u32[]{:S(2)}) collective-permute-start(bf16[64,384]{1,0:T(8,128)(2,1)S(1)} %fusion.1.refs_0_), channel_id=1, source_target_pairs={{0,8},{4,12},{8,0},{12,4},{1,9},{5,13},{9,1},{13,5},{2,10},{6,14},... | collective-permute-start | bytes 147464 | tf_op jit(solution)/shard_map/ppermute | solution.py:24
  23.2 2.4 %collective-permute-start.5 = (bf16[64,384]{1,0:T(8,128)(2,1)S(1)}, bf16[64,384]{1,0:T(8,128)(2,1)S(1)}, u32[]{:S(2)}, u32[]{:S(2)}) collective-permute-start(bf16[64,384]{1,0:T(8,128)(2,1)S(1)} %fusion.1.refs_0_), channel_id=1, source_target_pairs={{0,12},{4,8},{8,4},{12,0},{1,13},{5,9},{9,5},{13,1},{2,14},{6,10},... | collective-permute-start | bytes 147464 | tf_op jit(solution)/shard_map/ppermute | solution.py:24
  25.6 1.8 %collective-permute-start.12 = (bf16[1024,384]{1,0:T(8,128)(2,1)S(1)}, bf16[1024,384]{1,0:T(8,128)(2,1)S(1)}, u32[]{:S(2)}, u32[]{:S(2)}) collective-permute-start(bf16[1024,384]{1,0:T(8,128)(2,1)S(1)} %copy-done), channel_id=1, source_target_pairs={{0,4},{4,8},{8,12},{1,5},{5,9},{9,13},{2,6},{6,10},{10,14},{3,7},{... | collective-permute-start | bytes 2359304 | tf_op jit(solution)/shard_map/ppermute | solution.py:33
  27.4 1.3 %collective-permute-start.13 = (bf16[1024,384]{1,0:T(8,128)(2,1)S(1)}, bf16[1024,384]{1,0:T(8,128)(2,1)S(1)}, u32[]{:S(2)}, u32[]{:S(2)}) collective-permute-start(bf16[1024,384]{1,0:T(8,128)(2,1)S(1)} %copy-done), channel_id=1, source_target_pairs={{4,0},{8,4},{12,8},{5,1},{9,5},{13,9},{6,2},{10,6},{14,10},{7,3},{... | collective-permute-start | bytes 2359304 | tf_op jit(solution)/shard_map/ppermute | solution.py:33
  29.1 2.0 %shard_map.88.refs_4_ = bf16[288,384]{1,0:T(8,128)(2,1)S(1)} custom-call(s32[16]{0:T(128)S(1)} %copy-done.7, s32[2,16]{1,0:T(2,128)S(1)} %bitcast.13, bf16[512,384]{1,0:T(8,128)(2,1)S(1)} %copy-done.3, f32[1024,384]{1,0:T(8,128)S(1)} %get-tuple-element.68.slope, bf16[64,384]{1,0:T(8,128)(2,1)S(1)} %fusion.1.refs_0_, ...), custom_call_target="tpu_custom_call" | custom-call | flops 10000000000 | bytes 1000 | tf_op jit(solution)/shard_map/pallas_call | solution.py:435
  31.9 7.1 %collective-permute-done.9.refs_6_ = bf16[288,384]{1,0:T(8,128)(2,1)S(1)} collective-permute-done((bf16[288,384]{1,0:T(8,128)(2,1)S(1)}, bf16[288,384]{1,0:T(8,128)(2,1)S(1)}, u32[]{:S(2)}, u32[]{:S(2)}) %collective-permute-start.9) | collective-permute-done | bytes 221216 | tf_op jit(solution)/shard_map/ppermute | solution.py:24
  39.0 4.0 %collective-permute-done.12.refs_1_ = bf16[1024,384]{1,0:T(8,128)(2,1)S(1)} collective-permute-done((bf16[1024,384]{1,0:T(8,128)(2,1)S(1)}, bf16[1024,384]{1,0:T(8,128)(2,1)S(1)}, u32[]{:S(2)}, u32[]{:S(2)}) %collective-permute-start.12) | collective-permute-done | bytes 786464 | tf_op jit(solution)/shard_map/ppermute | solution.py:33
  43.0 3.7 %collective-permute-done.13.refs_2_ = bf16[1024,384]{1,0:T(8,128)(2,1)S(1)} collective-permute-done((bf16[1024,384]{1,0:T(8,128)(2,1)S(1)}, bf16[1024,384]{1,0:T(8,128)(2,1)S(1)}, u32[]{:S(2)}, u32[]{:S(2)}) %collective-permute-start.13) | collective-permute-done | bytes 786464 | tf_op jit(solution)/shard_map/ppermute | solution.py:33
  46.7 1.4 %shard_map.89 = (bf16[1024,384]{1,0:T(8,128)(2,1)S(1)}, bf16[1024,384]{1,0:T(8,128)(2,1)S(1)}, bf16[1024,384]{1,0:T(8,128)(2,1)S(1)}, bf16[1024,384]{1,0:T(8,128...) custom-call(s32[2,16]{1,0:T(2,128)S(1)} %bitcast.14, ...), custom_call_target="tpu_custom_call", output_to_operand_aliasing={{0}: (1, {}), {1}: (2, {}), {2}: (3, {}), {3}: (4, {})} | custom-call | flops 1000 | bytes 1000 | tf_op jit(solution)/shard_map/pallas_call | solution.py:511
  48.2 1.8 %collective-permute-start.14 = (bf16[272,384]{1,0:T(8,128)(2,1)S(1)}, bf16[272,384]{1,0:T(8,128)(2,1)S(1)}, u32[]{:S(2)}, u32[]{:S(2)}) collective-permute-start(bf16[272,384]{1,0:T(8,128)(2,1)S(1)} %get-tuple-element.84), channel_id=1, source_target_pairs={{0,4},{4,0},{8,12},{12,8},{1,5},{5,1},{9,13},{13,9},{2,6},{6,2},{1... | collective-permute-start | bytes 626696 | tf_op jit(solution)/shard_map/ppermute | solution.py:24
  50.0 1.5 %collective-permute-start.16 = (bf16[272,384]{1,0:T(8,128)(2,1)S(1)}, bf16[272,384]{1,0:T(8,128)(2,1)S(1)}, u32[]{:S(2)}, u32[]{:S(2)}) collective-permute-start(bf16[272,384]{1,0:T(8,128)(2,1)S(1)} %get-tuple-element.86), channel_id=1, source_target_pairs={{0,12},{4,8},{8,4},{12,0},{1,13},{5,9},{9,5},{13,1},{2,14},{6,10},... | collective-permute-start | bytes 626696 | tf_op jit(solution)/shard_map/ppermute | solution.py:24
  52.4 1.5 %collective-permute-start.19 = (bf16[1024,384]{1,0:T(8,128)(2,1)S(1)}, bf16[1024,384]{1,0:T(8,128)(2,1)S(1)}, u32[]{:S(2)}, u32[]{:S(2)}) collective-permute-start(bf16[1024,384]{1,0:T(8,128)(2,1)S(1)} %collective-permute-done.13.refs_2_), channel_id=1, source_target_pairs={{4,0},{8,4},{5,1},{9,5},{6,2},{10,6},{7,3},{11,7},{20,16},{24,20},... | collective-permute-start | bytes 2359304 | tf_op jit(solution)/shard_map/ppermute | solution.py:33
  54.0 2.8 %shard_map.90 = (f32[384,1920]{1,0:T(8,128)S(1)}, bf16[1536,1920]{1,0:T(8,128)(2,1)S(1)}) custom-call(bf16[16,384]{1,0:T(8,128)(2,1)S(1)} %slice.42.refs_0_, bf16[1024,384]{1,0:T(8,128)(2,1)S(1)} %copy-done, bf16[16,384]{1,0:T(8,128)(2,1)S(1)} %slice.43.refs_2_, bf16[1024,384]{1,0:T(8,128)(2,1)S(1)} %get-tuple-element.89.refs_3_, ...), custom_call_target="tpu_custom_call" | custom-call | flops 1000 | bytes 1000 | tf_op jit(solution)/shard_map/pallas_call | solution.py:258
  56.8 3.7 %shard_map.91.refs_6_ = bf16[512,384]{1,0:T(8,128)(2,1)S(1)} custom-call(bf16[1024,384]{1,0:T(8,128)(2,1)S(1)} %get-tuple-element.91.refs_0_, bf16[1024,384]{1,0:T(8,128)(2,1)S(1)} %get-tuple-element.92.refs_1_, bf16[1024,384]{1,0:T(8,128)(2,1)S(1)} %get-tuple-element.93.refs_2_, bf16[1024,384]{1,0:T(8,128)(2,1)S(1)} %get-tuple-element.94.refs_3_, ...), custom_call_target="tpu_custom_call" | custom-call | flops 1000 | bytes 1000 | tf_op jit(solution)/shard_map/pallas_call | solution.py:133
  60.5 8.5 %collective-permute-done.15.refs_9_.refs_7_ = bf16[256,384]{1,0:T(8,128)(2,1)S(1)} collective-permute-done((bf16[256,384]{1,0:T(8,128)(2,1)S(1)}, bf16[256,384]{1,0:T(8,128)(2,1)S(1)}, u32[]{:S(2)}, u32[]{:S(2)}) %collective-permute-start.15) | collective-permute-done | bytes 196640 | tf_op jit(solution)/shard_map/ppermute | solution.py:24
  69.7 4.8 %shard_map.92 = bf16[1024,384]{1,0:T(8,128)(2,1)} custom-call(bf16[1024,384]{1,0:T(8,128)(2,1)S(1)} %get-tuple-element.91.refs_0_, bf16[1024,384]{1,0:T(8,128)(2,1)S(1)} %get-tuple-element.92.refs_1_, bf16[1024,384]{1,0:T(8,128)(2,1)S(1)} %get-tuple-element.93.refs_2_, bf16[1024,384]{1,0:T(8,128)(2,1)S(1)} %get-tuple-element.94.refs_3_, ...), custom_call_target="tpu_custom_call" | custom-call | flops 1000 | bytes 1000 | tf_op jit(solution)/shard_map/pallas_call | solution.py:133
  74.5 5.3 %collective-permute-done.17 = bf16[768,384]{1,0:T(8,128)(2,1)S(1)} collective-permute-done((bf16[768,384]{1,0:T(8,128)(2,1)S(1)}, bf16[768,384]{1,0:T(8,128)(2,1)S(1)}, u32[]{:S(2)}, u32[]{:S(2)}) %collective-permute-start.17) | collective-permute-done | bytes 589856 | tf_op jit(solution)/shard_map/ppermute | solution.py:24
  79.9 0.7 collective-permute-start.20
  80.6 1.3 %collective-permute-start.21 = (bf16[1024,384]{1,0:T(8,128)(2,1)S(1)}, bf16[1024,384]{1,0:T(8,128)(2,1)S(1)}, u32[]{:S(2)}, u32[]{:S(2)}) collective-permute-start(bf16[1024,384]{1,0:T(8,128)(2,1)S(1)} %collective-permute-done.19.refs_4_), channel_id=1, source_target_pairs={{4,0},{5,1},{6,2},{7,3},{20,16},{21,17},{22,18},{23,19}} | collective-permute-start | bytes 2359304 | tf_op jit(solution)/shard_map/ppermute | solution.py:33
  82.1 6.4 %shard_map.93.refs_15_ = f32[384,1920]{1,0:T(8,128)S(1)} custom-call(bf16[1024,384]{1,0:T(8,128)(2,1)S(1)} %copy-done, bf16[1024,384]{1,0:T(8,128)(2,1)S(1)} %collective-permute-done.12.refs_1_, bf16[1024,384]{1,0:T(8,128)(2,1)S(1)} %collective-permute-done.13.refs_2_, bf16[1024,384]{1,0:T(8,128)(2,1)S(1)} %collective-permute-done.18.refs_3_, ...), custom_call_target="tpu_custom_call" | custom-call | flops 1000 | bytes 1000 | tf_op jit(solution)/shard_map/pallas_call | solution.py:258
  88.6 13.9 %collective-permute-done.21.refs_6_ = bf16[1024,384]{1,0:T(8,128)(2,1)S(1)} collective-permute-done((bf16[1024,384]{1,0:T(8,128)(2,1)S(1)}, bf16[1024,384]{1,0:T(8,128)(2,1)S(1)}, u32[]{:S(2)}, u32[]{:S(2)}) %collective-permute-start.21) | collective-permute-done | bytes 786464 | tf_op jit(solution)/shard_map/ppermute | solution.py:33
  102.4 6.9 %shard_map.94 = bf16[5,384,384]{2,1,0:T(8,128)(2,1)} custom-call(bf16[1024,384]{1,0:T(8,128)(2,1)S(1)} %copy-done, bf16[1024,384]{1,0:T(8,128)(2,1)S(1)} %collective-permute-done.12.refs_1_, bf16[1024,384]{1,0:T(8,128)(2,1)S(1)} %collective-permute-done.13.refs_2_, bf16[1024,384]{1,0:T(8,128)(2,1)S(1)} %collective-permute-done.18.refs_3_, ...), custom_call_target="tpu_custom_call" | custom-call | flops 1000 | bytes 1000 | tf_op jit(solution)/shard_map/pallas_call | solution.py:258
  (55 shorter events, 4.9 us)
Async XLA Ops:
  0.6 24.9 %copy-start = (bf16[1024,384]{1,0:T(8,128)(2,1)S(1)}, bf16[1024,384]{1,0:T(8,128)(2,1)}, u32[]{:S(2)}) copy-start(bf16[1024,384]{1,0:T(8,128)(2,1)} %refs_0_.3) | copy-start | bytes 2359300
  0.6 1.2 %copy-start.1 = (bf16[1024,384]{1,0:T(8,128)(2,1)S(1)}, bf16[1024,384]{1,0:T(8,128)(2,1)}, u32[]{:S(2)}) copy-start(bf16[1024,384]{1,0:T(8,128)(2,1)} %pre_act.2) | copy-start | bytes 2359300
  3.2 25.9 %copy-start.5 = (s32[16,2]{0,1:T(2,128)S(1)}, s32[16,2]{0,1:T(2,128)}, u32[]{:S(2)}) copy-start(s32[16,2]{0,1:T(2,128)} %param.13) | copy-start | bytes 388
  3.2 25.9 %copy-start.7 = (s32[16]{0:T(128)S(1)}, s32[16]{0:T(128)}, u32[]{:S(2)}) copy-start(s32[16]{0:T(128)} %owners.3) | copy-start | bytes 196
  4.6 1.0 copy-start.2
  5.6 23.6 %copy-start.3 = (bf16[512,384]{1,0:T(8,128)(2,1)S(1)}, bf16[512,384]{1,0:T(8,128)(2,1)}, u32[]{:S(2)}) copy-start(bf16[512,384]{1,0:T(8,128)(2,1)} %out_grad.2) | copy-start | bytes 1179652
  7.1 22.0 %collective-permute-start.6 = (bf16[1024,384]{1,0:T(8,128)(2,1)S(1)}, bf16[1024,384]{1,0:T(8,128)(2,1)S(1)}, u32[]{:S(2)}, u32[]{:S(2)}) collective-permute-start(bf16[1024,384]{1,0:T(8,128)(2,1)S(1)} %get-tuple-element.61.refs_0_), channel_id=1, source_target_pairs={{0,2},{1,3},{2,0},{3,1},{4,6},{5,7},{6,4},{7,5},{8,10},{9,11},{10,... | collective-permute-start | bytes 2359304 | tf_op jit(solution)/shard_map/ppermute | solution.py:24
  10.1 19.0 %collective-permute-start.7 = (bf16[1024,384]{1,0:T(8,128)(2,1)S(1)}, bf16[1024,384]{1,0:T(8,128)(2,1)S(1)}, u32[]{:S(2)}, u32[]{:S(2)}) collective-permute-start(bf16[1024,384]{1,0:T(8,128)(2,1)S(1)} %get-tuple-element.61.refs_0_), channel_id=1, source_target_pairs={{0,1},{1,0},{2,3},{3,2},{4,5},{5,4},{6,7},{7,6},{8,9},{9,8},{10,11... | collective-permute-start | bytes 2359304 | tf_op jit(solution)/shard_map/ppermute | solution.py:24
  10.1 4.4 %collective-permute-start = (bf16[64,384]{1,0:T(8,128)(2,1)S(1)}, bf16[64,384]{1,0:T(8,128)(2,1)S(1)}, u32[]{:S(2)}, u32[]{:S(2)}) collective-permute-start(bf16[64,384]{1,0:T(8,128)(2,1)S(1)} %get-tuple-element.54), channel_id=1, source_target_pairs={{0,4},{4,0},{8,12},{12,8},{1,5},{5,1},{9,13},{13,9},{2,6},{6,2},{1... | collective-permute-start | bytes 147464 | tf_op jit(solution)/shard_map/ppermute | solution.py:24
  11.7 6.2 %collective-permute-start.1 = (bf16[64,384]{1,0:T(8,128)(2,1)S(1)}, bf16[64,384]{1,0:T(8,128)(2,1)S(1)}, u32[]{:S(2)}, u32[]{:S(2)}) collective-permute-start(bf16[64,384]{1,0:T(8,128)(2,1)S(1)} %get-tuple-element.55), channel_id=1, source_target_pairs={{0,8},{4,12},{8,0},{12,4},{1,9},{5,13},{9,1},{13,5},{2,10},{6,14},... | collective-permute-start | bytes 147464 | tf_op jit(solution)/shard_map/ppermute | solution.py:24
  14.1 5.9 %collective-permute-start.2 = (bf16[64,384]{1,0:T(8,128)(2,1)S(1)}, bf16[64,384]{1,0:T(8,128)(2,1)S(1)}, u32[]{:S(2)}, u32[]{:S(2)}) collective-permute-start(bf16[64,384]{1,0:T(8,128)(2,1)S(1)} %get-tuple-element.56), channel_id=1, source_target_pairs={{0,12},{4,8},{8,4},{12,0},{1,13},{5,9},{9,5},{13,1},{2,14},{6,10},... | collective-permute-start | bytes 147464 | tf_op jit(solution)/shard_map/ppermute | solution.py:24
  20.0 33.9 %slice-start = ((s8[5898240]{0:T(1024)(128)(4,1)}), s8[4194304]{0:T(1024)(128)(4,1)S(1)}, s32[]{:S(2)}) async-start(s8[5898240]{0:T(1024)(128)(4,1)} %bitcast.9), calls=%async_computation | async-start | bytes 8388608
  21.1 32.8 %slice-start.1 = ((s8[5898240]{0:T(1024)(128)(4,1)}), s8[1703936]{0:T(1024)(128)(4,1)S(1)}, s32[]{:S(2)}) async-start(s8[5898240]{0:T(1024)(128)(4,1)} %bitcast.9), calls=%async_computation.1 | async-start | bytes 3407872
  21.1 4.5 %collective-permute-start.3 = (bf16[64,384]{1,0:T(8,128)(2,1)S(1)}, bf16[64,384]{1,0:T(8,128)(2,1)S(1)}, u32[]{:S(2)}, u32[]{:S(2)}) collective-permute-start(bf16[64,384]{1,0:T(8,128)(2,1)S(1)} %fusion.1.refs_0_), channel_id=1, source_target_pairs={{0,4},{4,0},{8,12},{12,8},{1,5},{5,1},{9,13},{13,9},{2,6},{6,2},{1... | collective-permute-start | bytes 147464 | tf_op jit(solution)/shard_map/ppermute | solution.py:24
  21.2 6.2 %collective-permute-start.4 = (bf16[64,384]{1,0:T(8,128)(2,1)S(1)}, bf16[64,384]{1,0:T(8,128)(2,1)S(1)}, u32[]{:S(2)}, u32[]{:S(2)}) collective-permute-start(bf16[64,384]{1,0:T(8,128)(2,1)S(1)} %fusion.1.refs_0_), channel_id=1, source_target_pairs={{0,8},{4,12},{8,0},{12,4},{1,9},{5,13},{9,1},{13,5},{2,10},{6,14},... | collective-permute-start | bytes 147464 | tf_op jit(solution)/shard_map/ppermute | solution.py:24
  23.2 5.9 %collective-permute-start.5 = (bf16[64,384]{1,0:T(8,128)(2,1)S(1)}, bf16[64,384]{1,0:T(8,128)(2,1)S(1)}, u32[]{:S(2)}, u32[]{:S(2)}) collective-permute-start(bf16[64,384]{1,0:T(8,128)(2,1)S(1)} %fusion.1.refs_0_), channel_id=1, source_target_pairs={{0,12},{4,8},{8,4},{12,0},{1,13},{5,9},{9,5},{13,1},{2,14},{6,10},... | collective-permute-start | bytes 147464 | tf_op jit(solution)/shard_map/ppermute | solution.py:24
  25.6 17.4 %collective-permute-start.12 = (bf16[1024,384]{1,0:T(8,128)(2,1)S(1)}, bf16[1024,384]{1,0:T(8,128)(2,1)S(1)}, u32[]{:S(2)}, u32[]{:S(2)}) collective-permute-start(bf16[1024,384]{1,0:T(8,128)(2,1)S(1)} %copy-done), channel_id=1, source_target_pairs={{0,4},{4,8},{8,12},{1,5},{5,9},{9,13},{2,6},{6,10},{10,14},{3,7},{... | collective-permute-start | bytes 2359304 | tf_op jit(solution)/shard_map/ppermute | solution.py:33
  27.4 19.4 %collective-permute-start.13 = (bf16[1024,384]{1,0:T(8,128)(2,1)S(1)}, bf16[1024,384]{1,0:T(8,128)(2,1)S(1)}, u32[]{:S(2)}, u32[]{:S(2)}) collective-permute-start(bf16[1024,384]{1,0:T(8,128)(2,1)S(1)} %copy-done), channel_id=1, source_target_pairs={{4,0},{8,4},{12,8},{5,1},{9,5},{13,9},{6,2},{10,6},{14,10},{7,3},{... | collective-permute-start | bytes 2359304 | tf_op jit(solution)/shard_map/ppermute | solution.py:33
  29.1 17.6 %collective-permute-start.11 = (bf16[1024,384]{1,0:T(8,128)(2,1)S(1)}, bf16[1024,384]{1,0:T(8,128)(2,1)S(1)}, u32[]{:S(2)}, u32[]{:S(2)}) collective-permute-start(bf16[1024,384]{1,0:T(8,128)(2,1)S(1)} %collective-permute-done.6.refs_2_), channel_id=1, source_target_pairs={{0,1},{1,0},{2,3},{3,2},{4,5},{5,4},{6,7},{7,6},{8,9},{9,8},{10,11... | collective-permute-start | bytes 2359304 | tf_op jit(solution)/shard_map/ppermute | solution.py:24
  31.1 7.9 %collective-permute-start.9 = (bf16[288,384]{1,0:T(8,128)(2,1)S(1)}, bf16[288,384]{1,0:T(8,128)(2,1)S(1)}, u32[]{:S(2)}, u32[]{:S(2)}) collective-permute-start(bf16[288,384]{1,0:T(8,128)(2,1)S(1)} %shard_map.88.refs_4_), channel_id=1, source_target_pairs={{0,2},{1,3},{2,0},{3,1},{4,6},{5,7},{6,4},{7,5},{8,10},{9,11},{10,... | collective-permute-start | bytes 663560 | tf_op jit(solution)/shard_map/ppermute | solution.py:24
  31.7 15.0 %collective-permute-start.8 = (bf16[288,384]{1,0:T(8,128)(2,1)S(1)}, bf16[288,384]{1,0:T(8,128)(2,1)S(1)}, u32[]{:S(2)}, u32[]{:S(2)}) collective-permute-start(bf16[288,384]{1,0:T(8,128)(2,1)S(1)} %shard_map.88.refs_4_), channel_id=1, source_target_pairs={{0,1},{1,0},{2,3},{3,2},{4,5},{5,4},{6,7},{7,6},{8,9},{9,8},{10,11... | collective-permute-start | bytes 663560 | tf_op jit(solution)/shard_map/ppermute | solution.py:24
  39.0 7.7 %collective-permute-start.10 = (bf16[288,384]{1,0:T(8,128)(2,1)S(1)}, bf16[288,384]{1,0:T(8,128)(2,1)S(1)}, u32[]{:S(2)}, u32[]{:S(2)}) collective-permute-start(bf16[288,384]{1,0:T(8,128)(2,1)S(1)} %collective-permute-done.9.refs_6_), channel_id=1, source_target_pairs={{0,1},{1,0},{2,3},{3,2},{4,5},{5,4},{6,7},{7,6},{8,9},{9,8},{10,11... | collective-permute-start | bytes 663560 | tf_op jit(solution)/shard_map/ppermute | solution.py:24
  48.2 20.8 %collective-permute-start.14 = (bf16[272,384]{1,0:T(8,128)(2,1)S(1)}, bf16[272,384]{1,0:T(8,128)(2,1)S(1)}, u32[]{:S(2)}, u32[]{:S(2)}) collective-permute-start(bf16[272,384]{1,0:T(8,128)(2,1)S(1)} %get-tuple-element.84), channel_id=1, source_target_pairs={{0,4},{4,0},{8,12},{12,8},{1,5},{5,1},{9,13},{13,9},{2,6},{6,2},{1... | collective-permute-start | bytes 626696 | tf_op jit(solution)/shard_map/ppermute | solution.py:24
  50.0 19.0 %collective-permute-start.16 = (bf16[272,384]{1,0:T(8,128)(2,1)S(1)}, bf16[272,384]{1,0:T(8,128)(2,1)S(1)}, u32[]{:S(2)}, u32[]{:S(2)}) collective-permute-start(bf16[272,384]{1,0:T(8,128)(2,1)S(1)} %get-tuple-element.86), channel_id=1, source_target_pairs={{0,12},{4,8},{8,4},{12,0},{1,13},{5,9},{9,5},{13,1},{2,14},{6,10},... | collective-permute-start | bytes 626696 | tf_op jit(solution)/shard_map/ppermute | solution.py:24
  51.5 17.5 %collective-permute-start.15 = (bf16[256,384]{1,0:T(8,128)(2,1)S(1)}, bf16[256,384]{1,0:T(8,128)(2,1)S(1)}, u32[]{:S(2)}, u32[]{:S(2)}) collective-permute-start(bf16[256,384]{1,0:T(8,128)(2,1)S(1)} %get-tuple-element.85), channel_id=1, source_target_pairs={{0,8},{4,12},{8,0},{12,4},{1,9},{5,13},{9,1},{13,5},{2,10},{6,14},... | collective-permute-start | bytes 589832 | tf_op jit(solution)/shard_map/ppermute | solution.py:24
  51.7 28.2 %collective-permute-start.18 = (bf16[1024,384]{1,0:T(8,128)(2,1)S(1)}, bf16[1024,384]{1,0:T(8,128)(2,1)S(1)}, u32[]{:S(2)}, u32[]{:S(2)}) collective-permute-start(bf16[1024,384]{1,0:T(8,128)(2,1)S(1)} %collective-permute-done.12.refs_1_), channel_id=1, source_target_pairs={{4,8},{8,12},{5,9},{9,13},{6,10},{10,14},{7,11},{11,15},{20,24},{2... | collective-permute-start | bytes 2359304 | tf_op jit(solution)/shard_map/ppermute | solution.py:33
  52.4 28.2 %collective-permute-start.19 = (bf16[1024,384]{1,0:T(8,128)(2,1)S(1)}, bf16[1024,384]{1,0:T(8,128)(2,1)S(1)}, u32[]{:S(2)}, u32[]{:S(2)}) collective-permute-start(bf16[1024,384]{1,0:T(8,128)(2,1)S(1)} %collective-permute-done.13.refs_2_), channel_id=1, source_target_pairs={{4,0},{8,4},{5,1},{9,5},{6,2},{10,6},{7,3},{11,7},{20,16},{24,20},... | collective-permute-start | bytes 2359304 | tf_op jit(solution)/shard_map/ppermute | solution.py:33
  69.1 10.7 %collective-permute-start.17 = (bf16[768,384]{1,0:T(8,128)(2,1)S(1)}, bf16[768,384]{1,0:T(8,128)(2,1)S(1)}, u32[]{:S(2)}, u32[]{:S(2)}) collective-permute-start(bf16[768,384]{1,0:T(8,128)(2,1)S(1)} %pad_maximum_fusion), channel_id=1, source_target_pairs={{0,2},{1,3},{2,0},{3,1},{4,6},{5,7},{6,4},{7,5},{8,10},{9,11},{10,... | collective-permute-start | bytes 1769480 | tf_op jit(solution)/shard_map/ppermute | solution.py:24
  69.7 12.2 %collective-permute-start.22 = (bf16[768,384]{1,0:T(8,128)(2,1)S(1)}, bf16[768,384]{1,0:T(8,128)(2,1)S(1)}, u32[]{:S(2)}, u32[]{:S(2)}) collective-permute-start(bf16[768,384]{1,0:T(8,128)(2,1)S(1)} %pad_maximum_fusion), channel_id=1, source_target_pairs={{0,1},{1,0},{2,3},{3,2},{4,5},{5,4},{6,7},{7,6},{8,9},{9,8},{10,11... | collective-permute-start | bytes 1769480 | tf_op jit(solution)/shard_map/ppermute | solution.py:24
  79.9 2.2 %collective-permute-start.23 = (bf16[768,384]{1,0:T(8,128)(2,1)S(1)}, bf16[768,384]{1,0:T(8,128)(2,1)S(1)}, u32[]{:S(2)}, u32[]{:S(2)}) collective-permute-start(bf16[768,384]{1,0:T(8,128)(2,1)S(1)} %collective-permute-done.17), channel_id=1, source_target_pairs={{0,1},{1,0},{2,3},{3,2},{4,5},{5,4},{6,7},{7,6},{8,9},{9,8},{10,11... | collective-permute-start | bytes 1769480 | tf_op jit(solution)/shard_map/ppermute | solution.py:24
  79.9 8.7 %collective-permute-start.20 = (bf16[1024,384]{1,0:T(8,128)(2,1)S(1)}, bf16[1024,384]{1,0:T(8,128)(2,1)S(1)}, u32[]{:S(2)}, u32[]{:S(2)}) collective-permute-start(bf16[1024,384]{1,0:T(8,128)(2,1)S(1)} %collective-permute-done.18.refs_3_), channel_id=1, source_target_pairs={{8,12},{9,13},{10,14},{11,15},{24,28},{25,29},{26,30},{27,31}} | collective-permute-start | bytes 2359304 | tf_op jit(solution)/shard_map/ppermute | solution.py:33
  80.6 21.8 %collective-permute-start.21 = (bf16[1024,384]{1,0:T(8,128)(2,1)S(1)}, bf16[1024,384]{1,0:T(8,128)(2,1)S(1)}, u32[]{:S(2)}, u32[]{:S(2)}) collective-permute-start(bf16[1024,384]{1,0:T(8,128)(2,1)S(1)} %collective-permute-done.19.refs_4_), channel_id=1, source_target_pairs={{4,0},{5,1},{6,2},{7,3},{20,16},{21,17},{22,18},{23,19}} | collective-permute-start | bytes 2359304 | tf_op jit(solution)/shard_map/ppermute | solution.py:33
  (2 other events, 1.3 us)

commit v9 on v7

--- a/solution.py
+++ b/solution.py
@@ -15,7 +15,7 @@
 HALF_ROOT = 0.7071067811865476
 DENSITY = 0.3989422804014327
 LANES = 128
-LONG = pl.CostEstimate(flops=10**10, bytes_accessed=1000, transcendentals=0)
+LONG = pl.CostEstimate(flops=5 * 10**9, bytes_accessed=1000, transcendentals=0)
 LITTLE = pl.CostEstimate(flops=1000, bytes_accessed=1000, transcendentals=0)
 
 
@@ -589,19 +589,18 @@
         return (in_grad, w_grad.transpose(1, 0, 2))
 
     outgoing = front(owners, exons, pre_act, most, size, nseq)
-    slope, plain = plain_gradient(pre_act, out_grad)
+    slope, plain = plain_gradient(*after([pre_act, out_grad], outgoing))
     arrived = [outgoing[0]] + [swap(outgoing[d], "seq", d) for d in range(1, nseq)]
     (source,) = after([x_saved], outgoing)
     up1, down1 = shift(source, "seq", 1), shift(source, "seq", -1)
-    *arrived, plain, slope = after([*arrived, plain, slope])
     far, near = swap(plain, "ch", 2), swap(plain, "ch", 1)
+    *arrived, plain, slope, near = after([*arrived, plain, slope, near])
     coverage = functools.reduce(jnp.add, [a.astype(jnp.float32) for a in arrived])
     splice = jnp.tanh(coverage - target).astype(jnp.bfloat16)
-    beside = swap(splice, "seq", 1)
-    both = swap(jnp.concatenate([splice, beside]), "seq", 2)
-    both, up1, down1 = after([both, up1, down1])
-    splices = [splice, beside, both]
+    splices = [splice] + [swap(splice, "seq", d) for d in range(1, nseq)]
+    *splices, far = after([*splices, far])
     gained = gained_rows(owners, exons, out_grad, slope, splices, most, size, nseq)
+    gained, up1, down1 = after([gained, up1, down1])
 
     far_gained, near_gained = swap(gained, "ch", 2), swap(gained, "ch", 1)
     up2, down2 = shift(up1, "seq", 1, 1), shift(down1, "seq", -1, 1)

time: 111 us -> 111 us (level)
    ppermute x17 -> x18, waiting for transfers between devices: 37 us -> 32.4 us  [swap(): return lax.ppermute(block, axis, [(i, i ^ flip) for i in range(count)])]
    ppermute x6, waiting for transfers between devices: 10.6 us -> 14.3 us  [shift(): return lax.ppermute(block, axis, pairs)]
    ppermute x17 -> x18, starting transfers between devices: 21 us -> 21.1 us  [swap(): return lax.ppermute(block, axis, [(i, i ^ flip) for i in range(count)])]
    unnamed x22 -> x20, local copies, waits for them, and re-layouts: 3.5 us -> 3.49 us
  transfers between devices with their start and end apart: 23 -> 24, of which waited for: 10 -> 12; matrix products, arithmetic and copies ran while one was open for 0% -> 1% of each run, Pallas kernels for 13% -> 12%
where the time goes in v9:
time: 111 us
  waiting for transfers between devices  46.7 us (42%)
  starting transfers between devices  29.8 us (27%)
  Pallas kernels  28.4 us (26%)
  local copies, waits for them, and re-layouts  3.72 us (3%)
  other arithmetic  1.15 us (1%)
    ppermute x18, waiting for transfers between devices, swap(): return lax.ppermute(block, axis, [(i, i ^ flip) for i in range(count)])  32.4 us
    ppermute x18, starting transfers between devices, swap(): return lax.ppermute(block, axis, [(i, i ^ flip) for i in range(count)])  21.1 us
    ppermute x6, waiting for transfers between devices, shift(): return lax.ppermute(block, axis, pairs)  14.3 us
    pallas_call x2, Pallas kernels, weight_gradient(): pl.pallas_call(functools.partial(weight_kernel, taps=taps, tile=min(1024,...  13.8 us
    ppermute x6, starting transfers between devices, shift(): return lax.ppermute(block, axis, pairs)  8.7 us
    pallas_call x2, Pallas kernels, pieces_gradient(): pl.pallas_call(functools.partial(pieces_kernel, taps=taps, pieces=len(par...  8.51 us
    unnamed x20, local copies, waits for them, and re-layouts  3.49 us
  transfers between devices with their start and end apart: 24, of which 12 were waited for; matrix products, arithmetic and copies ran while one was open for 1% of the time, Pallas kernels for 12%

profile of v9, /device:TPU:0, one launch (start us, length us, event | category | flops | bytes accessed | tf_op | source)
XLA Modules:
  0.0 110.9 jit_solution(10952234086386342029)
XLA Ops:
  0.7 1.1 %copy-done = bf16[1024,384]{1,0:T(8,128)(2,1)S(1)} copy-done((bf16[1024,384]{1,0:T(8,128)(2,1)S(1)}, bf16[1024,384]{1,0:T(8,128)(2,1)}, u32[]{:S(2)}) %copy-start) | copy-done | bytes 786456
  3.1 1.3 %shard_map.86 = (bf16[64,384]{1,0:T(8,128)(2,1)S(1)}, bf16[64,384]{1,0:T(8,128)(2,1)S(1)}, bf16[64,384]{1,0:T(8,128)(2,1)S(1)}, bf16[64,384]{1,0:T(8,128)(2,1)S(1)}) custom-call(s32[16]{0:T(128)S(1)} %copy-done.6, s32[2,16]{1,0:T(2,128)S(1)} %bitcast.12, bf16[1024,384]{1,0:T(8,128)(2,1)S(1)} %copy-done), custom_call_target="tpu_custom_call" | custom-call | flops 1000 | bytes 1000 | tf_op jit(solution)/shard_map/pallas_call | solution.py:361
  5.5 1.5 %shard_map.87 = (f32[1024,384]{1,0:T(8,128)S(1)}, bf16[1024,384]{1,0:T(8,128)(2,1)S(1)}) custom-call(bf16[1024,384]{1,0:T(8,128)(2,1)S(1)} %copy-done, bf16[512,384]{1,0:T(8,128)(2,1)S(1)} %copy-done.2), custom_call_target="tpu_custom_call" | custom-call | flops 1000 | bytes 1000 | tf_op jit(solution)/shard_map/pallas_call | solution.py:388
  7.5 2.6 %collective-permute-start.7 = (bf16[1024,384]{1,0:T(8,128)(2,1)S(1)}, bf16[1024,384]{1,0:T(8,128)(2,1)S(1)}, u32[]{:S(2)}, u32[]{:S(2)}) collective-permute-start(bf16[1024,384]{1,0:T(8,128)(2,1)S(1)} %get-tuple-element.65.refs_0_), channel_id=1, source_target_pairs={{0,2},{1,3},{2,0},{3,1},{4,6},{5,7},{6,4},{7,5},{8,10},{9,11},{10,... | collective-permute-start | bytes 2359304 | tf_op jit(solution)/shard_map/ppermute | solution.py:24
  10.0 1.6 %collective-permute-start = (bf16[64,384]{1,0:T(8,128)(2,1)S(1)}, bf16[64,384]{1,0:T(8,128)(2,1)S(1)}, u32[]{:S(2)}, u32[]{:S(2)}) collective-permute-start(bf16[64,384]{1,0:T(8,128)(2,1)S(1)} %get-tuple-element.58), channel_id=1, source_target_pairs={{0,4},{4,0},{8,12},{12,8},{1,5},{5,1},{9,13},{13,9},{2,6},{6,2},{1... | collective-permute-start | bytes 147464 | tf_op jit(solution)/shard_map/ppermute | solution.py:24
  11.6 2.6 %collective-permute-start.1 = (bf16[64,384]{1,0:T(8,128)(2,1)S(1)}, bf16[64,384]{1,0:T(8,128)(2,1)S(1)}, u32[]{:S(2)}, u32[]{:S(2)}) collective-permute-start(bf16[64,384]{1,0:T(8,128)(2,1)S(1)} %get-tuple-element.59), channel_id=1, source_target_pairs={{0,8},{4,12},{8,0},{12,4},{1,9},{5,13},{9,1},{13,5},{2,10},{6,14},... | collective-permute-start | bytes 147464 | tf_op jit(solution)/shard_map/ppermute | solution.py:24
  14.4 3.2 %collective-permute-start.8 = (bf16[1024,384]{1,0:T(8,128)(2,1)S(1)}, bf16[1024,384]{1,0:T(8,128)(2,1)S(1)}, u32[]{:S(2)}, u32[]{:S(2)}) collective-permute-start(bf16[1024,384]{1,0:T(8,128)(2,1)S(1)} %copy-done.1), channel_id=1, source_target_pairs={{0,4},{4,8},{8,12},{1,5},{5,9},{9,13},{2,6},{6,10},{10,14},{3,7},{... | collective-permute-start | bytes 2359304 | tf_op jit(solution)/shard_map/ppermute | solution.py:33
  17.7 1.3 %collective-permute-start.9 = (bf16[1024,384]{1,0:T(8,128)(2,1)S(1)}, bf16[1024,384]{1,0:T(8,128)(2,1)S(1)}, u32[]{:S(2)}, u32[]{:S(2)}) collective-permute-start(bf16[1024,384]{1,0:T(8,128)(2,1)S(1)} %copy-done.1), channel_id=1, source_target_pairs={{4,0},{8,4},{12,8},{5,1},{9,5},{13,9},{6,2},{10,6},{14,10},{7,3},{... | collective-permute-start | bytes 2359304 | tf_op jit(solution)/shard_map/ppermute | solution.py:33
  19.0 1.2 %collective-permute-done.2 = bf16[64,384]{1,0:T(8,128)(2,1)S(1)} collective-permute-done((bf16[64,384]{1,0:T(8,128)(2,1)S(1)}, bf16[64,384]{1,0:T(8,128)(2,1)S(1)}, u32[]{:S(2)}, u32[]{:S(2)}) %collective-permute-start.2) | collective-permute-done | bytes 49184 | tf_op jit(solution)/shard_map/ppermute | solution.py:24
  21.3 1.6 %collective-permute-start.4 = (bf16[64,384]{1,0:T(8,128)(2,1)S(1)}, bf16[64,384]{1,0:T(8,128)(2,1)S(1)}, u32[]{:S(2)}, u32[]{:S(2)}) collective-permute-start(bf16[64,384]{1,0:T(8,128)(2,1)S(1)} %fusion.1.refs_0_), channel_id=1, source_target_pairs={{0,4},{4,0},{8,12},{12,8},{1,5},{5,1},{9,13},{13,9},{2,6},{6,2},{1... | collective-permute-start | bytes 147464 | tf_op jit(solution)/shard_map/ppermute | solution.py:24
  22.8 3.2 %collective-permute-start.5 = (bf16[64,384]{1,0:T(8,128)(2,1)S(1)}, bf16[64,384]{1,0:T(8,128)(2,1)S(1)}, u32[]{:S(2)}, u32[]{:S(2)}) collective-permute-start(bf16[64,384]{1,0:T(8,128)(2,1)S(1)} %fusion.1.refs_0_), channel_id=1, source_target_pairs={{0,8},{4,12},{8,0},{12,4},{1,9},{5,13},{9,1},{13,5},{2,10},{6,14},... | collective-permute-start | bytes 147464 | tf_op jit(solution)/shard_map/ppermute | solution.py:24
  26.0 2.2 %collective-permute-done.7.refs_2_ = bf16[1024,384]{1,0:T(8,128)(2,1)S(1)} collective-permute-done((bf16[1024,384]{1,0:T(8,128)(2,1)S(1)}, bf16[1024,384]{1,0:T(8,128)(2,1)S(1)}, u32[]{:S(2)}, u32[]{:S(2)}) %collective-permute-start.7) | collective-permute-done | bytes 786464 | tf_op jit(solution)/shard_map/ppermute | solution.py:24
  28.2 3.9 %collective-permute-start.6 = (bf16[64,384]{1,0:T(8,128)(2,1)S(1)}, bf16[64,384]{1,0:T(8,128)(2,1)S(1)}, u32[]{:S(2)}, u32[]{:S(2)}) collective-permute-start(bf16[64,384]{1,0:T(8,128)(2,1)S(1)} %fusion.1.refs_0_), channel_id=1, source_target_pairs={{0,12},{4,8},{8,4},{12,0},{1,13},{5,9},{9,5},{13,1},{2,14},{6,10},... | collective-permute-start | bytes 147464 | tf_op jit(solution)/shard_map/ppermute | solution.py:24
  32.1 7.5 %collective-permute-done.4.refs_1_ = bf16[64,384]{1,0:T(8,128)(2,1)S(1)} collective-permute-done((bf16[64,384]{1,0:T(8,128)(2,1)S(1)}, bf16[64,384]{1,0:T(8,128)(2,1)S(1)}, u32[]{:S(2)}, u32[]{:S(2)}) %collective-permute-start.4) | collective-permute-done | bytes 49184 | tf_op jit(solution)/shard_map/ppermute | solution.py:24
  39.6 2.2 %collective-permute-done.5.refs_2_ = bf16[64,384]{1,0:T(8,128)(2,1)S(1)} collective-permute-done((bf16[64,384]{1,0:T(8,128)(2,1)S(1)}, bf16[64,384]{1,0:T(8,128)(2,1)S(1)}, u32[]{:S(2)}, u32[]{:S(2)}) %collective-permute-start.5) | collective-permute-done | bytes 49184 | tf_op jit(solution)/shard_map/ppermute | solution.py:24
  41.9 1.7 %collective-permute-done.6.refs_3_ = bf16[64,384]{1,0:T(8,128)(2,1)S(1)} collective-permute-done((bf16[64,384]{1,0:T(8,128)(2,1)S(1)}, bf16[64,384]{1,0:T(8,128)(2,1)S(1)}, u32[]{:S(2)}, u32[]{:S(2)}) %collective-permute-start.6) | collective-permute-done | bytes 49184 | tf_op jit(solution)/shard_map/ppermute | solution.py:24
  43.6 1.9 %shard_map.88.refs_4_ = bf16[288,384]{1,0:T(8,128)(2,1)S(1)} custom-call(s32[16]{0:T(128)S(1)} %copy-done.7, s32[2,16]{1,0:T(2,128)S(1)} %bitcast.13, bf16[512,384]{1,0:T(8,128)(2,1)S(1)} %copy-done.3, f32[1024,384]{1,0:T(8,128)S(1)} %get-tuple-element.72.slope, bf16[64,384]{1,0:T(8,128)(2,1)S(1)} %fusion.1.refs_0_, ...), custom_call_target="tpu_custom_call" | custom-call | flops 5000000000 | bytes 1000 | tf_op jit(solution)/shard_map/pallas_call | solution.py:435
  46.2 1.3 %collective-permute-start.15 = (bf16[1024,384]{1,0:T(8,128)(2,1)S(1)}, bf16[1024,384]{1,0:T(8,128)(2,1)S(1)}, u32[]{:S(2)}, u32[]{:S(2)}) collective-permute-start(bf16[1024,384]{1,0:T(8,128)(2,1)S(1)} %collective-permute-done.9.refs_2_), channel_id=1, source_target_pairs={{4,0},{8,4},{5,1},{9,5},{6,2},{10,6},{7,3},{11,7},{20,16},{24,20},... | collective-permute-start | bytes 2359304 | tf_op jit(solution)/shard_map/ppermute | solution.py:33
  48.4 7.1 %collective-permute-done.11.refs_6_ = bf16[288,384]{1,0:T(8,128)(2,1)S(1)} collective-permute-done((bf16[288,384]{1,0:T(8,128)(2,1)S(1)}, bf16[288,384]{1,0:T(8,128)(2,1)S(1)}, u32[]{:S(2)}, u32[]{:S(2)}) %collective-permute-start.11) | collective-permute-done | bytes 221216 | tf_op jit(solution)/shard_map/ppermute | solution.py:24
  55.5 1.5 %collective-permute-done.12.refs_7_ = bf16[288,384]{1,0:T(8,128)(2,1)S(1)} collective-permute-done((bf16[288,384]{1,0:T(8,128)(2,1)S(1)}, bf16[288,384]{1,0:T(8,128)(2,1)S(1)}, u32[]{:S(2)}, u32[]{:S(2)}) %collective-permute-start.12) | collective-permute-done | bytes 221216 | tf_op jit(solution)/shard_map/ppermute | solution.py:24
  56.9 8.2 %collective-permute-done.15.refs_4_ = bf16[1024,384]{1,0:T(8,128)(2,1)S(1)} collective-permute-done((bf16[1024,384]{1,0:T(8,128)(2,1)S(1)}, bf16[1024,384]{1,0:T(8,128)(2,1)S(1)}, u32[]{:S(2)}, u32[]{:S(2)}) %collective-permute-start.15) | collective-permute-done | bytes 786464 | tf_op jit(solution)/shard_map/ppermute | solution.py:33
  65.2 1.4 %shard_map.89 = (bf16[1024,384]{1,0:T(8,128)(2,1)S(1)}, bf16[1024,384]{1,0:T(8,128)(2,1)S(1)}, bf16[1024,384]{1,0:T(8,128)(2,1)S(1)}, bf16[1024,384]{1,0:T(8,128...) custom-call(s32[2,16]{1,0:T(2,128)S(1)} %bitcast.14, ...), custom_call_target="tpu_custom_call", output_to_operand_aliasing={{0}: (1, {}), {1}: (2, {}), {2}: (3, {}), {3}: (4, {})} | custom-call | flops 1000 | bytes 1000 | tf_op jit(solution)/shard_map/pallas_call | solution.py:511
  67.5 2.7 %collective-permute-start.17 = (bf16[256,384]{1,0:T(8,128)(2,1)S(1)}, bf16[256,384]{1,0:T(8,128)(2,1)S(1)}, u32[]{:S(2)}, u32[]{:S(2)}) collective-permute-start(bf16[256,384]{1,0:T(8,128)(2,1)S(1)} %get-tuple-element.92), channel_id=1, source_target_pairs={{0,8},{4,12},{8,0},{12,4},{1,9},{5,13},{9,1},{13,5},{2,10},{6,14},... | collective-permute-start | bytes 589832 | tf_op jit(solution)/shard_map/ppermute | solution.py:24
  70.8 1.5 %collective-permute-start.21 = (bf16[1024,384]{1,0:T(8,128)(2,1)S(1)}, bf16[1024,384]{1,0:T(8,128)(2,1)S(1)}, u32[]{:S(2)}, u32[]{:S(2)}) collective-permute-start(bf16[1024,384]{1,0:T(8,128)(2,1)S(1)} %collective-permute-done.15.refs_4_), channel_id=1, source_target_pairs={{4,0},{5,1},{6,2},{7,3},{20,16},{21,17},{22,18},{23,19}} | collective-permute-start | bytes 2359304 | tf_op jit(solution)/shard_map/ppermute | solution.py:33
  72.4 2.8 %shard_map.90 = (f32[384,1920]{1,0:T(8,128)S(1)}, bf16[1536,1920]{1,0:T(8,128)(2,1)S(1)}) custom-call(bf16[16,384]{1,0:T(8,128)(2,1)S(1)} %slice.39.refs_0_, bf16[1024,384]{1,0:T(8,128)(2,1)S(1)} %copy-done.1, bf16[16,384]{1,0:T(8,128)(2,1)S(1)} %slice.40.refs_2_, bf16[1024,384]{1,0:T(8,128)(2,1)S(1)} %get-tuple-element.94.refs_3_, ...), custom_call_target="tpu_custom_call" | custom-call | flops 1000 | bytes 1000 | tf_op jit(solution)/shard_map/pallas_call | solution.py:258
  75.2 3.7 %shard_map.91.refs_6_ = bf16[512,384]{1,0:T(8,128)(2,1)S(1)} custom-call(bf16[1024,384]{1,0:T(8,128)(2,1)S(1)} %get-tuple-element.96.refs_0_, bf16[1024,384]{1,0:T(8,128)(2,1)S(1)} %get-tuple-element.97.refs_1_, bf16[1024,384]{1,0:T(8,128)(2,1)S(1)} %get-tuple-element.98.refs_2_, bf16[1024,384]{1,0:T(8,128)(2,1)S(1)} %get-tuple-element.99.refs_3_, ...), custom_call_target="tpu_custom_call" | custom-call | flops 1000 | bytes 1000 | tf_op jit(solution)/shard_map/pallas_call | solution.py:133
  78.9 5.7 %collective-permute-done.17.refs_11_ = bf16[256,384]{1,0:T(8,128)(2,1)S(1)} collective-permute-done((bf16[256,384]{1,0:T(8,128)(2,1)S(1)}, bf16[256,384]{1,0:T(8,128)(2,1)S(1)}, u32[]{:S(2)}, u32[]{:S(2)}) %collective-permute-start.17) | collective-permute-done | bytes 196640 | tf_op jit(solution)/shard_map/ppermute | solution.py:24
  85.4 4.8 %shard_map.92 = bf16[1024,384]{1,0:T(8,128)(2,1)} custom-call(bf16[1024,384]{1,0:T(8,128)(2,1)S(1)} %get-tuple-element.96.refs_0_, bf16[1024,384]{1,0:T(8,128)(2,1)S(1)} %get-tuple-element.97.refs_1_, bf16[1024,384]{1,0:T(8,128)(2,1)S(1)} %get-tuple-element.98.refs_2_, bf16[1024,384]{1,0:T(8,128)(2,1)S(1)} %get-tuple-element.99.refs_3_, ...), custom_call_target="tpu_custom_call" | custom-call | flops 1000 | bytes 1000 | tf_op jit(solution)/shard_map/pallas_call | solution.py:133
  90.2 6.0 %collective-permute-done.21.refs_6_ = bf16[1024,384]{1,0:T(8,128)(2,1)S(1)} collective-permute-done((bf16[1024,384]{1,0:T(8,128)(2,1)S(1)}, bf16[1024,384]{1,0:T(8,128)(2,1)S(1)}, u32[]{:S(2)}, u32[]{:S(2)}) %collective-permute-start.21) | collective-permute-done | bytes 786464 | tf_op jit(solution)/shard_map/ppermute | solution.py:33
  96.2 1.4 %collective-permute-done.19 = bf16[768,384]{1,0:T(8,128)(2,1)S(1)} collective-permute-done((bf16[768,384]{1,0:T(8,128)(2,1)S(1)}, bf16[768,384]{1,0:T(8,128)(2,1)S(1)}, u32[]{:S(2)}, u32[]{:S(2)}) %collective-permute-start.19) | collective-permute-done | bytes 589856 | tf_op jit(solution)/shard_map/ppermute | solution.py:24
  97.8 1.9 %collective-permute-done.23 = bf16[768,384]{1,0:T(8,128)(2,1)S(1)} collective-permute-done((bf16[768,384]{1,0:T(8,128)(2,1)S(1)}, bf16[768,384]{1,0:T(8,128)(2,1)S(1)}, u32[]{:S(2)}, u32[]{:S(2)}) %collective-permute-start.23) | collective-permute-done | bytes 589856 | tf_op jit(solution)/shard_map/ppermute | solution.py:24
  99.7 11.0 %shard_map.93 = bf16[5,384,384]{2,1,0:T(8,128)(2,1)} custom-call(bf16[1024,384]{1,0:T(8,128)(2,1)S(1)} %copy-done.1, bf16[1024,384]{1,0:T(8,128)(2,1)S(1)} %collective-permute-done.8.refs_1_, bf16[1024,384]{1,0:T(8,128)(2,1)S(1)} %collective-permute-done.9.refs_2_, bf16[1024,384]{1,0:T(8,128)(2,1)S(1)} %collective-permute-done.14.refs_3_, ...), custom_call_target="tpu_custom_call" | custom-call | flops 1000 | bytes 1000 | tf_op jit(solution)/shard_map/pallas_call | solution.py:258
  (54 shorter events, 8.2 us)
Async XLA Ops:
  0.6 42.9 %copy-start.5 = (s32[16,2]{0,1:T(2,128)S(1)}, s32[16,2]{0,1:T(2,128)}, u32[]{:S(2)}) copy-start(s32[16,2]{0,1:T(2,128)} %param.13) | copy-start | bytes 388
  0.6 42.9 %copy-start.7 = (s32[16]{0:T(128)S(1)}, s32[16]{0:T(128)}, u32[]{:S(2)}) copy-start(s32[16]{0:T(128)} %owners.3) | copy-start | bytes 196
  0.7 1.1 %copy-start = (bf16[1024,384]{1,0:T(8,128)(2,1)S(1)}, bf16[1024,384]{1,0:T(8,128)(2,1)}, u32[]{:S(2)}) copy-start(bf16[1024,384]{1,0:T(8,128)(2,1)} %pre_act.2) | copy-start | bytes 2359300
  3.1 11.3 %copy-start.1 = (bf16[1024,384]{1,0:T(8,128)(2,1)S(1)}, bf16[1024,384]{1,0:T(8,128)(2,1)}, u32[]{:S(2)}) copy-start(bf16[1024,384]{1,0:T(8,128)(2,1)} %refs_0_.1) | copy-start | bytes 2359300
  4.5 1.0 copy-start.2
  5.5 38.1 %copy-start.3 = (bf16[512,384]{1,0:T(8,128)(2,1)S(1)}, bf16[512,384]{1,0:T(8,128)(2,1)}, u32[]{:S(2)}) copy-start(bf16[512,384]{1,0:T(8,128)(2,1)} %out_grad.2) | copy-start | bytes 1179652
  7.0 13.2 %collective-permute-start.3 = (bf16[1024,384]{1,0:T(8,128)(2,1)S(1)}, bf16[1024,384]{1,0:T(8,128)(2,1)S(1)}, u32[]{:S(2)}, u32[]{:S(2)}) collective-permute-start(bf16[1024,384]{1,0:T(8,128)(2,1)S(1)} %get-tuple-element.65.refs_0_), channel_id=1, source_target_pairs={{0,1},{1,0},{2,3},{3,2},{4,5},{5,4},{6,7},{7,6},{8,9},{9,8},{10,11... | collective-permute-start | bytes 2359304 | tf_op jit(solution)/shard_map/ppermute | solution.py:24
  7.5 20.7 %collective-permute-start.7 = (bf16[1024,384]{1,0:T(8,128)(2,1)S(1)}, bf16[1024,384]{1,0:T(8,128)(2,1)S(1)}, u32[]{:S(2)}, u32[]{:S(2)}) collective-permute-start(bf16[1024,384]{1,0:T(8,128)(2,1)S(1)} %get-tuple-element.65.refs_0_), channel_id=1, source_target_pairs={{0,2},{1,3},{2,0},{3,1},{4,6},{5,7},{6,4},{7,5},{8,10},{9,11},{10,... | collective-permute-start | bytes 2359304 | tf_op jit(solution)/shard_map/ppermute | solution.py:24
  10.0 4.4 %collective-permute-start = (bf16[64,384]{1,0:T(8,128)(2,1)S(1)}, bf16[64,384]{1,0:T(8,128)(2,1)S(1)}, u32[]{:S(2)}, u32[]{:S(2)}) collective-permute-start(bf16[64,384]{1,0:T(8,128)(2,1)S(1)} %get-tuple-element.58), channel_id=1, source_target_pairs={{0,4},{4,0},{8,12},{12,8},{1,5},{5,1},{9,13},{13,9},{2,6},{6,2},{1... | collective-permute-start | bytes 147464 | tf_op jit(solution)/shard_map/ppermute | solution.py:24
  11.6 6.0 %collective-permute-start.1 = (bf16[64,384]{1,0:T(8,128)(2,1)S(1)}, bf16[64,384]{1,0:T(8,128)(2,1)S(1)}, u32[]{:S(2)}, u32[]{:S(2)}) collective-permute-start(bf16[64,384]{1,0:T(8,128)(2,1)S(1)} %get-tuple-element.59), channel_id=1, source_target_pairs={{0,8},{4,12},{8,0},{12,4},{1,9},{5,13},{9,1},{13,5},{2,10},{6,14},... | collective-permute-start | bytes 147464 | tf_op jit(solution)/shard_map/ppermute | solution.py:24
  14.3 5.9 %collective-permute-start.2 = (bf16[64,384]{1,0:T(8,128)(2,1)S(1)}, bf16[64,384]{1,0:T(8,128)(2,1)S(1)}, u32[]{:S(2)}, u32[]{:S(2)}) collective-permute-start(bf16[64,384]{1,0:T(8,128)(2,1)S(1)} %get-tuple-element.60), channel_id=1, source_target_pairs={{0,12},{4,8},{8,4},{12,0},{1,13},{5,9},{9,5},{13,1},{2,14},{6,10},... | collective-permute-start | bytes 147464 | tf_op jit(solution)/shard_map/ppermute | solution.py:24
  14.4 31.1 %collective-permute-start.8 = (bf16[1024,384]{1,0:T(8,128)(2,1)S(1)}, bf16[1024,384]{1,0:T(8,128)(2,1)S(1)}, u32[]{:S(2)}, u32[]{:S(2)}) collective-permute-start(bf16[1024,384]{1,0:T(8,128)(2,1)S(1)} %copy-done.1), channel_id=1, source_target_pairs={{0,4},{4,8},{8,12},{1,5},{5,9},{9,13},{2,6},{6,10},{10,14},{3,7},{... | collective-permute-start | bytes 2359304 | tf_op jit(solution)/shard_map/ppermute | solution.py:33
  17.7 27.8 %collective-permute-start.9 = (bf16[1024,384]{1,0:T(8,128)(2,1)S(1)}, bf16[1024,384]{1,0:T(8,128)(2,1)S(1)}, u32[]{:S(2)}, u32[]{:S(2)}) collective-permute-start(bf16[1024,384]{1,0:T(8,128)(2,1)S(1)} %copy-done.1), channel_id=1, source_target_pairs={{4,0},{8,4},{12,8},{5,1},{9,5},{13,9},{6,2},{10,6},{14,10},{7,3},{... | collective-permute-start | bytes 2359304 | tf_op jit(solution)/shard_map/ppermute | solution.py:33
  20.2 52.2 %slice-start = ((s8[5898240]{0:T(1024)(128)(4,1)}), s8[4194304]{0:T(1024)(128)(4,1)S(1)}, s32[]{:S(2)}) async-start(s8[5898240]{0:T(1024)(128)(4,1)} %bitcast.9), calls=%async_computation | async-start | bytes 8388608
  21.3 51.1 %slice-start.1 = ((s8[5898240]{0:T(1024)(128)(4,1)}), s8[1703936]{0:T(1024)(128)(4,1)S(1)}, s32[]{:S(2)}) async-start(s8[5898240]{0:T(1024)(128)(4,1)} %bitcast.9), calls=%async_computation.1 | async-start | bytes 3407872
  21.3 18.4 %collective-permute-start.4 = (bf16[64,384]{1,0:T(8,128)(2,1)S(1)}, bf16[64,384]{1,0:T(8,128)(2,1)S(1)}, u32[]{:S(2)}, u32[]{:S(2)}) collective-permute-start(bf16[64,384]{1,0:T(8,128)(2,1)S(1)} %fusion.1.refs_0_), channel_id=1, source_target_pairs={{0,4},{4,0},{8,12},{12,8},{1,5},{5,1},{9,13},{13,9},{2,6},{6,2},{1... | collective-permute-start | bytes 147464 | tf_op jit(solution)/shard_map/ppermute | solution.py:24
  22.8 19.0 %collective-permute-start.5 = (bf16[64,384]{1,0:T(8,128)(2,1)S(1)}, bf16[64,384]{1,0:T(8,128)(2,1)S(1)}, u32[]{:S(2)}, u32[]{:S(2)}) collective-permute-start(bf16[64,384]{1,0:T(8,128)(2,1)S(1)} %fusion.1.refs_0_), channel_id=1, source_target_pairs={{0,8},{4,12},{8,0},{12,4},{1,9},{5,13},{9,1},{13,5},{2,10},{6,14},... | collective-permute-start | bytes 147464 | tf_op jit(solution)/shard_map/ppermute | solution.py:24
  28.2 15.4 %collective-permute-start.6 = (bf16[64,384]{1,0:T(8,128)(2,1)S(1)}, bf16[64,384]{1,0:T(8,128)(2,1)S(1)}, u32[]{:S(2)}, u32[]{:S(2)}) collective-permute-start(bf16[64,384]{1,0:T(8,128)(2,1)S(1)} %fusion.1.refs_0_), channel_id=1, source_target_pairs={{0,12},{4,8},{8,4},{12,0},{1,13},{5,9},{9,5},{13,1},{2,14},{6,10},... | collective-permute-start | bytes 147464 | tf_op jit(solution)/shard_map/ppermute | solution.py:24
  45.5 11.4 %collective-permute-start.14 = (bf16[1024,384]{1,0:T(8,128)(2,1)S(1)}, bf16[1024,384]{1,0:T(8,128)(2,1)S(1)}, u32[]{:S(2)}, u32[]{:S(2)}) collective-permute-start(bf16[1024,384]{1,0:T(8,128)(2,1)S(1)} %collective-permute-done.8.refs_1_), channel_id=1, source_target_pairs={{4,8},{8,12},{5,9},{9,13},{6,10},{10,14},{7,11},{11,15},{20,24},{2... | collective-permute-start | bytes 2359304 | tf_op jit(solution)/shard_map/ppermute | solution.py:33
  46.2 18.9 %collective-permute-start.15 = (bf16[1024,384]{1,0:T(8,128)(2,1)S(1)}, bf16[1024,384]{1,0:T(8,128)(2,1)S(1)}, u32[]{:S(2)}, u32[]{:S(2)}) collective-permute-start(bf16[1024,384]{1,0:T(8,128)(2,1)S(1)} %collective-permute-done.9.refs_2_), channel_id=1, source_target_pairs={{4,0},{8,4},{5,1},{9,5},{6,2},{10,6},{7,3},{11,7},{20,16},{24,20},... | collective-permute-start | bytes 2359304 | tf_op jit(solution)/shard_map/ppermute | solution.py:33
  47.5 17.7 %collective-permute-start.13 = (bf16[1024,384]{1,0:T(8,128)(2,1)S(1)}, bf16[1024,384]{1,0:T(8,128)(2,1)S(1)}, u32[]{:S(2)}, u32[]{:S(2)}) collective-permute-start(bf16[1024,384]{1,0:T(8,128)(2,1)S(1)} %collective-permute-done.7.refs_2_), channel_id=1, source_target_pairs={{0,1},{1,0},{2,3},{3,2},{4,5},{5,4},{6,7},{7,6},{8,9},{9,8},{10,11... | collective-permute-start | bytes 2359304 | tf_op jit(solution)/shard_map/ppermute | solution.py:24
  47.6 7.8 %collective-permute-start.11 = (bf16[288,384]{1,0:T(8,128)(2,1)S(1)}, bf16[288,384]{1,0:T(8,128)(2,1)S(1)}, u32[]{:S(2)}, u32[]{:S(2)}) collective-permute-start(bf16[288,384]{1,0:T(8,128)(2,1)S(1)} %shard_map.88.refs_4_), channel_id=1, source_target_pairs={{0,2},{1,3},{2,0},{3,1},{4,6},{5,7},{6,4},{7,5},{8,10},{9,11},{10,... | collective-permute-start | bytes 663560 | tf_op jit(solution)/shard_map/ppermute | solution.py:24
  48.2 7.2 %collective-permute-start.10 = (bf16[288,384]{1,0:T(8,128)(2,1)S(1)}, bf16[288,384]{1,0:T(8,128)(2,1)S(1)}, u32[]{:S(2)}, u32[]{:S(2)}) collective-permute-start(bf16[288,384]{1,0:T(8,128)(2,1)S(1)} %shard_map.88.refs_4_), channel_id=1, source_target_pairs={{0,1},{1,0},{2,3},{3,2},{4,5},{5,4},{6,7},{7,6},{8,9},{9,8},{10,11... | collective-permute-start | bytes 663560 | tf_op jit(solution)/shard_map/ppermute | solution.py:24
  55.5 1.5 %collective-permute-start.12 = (bf16[288,384]{1,0:T(8,128)(2,1)S(1)}, bf16[288,384]{1,0:T(8,128)(2,1)S(1)}, u32[]{:S(2)}, u32[]{:S(2)}) collective-permute-start(bf16[288,384]{1,0:T(8,128)(2,1)S(1)} %collective-permute-done.11.refs_6_), channel_id=1, source_target_pairs={{0,1},{1,0},{2,3},{3,2},{4,5},{5,4},{6,7},{7,6},{8,9},{9,8},{10,11... | collective-permute-start | bytes 663560 | tf_op jit(solution)/shard_map/ppermute | solution.py:24
  66.6 18.1 %collective-permute-start.16 = (bf16[272,384]{1,0:T(8,128)(2,1)S(1)}, bf16[272,384]{1,0:T(8,128)(2,1)S(1)}, u32[]{:S(2)}, u32[]{:S(2)}) collective-permute-start(bf16[272,384]{1,0:T(8,128)(2,1)S(1)} %get-tuple-element.91), channel_id=1, source_target_pairs={{0,4},{4,0},{8,12},{12,8},{1,5},{5,1},{9,13},{13,9},{2,6},{6,2},{1... | collective-permute-start | bytes 626696 | tf_op jit(solution)/shard_map/ppermute | solution.py:24
  67.0 17.6 %collective-permute-start.18 = (bf16[272,384]{1,0:T(8,128)(2,1)S(1)}, bf16[272,384]{1,0:T(8,128)(2,1)S(1)}, u32[]{:S(2)}, u32[]{:S(2)}) collective-permute-start(bf16[272,384]{1,0:T(8,128)(2,1)S(1)} %get-tuple-element.93), channel_id=1, source_target_pairs={{0,12},{4,8},{8,4},{12,0},{1,13},{5,9},{9,5},{13,1},{2,14},{6,10},... | collective-permute-start | bytes 626696 | tf_op jit(solution)/shard_map/ppermute | solution.py:24
  67.5 17.2 %collective-permute-start.17 = (bf16[256,384]{1,0:T(8,128)(2,1)S(1)}, bf16[256,384]{1,0:T(8,128)(2,1)S(1)}, u32[]{:S(2)}, u32[]{:S(2)}) collective-permute-start(bf16[256,384]{1,0:T(8,128)(2,1)S(1)} %get-tuple-element.92), channel_id=1, source_target_pairs={{0,8},{4,12},{8,0},{12,4},{1,9},{5,13},{9,1},{13,5},{2,10},{6,14},... | collective-permute-start | bytes 589832 | tf_op jit(solution)/shard_map/ppermute | solution.py:24
  70.1 20.1 %collective-permute-start.20 = (bf16[1024,384]{1,0:T(8,128)(2,1)S(1)}, bf16[1024,384]{1,0:T(8,128)(2,1)S(1)}, u32[]{:S(2)}, u32[]{:S(2)}) collective-permute-start(bf16[1024,384]{1,0:T(8,128)(2,1)S(1)} %collective-permute-done.14.refs_3_), channel_id=1, source_target_pairs={{8,12},{9,13},{10,14},{11,15},{24,28},{25,29},{26,30},{27,31}} | collective-permute-start | bytes 2359304 | tf_op jit(solution)/shard_map/ppermute | solution.py:33
  70.8 25.4 %collective-permute-start.21 = (bf16[1024,384]{1,0:T(8,128)(2,1)S(1)}, bf16[1024,384]{1,0:T(8,128)(2,1)S(1)}, u32[]{:S(2)}, u32[]{:S(2)}) collective-permute-start(bf16[1024,384]{1,0:T(8,128)(2,1)S(1)} %collective-permute-done.15.refs_4_), channel_id=1, source_target_pairs={{4,0},{5,1},{6,2},{7,3},{20,16},{21,17},{22,18},{23,19}} | collective-permute-start | bytes 2359304 | tf_op jit(solution)/shard_map/ppermute | solution.py:33
  84.8 12.9 %collective-permute-start.19 = (bf16[768,384]{1,0:T(8,128)(2,1)S(1)}, bf16[768,384]{1,0:T(8,128)(2,1)S(1)}, u32[]{:S(2)}, u32[]{:S(2)}) collective-permute-start(bf16[768,384]{1,0:T(8,128)(2,1)S(1)} %pad_maximum_fusion), channel_id=1, source_target_pairs={{0,2},{1,3},{2,0},{3,1},{4,6},{5,7},{6,4},{7,5},{8,10},{9,11},{10,... | collective-permute-start | bytes 1769480 | tf_op jit(solution)/shard_map/ppermute | solution.py:24
  85.4 12.4 %collective-permute-start.22 = (bf16[768,384]{1,0:T(8,128)(2,1)S(1)}, bf16[768,384]{1,0:T(8,128)(2,1)S(1)}, u32[]{:S(2)}, u32[]{:S(2)}) collective-permute-start(bf16[768,384]{1,0:T(8,128)(2,1)S(1)} %pad_maximum_fusion), channel_id=1, source_target_pairs={{0,1},{1,0},{2,3},{3,2},{4,5},{5,4},{6,7},{7,6},{8,9},{9,8},{10,11... | collective-permute-start | bytes 1769480 | tf_op jit(solution)/shard_map/ppermute | solution.py:24
  97.7 2.0 %collective-permute-start.23 = (bf16[768,384]{1,0:T(8,128)(2,1)S(1)}, bf16[768,384]{1,0:T(8,128)(2,1)S(1)}, u32[]{:S(2)}, u32[]{:S(2)}) collective-permute-start(bf16[768,384]{1,0:T(8,128)(2,1)S(1)} %collective-permute-done.19), channel_id=1, source_target_pairs={{0,1},{1,0},{2,3},{3,2},{4,5},{5,4},{6,7},{7,6},{8,9},{9,8},{10,11... | collective-permute-start | bytes 1769480 | tf_op jit(solution)/shard_map/ppermute | solution.py:24
  (2 other events, 1.3 us)

commit v10 on v7

--- a/solution.py
+++ b/solution.py
@@ -15,7 +15,7 @@
 HALF_ROOT = 0.7071067811865476
 DENSITY = 0.3989422804014327
 LANES = 128
-LONG = pl.CostEstimate(flops=10**10, bytes_accessed=1000, transcendentals=0)
+LONG = pl.CostEstimate(flops=4 * 10**9, bytes_accessed=1000, transcendentals=0)
 LITTLE = pl.CostEstimate(flops=1000, bytes_accessed=1000, transcendentals=0)
 
 
@@ -597,10 +597,8 @@
     far, near = swap(plain, "ch", 2), swap(plain, "ch", 1)
     coverage = functools.reduce(jnp.add, [a.astype(jnp.float32) for a in arrived])
     splice = jnp.tanh(coverage - target).astype(jnp.bfloat16)
-    beside = swap(splice, "seq", 1)
-    both = swap(jnp.concatenate([splice, beside]), "seq", 2)
-    both, up1, down1 = after([both, up1, down1])
-    splices = [splice, beside, both]
+    (last_splice,) = after([splice], [up1, down1])
+    splices = [splice, swap(splice, "seq", 1), swap(splice, "seq", 2), swap(last_splice, "seq", 3)]
     gained = gained_rows(owners, exons, out_grad, slope, splices, most, size, nseq)
 
     far_gained, near_gained = swap(gained, "ch", 2), swap(gained, "ch", 1)

time: 111 us -> 110 us (level)
  waiting for transfers between devices: 47.6 us -> 44.3 us
  starting transfers between devices: 29.5 us -> 31.7 us
    ppermute x17 -> x18, waiting for transfers between devices: 37 us -> 21.1 us  [swap(): return lax.ppermute(block, axis, [(i, i ^ flip) for i in range(count)])]
    ppermute x6, waiting for transfers between devices: 10.6 us -> 23.2 us  [shift(): return lax.ppermute(block, axis, pairs)]
    ppermute x17 -> x18, starting transfers between devices: 21 us -> 23.3 us  [swap(): return lax.ppermute(block, axis, [(i, i ^ flip) for i in range(count)])]
  transfers between devices with their start and end apart: 23 -> 24, of which waited for: 10 -> 11; matrix products, arithmetic and copies ran while one was open for 0% -> 0% of each run, Pallas kernels for 13% -> 14%
where the time goes in v10:
time: 110 us
  waiting for transfers between devices  44.3 us (40%)
  starting transfers between devices  31.7 us (29%)
  Pallas kernels  28.7 us (26%)
  local copies, waits for them, and re-layouts  3.73 us (3%)
  between operations  1.11 us (1%)
    ppermute x18, starting transfers between devices, swap(): return lax.ppermute(block, axis, [(i, i ^ flip) for i in range(count)])  23.3 us
    ppermute x6, waiting for transfers between devices, shift(): return lax.ppermute(block, axis, pairs)  23.2 us
    ppermute x18, waiting for transfers between devices, swap(): return lax.ppermute(block, axis, [(i, i ^ flip) for i in range(count)])  21.1 us
    pallas_call x2, Pallas kernels, weight_gradient(): pl.pallas_call(functools.partial(weight_kernel, taps=taps, tile=min(1024,...  13.8 us
    pallas_call x2, Pallas kernels, pieces_gradient(): pl.pallas_call(functools.partial(pieces_kernel, taps=taps, pieces=len(par...  8.51 us
    ppermute x6, starting transfers between devices, shift(): return lax.ppermute(block, axis, pairs)  8.45 us
    unnamed x22, local copies, waits for them, and re-layouts  3.5 us
  transfers between devices with their start and end apart: 24, of which 11 were waited for; matrix products, arithmetic and copies ran while one was open for 0% of the time, Pallas kernels for 14%

profile of v10, /device:TPU:0, one launch (start us, length us, event | category | flops | bytes accessed | tf_op | source)
XLA Modules:
  0.0 109.7 jit_solution(12138230471206387006)
XLA Ops:
  3.1 1.4 %shard_map.86 = (bf16[64,384]{1,0:T(8,128)(2,1)S(1)}, bf16[64,384]{1,0:T(8,128)(2,1)S(1)}, bf16[64,384]{1,0:T(8,128)(2,1)S(1)}, bf16[64,384]{1,0:T(8,128)(2,1)S(1)}) custom-call(s32[16]{0:T(128)S(1)} %copy-done.6, s32[2,16]{1,0:T(2,128)S(1)} %bitcast.12, bf16[1024,384]{1,0:T(8,128)(2,1)S(1)} %copy-done), custom_call_target="tpu_custom_call" | custom-call | flops 1000 | bytes 1000 | tf_op jit(solution)/shard_map/pallas_call | solution.py:361
  4.6 3.1 %collective-permute-start = (bf16[64,384]{1,0:T(8,128)(2,1)S(1)}, bf16[64,384]{1,0:T(8,128)(2,1)S(1)}, u32[]{:S(2)}, u32[]{:S(2)}) collective-permute-start(bf16[64,384]{1,0:T(8,128)(2,1)S(1)} %get-tuple-element.48), channel_id=1, source_target_pairs={{0,4},{4,0},{8,12},{12,8},{1,5},{5,1},{9,13},{13,9},{2,6},{6,2},{1... | collective-permute-start | bytes 147464 | tf_op jit(solution)/shard_map/ppermute | solution.py:24
  7.7 2.4 %collective-permute-start.1 = (bf16[64,384]{1,0:T(8,128)(2,1)S(1)}, bf16[64,384]{1,0:T(8,128)(2,1)S(1)}, u32[]{:S(2)}, u32[]{:S(2)}) collective-permute-start(bf16[64,384]{1,0:T(8,128)(2,1)S(1)} %get-tuple-element.49), channel_id=1, source_target_pairs={{0,8},{4,12},{8,0},{12,4},{1,9},{5,13},{9,1},{13,5},{2,10},{6,14},... | collective-permute-start | bytes 147464 | tf_op jit(solution)/shard_map/ppermute | solution.py:24
  10.1 3.0 %collective-permute-start.7 = (bf16[1024,384]{1,0:T(8,128)(2,1)}, bf16[1024,384]{1,0:T(8,128)(2,1)S(1)}, u32[]{:S(2)}, u32[]{:S(2)}) collective-permute-start(bf16[1024,384]{1,0:T(8,128)(2,1)} %refs_0_.1), channel_id=1, source_target_pairs={{0,4},{4,8},{8,12},{1,5},{5,9},{9,13},{2,6},{6,10},{10,14},{3,7},{... | collective-permute-start | bytes 2359304 | tf_op jit(solution)/shard_map/ppermute | solution.py:33
  13.1 1.3 %collective-permute-start.8 = (bf16[1024,384]{1,0:T(8,128)(2,1)}, bf16[1024,384]{1,0:T(8,128)(2,1)S(1)}, u32[]{:S(2)}, u32[]{:S(2)}) collective-permute-start(bf16[1024,384]{1,0:T(8,128)(2,1)} %refs_0_.1), channel_id=1, source_target_pairs={{4,0},{8,4},{12,8},{5,1},{9,5},{13,9},{6,2},{10,6},{14,10},{7,3},{... | collective-permute-start | bytes 2359304 | tf_op jit(solution)/shard_map/ppermute | solution.py:33
  15.4 1.5 %shard_map.87 = (f32[1024,384]{1,0:T(8,128)S(1)}, bf16[1024,384]{1,0:T(8,128)(2,1)S(1)}) custom-call(bf16[1024,384]{1,0:T(8,128)(2,1)S(1)} %copy-done, bf16[512,384]{1,0:T(8,128)(2,1)S(1)} %copy-done.2), custom_call_target="tpu_custom_call" | custom-call | flops 1000 | bytes 1000 | tf_op jit(solution)/shard_map/pallas_call | solution.py:388
  17.0 1.6 %collective-permute-start.4 = (bf16[1024,384]{1,0:T(8,128)(2,1)S(1)}, bf16[1024,384]{1,0:T(8,128)(2,1)S(1)}, u32[]{:S(2)}, u32[]{:S(2)}) collective-permute-start(bf16[1024,384]{1,0:T(8,128)(2,1)S(1)} %get-tuple-element.53.refs_0_), channel_id=1, source_target_pairs={{0,2},{1,3},{2,0},{3,1},{4,6},{5,7},{6,4},{7,5},{8,10},{9,11},{10,... | collective-permute-start | bytes 2359304 | tf_op jit(solution)/shard_map/ppermute | solution.py:24
  18.6 2.7 %collective-permute-start.5 = (bf16[64,384]{1,0:T(8,128)(2,1)S(1)}, bf16[64,384]{1,0:T(8,128)(2,1)S(1)}, u32[]{:S(2)}, u32[]{:S(2)}) collective-permute-start(bf16[64,384]{1,0:T(8,128)(2,1)S(1)} %fusion.1.refs_0_), channel_id=1, source_target_pairs={{0,4},{4,0},{8,12},{12,8},{1,5},{5,1},{9,13},{13,9},{2,6},{6,2},{1... | collective-permute-start | bytes 147464 | tf_op jit(solution)/shard_map/ppermute | solution.py:24
  21.3 3.3 %collective-permute-start.6 = (bf16[64,384]{1,0:T(8,128)(2,1)S(1)}, bf16[64,384]{1,0:T(8,128)(2,1)S(1)}, u32[]{:S(2)}, u32[]{:S(2)}) collective-permute-start(bf16[64,384]{1,0:T(8,128)(2,1)S(1)} %fusion.1.refs_0_), channel_id=1, source_target_pairs={{0,8},{4,12},{8,0},{12,4},{1,9},{5,13},{9,1},{13,5},{2,10},{6,14},... | collective-permute-start | bytes 147464 | tf_op jit(solution)/shard_map/ppermute | solution.py:24
  24.6 5.8 %collective-permute-done.7.refs_1_ = bf16[1024,384]{1,0:T(8,128)(2,1)S(1)} collective-permute-done((bf16[1024,384]{1,0:T(8,128)(2,1)}, bf16[1024,384]{1,0:T(8,128)(2,1)S(1)}, u32[]{:S(2)}, u32[]{:S(2)}) %collective-permute-start.7) | collective-permute-done | bytes 786464 | tf_op jit(solution)/shard_map/ppermute | solution.py:33
  30.4 4.1 %collective-permute-done.8.refs_2_ = bf16[1024,384]{1,0:T(8,128)(2,1)S(1)} collective-permute-done((bf16[1024,384]{1,0:T(8,128)(2,1)}, bf16[1024,384]{1,0:T(8,128)(2,1)S(1)}, u32[]{:S(2)}, u32[]{:S(2)}) %collective-permute-start.8) | collective-permute-done | bytes 786464 | tf_op jit(solution)/shard_map/ppermute | solution.py:33
  34.5 2.8 %collective-permute-start.9 = (bf16[64,384]{1,0:T(8,128)(2,1)S(1)}, bf16[64,384]{1,0:T(8,128)(2,1)S(1)}, u32[]{:S(2)}, u32[]{:S(2)}) collective-permute-start(bf16[64,384]{1,0:T(8,128)(2,1)S(1)} %fusion.1.refs_0_), channel_id=1, source_target_pairs={{0,12},{4,8},{8,4},{12,0},{1,13},{5,9},{9,5},{13,1},{2,14},{6,10},... | collective-permute-start | bytes 147464 | tf_op jit(solution)/shard_map/ppermute | solution.py:24
  38.0 1.3 %collective-permute-start.15 = (bf16[1024,384]{1,0:T(8,128)(2,1)S(1)}, bf16[1024,384]{1,0:T(8,128)(2,1)S(1)}, u32[]{:S(2)}, u32[]{:S(2)}) collective-permute-start(bf16[1024,384]{1,0:T(8,128)(2,1)S(1)} %collective-permute-done.8.refs_2_), channel_id=1, source_target_pairs={{4,0},{8,4},{5,1},{9,5},{6,2},{10,6},{7,3},{11,7},{20,16},{24,20},... | collective-permute-start | bytes 2359304 | tf_op jit(solution)/shard_map/ppermute | solution.py:33
  40.4 2.0 %shard_map.88.refs_4_ = bf16[288,384]{1,0:T(8,128)(2,1)S(1)} custom-call(s32[16]{0:T(128)S(1)} %copy-done.7, s32[2,16]{1,0:T(2,128)S(1)} %bitcast.13, bf16[512,384]{1,0:T(8,128)(2,1)S(1)} %copy-done.3, f32[1024,384]{1,0:T(8,128)S(1)} %get-tuple-element.54.slope, bf16[64,384]{1,0:T(8,128)(2,1)S(1)} %fusion.1.refs_0_, ...), custom_call_target="tpu_custom_call" | custom-call | flops 4000000000 | bytes 1000 | tf_op jit(solution)/shard_map/pallas_call | solution.py:435
  42.4 1.6 %collective-permute-start.11 = (bf16[288,384]{1,0:T(8,128)(2,1)S(1)}, bf16[288,384]{1,0:T(8,128)(2,1)S(1)}, u32[]{:S(2)}, u32[]{:S(2)}) collective-permute-start(bf16[288,384]{1,0:T(8,128)(2,1)S(1)} %shard_map.88.refs_4_), channel_id=1, source_target_pairs={{0,2},{1,3},{2,0},{3,1},{4,6},{5,7},{6,4},{7,5},{8,10},{9,11},{10,... | collective-permute-start | bytes 663560 | tf_op jit(solution)/shard_map/ppermute | solution.py:24
  44.0 5.4 %collective-permute-done.11.refs_6_ = bf16[288,384]{1,0:T(8,128)(2,1)S(1)} collective-permute-done((bf16[288,384]{1,0:T(8,128)(2,1)S(1)}, bf16[288,384]{1,0:T(8,128)(2,1)S(1)}, u32[]{:S(2)}, u32[]{:S(2)}) %collective-permute-start.11) | collective-permute-done | bytes 221216 | tf_op jit(solution)/shard_map/ppermute | solution.py:24
  49.4 1.5 %collective-permute-done.10.refs_5_ = bf16[288,384]{1,0:T(8,128)(2,1)S(1)} collective-permute-done((bf16[288,384]{1,0:T(8,128)(2,1)S(1)}, bf16[288,384]{1,0:T(8,128)(2,1)S(1)}, u32[]{:S(2)}, u32[]{:S(2)}) %collective-permute-start.10) | collective-permute-done | bytes 221216 | tf_op jit(solution)/shard_map/ppermute | solution.py:24
  51.0 1.3 %collective-permute-done.12.refs_7_ = bf16[288,384]{1,0:T(8,128)(2,1)S(1)} collective-permute-done((bf16[288,384]{1,0:T(8,128)(2,1)S(1)}, bf16[288,384]{1,0:T(8,128)(2,1)S(1)}, u32[]{:S(2)}, u32[]{:S(2)}) %collective-permute-start.12) | collective-permute-done | bytes 221216 | tf_op jit(solution)/shard_map/ppermute | solution.py:24
  52.3 8.4 %collective-permute-done.15.refs_4_ = bf16[1024,384]{1,0:T(8,128)(2,1)S(1)} collective-permute-done((bf16[1024,384]{1,0:T(8,128)(2,1)S(1)}, bf16[1024,384]{1,0:T(8,128)(2,1)S(1)}, u32[]{:S(2)}, u32[]{:S(2)}) %collective-permute-start.15) | collective-permute-done | bytes 786464 | tf_op jit(solution)/shard_map/ppermute | solution.py:33
  60.8 1.4 %shard_map.89 = (bf16[1024,384]{1,0:T(8,128)(2,1)S(1)}, bf16[1024,384]{1,0:T(8,128)(2,1)S(1)}, bf16[1024,384]{1,0:T(8,128)(2,1)S(1)}, bf16[1024,384]{1,0:T(8,128...) custom-call(s32[2,16]{1,0:T(2,128)S(1)} %bitcast.14, ...), custom_call_target="tpu_custom_call", output_to_operand_aliasing={{0}: (1, {}), {1}: (2, {}), {2}: (3, {}), {3}: (4, {})} | custom-call | flops 1000 | bytes 1000 | tf_op jit(solution)/shard_map/pallas_call | solution.py:511
  62.2 1.8 %collective-permute-start.16 = (bf16[272,384]{1,0:T(8,128)(2,1)S(1)}, bf16[272,384]{1,0:T(8,128)(2,1)S(1)}, u32[]{:S(2)}, u32[]{:S(2)}) collective-permute-start(bf16[272,384]{1,0:T(8,128)(2,1)S(1)} %get-tuple-element.71), channel_id=1, source_target_pairs={{0,4},{4,0},{8,12},{12,8},{1,5},{5,1},{9,13},{13,9},{2,6},{6,2},{1... | collective-permute-start | bytes 626696 | tf_op jit(solution)/shard_map/ppermute | solution.py:24
  64.4 1.4 %collective-permute-start.17 = (bf16[256,384]{1,0:T(8,128)(2,1)S(1)}, bf16[256,384]{1,0:T(8,128)(2,1)S(1)}, u32[]{:S(2)}, u32[]{:S(2)}) collective-permute-start(bf16[256,384]{1,0:T(8,128)(2,1)S(1)} %get-tuple-element.72), channel_id=1, source_target_pairs={{0,8},{4,12},{8,0},{12,4},{1,9},{5,13},{9,1},{13,5},{2,10},{6,14},... | collective-permute-start | bytes 589832 | tf_op jit(solution)/shard_map/ppermute | solution.py:24
  66.5 1.5 %collective-permute-start.21 = (bf16[1024,384]{1,0:T(8,128)(2,1)S(1)}, bf16[1024,384]{1,0:T(8,128)(2,1)S(1)}, u32[]{:S(2)}, u32[]{:S(2)}) collective-permute-start(bf16[1024,384]{1,0:T(8,128)(2,1)S(1)} %collective-permute-done.15.refs_4_), channel_id=1, source_target_pairs={{4,0},{5,1},{6,2},{7,3},{20,16},{21,17},{22,18},{23,19}} | collective-permute-start | bytes 2359304 | tf_op jit(solution)/shard_map/ppermute | solution.py:33
  68.0 2.8 %shard_map.90 = (f32[384,1920]{1,0:T(8,128)S(1)}, bf16[1536,1920]{1,0:T(8,128)(2,1)S(1)}) custom-call(bf16[16,384]{1,0:T(8,128)(2,1)S(1)} %slice.52.refs_0_, bf16[1024,384]{1,0:T(8,128)(2,1)S(1)} %copy-done.1, bf16[16,384]{1,0:T(8,128)(2,1)S(1)} %slice.53.refs_2_, bf16[1024,384]{1,0:T(8,128)(2,1)S(1)} %get-tuple-element.74.refs_3_, ...), custom_call_target="tpu_custom_call" | custom-call | flops 1000 | bytes 1000 | tf_op jit(solution)/shard_map/pallas_call | solution.py:258
  70.9 3.7 %shard_map.91.refs_6_ = bf16[512,384]{1,0:T(8,128)(2,1)S(1)} custom-call(bf16[1024,384]{1,0:T(8,128)(2,1)S(1)} %get-tuple-element.76.refs_0_, bf16[1024,384]{1,0:T(8,128)(2,1)S(1)} %get-tuple-element.77.refs_1_, bf16[1024,384]{1,0:T(8,128)(2,1)S(1)} %get-tuple-element.78.refs_2_, bf16[1024,384]{1,0:T(8,128)(2,1)S(1)} %get-tuple-element.79.refs_3_, ...), custom_call_target="tpu_custom_call" | custom-call | flops 1000 | bytes 1000 | tf_op jit(solution)/shard_map/pallas_call | solution.py:133
  74.6 8.3 %collective-permute-done.17.refs_11_ = bf16[256,384]{1,0:T(8,128)(2,1)S(1)} collective-permute-done((bf16[256,384]{1,0:T(8,128)(2,1)S(1)}, bf16[256,384]{1,0:T(8,128)(2,1)S(1)}, u32[]{:S(2)}, u32[]{:S(2)}) %collective-permute-start.17) | collective-permute-done | bytes 196640 | tf_op jit(solution)/shard_map/ppermute | solution.py:24
  83.1 1.6 %collective-permute-start.19 = (bf16[768,384]{1,0:T(8,128)(2,1)S(1)}, bf16[768,384]{1,0:T(8,128)(2,1)S(1)}, u32[]{:S(2)}, u32[]{:S(2)}) collective-permute-start(bf16[768,384]{1,0:T(8,128)(2,1)S(1)} %pad_maximum_fusion), channel_id=1, source_target_pairs={{0,2},{1,3},{2,0},{3,1},{4,6},{5,7},{6,4},{7,5},{8,10},{9,11},{10,... | collective-permute-start | bytes 1769480 | tf_op jit(solution)/shard_map/ppermute | solution.py:24
  84.6 4.8 %shard_map.92 = bf16[1024,384]{1,0:T(8,128)(2,1)} custom-call(bf16[1024,384]{1,0:T(8,128)(2,1)S(1)} %get-tuple-element.76.refs_0_, bf16[1024,384]{1,0:T(8,128)(2,1)S(1)} %get-tuple-element.77.refs_1_, bf16[1024,384]{1,0:T(8,128)(2,1)S(1)} %get-tuple-element.78.refs_2_, bf16[1024,384]{1,0:T(8,128)(2,1)S(1)} %get-tuple-element.79.refs_3_, ...), custom_call_target="tpu_custom_call" | custom-call | flops 1000 | bytes 1000 | tf_op jit(solution)/shard_map/pallas_call | solution.py:133
  89.4 4.8 %collective-permute-done.21.refs_6_ = bf16[1024,384]{1,0:T(8,128)(2,1)S(1)} collective-permute-done((bf16[1024,384]{1,0:T(8,128)(2,1)S(1)}, bf16[1024,384]{1,0:T(8,128)(2,1)S(1)}, u32[]{:S(2)}, u32[]{:S(2)}) %collective-permute-start.21) | collective-permute-done | bytes 786464 | tf_op jit(solution)/shard_map/ppermute | solution.py:33
  94.3 2.2 %collective-permute-done.19 = bf16[768,384]{1,0:T(8,128)(2,1)S(1)} collective-permute-done((bf16[768,384]{1,0:T(8,128)(2,1)S(1)}, bf16[768,384]{1,0:T(8,128)(2,1)S(1)}, u32[]{:S(2)}, u32[]{:S(2)}) %collective-permute-start.19) | collective-permute-done | bytes 589856 | tf_op jit(solution)/shard_map/ppermute | solution.py:24
  96.6 1.9 %collective-permute-done.23 = bf16[768,384]{1,0:T(8,128)(2,1)S(1)} collective-permute-done((bf16[768,384]{1,0:T(8,128)(2,1)S(1)}, bf16[768,384]{1,0:T(8,128)(2,1)S(1)}, u32[]{:S(2)}, u32[]{:S(2)}) %collective-permute-start.23) | collective-permute-done | bytes 589856 | tf_op jit(solution)/shard_map/ppermute | solution.py:24
  98.5 11.0 %shard_map.93 = bf16[5,384,384]{2,1,0:T(8,128)(2,1)} custom-call(bf16[1024,384]{1,0:T(8,128)(2,1)S(1)} %copy-done.1, bf16[1024,384]{1,0:T(8,128)(2,1)S(1)} %collective-permute-done.7.refs_1_, bf16[1024,384]{1,0:T(8,128)(2,1)S(1)} %collective-permute-done.8.refs_2_, bf16[1024,384]{1,0:T(8,128)(2,1)S(1)} %collective-permute-done.14.refs_3_, ...), custom_call_target="tpu_custom_call" | custom-call | flops 1000 | bytes 1000 | tf_op jit(solution)/shard_map/pallas_call | solution.py:258
  (56 shorter events, 6.9 us)
Async XLA Ops:
  0.6 39.8 %copy-start.5 = (s32[16,2]{0,1:T(2,128)S(1)}, s32[16,2]{0,1:T(2,128)}, u32[]{:S(2)}) copy-start(s32[16,2]{0,1:T(2,128)} %param.13) | copy-start | bytes 388
  0.6 39.8 %copy-start.7 = (s32[16]{0:T(128)S(1)}, s32[16]{0:T(128)}, u32[]{:S(2)}) copy-start(s32[16]{0:T(128)} %owners.3) | copy-start | bytes 196
  0.7 1.1 %copy-start = (bf16[1024,384]{1,0:T(8,128)(2,1)S(1)}, bf16[1024,384]{1,0:T(8,128)(2,1)}, u32[]{:S(2)}) copy-start(bf16[1024,384]{1,0:T(8,128)(2,1)} %pre_act.3) | copy-start | bytes 2359300
  3.1 15.4 %copy-start.8 = (f32[1,8,8,384]{3,2,1,0:T(8,128)S(1)}, f32[1,8,8,384]{3,2,1,0:T(8,128)}, u32[]{:S(2)}) copy-start(f32[1,8,8,384]{3,2,1,0:T(8,128)} %param.11) | copy-start | bytes 294916
  3.1 37.3 %copy-start.3 = (bf16[512,384]{1,0:T(8,128)(2,1)S(1)}, bf16[512,384]{1,0:T(8,128)(2,1)}, u32[]{:S(2)}) copy-start(bf16[512,384]{1,0:T(8,128)(2,1)} %out_grad.3) | copy-start | bytes 1179652
  4.6 12.4 %collective-permute-start = (bf16[64,384]{1,0:T(8,128)(2,1)S(1)}, bf16[64,384]{1,0:T(8,128)(2,1)S(1)}, u32[]{:S(2)}, u32[]{:S(2)}) collective-permute-start(bf16[64,384]{1,0:T(8,128)(2,1)S(1)} %get-tuple-element.48), channel_id=1, source_target_pairs={{0,4},{4,0},{8,12},{12,8},{1,5},{5,1},{9,13},{13,9},{2,6},{6,2},{1... | collective-permute-start | bytes 147464 | tf_op jit(solution)/shard_map/ppermute | solution.py:24
  7.7 9.3 %collective-permute-start.1 = (bf16[64,384]{1,0:T(8,128)(2,1)S(1)}, bf16[64,384]{1,0:T(8,128)(2,1)S(1)}, u32[]{:S(2)}, u32[]{:S(2)}) collective-permute-start(bf16[64,384]{1,0:T(8,128)(2,1)S(1)} %get-tuple-element.49), channel_id=1, source_target_pairs={{0,8},{4,12},{8,0},{12,4},{1,9},{5,13},{9,1},{13,5},{2,10},{6,14},... | collective-permute-start | bytes 147464 | tf_op jit(solution)/shard_map/ppermute | solution.py:24
  10.1 6.9 %collective-permute-start.2 = (bf16[64,384]{1,0:T(8,128)(2,1)S(1)}, bf16[64,384]{1,0:T(8,128)(2,1)S(1)}, u32[]{:S(2)}, u32[]{:S(2)}) collective-permute-start(bf16[64,384]{1,0:T(8,128)(2,1)S(1)} %get-tuple-element.50), channel_id=1, source_target_pairs={{0,12},{4,8},{8,4},{12,0},{1,13},{5,9},{9,5},{13,1},{2,14},{6,10},... | collective-permute-start | bytes 147464 | tf_op jit(solution)/shard_map/ppermute | solution.py:24
  10.1 20.3 %collective-permute-start.7 = (bf16[1024,384]{1,0:T(8,128)(2,1)}, bf16[1024,384]{1,0:T(8,128)(2,1)S(1)}, u32[]{:S(2)}, u32[]{:S(2)}) collective-permute-start(bf16[1024,384]{1,0:T(8,128)(2,1)} %refs_0_.1), channel_id=1, source_target_pairs={{0,4},{4,8},{8,12},{1,5},{5,9},{9,13},{2,6},{6,10},{10,14},{3,7},{... | collective-permute-start | bytes 2359304 | tf_op jit(solution)/shard_map/ppermute | solution.py:33
  13.1 21.3 %collective-permute-start.8 = (bf16[1024,384]{1,0:T(8,128)(2,1)}, bf16[1024,384]{1,0:T(8,128)(2,1)S(1)}, u32[]{:S(2)}, u32[]{:S(2)}) collective-permute-start(bf16[1024,384]{1,0:T(8,128)(2,1)} %refs_0_.1), channel_id=1, source_target_pairs={{4,0},{8,4},{12,8},{5,1},{9,5},{13,9},{6,2},{10,6},{14,10},{7,3},{... | collective-permute-start | bytes 2359304 | tf_op jit(solution)/shard_map/ppermute | solution.py:33
  17.0 22.3 %collective-permute-start.4 = (bf16[1024,384]{1,0:T(8,128)(2,1)S(1)}, bf16[1024,384]{1,0:T(8,128)(2,1)S(1)}, u32[]{:S(2)}, u32[]{:S(2)}) collective-permute-start(bf16[1024,384]{1,0:T(8,128)(2,1)S(1)} %get-tuple-element.53.refs_0_), channel_id=1, source_target_pairs={{0,2},{1,3},{2,0},{3,1},{4,6},{5,7},{6,4},{7,5},{8,10},{9,11},{10,... | collective-permute-start | bytes 2359304 | tf_op jit(solution)/shard_map/ppermute | solution.py:24
  18.5 49.5 %slice-start = ((s8[5898240]{0:T(1024)(128)(4,1)}), s8[4194304]{0:T(1024)(128)(4,1)S(1)}, s32[]{:S(2)}) async-start(s8[5898240]{0:T(1024)(128)(4,1)} %bitcast.9), calls=%async_computation | async-start | bytes 8388608
  18.6 49.4 %slice-start.1 = ((s8[5898240]{0:T(1024)(128)(4,1)}), s8[1703936]{0:T(1024)(128)(4,1)S(1)}, s32[]{:S(2)}) async-start(s8[5898240]{0:T(1024)(128)(4,1)} %bitcast.9), calls=%async_computation.1 | async-start | bytes 3407872
  18.6 18.7 %collective-permute-start.5 = (bf16[64,384]{1,0:T(8,128)(2,1)S(1)}, bf16[64,384]{1,0:T(8,128)(2,1)S(1)}, u32[]{:S(2)}, u32[]{:S(2)}) collective-permute-start(bf16[64,384]{1,0:T(8,128)(2,1)S(1)} %fusion.1.refs_0_), channel_id=1, source_target_pairs={{0,4},{4,0},{8,12},{12,8},{1,5},{5,1},{9,13},{13,9},{2,6},{6,2},{1... | collective-permute-start | bytes 147464 | tf_op jit(solution)/shard_map/ppermute | solution.py:24
  21.3 16.7 %collective-permute-start.6 = (bf16[64,384]{1,0:T(8,128)(2,1)S(1)}, bf16[64,384]{1,0:T(8,128)(2,1)S(1)}, u32[]{:S(2)}, u32[]{:S(2)}) collective-permute-start(bf16[64,384]{1,0:T(8,128)(2,1)S(1)} %fusion.1.refs_0_), channel_id=1, source_target_pairs={{0,8},{4,12},{8,0},{12,4},{1,9},{5,13},{9,1},{13,5},{2,10},{6,14},... | collective-permute-start | bytes 147464 | tf_op jit(solution)/shard_map/ppermute | solution.py:24
  34.5 5.9 %collective-permute-start.9 = (bf16[64,384]{1,0:T(8,128)(2,1)S(1)}, bf16[64,384]{1,0:T(8,128)(2,1)S(1)}, u32[]{:S(2)}, u32[]{:S(2)}) collective-permute-start(bf16[64,384]{1,0:T(8,128)(2,1)S(1)} %fusion.1.refs_0_), channel_id=1, source_target_pairs={{0,12},{4,8},{8,4},{12,0},{1,13},{5,9},{9,5},{13,1},{2,14},{6,10},... | collective-permute-start | bytes 147464 | tf_op jit(solution)/shard_map/ppermute | solution.py:24
  37.3 23.5 %collective-permute-start.3 = (bf16[1024,384]{1,0:T(8,128)(2,1)S(1)}, bf16[1024,384]{1,0:T(8,128)(2,1)S(1)}, u32[]{:S(2)}, u32[]{:S(2)}) collective-permute-start(bf16[1024,384]{1,0:T(8,128)(2,1)S(1)} %get-tuple-element.53.refs_0_), channel_id=1, source_target_pairs={{0,1},{1,0},{2,3},{3,2},{4,5},{5,4},{6,7},{7,6},{8,9},{9,8},{10,11... | collective-permute-start | bytes 2359304 | tf_op jit(solution)/shard_map/ppermute | solution.py:24
  37.3 15.0 %collective-permute-start.14 = (bf16[1024,384]{1,0:T(8,128)(2,1)S(1)}, bf16[1024,384]{1,0:T(8,128)(2,1)S(1)}, u32[]{:S(2)}, u32[]{:S(2)}) collective-permute-start(bf16[1024,384]{1,0:T(8,128)(2,1)S(1)} %collective-permute-done.7.refs_1_), channel_id=1, source_target_pairs={{4,8},{8,12},{5,9},{9,13},{6,10},{10,14},{7,11},{11,15},{20,24},{2... | collective-permute-start | bytes 2359304 | tf_op jit(solution)/shard_map/ppermute | solution.py:33
  38.0 22.8 %collective-permute-start.15 = (bf16[1024,384]{1,0:T(8,128)(2,1)S(1)}, bf16[1024,384]{1,0:T(8,128)(2,1)S(1)}, u32[]{:S(2)}, u32[]{:S(2)}) collective-permute-start(bf16[1024,384]{1,0:T(8,128)(2,1)S(1)} %collective-permute-done.8.refs_2_), channel_id=1, source_target_pairs={{4,0},{8,4},{5,1},{9,5},{6,2},{10,6},{7,3},{11,7},{20,16},{24,20},... | collective-permute-start | bytes 2359304 | tf_op jit(solution)/shard_map/ppermute | solution.py:33
  39.3 21.5 %collective-permute-start.13 = (bf16[1024,384]{1,0:T(8,128)(2,1)S(1)}, bf16[1024,384]{1,0:T(8,128)(2,1)S(1)}, u32[]{:S(2)}, u32[]{:S(2)}) collective-permute-start(bf16[1024,384]{1,0:T(8,128)(2,1)S(1)} %collective-permute-done.4.refs_2_), channel_id=1, source_target_pairs={{0,1},{1,0},{2,3},{3,2},{4,5},{5,4},{6,7},{7,6},{8,9},{9,8},{10,11... | collective-permute-start | bytes 2359304 | tf_op jit(solution)/shard_map/ppermute | solution.py:24
  42.4 25.6 %copy-start.1 = (bf16[1024,384]{1,0:T(8,128)(2,1)S(1)}, bf16[1024,384]{1,0:T(8,128)(2,1)}, u32[]{:S(2)}) copy-start(bf16[1024,384]{1,0:T(8,128)(2,1)} %refs_0_.1) | copy-start | bytes 2359300
  42.4 6.9 %collective-permute-start.11 = (bf16[288,384]{1,0:T(8,128)(2,1)S(1)}, bf16[288,384]{1,0:T(8,128)(2,1)S(1)}, u32[]{:S(2)}, u32[]{:S(2)}) collective-permute-start(bf16[288,384]{1,0:T(8,128)(2,1)S(1)} %shard_map.88.refs_4_), channel_id=1, source_target_pairs={{0,2},{1,3},{2,0},{3,1},{4,6},{5,7},{6,4},{7,5},{8,10},{9,11},{10,... | collective-permute-start | bytes 663560 | tf_op jit(solution)/shard_map/ppermute | solution.py:24
  49.4 1.5 %collective-permute-start.10 = (bf16[288,384]{1,0:T(8,128)(2,1)S(1)}, bf16[288,384]{1,0:T(8,128)(2,1)S(1)}, u32[]{:S(2)}, u32[]{:S(2)}) collective-permute-start(bf16[288,384]{1,0:T(8,128)(2,1)S(1)} %shard_map.88.refs_4_), channel_id=1, source_target_pairs={{0,1},{1,0},{2,3},{3,2},{4,5},{5,4},{6,7},{7,6},{8,9},{9,8},{10,11... | collective-permute-start | bytes 663560 | tf_op jit(solution)/shard_map/ppermute | solution.py:24
  50.9 1.5 %collective-permute-start.12 = (bf16[288,384]{1,0:T(8,128)(2,1)S(1)}, bf16[288,384]{1,0:T(8,128)(2,1)S(1)}, u32[]{:S(2)}, u32[]{:S(2)}) collective-permute-start(bf16[288,384]{1,0:T(8,128)(2,1)S(1)} %collective-permute-done.11.refs_6_), channel_id=1, source_target_pairs={{0,1},{1,0},{2,3},{3,2},{4,5},{5,4},{6,7},{7,6},{8,9},{9,8},{10,11... | collective-permute-start | bytes 663560 | tf_op jit(solution)/shard_map/ppermute | solution.py:24
  62.2 20.7 %collective-permute-start.16 = (bf16[272,384]{1,0:T(8,128)(2,1)S(1)}, bf16[272,384]{1,0:T(8,128)(2,1)S(1)}, u32[]{:S(2)}, u32[]{:S(2)}) collective-permute-start(bf16[272,384]{1,0:T(8,128)(2,1)S(1)} %get-tuple-element.71), channel_id=1, source_target_pairs={{0,4},{4,0},{8,12},{12,8},{1,5},{5,1},{9,13},{13,9},{2,6},{6,2},{1... | collective-permute-start | bytes 626696 | tf_op jit(solution)/shard_map/ppermute | solution.py:24
  64.0 18.9 %collective-permute-start.18 = (bf16[272,384]{1,0:T(8,128)(2,1)S(1)}, bf16[272,384]{1,0:T(8,128)(2,1)S(1)}, u32[]{:S(2)}, u32[]{:S(2)}) collective-permute-start(bf16[272,384]{1,0:T(8,128)(2,1)S(1)} %get-tuple-element.73), channel_id=1, source_target_pairs={{0,12},{4,8},{8,4},{12,0},{1,13},{5,9},{9,5},{13,1},{2,14},{6,10},... | collective-permute-start | bytes 626696 | tf_op jit(solution)/shard_map/ppermute | solution.py:24
  64.4 18.5 %collective-permute-start.17 = (bf16[256,384]{1,0:T(8,128)(2,1)S(1)}, bf16[256,384]{1,0:T(8,128)(2,1)S(1)}, u32[]{:S(2)}, u32[]{:S(2)}) collective-permute-start(bf16[256,384]{1,0:T(8,128)(2,1)S(1)} %get-tuple-element.72), channel_id=1, source_target_pairs={{0,8},{4,12},{8,0},{12,4},{1,9},{5,13},{9,1},{13,5},{2,10},{6,14},... | collective-permute-start | bytes 589832 | tf_op jit(solution)/shard_map/ppermute | solution.py:24
  65.8 23.7 %collective-permute-start.20 = (bf16[1024,384]{1,0:T(8,128)(2,1)S(1)}, bf16[1024,384]{1,0:T(8,128)(2,1)S(1)}, u32[]{:S(2)}, u32[]{:S(2)}) collective-permute-start(bf16[1024,384]{1,0:T(8,128)(2,1)S(1)} %collective-permute-done.14.refs_3_), channel_id=1, source_target_pairs={{8,12},{9,13},{10,14},{11,15},{24,28},{25,29},{26,30},{27,31}} | collective-permute-start | bytes 2359304 | tf_op jit(solution)/shard_map/ppermute | solution.py:33
  66.5 27.8 %collective-permute-start.21 = (bf16[1024,384]{1,0:T(8,128)(2,1)S(1)}, bf16[1024,384]{1,0:T(8,128)(2,1)S(1)}, u32[]{:S(2)}, u32[]{:S(2)}) collective-permute-start(bf16[1024,384]{1,0:T(8,128)(2,1)S(1)} %collective-permute-done.15.refs_4_), channel_id=1, source_target_pairs={{4,0},{5,1},{6,2},{7,3},{20,16},{21,17},{22,18},{23,19}} | collective-permute-start | bytes 2359304 | tf_op jit(solution)/shard_map/ppermute | solution.py:33
  83.1 13.4 %collective-permute-start.19 = (bf16[768,384]{1,0:T(8,128)(2,1)S(1)}, bf16[768,384]{1,0:T(8,128)(2,1)S(1)}, u32[]{:S(2)}, u32[]{:S(2)}) collective-permute-start(bf16[768,384]{1,0:T(8,128)(2,1)S(1)} %pad_maximum_fusion), channel_id=1, source_target_pairs={{0,2},{1,3},{2,0},{3,1},{4,6},{5,7},{6,4},{7,5},{8,10},{9,11},{10,... | collective-permute-start | bytes 1769480 | tf_op jit(solution)/shard_map/ppermute | solution.py:24
  84.6 11.9 %collective-permute-start.22 = (bf16[768,384]{1,0:T(8,128)(2,1)S(1)}, bf16[768,384]{1,0:T(8,128)(2,1)S(1)}, u32[]{:S(2)}, u32[]{:S(2)}) collective-permute-start(bf16[768,384]{1,0:T(8,128)(2,1)S(1)} %pad_maximum_fusion), channel_id=1, source_target_pairs={{0,1},{1,0},{2,3},{3,2},{4,5},{5,4},{6,7},{7,6},{8,9},{9,8},{10,11... | collective-permute-start | bytes 1769480 | tf_op jit(solution)/shard_map/ppermute | solution.py:24
  96.5 2.0 %collective-permute-start.23 = (bf16[768,384]{1,0:T(8,128)(2,1)S(1)}, bf16[768,384]{1,0:T(8,128)(2,1)S(1)}, u32[]{:S(2)}, u32[]{:S(2)}) collective-permute-start(bf16[768,384]{1,0:T(8,128)(2,1)S(1)} %collective-permute-done.19), channel_id=1, source_target_pairs={{0,1},{1,0},{2,3},{3,2},{4,5},{5,4},{6,7},{7,6},{8,9},{9,8},{10,11... | collective-permute-start | bytes 1769480 | tf_op jit(solution)/shard_map/ppermute | solution.py:24
  (3 other events, 2.3 us)

commit v11 on v10

--- a/solution.py
+++ b/solution.py
@@ -196,11 +196,13 @@
                 )
         for move in moves:
             move.start()
-    acc[...] = jnp.zeros_like(acc) if first else before[...]
+    short = size == tile and not seams and width % LANES == 0
+    if not short:
+        acc[...] = jnp.zeros_like(acc) if first else before[...]
     if not stages:
         each(lambda at: copy(at).wait())
 
-    def add(start, count, side=None):
+    def add(start, count, side=None, base=None, close=False):
         grad = gbuf[pl.ds(start, count), :].T
         block = xbuf[pl.ds(start, count + 2 * PAD), :].astype(jnp.float32)
         if side is not None:
@@ -215,20 +217,36 @@
                 acc[tap] += jnp.dot(grad, moved[tap], preferred_element_type=jnp.float32)
         else:
             moved = jnp.concatenate(moved, axis=1)
-            acc[...] += jnp.dot(grad, moved, preferred_element_type=jnp.float32)
+            total = jnp.dot(grad, moved, preferred_element_type=jnp.float32)
+            if base is not None:
+                total = base[...] + total
+            if not close:
+                acc[...] = total
+            elif last:
+                for tap in range(taps):
+                    out[tap] = total[:, tap * width : (tap + 1) * width].astype(out.dtype)
+            else:
+                out[...] = total
 
     for stage, begin in enumerate(starts):
         if stages:
             each(lambda at: copy(at).wait(), stage)
 
+        if short:
+            base = acc if stage else before
+            add(pl.multiple_of(begin, 16), tile, None, base, stage == len(starts) - 1)
+            continue
+
         def body(step, carry):
-            add(pl.multiple_of(begin + step * tile, 16), tile)
+            add(pl.multiple_of(begin + step * tile, 16), tile, None, acc)
             return carry
 
         lax.fori_loop(0, size // tile, body, 0)
     for wanted, row, side in seams:
-        pl.when(wanted)(functools.partial(add, row, PAD, side))
-    if last and width % LANES == 0:
+        pl.when(wanted)(functools.partial(add, row, PAD, side, acc))
+    if short:
+        pass
+    elif last and width % LANES == 0:
         for tap in range(taps):
             out[tap] = acc[:, tap * width : (tap + 1) * width].astype(out.dtype)
     else:
@@ -629,47 +647,59 @@
         origins=origins,
     )
     center = pieces_gradient(parts, laid, taps)
-    *got, partial, center = after([*got, partial, center])
-
-    crossing = jnp.concatenate([block[:quarter] for block in got])
+    first, *rest, partial, center = after([*got, partial, center])
+    across_first = swap(first, "ch", 2)
+    crossing = jnp.concatenate([block[:quarter] for block in rest])
     across = swap(crossing, "ch", 2)
     beside = swap(crossing, "ch", 1)
-    in_grad = pieces_gradient(parts, laid, taps, [got[0], got[2], center])
-    across, in_grad, up3, down3 = after([across, in_grad, up3, down3])
-    beyond = swap(across, "ch", 1)
-
-    def layout():
+    beside_first = swap(first, "ch", 1)
+    in_grad = pieces_gradient(parts, laid, taps, [first, rest[1], center])
+    across_first, in_grad = after([across_first, in_grad])
+    beyond_first = swap(across_first, "ch", 1)
+
+    def layout(hops, blocks):
         mine = lax.axis_index("seq")
         place = lax.axis_index("ch")
         x_rows = [PAD + mine * rows]
-        for hop in range(1, nseq):
+        for hop in range(1, hops):
             low_at, high_at = mine - hop, mine + hop
             x_rows += [
                 jnp.where(low_at >= 0, PAD + low_at * rows, -1),
                 jnp.where(high_at < nseq, PAD + high_at * rows, -1),
             ]
         g_rows = [
-            (mine ^ d) * rows + (place ^ tag) * quarter
-            for d in range(1, nseq)
-            for tag in range(nch)
+            (mine ^ d) * rows + (place ^ tag) * quarter for d in blocks for tag in range(nch)
         ]
-        return x_rows, g_rows, [(mine ^ d) * rows for d in range(1, nseq)], [], []
-
-    g_pieces, stages = [], [0] * 5 + [1] * 2
-    for d in range(nseq - 1):
+        return x_rows, g_rows, [(mine ^ d) * rows for d in blocks], [], []
+
+    (partial,) = weight_gradient(
+        [x_saved, up1, down1, up2, down2],
+        [first, beside_first, across_first, beyond_first],
+        functools.partial(layout, 3, (1,)),
+        rows,
+        taps,
+        nseq * rows,
+        before=partial,
+        last=False,
+        vmem=32,
+        span=quarter,
+    )
+    across, in_grad, partial, up3, down3 = after([across, in_grad, partial, up3, down3])
+    beyond = swap(across, "ch", 1)
+
+    g_pieces = []
+    for d in range(nseq - 2):
         for piece in (crossing, beside, across, beyond):
             g_pieces.append(piece[d * quarter : (d + 1) * quarter])
-            stages.append(d)
     (w_grad,) = weight_gradient(
         [x_saved, up1, down1, up2, down2, up3, down3],
         g_pieces,
-        layout,
+        functools.partial(layout, nseq, (2, 3)),
         rows,
         taps,
         nseq * rows,
         before=partial,
         vmem=32,
-        stages=stages,
     )
     return (in_grad, w_grad.transpose(1, 0, 2))
 

time: 110 us -> 110 us (level)
  waiting for transfers between devices: 44.3 us -> 39.2 us
  local copies, waits for them, and re-layouts: 3.73 us -> 5.95 us
  starting transfers between devices: 31.7 us -> 33.6 us
    ppermute x6, waiting for transfers between devices: 23.2 us -> 15.1 us  [shift(): return lax.ppermute(block, axis, pairs)]
    ppermute x18 -> x21, waiting for transfers between devices: 21.1 us -> 24.1 us  [swap(): return lax.ppermute(block, axis, [(i, i ^ flip) for i in range(count)])]
    unnamed x22, local copies, waits for them, and re-layouts: 3.5 us -> 5.8 us
    ppermute x18 -> x21, starting transfers between devices: 23.3 us -> 25.3 us  [swap(): return lax.ppermute(block, axis, [(i, i ^ flip) for i in range(count)])]
    pallas_call x2 -> x3, Pallas kernels: 13.8 us -> 13.7 us  [weight_gradient(): pl.pallas_call(functools.partial(weight_kernel, taps=taps, tile=min(1024,...]
  transfers between devices with their start and end apart: 24 -> 27, of which waited for: 11 -> 11; matrix products, arithmetic and copies ran while one was open for 0% -> 1% of each run, Pallas kernels for 14% -> 16%
where the time goes in v11:
time: 110 us; the launch traced here: 109 us
  waiting for transfers between devices  39.2 us (36%)
  starting transfers between devices  33.6 us (31%)
  Pallas kernels  28 us (25%)
  local copies, waits for them, and re-layouts  5.95 us (5%)
  other arithmetic  1.12 us (1%)
  between operations  1.12 us (1%)
    ppermute x21, starting transfers between devices, swap(): return lax.ppermute(block, axis, [(i, i ^ flip) for i in range(count)])  25.3 us
    ppermute x21, waiting for transfers between devices, swap(): return lax.ppermute(block, axis, [(i, i ^ flip) for i in range(count)])  24.1 us
    ppermute x6, waiting for transfers between devices, shift(): return lax.ppermute(block, axis, pairs)  15.1 us
    pallas_call x3, Pallas kernels, weight_gradient(): pl.pallas_call(functools.partial(weight_kernel, taps=taps, tile=min(1024,...  13.7 us
    pallas_call x2, Pallas kernels, pieces_gradient(): pl.pallas_call(functools.partial(pieces_kernel, taps=taps, pieces=len(par...  8.51 us
    ppermute x6, starting transfers between devices, shift(): return lax.ppermute(block, axis, pairs)  8.33 us
    unnamed x22, local copies, waits for them, and re-layouts  5.8 us
  transfers between devices with their start and end apart: 27, of which 11 were waited for; matrix products, arithmetic and copies ran while one was open for 1% of the time, Pallas kernels for 16%

profile of v11, /device:TPU:0, one launch (start us, length us, event | category | flops | bytes accessed | tf_op | source)
XLA Modules:
  0.0 109.0 jit_solution(9597831100954574501)
XLA Ops:
  3.1 1.2 %shard_map.86 = (bf16[64,384]{1,0:T(8,128)(2,1)S(1)}, bf16[64,384]{1,0:T(8,128)(2,1)S(1)}, bf16[64,384]{1,0:T(8,128)(2,1)S(1)}, bf16[64,384]{1,0:T(8,128)(2,1)S(1)}) custom-call(s32[16]{0:T(128)S(1)} %copy-done.7, s32[2,16]{1,0:T(2,128)S(1)} %bitcast.12, bf16[1024,384]{1,0:T(8,128)(2,1)S(1)} %copy-done.1), custom_call_target="tpu_custom_call" | custom-call | flops 1000 | bytes 1000 | tf_op jit(solution)/shard_map/pallas_call | solution.py:379
  4.3 3.3 %collective-permute-start = (bf16[64,384]{1,0:T(8,128)(2,1)S(1)}, bf16[64,384]{1,0:T(8,128)(2,1)S(1)}, u32[]{:S(2)}, u32[]{:S(2)}) collective-permute-start(bf16[64,384]{1,0:T(8,128)(2,1)S(1)} %get-tuple-element.51), channel_id=1, source_target_pairs={{0,4},{4,0},{8,12},{12,8},{1,5},{5,1},{9,13},{13,9},{2,6},{6,2},{1... | collective-permute-start | bytes 147464 | tf_op jit(solution)/shard_map/ppermute | solution.py:24
  7.6 2.5 %collective-permute-start.1 = (bf16[64,384]{1,0:T(8,128)(2,1)S(1)}, bf16[64,384]{1,0:T(8,128)(2,1)S(1)}, u32[]{:S(2)}, u32[]{:S(2)}) collective-permute-start(bf16[64,384]{1,0:T(8,128)(2,1)S(1)} %get-tuple-element.52), channel_id=1, source_target_pairs={{0,8},{4,12},{8,0},{12,4},{1,9},{5,13},{9,1},{13,5},{2,10},{6,14},... | collective-permute-start | bytes 147464 | tf_op jit(solution)/shard_map/ppermute | solution.py:24
  10.2 2.9 %collective-permute-start.7 = (bf16[1024,384]{1,0:T(8,128)(2,1)}, bf16[1024,384]{1,0:T(8,128)(2,1)S(1)}, u32[]{:S(2)}, u32[]{:S(2)}) collective-permute-start(bf16[1024,384]{1,0:T(8,128)(2,1)} %refs_0_.3), channel_id=1, source_target_pairs={{0,4},{4,8},{8,12},{1,5},{5,9},{9,13},{2,6},{6,10},{10,14},{3,7},{... | collective-permute-start | bytes 2359304 | tf_op jit(solution)/shard_map/ppermute | solution.py:33
  13.0 1.3 %collective-permute-start.8 = (bf16[1024,384]{1,0:T(8,128)(2,1)}, bf16[1024,384]{1,0:T(8,128)(2,1)S(1)}, u32[]{:S(2)}, u32[]{:S(2)}) collective-permute-start(bf16[1024,384]{1,0:T(8,128)(2,1)} %refs_0_.3), channel_id=1, source_target_pairs={{4,0},{8,4},{12,8},{5,1},{9,5},{13,9},{6,2},{10,6},{14,10},{7,3},{... | collective-permute-start | bytes 2359304 | tf_op jit(solution)/shard_map/ppermute | solution.py:33
  15.3 1.4 %shard_map.87 = (f32[1024,384]{1,0:T(8,128)S(1)}, bf16[1024,384]{1,0:T(8,128)(2,1)S(1)}) custom-call(bf16[1024,384]{1,0:T(8,128)(2,1)S(1)} %copy-done.1, bf16[512,384]{1,0:T(8,128)(2,1)S(1)} %copy-done.2), custom_call_target="tpu_custom_call" | custom-call | flops 1000 | bytes 1000 | tf_op jit(solution)/shard_map/pallas_call | solution.py:406
  16.8 1.6 %collective-permute-start.4 = (bf16[1024,384]{1,0:T(8,128)(2,1)S(1)}, bf16[1024,384]{1,0:T(8,128)(2,1)S(1)}, u32[]{:S(2)}, u32[]{:S(2)}) collective-permute-start(bf16[1024,384]{1,0:T(8,128)(2,1)S(1)} %get-tuple-element.56.refs_0_), channel_id=1, source_target_pairs={{0,2},{1,3},{2,0},{3,1},{4,6},{5,7},{6,4},{7,5},{8,10},{9,11},{10,... | collective-permute-start | bytes 2359304 | tf_op jit(solution)/shard_map/ppermute | solution.py:24
  19.5 2.7 %collective-permute-start.5 = (bf16[64,384]{1,0:T(8,128)(2,1)S(1)}, bf16[64,384]{1,0:T(8,128)(2,1)S(1)}, u32[]{:S(2)}, u32[]{:S(2)}) collective-permute-start(bf16[64,384]{1,0:T(8,128)(2,1)S(1)} %fusion.1.refs_0_), channel_id=1, source_target_pairs={{0,4},{4,0},{8,12},{12,8},{1,5},{5,1},{9,13},{13,9},{2,6},{6,2},{1... | collective-permute-start | bytes 147464 | tf_op jit(solution)/shard_map/ppermute | solution.py:24
  22.2 3.4 %collective-permute-start.6 = (bf16[64,384]{1,0:T(8,128)(2,1)S(1)}, bf16[64,384]{1,0:T(8,128)(2,1)S(1)}, u32[]{:S(2)}, u32[]{:S(2)}) collective-permute-start(bf16[64,384]{1,0:T(8,128)(2,1)S(1)} %fusion.1.refs_0_), channel_id=1, source_target_pairs={{0,8},{4,12},{8,0},{12,4},{1,9},{5,13},{9,1},{13,5},{2,10},{6,14},... | collective-permute-start | bytes 147464 | tf_op jit(solution)/shard_map/ppermute | solution.py:24
  25.5 4.8 %collective-permute-done.7.refs_1_ = bf16[1024,384]{1,0:T(8,128)(2,1)S(1)} collective-permute-done((bf16[1024,384]{1,0:T(8,128)(2,1)}, bf16[1024,384]{1,0:T(8,128)(2,1)S(1)}, u32[]{:S(2)}, u32[]{:S(2)}) %collective-permute-start.7) | collective-permute-done | bytes 786464 | tf_op jit(solution)/shard_map/ppermute | solution.py:33
  30.3 4.1 %collective-permute-done.8.refs_2_ = bf16[1024,384]{1,0:T(8,128)(2,1)S(1)} collective-permute-done((bf16[1024,384]{1,0:T(8,128)(2,1)}, bf16[1024,384]{1,0:T(8,128)(2,1)S(1)}, u32[]{:S(2)}, u32[]{:S(2)}) %collective-permute-start.8) | collective-permute-done | bytes 786464 | tf_op jit(solution)/shard_map/ppermute | solution.py:33
  34.4 2.9 %collective-permute-start.9 = (bf16[64,384]{1,0:T(8,128)(2,1)S(1)}, bf16[64,384]{1,0:T(8,128)(2,1)S(1)}, u32[]{:S(2)}, u32[]{:S(2)}) collective-permute-start(bf16[64,384]{1,0:T(8,128)(2,1)S(1)} %fusion.1.refs_0_), channel_id=1, source_target_pairs={{0,12},{4,8},{8,4},{12,0},{1,13},{5,9},{9,5},{13,1},{2,14},{6,10},... | collective-permute-start | bytes 147464 | tf_op jit(solution)/shard_map/ppermute | solution.py:24
  38.0 1.3 %collective-permute-start.15 = (bf16[1024,384]{1,0:T(8,128)(2,1)S(1)}, bf16[1024,384]{1,0:T(8,128)(2,1)S(1)}, u32[]{:S(2)}, u32[]{:S(2)}) collective-permute-start(bf16[1024,384]{1,0:T(8,128)(2,1)S(1)} %collective-permute-done.8.refs_2_), channel_id=1, source_target_pairs={{4,0},{8,4},{5,1},{9,5},{6,2},{10,6},{7,3},{11,7},{20,16},{24,20},... | collective-permute-start | bytes 2359304 | tf_op jit(solution)/shard_map/ppermute | solution.py:33
  42.6 1.8 %shard_map.88.refs_4_ = bf16[288,384]{1,0:T(8,128)(2,1)S(1)} custom-call(s32[16]{0:T(128)S(1)} %copy-done.8, s32[2,16]{1,0:T(2,128)S(1)} %bitcast.13, bf16[512,384]{1,0:T(8,128)(2,1)S(1)} %copy-done.3, f32[1024,384]{1,0:T(8,128)S(1)} %get-tuple-element.57.slope, bf16[64,384]{1,0:T(8,128)(2,1)S(1)} %fusion.1.refs_0_, ...), custom_call_target="tpu_custom_call" | custom-call | flops 4000000000 | bytes 1000 | tf_op jit(solution)/shard_map/pallas_call | solution.py:453
  44.5 1.6 %collective-permute-start.11 = (bf16[288,384]{1,0:T(8,128)(2,1)S(1)}, bf16[288,384]{1,0:T(8,128)(2,1)S(1)}, u32[]{:S(2)}, u32[]{:S(2)}) collective-permute-start(bf16[288,384]{1,0:T(8,128)(2,1)S(1)} %shard_map.88.refs_4_), channel_id=1, source_target_pairs={{0,2},{1,3},{2,0},{3,1},{4,6},{5,7},{6,4},{7,5},{8,10},{9,11},{10,... | collective-permute-start | bytes 663560 | tf_op jit(solution)/shard_map/ppermute | solution.py:24
  46.0 5.5 %collective-permute-done.11.refs_6_ = bf16[288,384]{1,0:T(8,128)(2,1)S(1)} collective-permute-done((bf16[288,384]{1,0:T(8,128)(2,1)S(1)}, bf16[288,384]{1,0:T(8,128)(2,1)S(1)}, u32[]{:S(2)}, u32[]{:S(2)}) %collective-permute-start.11) | collective-permute-done | bytes 221216 | tf_op jit(solution)/shard_map/ppermute | solution.py:24
  51.5 1.5 %collective-permute-done.10.refs_5_ = bf16[288,384]{1,0:T(8,128)(2,1)S(1)} collective-permute-done((bf16[288,384]{1,0:T(8,128)(2,1)S(1)}, bf16[288,384]{1,0:T(8,128)(2,1)S(1)}, u32[]{:S(2)}, u32[]{:S(2)}) %collective-permute-start.10) | collective-permute-done | bytes 221216 | tf_op jit(solution)/shard_map/ppermute | solution.py:24
  53.1 1.3 %collective-permute-done.12.refs_7_ = bf16[288,384]{1,0:T(8,128)(2,1)S(1)} collective-permute-done((bf16[288,384]{1,0:T(8,128)(2,1)S(1)}, bf16[288,384]{1,0:T(8,128)(2,1)S(1)}, u32[]{:S(2)}, u32[]{:S(2)}) %collective-permute-start.12) | collective-permute-done | bytes 221216 | tf_op jit(solution)/shard_map/ppermute | solution.py:24
  54.5 6.3 %collective-permute-done.15.refs_4_ = bf16[1024,384]{1,0:T(8,128)(2,1)S(1)} collective-permute-done((bf16[1024,384]{1,0:T(8,128)(2,1)S(1)}, bf16[1024,384]{1,0:T(8,128)(2,1)S(1)}, u32[]{:S(2)}, u32[]{:S(2)}) %collective-permute-start.15) | collective-permute-done | bytes 786464 | tf_op jit(solution)/shard_map/ppermute | solution.py:33
  60.8 1.4 %shard_map.89 = (bf16[1024,384]{1,0:T(8,128)(2,1)S(1)}, bf16[1024,384]{1,0:T(8,128)(2,1)S(1)}, bf16[1024,384]{1,0:T(8,128)(2,1)S(1)}, bf16[1024,384]{1,0:T(8,128...) custom-call(s32[2,16]{1,0:T(2,128)S(1)} %bitcast.14, ...), custom_call_target="tpu_custom_call", output_to_operand_aliasing={{0}: (1, {}), {1}: (2, {}), {2}: (3, {}), {3}: (4, {})} | custom-call | flops 1000 | bytes 1000 | tf_op jit(solution)/shard_map/pallas_call | solution.py:529
  62.2 1.9 %collective-permute-start.16 = (bf16[272,384]{1,0:T(8,128)(2,1)S(1)}, bf16[272,384]{1,0:T(8,128)(2,1)S(1)}, u32[]{:S(2)}, u32[]{:S(2)}) collective-permute-start(bf16[272,384]{1,0:T(8,128)(2,1)S(1)} %get-tuple-element.74), channel_id=1, source_target_pairs={{0,4},{4,0},{8,12},{12,8},{1,5},{5,1},{9,13},{13,9},{2,6},{6,2},{1... | collective-permute-start | bytes 626696 | tf_op jit(solution)/shard_map/ppermute | solution.py:24
  64.5 1.2 %collective-permute-start.17 = (bf16[256,384]{1,0:T(8,128)(2,1)S(1)}, bf16[256,384]{1,0:T(8,128)(2,1)S(1)}, u32[]{:S(2)}, u32[]{:S(2)}) collective-permute-start(bf16[256,384]{1,0:T(8,128)(2,1)S(1)} %get-tuple-element.75), channel_id=1, source_target_pairs={{0,8},{4,12},{8,0},{12,4},{1,9},{5,13},{9,1},{13,5},{2,10},{6,14},... | collective-permute-start | bytes 589832 | tf_op jit(solution)/shard_map/ppermute | solution.py:24
  66.4 1.5 %collective-permute-start.24 = (bf16[1024,384]{1,0:T(8,128)(2,1)S(1)}, bf16[1024,384]{1,0:T(8,128)(2,1)S(1)}, u32[]{:S(2)}, u32[]{:S(2)}) collective-permute-start(bf16[1024,384]{1,0:T(8,128)(2,1)S(1)} %collective-permute-done.15.refs_4_), channel_id=1, source_target_pairs={{4,0},{5,1},{6,2},{7,3},{20,16},{21,17},{22,18},{23,19}} | collective-permute-start | bytes 2359304 | tf_op jit(solution)/shard_map/ppermute | solution.py:33
  68.0 2.8 %shard_map.90 = (f32[384,1920]{1,0:T(8,128)S(1)}, bf16[1536,1920]{1,0:T(8,128)(2,1)S(1)}) custom-call(bf16[16,384]{1,0:T(8,128)(2,1)S(1)} %slice.36.refs_0_, bf16[1024,384]{1,0:T(8,128)(2,1)S(1)} %copy-done, bf16[16,384]{1,0:T(8,128)(2,1)S(1)} %slice.37.refs_2_, bf16[1024,384]{1,0:T(8,128)(2,1)S(1)} %get-tuple-element.77.refs_3_, ...), custom_call_target="tpu_custom_call" | custom-call | flops 1000 | bytes 1000 | tf_op jit(solution)/shard_map/pallas_call | solution.py:276
  70.8 3.7 %shard_map.91.refs_6_ = bf16[512,384]{1,0:T(8,128)(2,1)S(1)} custom-call(bf16[1024,384]{1,0:T(8,128)(2,1)S(1)} %get-tuple-element.79.refs_0_, bf16[1024,384]{1,0:T(8,128)(2,1)S(1)} %get-tuple-element.80.refs_1_, bf16[1024,384]{1,0:T(8,128)(2,1)S(1)} %get-tuple-element.81.refs_2_, bf16[1024,384]{1,0:T(8,128)(2,1)S(1)} %get-tuple-element.82.refs_3_, ...), custom_call_target="tpu_custom_call" | custom-call | flops 1000 | bytes 1000 | tf_op jit(solution)/shard_map/pallas_call | solution.py:133
  74.5 8.3 %collective-permute-done.17.refs_7_ = bf16[256,384]{1,0:T(8,128)(2,1)S(1)} collective-permute-done((bf16[256,384]{1,0:T(8,128)(2,1)S(1)}, bf16[256,384]{1,0:T(8,128)(2,1)S(1)}, u32[]{:S(2)}, u32[]{:S(2)}) %collective-permute-start.17) | collective-permute-done | bytes 196640 | tf_op jit(solution)/shard_map/ppermute | solution.py:24
  82.9 1.5 %collective-permute-start.20 = (bf16[272,384]{1,0:T(8,128)(2,1)S(1)}, bf16[272,384]{1,0:T(8,128)(2,1)S(1)}, u32[]{:S(2)}, u32[]{:S(2)}) collective-permute-start(bf16[272,384]{1,0:T(8,128)(2,1)S(1)} %collective-permute-done.16.refs_4_.refs_5_), channel_id=1, source_target_pairs={{0,2},{1,3},{2,0},{3,1},{4,6},{5,7},{6,4},{7,5},{8,10},{9,11},{10,... | collective-permute-start | bytes 626696 | tf_op jit(solution)/shard_map/ppermute | solution.py:24
  85.1 4.7 %collective-permute-done.20.refs_7_ = bf16[272,384]{1,0:T(8,128)(2,1)S(1)} collective-permute-done((bf16[272,384]{1,0:T(8,128)(2,1)S(1)}, bf16[272,384]{1,0:T(8,128)(2,1)S(1)}, u32[]{:S(2)}, u32[]{:S(2)}) %collective-permute-start.20) | collective-permute-done | bytes 208928 | tf_op jit(solution)/shard_map/ppermute | solution.py:24
  89.7 4.8 %shard_map.92 = bf16[1024,384]{1,0:T(8,128)(2,1)} custom-call(bf16[1024,384]{1,0:T(8,128)(2,1)S(1)} %get-tuple-element.79.refs_0_, bf16[1024,384]{1,0:T(8,128)(2,1)S(1)} %get-tuple-element.80.refs_1_, bf16[1024,384]{1,0:T(8,128)(2,1)S(1)} %get-tuple-element.81.refs_2_, bf16[1024,384]{1,0:T(8,128)(2,1)S(1)} %get-tuple-element.82.refs_3_, ...), custom_call_target="tpu_custom_call" | custom-call | flops 1000 | bytes 1000 | tf_op jit(solution)/shard_map/pallas_call | solution.py:133
  96.2 3.1 %shard_map.93.refs_15_ = f32[384,1920]{1,0:T(8,128)S(1)} custom-call(bf16[1024,384]{1,0:T(8,128)(2,1)S(1)} %copy-done, bf16[1024,384]{1,0:T(8,128)(2,1)S(1)} %collective-permute-done.7.refs_1_, bf16[1024,384]{1,0:T(8,128)(2,1)S(1)} %collective-permute-done.8.refs_2_, bf16[1024,384]{1,0:T(8,128)(2,1)S(1)} %collective-permute-done.14.refs_3_, ...), custom_call_target="tpu_custom_call" | custom-call | flops 1000 | bytes 1000 | tf_op jit(solution)/shard_map/pallas_call | solution.py:276
  99.9 1.3 %collective-permute-done.26 = bf16[512,384]{1,0:T(8,128)(2,1)S(1)} collective-permute-done((bf16[512,384]{1,0:T(8,128)(2,1)S(1)}, bf16[512,384]{1,0:T(8,128)(2,1)S(1)}, u32[]{:S(2)}, u32[]{:S(2)}) %collective-permute-start.26) | collective-permute-done | bytes 393248 | tf_op jit(solution)/shard_map/ppermute | solution.py:24
  101.2 7.7 %shard_map.94 = bf16[5,384,384]{2,1,0:T(8,128)(2,1)} custom-call(bf16[1024,384]{1,0:T(8,128)(2,1)S(1)} %copy-done, bf16[1024,384]{1,0:T(8,128)(2,1)S(1)} %collective-permute-done.7.refs_1_, bf16[1024,384]{1,0:T(8,128)(2,1)S(1)} %collective-permute-done.8.refs_2_, bf16[1024,384]{1,0:T(8,128)(2,1)S(1)} %collective-permute-done.14.refs_3_, ...), custom_call_target="tpu_custom_call" | custom-call | flops 1000 | bytes 1000 | tf_op jit(solution)/shard_map/pallas_call | solution.py:276
  (62 shorter events, 12.8 us)
Async XLA Ops:
  0.6 1.1 %copy-start.1 = (bf16[1024,384]{1,0:T(8,128)(2,1)S(1)}, bf16[1024,384]{1,0:T(8,128)(2,1)}, u32[]{:S(2)}) copy-start(bf16[1024,384]{1,0:T(8,128)(2,1)} %pre_act.3) | copy-start | bytes 2359300
  4.3 12.4 %collective-permute-start = (bf16[64,384]{1,0:T(8,128)(2,1)S(1)}, bf16[64,384]{1,0:T(8,128)(2,1)S(1)}, u32[]{:S(2)}, u32[]{:S(2)}) collective-permute-start(bf16[64,384]{1,0:T(8,128)(2,1)S(1)} %get-tuple-element.51), channel_id=1, source_target_pairs={{0,4},{4,0},{8,12},{12,8},{1,5},{5,1},{9,13},{13,9},{2,6},{6,2},{1... | collective-permute-start | bytes 147464 | tf_op jit(solution)/shard_map/ppermute | solution.py:24
  7.6 9.2 %collective-permute-start.1 = (bf16[64,384]{1,0:T(8,128)(2,1)S(1)}, bf16[64,384]{1,0:T(8,128)(2,1)S(1)}, u32[]{:S(2)}, u32[]{:S(2)}) collective-permute-start(bf16[64,384]{1,0:T(8,128)(2,1)S(1)} %get-tuple-element.52), channel_id=1, source_target_pairs={{0,8},{4,12},{8,0},{12,4},{1,9},{5,13},{9,1},{13,5},{2,10},{6,14},... | collective-permute-start | bytes 147464 | tf_op jit(solution)/shard_map/ppermute | solution.py:24
  10.1 6.7 %collective-permute-start.2 = (bf16[64,384]{1,0:T(8,128)(2,1)S(1)}, bf16[64,384]{1,0:T(8,128)(2,1)S(1)}, u32[]{:S(2)}, u32[]{:S(2)}) collective-permute-start(bf16[64,384]{1,0:T(8,128)(2,1)S(1)} %get-tuple-element.53), channel_id=1, source_target_pairs={{0,12},{4,8},{8,4},{12,0},{1,13},{5,9},{9,5},{13,1},{2,14},{6,10},... | collective-permute-start | bytes 147464 | tf_op jit(solution)/shard_map/ppermute | solution.py:24
  10.2 20.1 %collective-permute-start.7 = (bf16[1024,384]{1,0:T(8,128)(2,1)}, bf16[1024,384]{1,0:T(8,128)(2,1)S(1)}, u32[]{:S(2)}, u32[]{:S(2)}) collective-permute-start(bf16[1024,384]{1,0:T(8,128)(2,1)} %refs_0_.3), channel_id=1, source_target_pairs={{0,4},{4,8},{8,12},{1,5},{5,9},{9,13},{2,6},{6,10},{10,14},{3,7},{... | collective-permute-start | bytes 2359304 | tf_op jit(solution)/shard_map/ppermute | solution.py:33
  13.0 21.3 %collective-permute-start.8 = (bf16[1024,384]{1,0:T(8,128)(2,1)}, bf16[1024,384]{1,0:T(8,128)(2,1)S(1)}, u32[]{:S(2)}, u32[]{:S(2)}) collective-permute-start(bf16[1024,384]{1,0:T(8,128)(2,1)} %refs_0_.3), channel_id=1, source_target_pairs={{4,0},{8,4},{12,8},{5,1},{9,5},{13,9},{6,2},{10,6},{14,10},{7,3},{... | collective-permute-start | bytes 2359304 | tf_op jit(solution)/shard_map/ppermute | solution.py:33
  16.8 44.0 %copy-start.6 = (s32[16,2]{0,1:T(2,128)S(1)}, s32[16,2]{0,1:T(2,128)}, u32[]{:S(2)}) copy-start(s32[16,2]{0,1:T(2,128)} %param.13) | copy-start | bytes 388
  16.8 22.5 %collective-permute-start.4 = (bf16[1024,384]{1,0:T(8,128)(2,1)S(1)}, bf16[1024,384]{1,0:T(8,128)(2,1)S(1)}, u32[]{:S(2)}, u32[]{:S(2)}) collective-permute-start(bf16[1024,384]{1,0:T(8,128)(2,1)S(1)} %get-tuple-element.56.refs_0_), channel_id=1, source_target_pairs={{0,2},{1,3},{2,0},{3,1},{4,6},{5,7},{6,4},{7,5},{8,10},{9,11},{10,... | collective-permute-start | bytes 2359304 | tf_op jit(solution)/shard_map/ppermute | solution.py:24
  18.4 49.6 %slice-start = ((s8[5898240]{0:T(1024)(128)(4,1)}), s8[4194304]{0:T(1024)(128)(4,1)S(1)}, s32[]{:S(2)}) async-start(s8[5898240]{0:T(1024)(128)(4,1)} %bitcast.9), calls=%async_computation | async-start | bytes 8388608
  19.4 48.5 %slice-start.1 = ((s8[5898240]{0:T(1024)(128)(4,1)}), s8[1703936]{0:T(1024)(128)(4,1)S(1)}, s32[]{:S(2)}) async-start(s8[5898240]{0:T(1024)(128)(4,1)} %bitcast.9), calls=%async_computation.1 | async-start | bytes 3407872
  19.5 17.9 %collective-permute-start.5 = (bf16[64,384]{1,0:T(8,128)(2,1)S(1)}, bf16[64,384]{1,0:T(8,128)(2,1)S(1)}, u32[]{:S(2)}, u32[]{:S(2)}) collective-permute-start(bf16[64,384]{1,0:T(8,128)(2,1)S(1)} %fusion.1.refs_0_), channel_id=1, source_target_pairs={{0,4},{4,0},{8,12},{12,8},{1,5},{5,1},{9,13},{13,9},{2,6},{6,2},{1... | collective-permute-start | bytes 147464 | tf_op jit(solution)/shard_map/ppermute | solution.py:24
  22.2 15.9 %collective-permute-start.6 = (bf16[64,384]{1,0:T(8,128)(2,1)S(1)}, bf16[64,384]{1,0:T(8,128)(2,1)S(1)}, u32[]{:S(2)}, u32[]{:S(2)}) collective-permute-start(bf16[64,384]{1,0:T(8,128)(2,1)S(1)} %fusion.1.refs_0_), channel_id=1, source_target_pairs={{0,8},{4,12},{8,0},{12,4},{1,9},{5,13},{9,1},{13,5},{2,10},{6,14},... | collective-permute-start | bytes 147464 | tf_op jit(solution)/shard_map/ppermute | solution.py:24
  34.4 5.9 %collective-permute-start.9 = (bf16[64,384]{1,0:T(8,128)(2,1)S(1)}, bf16[64,384]{1,0:T(8,128)(2,1)S(1)}, u32[]{:S(2)}, u32[]{:S(2)}) collective-permute-start(bf16[64,384]{1,0:T(8,128)(2,1)S(1)} %fusion.1.refs_0_), channel_id=1, source_target_pairs={{0,12},{4,8},{8,4},{12,0},{1,13},{5,9},{9,5},{13,1},{2,14},{6,10},... | collective-permute-start | bytes 147464 | tf_op jit(solution)/shard_map/ppermute | solution.py:24
  37.3 23.5 %collective-permute-start.3 = (bf16[1024,384]{1,0:T(8,128)(2,1)S(1)}, bf16[1024,384]{1,0:T(8,128)(2,1)S(1)}, u32[]{:S(2)}, u32[]{:S(2)}) collective-permute-start(bf16[1024,384]{1,0:T(8,128)(2,1)S(1)} %get-tuple-element.56.refs_0_), channel_id=1, source_target_pairs={{0,1},{1,0},{2,3},{3,2},{4,5},{5,4},{6,7},{7,6},{8,9},{9,8},{10,11... | collective-permute-start | bytes 2359304 | tf_op jit(solution)/shard_map/ppermute | solution.py:24
  37.3 17.2 %collective-permute-start.14 = (bf16[1024,384]{1,0:T(8,128)(2,1)S(1)}, bf16[1024,384]{1,0:T(8,128)(2,1)S(1)}, u32[]{:S(2)}, u32[]{:S(2)}) collective-permute-start(bf16[1024,384]{1,0:T(8,128)(2,1)S(1)} %collective-permute-done.7.refs_1_), channel_id=1, source_target_pairs={{4,8},{8,12},{5,9},{9,13},{6,10},{10,14},{7,11},{11,15},{20,24},{2... | collective-permute-start | bytes 2359304 | tf_op jit(solution)/shard_map/ppermute | solution.py:33
  38.0 22.8 %collective-permute-start.15 = (bf16[1024,384]{1,0:T(8,128)(2,1)S(1)}, bf16[1024,384]{1,0:T(8,128)(2,1)S(1)}, u32[]{:S(2)}, u32[]{:S(2)}) collective-permute-start(bf16[1024,384]{1,0:T(8,128)(2,1)S(1)} %collective-permute-done.8.refs_2_), channel_id=1, source_target_pairs={{4,0},{8,4},{5,1},{9,5},{6,2},{10,6},{7,3},{11,7},{20,16},{24,20},... | collective-permute-start | bytes 2359304 | tf_op jit(solution)/shard_map/ppermute | solution.py:33
  39.3 21.5 %collective-permute-start.13 = (bf16[1024,384]{1,0:T(8,128)(2,1)S(1)}, bf16[1024,384]{1,0:T(8,128)(2,1)S(1)}, u32[]{:S(2)}, u32[]{:S(2)}) collective-permute-start(bf16[1024,384]{1,0:T(8,128)(2,1)S(1)} %collective-permute-done.4.refs_2_), channel_id=1, source_target_pairs={{0,1},{1,0},{2,3},{3,2},{4,5},{5,4},{6,7},{7,6},{8,9},{9,8},{10,11... | collective-permute-start | bytes 2359304 | tf_op jit(solution)/shard_map/ppermute | solution.py:24
  44.5 23.5 %copy-start = (bf16[1024,384]{1,0:T(8,128)(2,1)S(1)}, bf16[1024,384]{1,0:T(8,128)(2,1)}, u32[]{:S(2)}) copy-start(bf16[1024,384]{1,0:T(8,128)(2,1)} %refs_0_.3) | copy-start | bytes 2359300
  44.5 7.1 %collective-permute-start.11 = (bf16[288,384]{1,0:T(8,128)(2,1)S(1)}, bf16[288,384]{1,0:T(8,128)(2,1)S(1)}, u32[]{:S(2)}, u32[]{:S(2)}) collective-permute-start(bf16[288,384]{1,0:T(8,128)(2,1)S(1)} %shard_map.88.refs_4_), channel_id=1, source_target_pairs={{0,2},{1,3},{2,0},{3,1},{4,6},{5,7},{6,4},{7,5},{8,10},{9,11},{10,... | collective-permute-start | bytes 663560 | tf_op jit(solution)/shard_map/ppermute | solution.py:24
  51.5 1.5 %collective-permute-start.10 = (bf16[288,384]{1,0:T(8,128)(2,1)S(1)}, bf16[288,384]{1,0:T(8,128)(2,1)S(1)}, u32[]{:S(2)}, u32[]{:S(2)}) collective-permute-start(bf16[288,384]{1,0:T(8,128)(2,1)S(1)} %shard_map.88.refs_4_), channel_id=1, source_target_pairs={{0,1},{1,0},{2,3},{3,2},{4,5},{5,4},{6,7},{7,6},{8,9},{9,8},{10,11... | collective-permute-start | bytes 663560 | tf_op jit(solution)/shard_map/ppermute | solution.py:24
  53.0 1.5 %collective-permute-start.12 = (bf16[288,384]{1,0:T(8,128)(2,1)S(1)}, bf16[288,384]{1,0:T(8,128)(2,1)S(1)}, u32[]{:S(2)}, u32[]{:S(2)}) collective-permute-start(bf16[288,384]{1,0:T(8,128)(2,1)S(1)} %collective-permute-done.11.refs_6_), channel_id=1, source_target_pairs={{0,1},{1,0},{2,3},{3,2},{4,5},{5,4},{6,7},{7,6},{8,9},{9,8},{10,11... | collective-permute-start | bytes 663560 | tf_op jit(solution)/shard_map/ppermute | solution.py:24
  62.2 20.7 %collective-permute-start.16 = (bf16[272,384]{1,0:T(8,128)(2,1)S(1)}, bf16[272,384]{1,0:T(8,128)(2,1)S(1)}, u32[]{:S(2)}, u32[]{:S(2)}) collective-permute-start(bf16[272,384]{1,0:T(8,128)(2,1)S(1)} %get-tuple-element.74), channel_id=1, source_target_pairs={{0,4},{4,0},{8,12},{12,8},{1,5},{5,1},{9,13},{13,9},{2,6},{6,2},{1... | collective-permute-start | bytes 626696 | tf_op jit(solution)/shard_map/ppermute | solution.py:24
  64.0 18.8 %collective-permute-start.18 = (bf16[272,384]{1,0:T(8,128)(2,1)S(1)}, bf16[272,384]{1,0:T(8,128)(2,1)S(1)}, u32[]{:S(2)}, u32[]{:S(2)}) collective-permute-start(bf16[272,384]{1,0:T(8,128)(2,1)S(1)} %get-tuple-element.76), channel_id=1, source_target_pairs={{0,12},{4,8},{8,4},{12,0},{1,13},{5,9},{9,5},{13,1},{2,14},{6,10},... | collective-permute-start | bytes 626696 | tf_op jit(solution)/shard_map/ppermute | solution.py:24
  64.5 18.4 %collective-permute-start.17 = (bf16[256,384]{1,0:T(8,128)(2,1)S(1)}, bf16[256,384]{1,0:T(8,128)(2,1)S(1)}, u32[]{:S(2)}, u32[]{:S(2)}) collective-permute-start(bf16[256,384]{1,0:T(8,128)(2,1)S(1)} %get-tuple-element.75), channel_id=1, source_target_pairs={{0,8},{4,12},{8,0},{12,4},{1,9},{5,13},{9,1},{13,5},{2,10},{6,14},... | collective-permute-start | bytes 589832 | tf_op jit(solution)/shard_map/ppermute | solution.py:24
  65.7 33.6 %collective-permute-start.23 = (bf16[1024,384]{1,0:T(8,128)(2,1)S(1)}, bf16[1024,384]{1,0:T(8,128)(2,1)S(1)}, u32[]{:S(2)}, u32[]{:S(2)}) collective-permute-start(bf16[1024,384]{1,0:T(8,128)(2,1)S(1)} %collective-permute-done.14.refs_3_), channel_id=1, source_target_pairs={{8,12},{9,13},{10,14},{11,15},{24,28},{25,29},{26,30},{27,31}} | collective-permute-start | bytes 2359304 | tf_op jit(solution)/shard_map/ppermute | solution.py:33
  66.4 32.9 %collective-permute-start.24 = (bf16[1024,384]{1,0:T(8,128)(2,1)S(1)}, bf16[1024,384]{1,0:T(8,128)(2,1)S(1)}, u32[]{:S(2)}, u32[]{:S(2)}) collective-permute-start(bf16[1024,384]{1,0:T(8,128)(2,1)S(1)} %collective-permute-done.15.refs_4_), channel_id=1, source_target_pairs={{4,0},{5,1},{6,2},{7,3},{20,16},{21,17},{22,18},{23,19}} | collective-permute-start | bytes 2359304 | tf_op jit(solution)/shard_map/ppermute | solution.py:33
  82.9 6.8 %collective-permute-start.20 = (bf16[272,384]{1,0:T(8,128)(2,1)S(1)}, bf16[272,384]{1,0:T(8,128)(2,1)S(1)}, u32[]{:S(2)}, u32[]{:S(2)}) collective-permute-start(bf16[272,384]{1,0:T(8,128)(2,1)S(1)} %collective-permute-done.16.refs_4_.refs_5_), channel_id=1, source_target_pairs={{0,2},{1,3},{2,0},{3,1},{4,6},{5,7},{6,4},{7,5},{8,10},{9,11},{10,... | collective-permute-start | bytes 626696 | tf_op jit(solution)/shard_map/ppermute | solution.py:24
  84.4 10.2 %collective-permute-start.21 = (bf16[272,384]{1,0:T(8,128)(2,1)S(1)}, bf16[272,384]{1,0:T(8,128)(2,1)S(1)}, u32[]{:S(2)}, u32[]{:S(2)}) collective-permute-start(bf16[272,384]{1,0:T(8,128)(2,1)S(1)} %collective-permute-done.16.refs_4_.refs_5_), channel_id=1, source_target_pairs={{0,1},{1,0},{2,3},{3,2},{4,5},{5,4},{6,7},{7,6},{8,9},{9,8},{10,11... | collective-permute-start | bytes 626696 | tf_op jit(solution)/shard_map/ppermute | solution.py:24
  84.5 14.8 %collective-permute-start.19 = (bf16[512,384]{1,0:T(8,128)(2,1)S(1)}, bf16[512,384]{1,0:T(8,128)(2,1)S(1)}, u32[]{:S(2)}, u32[]{:S(2)}) collective-permute-start(bf16[512,384]{1,0:T(8,128)(2,1)S(1)} %pad_maximum_fusion), channel_id=1, source_target_pairs={{0,2},{1,3},{2,0},{3,1},{4,6},{5,7},{6,4},{7,5},{8,10},{9,11},{10,... | collective-permute-start | bytes 1179656 | tf_op jit(solution)/shard_map/ppermute | solution.py:24
  89.7 10.0 %collective-permute-start.25 = (bf16[512,384]{1,0:T(8,128)(2,1)S(1)}, bf16[512,384]{1,0:T(8,128)(2,1)S(1)}, u32[]{:S(2)}, u32[]{:S(2)}) collective-permute-start(bf16[512,384]{1,0:T(8,128)(2,1)S(1)} %pad_maximum_fusion), channel_id=1, source_target_pairs={{0,1},{1,0},{2,3},{3,2},{4,5},{5,4},{6,7},{7,6},{8,9},{9,8},{10,11... | collective-permute-start | bytes 1179656 | tf_op jit(solution)/shard_map/ppermute | solution.py:24
  94.6 1.6 %collective-permute-start.22 = (bf16[272,384]{1,0:T(8,128)(2,1)S(1)}, bf16[272,384]{1,0:T(8,128)(2,1)S(1)}, u32[]{:S(2)}, u32[]{:S(2)}) collective-permute-start(bf16[272,384]{1,0:T(8,128)(2,1)S(1)} %collective-permute-done.20.refs_7_), channel_id=1, source_target_pairs={{0,1},{1,0},{2,3},{3,2},{4,5},{5,4},{6,7},{7,6},{8,9},{9,8},{10,11... | collective-permute-start | bytes 626696 | tf_op jit(solution)/shard_map/ppermute | solution.py:24
  99.3 1.8 %collective-permute-start.26 = (bf16[512,384]{1,0:T(8,128)(2,1)S(1)}, bf16[512,384]{1,0:T(8,128)(2,1)S(1)}, u32[]{:S(2)}, u32[]{:S(2)}) collective-permute-start(bf16[512,384]{1,0:T(8,128)(2,1)S(1)} %collective-permute-done.19), channel_id=1, source_target_pairs={{0,1},{1,0},{2,3},{3,2},{4,5},{5,4},{6,7},{7,6},{8,9},{9,8},{10,11... | collective-permute-start | bytes 1179656 | tf_op jit(solution)/shard_map/ppermute | solution.py:24
  (6 other events, 4.7 us)

commit v12 on v11

--- a/solution.py
+++ b/solution.py
@@ -629,6 +629,7 @@
     parts, sent, own = mend(exons, [plain, near, far, beyond], gained, size)
     *sent, up2, down2 = after([*sent, up2, down2])
     got = [swap(block, "seq", d) for d, block in zip(range(1, nseq), sent)]
+    up2, down2 = after([up2, down2], got[:1])
     up3, down3 = shift(up2, "seq", 1, 2), shift(down2, "seq", -1, 2)
 
     def origins():
@@ -651,10 +652,10 @@
     across_first = swap(first, "ch", 2)
     crossing = jnp.concatenate([block[:quarter] for block in rest])
     across = swap(crossing, "ch", 2)
-    beside = swap(crossing, "ch", 1)
     beside_first = swap(first, "ch", 1)
     in_grad = pieces_gradient(parts, laid, taps, [first, rest[1], center])
-    across_first, in_grad = after([across_first, in_grad])
+    across_first, in_grad, crossing = after([across_first, in_grad, crossing])
+    beside = swap(crossing, "ch", 1)
     beyond_first = swap(across_first, "ch", 1)
 
     def layout(hops, blocks):

time: 110 us -> 107 us (0.973)
  waiting for transfers between devices: 39.2 us -> 37.5 us
    ppermute x21, waiting for transfers between devices: 24.1 us -> 22.2 us  [swap(): return lax.ppermute(block, axis, [(i, i ^ flip) for i in range(count)])]
  transfers between devices with their start and end apart: 27 -> 27, of which waited for: 11 -> 12; matrix products, arithmetic and copies ran while one was open for 1% -> 1% of each run, Pallas kernels for 16% -> 17%
where the time goes in v12:
time: 107 us
  waiting for transfers between devices  37.5 us (35%)
  starting transfers between devices  32.9 us (31%)
  Pallas kernels  28.1 us (26%)
  local copies, waits for them, and re-layouts  5.99 us (6%)
  other arithmetic  1.12 us (1%)
  between operations  1.12 us (1%)
    ppermute x21, starting transfers between devices, swap(): return lax.ppermute(block, axis, [(i, i ^ flip) for i in range(count)])  24.5 us
    ppermute x21, waiting for transfers between devices, swap(): return lax.ppermute(block, axis, [(i, i ^ flip) for i in range(count)])  22.2 us
    ppermute x6, waiting for transfers between devices, shift(): return lax.ppermute(block, axis, pairs)  15.3 us
    pallas_call x3, Pallas kernels, weight_gradient(): pl.pallas_call(functools.partial(weight_kernel, taps=taps, tile=min(1024,...  13.7 us
    pallas_call x2, Pallas kernels, pieces_gradient(): pl.pallas_call(functools.partial(pieces_kernel, taps=taps, pieces=len(par...  8.5 us
    ppermute x6, starting transfers between devices, shift(): return lax.ppermute(block, axis, pairs)  8.43 us
    unnamed x22, local copies, waits for them, and re-layouts  5.8 us
  transfers between devices with their start and end apart: 27, of which 12 were waited for; matrix products, arithmetic and copies ran while one was open for 1% of the time, Pallas kernels for 17%

profile of v12, /device:TPU:0, one launch (start us, length us, event | category | flops | bytes accessed | tf_op | source)
XLA Modules:
  0.0 106.7 jit_solution(16784101536387064418)
XLA Ops:
  4.3 3.3 %collective-permute-start = (bf16[64,384]{1,0:T(8,128)(2,1)S(1)}, bf16[64,384]{1,0:T(8,128)(2,1)S(1)}, u32[]{:S(2)}, u32[]{:S(2)}) collective-permute-start(bf16[64,384]{1,0:T(8,128)(2,1)S(1)} %get-tuple-element.54), channel_id=1, source_target_pairs={{0,4},{4,0},{8,12},{12,8},{1,5},{5,1},{9,13},{13,9},{2,6},{6,2},{1... | collective-permute-start | bytes 147464 | tf_op jit(solution)/shard_map/ppermute | solution.py:24
  7.7 2.3 %collective-permute-start.1 = (bf16[64,384]{1,0:T(8,128)(2,1)S(1)}, bf16[64,384]{1,0:T(8,128)(2,1)S(1)}, u32[]{:S(2)}, u32[]{:S(2)}) collective-permute-start(bf16[64,384]{1,0:T(8,128)(2,1)S(1)} %get-tuple-element.55), channel_id=1, source_target_pairs={{0,8},{4,12},{8,0},{12,4},{1,9},{5,13},{9,1},{13,5},{2,10},{6,14},... | collective-permute-start | bytes 147464 | tf_op jit(solution)/shard_map/ppermute | solution.py:24
  10.1 3.0 %collective-permute-start.7 = (bf16[1024,384]{1,0:T(8,128)(2,1)}, bf16[1024,384]{1,0:T(8,128)(2,1)S(1)}, u32[]{:S(2)}, u32[]{:S(2)}) collective-permute-start(bf16[1024,384]{1,0:T(8,128)(2,1)} %refs_0_.3), channel_id=1, source_target_pairs={{0,4},{4,8},{8,12},{1,5},{5,9},{9,13},{2,6},{6,10},{10,14},{3,7},{... | collective-permute-start | bytes 2359304 | tf_op jit(solution)/shard_map/ppermute | solution.py:33
  13.1 1.3 %collective-permute-start.8 = (bf16[1024,384]{1,0:T(8,128)(2,1)}, bf16[1024,384]{1,0:T(8,128)(2,1)S(1)}, u32[]{:S(2)}, u32[]{:S(2)}) collective-permute-start(bf16[1024,384]{1,0:T(8,128)(2,1)} %refs_0_.3), channel_id=1, source_target_pairs={{4,0},{8,4},{12,8},{5,1},{9,5},{13,9},{6,2},{10,6},{14,10},{7,3},{... | collective-permute-start | bytes 2359304 | tf_op jit(solution)/shard_map/ppermute | solution.py:33
  15.4 1.4 %shard_map.87 = (f32[1024,384]{1,0:T(8,128)S(1)}, bf16[1024,384]{1,0:T(8,128)(2,1)S(1)}) custom-call(bf16[1024,384]{1,0:T(8,128)(2,1)S(1)} %copy-done.1, bf16[512,384]{1,0:T(8,128)(2,1)S(1)} %copy-done.2), custom_call_target="tpu_custom_call" | custom-call | flops 1000 | bytes 1000 | tf_op jit(solution)/shard_map/pallas_call | solution.py:406
  16.9 1.6 %collective-permute-start.4 = (bf16[1024,384]{1,0:T(8,128)(2,1)S(1)}, bf16[1024,384]{1,0:T(8,128)(2,1)S(1)}, u32[]{:S(2)}, u32[]{:S(2)}) collective-permute-start(bf16[1024,384]{1,0:T(8,128)(2,1)S(1)} %get-tuple-element.59.refs_0_), channel_id=1, source_target_pairs={{0,2},{1,3},{2,0},{3,1},{4,6},{5,7},{6,4},{7,5},{8,10},{9,11},{10,... | collective-permute-start | bytes 2359304 | tf_op jit(solution)/shard_map/ppermute | solution.py:24
  19.5 2.7 %collective-permute-start.5 = (bf16[64,384]{1,0:T(8,128)(2,1)S(1)}, bf16[64,384]{1,0:T(8,128)(2,1)S(1)}, u32[]{:S(2)}, u32[]{:S(2)}) collective-permute-start(bf16[64,384]{1,0:T(8,128)(2,1)S(1)} %fusion.1.refs_0_), channel_id=1, source_target_pairs={{0,4},{4,0},{8,12},{12,8},{1,5},{5,1},{9,13},{13,9},{2,6},{6,2},{1... | collective-permute-start | bytes 147464 | tf_op jit(solution)/shard_map/ppermute | solution.py:24
  22.2 3.2 %collective-permute-start.6 = (bf16[64,384]{1,0:T(8,128)(2,1)S(1)}, bf16[64,384]{1,0:T(8,128)(2,1)S(1)}, u32[]{:S(2)}, u32[]{:S(2)}) collective-permute-start(bf16[64,384]{1,0:T(8,128)(2,1)S(1)} %fusion.1.refs_0_), channel_id=1, source_target_pairs={{0,8},{4,12},{8,0},{12,4},{1,9},{5,13},{9,1},{13,5},{2,10},{6,14},... | collective-permute-start | bytes 147464 | tf_op jit(solution)/shard_map/ppermute | solution.py:24
  25.5 4.9 %collective-permute-done.7.refs_1_ = bf16[1024,384]{1,0:T(8,128)(2,1)S(1)} collective-permute-done((bf16[1024,384]{1,0:T(8,128)(2,1)}, bf16[1024,384]{1,0:T(8,128)(2,1)S(1)}, u32[]{:S(2)}, u32[]{:S(2)}) %collective-permute-start.7) | collective-permute-done | bytes 786464 | tf_op jit(solution)/shard_map/ppermute | solution.py:33
  30.4 4.1 %collective-permute-done.8.refs_2_ = bf16[1024,384]{1,0:T(8,128)(2,1)S(1)} collective-permute-done((bf16[1024,384]{1,0:T(8,128)(2,1)}, bf16[1024,384]{1,0:T(8,128)(2,1)S(1)}, u32[]{:S(2)}, u32[]{:S(2)}) %collective-permute-start.8) | collective-permute-done | bytes 786464 | tf_op jit(solution)/shard_map/ppermute | solution.py:33
  34.4 2.8 %collective-permute-start.9 = (bf16[64,384]{1,0:T(8,128)(2,1)S(1)}, bf16[64,384]{1,0:T(8,128)(2,1)S(1)}, u32[]{:S(2)}, u32[]{:S(2)}) collective-permute-start(bf16[64,384]{1,0:T(8,128)(2,1)S(1)} %fusion.1.refs_0_), channel_id=1, source_target_pairs={{0,12},{4,8},{8,4},{12,0},{1,13},{5,9},{9,5},{13,1},{2,14},{6,10},... | collective-permute-start | bytes 147464 | tf_op jit(solution)/shard_map/ppermute | solution.py:24
  38.0 1.3 %collective-permute-start.15 = (bf16[1024,384]{1,0:T(8,128)(2,1)S(1)}, bf16[1024,384]{1,0:T(8,128)(2,1)S(1)}, u32[]{:S(2)}, u32[]{:S(2)}) collective-permute-start(bf16[1024,384]{1,0:T(8,128)(2,1)S(1)} %collective-permute-done.8.refs_2_), channel_id=1, source_target_pairs={{4,0},{8,4},{5,1},{9,5},{6,2},{10,6},{7,3},{11,7},{20,16},{24,20},... | collective-permute-start | bytes 2359304 | tf_op jit(solution)/shard_map/ppermute | solution.py:33
  42.7 1.9 %shard_map.88.refs_4_ = bf16[288,384]{1,0:T(8,128)(2,1)S(1)} custom-call(s32[16]{0:T(128)S(1)} %copy-done.8, s32[2,16]{1,0:T(2,128)S(1)} %bitcast.13, bf16[512,384]{1,0:T(8,128)(2,1)S(1)} %copy-done.3, f32[1024,384]{1,0:T(8,128)S(1)} %get-tuple-element.60.slope, bf16[64,384]{1,0:T(8,128)(2,1)S(1)} %fusion.1.refs_0_, ...), custom_call_target="tpu_custom_call" | custom-call | flops 4000000000 | bytes 1000 | tf_op jit(solution)/shard_map/pallas_call | solution.py:453
  44.6 1.6 %collective-permute-start.11 = (bf16[288,384]{1,0:T(8,128)(2,1)S(1)}, bf16[288,384]{1,0:T(8,128)(2,1)S(1)}, u32[]{:S(2)}, u32[]{:S(2)}) collective-permute-start(bf16[288,384]{1,0:T(8,128)(2,1)S(1)} %shard_map.88.refs_4_), channel_id=1, source_target_pairs={{0,2},{1,3},{2,0},{3,1},{4,6},{5,7},{6,4},{7,5},{8,10},{9,11},{10,... | collective-permute-start | bytes 663560 | tf_op jit(solution)/shard_map/ppermute | solution.py:24
  46.1 5.3 %collective-permute-done.11.refs_6_ = bf16[288,384]{1,0:T(8,128)(2,1)S(1)} collective-permute-done((bf16[288,384]{1,0:T(8,128)(2,1)S(1)}, bf16[288,384]{1,0:T(8,128)(2,1)S(1)}, u32[]{:S(2)}, u32[]{:S(2)}) %collective-permute-start.11) | collective-permute-done | bytes 221216 | tf_op jit(solution)/shard_map/ppermute | solution.py:24
  51.5 1.5 %collective-permute-done.10.refs_5_ = bf16[288,384]{1,0:T(8,128)(2,1)S(1)} collective-permute-done((bf16[288,384]{1,0:T(8,128)(2,1)S(1)}, bf16[288,384]{1,0:T(8,128)(2,1)S(1)}, u32[]{:S(2)}, u32[]{:S(2)}) %collective-permute-start.10) | collective-permute-done | bytes 221216 | tf_op jit(solution)/shard_map/ppermute | solution.py:24
  53.1 1.3 %collective-permute-done.12.refs_7_ = bf16[288,384]{1,0:T(8,128)(2,1)S(1)} collective-permute-done((bf16[288,384]{1,0:T(8,128)(2,1)S(1)}, bf16[288,384]{1,0:T(8,128)(2,1)S(1)}, u32[]{:S(2)}, u32[]{:S(2)}) %collective-permute-start.12) | collective-permute-done | bytes 221216 | tf_op jit(solution)/shard_map/ppermute | solution.py:24
  54.4 6.3 %collective-permute-done.15.refs_4_ = bf16[1024,384]{1,0:T(8,128)(2,1)S(1)} collective-permute-done((bf16[1024,384]{1,0:T(8,128)(2,1)S(1)}, bf16[1024,384]{1,0:T(8,128)(2,1)S(1)}, u32[]{:S(2)}, u32[]{:S(2)}) %collective-permute-start.15) | collective-permute-done | bytes 786464 | tf_op jit(solution)/shard_map/ppermute | solution.py:33
  60.7 1.4 %shard_map.89 = (bf16[1024,384]{1,0:T(8,128)(2,1)S(1)}, bf16[1024,384]{1,0:T(8,128)(2,1)S(1)}, bf16[1024,384]{1,0:T(8,128)(2,1)S(1)}, bf16[1024,384]{1,0:T(8,128...) custom-call(s32[2,16]{1,0:T(2,128)S(1)} %bitcast.14, ...), custom_call_target="tpu_custom_call", output_to_operand_aliasing={{0}: (1, {}), {1}: (2, {}), {2}: (3, {}), {3}: (4, {})} | custom-call | flops 1000 | bytes 1000 | tf_op jit(solution)/shard_map/pallas_call | solution.py:529
  62.1 1.9 %collective-permute-start.16 = (bf16[272,384]{1,0:T(8,128)(2,1)S(1)}, bf16[272,384]{1,0:T(8,128)(2,1)S(1)}, u32[]{:S(2)}, u32[]{:S(2)}) collective-permute-start(bf16[272,384]{1,0:T(8,128)(2,1)S(1)} %get-tuple-element.77), channel_id=1, source_target_pairs={{0,4},{4,0},{8,12},{12,8},{1,5},{5,1},{9,13},{13,9},{2,6},{6,2},{1... | collective-permute-start | bytes 626696 | tf_op jit(solution)/shard_map/ppermute | solution.py:24
  65.7 7.0 %collective-permute-done.16.refs_4_.refs_5_ = bf16[272,384]{1,0:T(8,128)(2,1)S(1)} collective-permute-done((bf16[272,384]{1,0:T(8,128)(2,1)S(1)}, bf16[272,384]{1,0:T(8,128)(2,1)S(1)}, u32[]{:S(2)}, u32[]{:S(2)}) %collective-permute-start.16) | collective-permute-done | bytes 208928 | tf_op jit(solution)/shard_map/ppermute | solution.py:24
  73.3 1.5 %collective-permute-start.24 = (bf16[1024,384]{1,0:T(8,128)(2,1)S(1)}, bf16[1024,384]{1,0:T(8,128)(2,1)S(1)}, u32[]{:S(2)}, u32[]{:S(2)}) collective-permute-start(bf16[1024,384]{1,0:T(8,128)(2,1)S(1)} %collective-permute-done.15.refs_4_), channel_id=1, source_target_pairs={{4,0},{5,1},{6,2},{7,3},{20,16},{21,17},{22,18},{23,19}} | collective-permute-start | bytes 2359304 | tf_op jit(solution)/shard_map/ppermute | solution.py:33
  74.9 2.8 %shard_map.90 = (f32[384,1920]{1,0:T(8,128)S(1)}, bf16[1536,1920]{1,0:T(8,128)(2,1)S(1)}) custom-call(bf16[16,384]{1,0:T(8,128)(2,1)S(1)} %slice.44.refs_0_, bf16[1024,384]{1,0:T(8,128)(2,1)S(1)} %copy-done, bf16[16,384]{1,0:T(8,128)(2,1)S(1)} %slice.45.refs_2_, bf16[1024,384]{1,0:T(8,128)(2,1)S(1)} %get-tuple-element.80.refs_3_, ...), custom_call_target="tpu_custom_call" | custom-call | flops 1000 | bytes 1000 | tf_op jit(solution)/shard_map/pallas_call | solution.py:276
  77.7 3.7 %shard_map.91.refs_6_ = bf16[512,384]{1,0:T(8,128)(2,1)S(1)} custom-call(bf16[1024,384]{1,0:T(8,128)(2,1)S(1)} %get-tuple-element.82.refs_0_, bf16[1024,384]{1,0:T(8,128)(2,1)S(1)} %get-tuple-element.83.refs_1_, bf16[1024,384]{1,0:T(8,128)(2,1)S(1)} %get-tuple-element.84.refs_2_, bf16[1024,384]{1,0:T(8,128)(2,1)S(1)} %get-tuple-element.85.refs_3_, ...), custom_call_target="tpu_custom_call" | custom-call | flops 1000 | bytes 1000 | tf_op jit(solution)/shard_map/pallas_call | solution.py:133
  81.4 1.4 %collective-permute-done.17 = bf16[256,384]{1,0:T(8,128)(2,1)S(1)} collective-permute-done((bf16[256,384]{1,0:T(8,128)(2,1)S(1)}, bf16[256,384]{1,0:T(8,128)(2,1)S(1)}, u32[]{:S(2)}, u32[]{:S(2)}) %collective-permute-start.17) | collective-permute-done | bytes 196640 | tf_op jit(solution)/shard_map/ppermute | solution.py:24
  82.8 1.5 %collective-permute-start.20 = (bf16[272,384]{1,0:T(8,128)(2,1)S(1)}, bf16[272,384]{1,0:T(8,128)(2,1)S(1)}, u32[]{:S(2)}, u32[]{:S(2)}) collective-permute-start(bf16[272,384]{1,0:T(8,128)(2,1)S(1)} %collective-permute-done.16.refs_4_.refs_5_), channel_id=1, source_target_pairs={{0,2},{1,3},{2,0},{3,1},{4,6},{5,7},{6,4},{7,5},{8,10},{9,11},{10,... | collective-permute-start | bytes 626696 | tf_op jit(solution)/shard_map/ppermute | solution.py:24
  85.0 4.8 %shard_map.92 = bf16[1024,384]{1,0:T(8,128)(2,1)} custom-call(bf16[1024,384]{1,0:T(8,128)(2,1)S(1)} %get-tuple-element.82.refs_0_, bf16[1024,384]{1,0:T(8,128)(2,1)S(1)} %get-tuple-element.83.refs_1_, bf16[1024,384]{1,0:T(8,128)(2,1)S(1)} %get-tuple-element.84.refs_2_, bf16[1024,384]{1,0:T(8,128)(2,1)S(1)} %get-tuple-element.85.refs_3_, ...), custom_call_target="tpu_custom_call" | custom-call | flops 1000 | bytes 1000 | tf_op jit(solution)/shard_map/pallas_call | solution.py:133
  90.4 1.5 %collective-permute-done.22.refs_8_ = bf16[272,384]{1,0:T(8,128)(2,1)S(1)} collective-permute-done((bf16[272,384]{1,0:T(8,128)(2,1)S(1)}, bf16[272,384]{1,0:T(8,128)(2,1)S(1)}, u32[]{:S(2)}, u32[]{:S(2)}) %collective-permute-start.22) | collective-permute-done | bytes 208928 | tf_op jit(solution)/shard_map/ppermute | solution.py:24
  91.8 3.1 %shard_map.93.refs_15_ = f32[384,1920]{1,0:T(8,128)S(1)} custom-call(bf16[1024,384]{1,0:T(8,128)(2,1)S(1)} %copy-done, bf16[1024,384]{1,0:T(8,128)(2,1)S(1)} %collective-permute-done.7.refs_1_, bf16[1024,384]{1,0:T(8,128)(2,1)S(1)} %collective-permute-done.8.refs_2_, bf16[1024,384]{1,0:T(8,128)(2,1)S(1)} %collective-permute-done.14.refs_3_, ...), custom_call_target="tpu_custom_call" | custom-call | flops 1000 | bytes 1000 | tf_op jit(solution)/shard_map/pallas_call | solution.py:276
  95.0 2.1 %collective-permute-done.19 = bf16[512,384]{1,0:T(8,128)(2,1)S(1)} collective-permute-done((bf16[512,384]{1,0:T(8,128)(2,1)S(1)}, bf16[512,384]{1,0:T(8,128)(2,1)S(1)}, u32[]{:S(2)}, u32[]{:S(2)}) %collective-permute-start.19) | collective-permute-done | bytes 393248 | tf_op jit(solution)/shard_map/ppermute | solution.py:24
  97.2 1.6 %collective-permute-done.26 = bf16[512,384]{1,0:T(8,128)(2,1)S(1)} collective-permute-done((bf16[512,384]{1,0:T(8,128)(2,1)S(1)}, bf16[512,384]{1,0:T(8,128)(2,1)S(1)}, u32[]{:S(2)}, u32[]{:S(2)}) %collective-permute-start.26) | collective-permute-done | bytes 393248 | tf_op jit(solution)/shard_map/ppermute | solution.py:24
  98.8 7.7 %shard_map.94 = bf16[5,384,384]{2,1,0:T(8,128)(2,1)} custom-call(bf16[1024,384]{1,0:T(8,128)(2,1)S(1)} %copy-done, bf16[1024,384]{1,0:T(8,128)(2,1)S(1)} %collective-permute-done.7.refs_1_, bf16[1024,384]{1,0:T(8,128)(2,1)S(1)} %collective-permute-done.8.refs_2_, bf16[1024,384]{1,0:T(8,128)(2,1)S(1)} %collective-permute-done.14.refs_3_, ...), custom_call_target="tpu_custom_call" | custom-call | flops 1000 | bytes 1000 | tf_op jit(solution)/shard_map/pallas_call | solution.py:276
  (63 shorter events, 14.0 us)
Async XLA Ops:
  0.6 1.1 %copy-start.1 = (bf16[1024,384]{1,0:T(8,128)(2,1)S(1)}, bf16[1024,384]{1,0:T(8,128)(2,1)}, u32[]{:S(2)}) copy-start(bf16[1024,384]{1,0:T(8,128)(2,1)} %pre_act.3) | copy-start | bytes 2359300
  4.3 12.5 %collective-permute-start = (bf16[64,384]{1,0:T(8,128)(2,1)S(1)}, bf16[64,384]{1,0:T(8,128)(2,1)S(1)}, u32[]{:S(2)}, u32[]{:S(2)}) collective-permute-start(bf16[64,384]{1,0:T(8,128)(2,1)S(1)} %get-tuple-element.54), channel_id=1, source_target_pairs={{0,4},{4,0},{8,12},{12,8},{1,5},{5,1},{9,13},{13,9},{2,6},{6,2},{1... | collective-permute-start | bytes 147464 | tf_op jit(solution)/shard_map/ppermute | solution.py:24
  7.7 9.2 %collective-permute-start.1 = (bf16[64,384]{1,0:T(8,128)(2,1)S(1)}, bf16[64,384]{1,0:T(8,128)(2,1)S(1)}, u32[]{:S(2)}, u32[]{:S(2)}) collective-permute-start(bf16[64,384]{1,0:T(8,128)(2,1)S(1)} %get-tuple-element.55), channel_id=1, source_target_pairs={{0,8},{4,12},{8,0},{12,4},{1,9},{5,13},{9,1},{13,5},{2,10},{6,14},... | collective-permute-start | bytes 147464 | tf_op jit(solution)/shard_map/ppermute | solution.py:24
  10.0 6.9 %collective-permute-start.2 = (bf16[64,384]{1,0:T(8,128)(2,1)S(1)}, bf16[64,384]{1,0:T(8,128)(2,1)S(1)}, u32[]{:S(2)}, u32[]{:S(2)}) collective-permute-start(bf16[64,384]{1,0:T(8,128)(2,1)S(1)} %get-tuple-element.56), channel_id=1, source_target_pairs={{0,12},{4,8},{8,4},{12,0},{1,13},{5,9},{9,5},{13,1},{2,14},{6,10},... | collective-permute-start | bytes 147464 | tf_op jit(solution)/shard_map/ppermute | solution.py:24
  10.1 20.2 %collective-permute-start.7 = (bf16[1024,384]{1,0:T(8,128)(2,1)}, bf16[1024,384]{1,0:T(8,128)(2,1)S(1)}, u32[]{:S(2)}, u32[]{:S(2)}) collective-permute-start(bf16[1024,384]{1,0:T(8,128)(2,1)} %refs_0_.3), channel_id=1, source_target_pairs={{0,4},{4,8},{8,12},{1,5},{5,9},{9,13},{2,6},{6,10},{10,14},{3,7},{... | collective-permute-start | bytes 2359304 | tf_op jit(solution)/shard_map/ppermute | solution.py:33
  13.1 21.3 %collective-permute-start.8 = (bf16[1024,384]{1,0:T(8,128)(2,1)}, bf16[1024,384]{1,0:T(8,128)(2,1)S(1)}, u32[]{:S(2)}, u32[]{:S(2)}) collective-permute-start(bf16[1024,384]{1,0:T(8,128)(2,1)} %refs_0_.3), channel_id=1, source_target_pairs={{4,0},{8,4},{12,8},{5,1},{9,5},{13,9},{6,2},{10,6},{14,10},{7,3},{... | collective-permute-start | bytes 2359304 | tf_op jit(solution)/shard_map/ppermute | solution.py:33
  16.9 43.9 %copy-start.6 = (s32[16,2]{0,1:T(2,128)S(1)}, s32[16,2]{0,1:T(2,128)}, u32[]{:S(2)}) copy-start(s32[16,2]{0,1:T(2,128)} %param.13) | copy-start | bytes 388
  16.9 22.4 %collective-permute-start.4 = (bf16[1024,384]{1,0:T(8,128)(2,1)S(1)}, bf16[1024,384]{1,0:T(8,128)(2,1)S(1)}, u32[]{:S(2)}, u32[]{:S(2)}) collective-permute-start(bf16[1024,384]{1,0:T(8,128)(2,1)S(1)} %get-tuple-element.59.refs_0_), channel_id=1, source_target_pairs={{0,2},{1,3},{2,0},{3,1},{4,6},{5,7},{6,4},{7,5},{8,10},{9,11},{10,... | collective-permute-start | bytes 2359304 | tf_op jit(solution)/shard_map/ppermute | solution.py:24
  18.4 56.4 %slice-start = ((s8[5898240]{0:T(1024)(128)(4,1)}), s8[4194304]{0:T(1024)(128)(4,1)S(1)}, s32[]{:S(2)}) async-start(s8[5898240]{0:T(1024)(128)(4,1)} %bitcast.9), calls=%async_computation | async-start | bytes 8388608
  19.5 55.3 %slice-start.1 = ((s8[5898240]{0:T(1024)(128)(4,1)}), s8[1703936]{0:T(1024)(128)(4,1)S(1)}, s32[]{:S(2)}) async-start(s8[5898240]{0:T(1024)(128)(4,1)} %bitcast.9), calls=%async_computation.1 | async-start | bytes 3407872
  19.5 17.7 %collective-permute-start.5 = (bf16[64,384]{1,0:T(8,128)(2,1)S(1)}, bf16[64,384]{1,0:T(8,128)(2,1)S(1)}, u32[]{:S(2)}, u32[]{:S(2)}) collective-permute-start(bf16[64,384]{1,0:T(8,128)(2,1)S(1)} %fusion.1.refs_0_), channel_id=1, source_target_pairs={{0,4},{4,0},{8,12},{12,8},{1,5},{5,1},{9,13},{13,9},{2,6},{6,2},{1... | collective-permute-start | bytes 147464 | tf_op jit(solution)/shard_map/ppermute | solution.py:24
  22.2 15.7 %collective-permute-start.6 = (bf16[64,384]{1,0:T(8,128)(2,1)S(1)}, bf16[64,384]{1,0:T(8,128)(2,1)S(1)}, u32[]{:S(2)}, u32[]{:S(2)}) collective-permute-start(bf16[64,384]{1,0:T(8,128)(2,1)S(1)} %fusion.1.refs_0_), channel_id=1, source_target_pairs={{0,8},{4,12},{8,0},{12,4},{1,9},{5,13},{9,1},{13,5},{2,10},{6,14},... | collective-permute-start | bytes 147464 | tf_op jit(solution)/shard_map/ppermute | solution.py:24
  34.4 5.9 %collective-permute-start.9 = (bf16[64,384]{1,0:T(8,128)(2,1)S(1)}, bf16[64,384]{1,0:T(8,128)(2,1)S(1)}, u32[]{:S(2)}, u32[]{:S(2)}) collective-permute-start(bf16[64,384]{1,0:T(8,128)(2,1)S(1)} %fusion.1.refs_0_), channel_id=1, source_target_pairs={{0,12},{4,8},{8,4},{12,0},{1,13},{5,9},{9,5},{13,1},{2,14},{6,10},... | collective-permute-start | bytes 147464 | tf_op jit(solution)/shard_map/ppermute | solution.py:24
  37.2 23.5 %collective-permute-start.3 = (bf16[1024,384]{1,0:T(8,128)(2,1)S(1)}, bf16[1024,384]{1,0:T(8,128)(2,1)S(1)}, u32[]{:S(2)}, u32[]{:S(2)}) collective-permute-start(bf16[1024,384]{1,0:T(8,128)(2,1)S(1)} %get-tuple-element.59.refs_0_), channel_id=1, source_target_pairs={{0,1},{1,0},{2,3},{3,2},{4,5},{5,4},{6,7},{7,6},{8,9},{9,8},{10,11... | collective-permute-start | bytes 2359304 | tf_op jit(solution)/shard_map/ppermute | solution.py:24
  37.2 17.2 %collective-permute-start.14 = (bf16[1024,384]{1,0:T(8,128)(2,1)S(1)}, bf16[1024,384]{1,0:T(8,128)(2,1)S(1)}, u32[]{:S(2)}, u32[]{:S(2)}) collective-permute-start(bf16[1024,384]{1,0:T(8,128)(2,1)S(1)} %collective-permute-done.7.refs_1_), channel_id=1, source_target_pairs={{4,8},{8,12},{5,9},{9,13},{6,10},{10,14},{7,11},{11,15},{20,24},{2... | collective-permute-start | bytes 2359304 | tf_op jit(solution)/shard_map/ppermute | solution.py:33
  38.0 22.8 %collective-permute-start.15 = (bf16[1024,384]{1,0:T(8,128)(2,1)S(1)}, bf16[1024,384]{1,0:T(8,128)(2,1)S(1)}, u32[]{:S(2)}, u32[]{:S(2)}) collective-permute-start(bf16[1024,384]{1,0:T(8,128)(2,1)S(1)} %collective-permute-done.8.refs_2_), channel_id=1, source_target_pairs={{4,0},{8,4},{5,1},{9,5},{6,2},{10,6},{7,3},{11,7},{20,16},{24,20},... | collective-permute-start | bytes 2359304 | tf_op jit(solution)/shard_map/ppermute | solution.py:33
  39.3 21.5 %collective-permute-start.13 = (bf16[1024,384]{1,0:T(8,128)(2,1)S(1)}, bf16[1024,384]{1,0:T(8,128)(2,1)S(1)}, u32[]{:S(2)}, u32[]{:S(2)}) collective-permute-start(bf16[1024,384]{1,0:T(8,128)(2,1)S(1)} %collective-permute-done.4.refs_2_), channel_id=1, source_target_pairs={{0,1},{1,0},{2,3},{3,2},{4,5},{5,4},{6,7},{7,6},{8,9},{9,8},{10,11... | collective-permute-start | bytes 2359304 | tf_op jit(solution)/shard_map/ppermute | solution.py:24
  44.6 30.3 %copy-start = (bf16[1024,384]{1,0:T(8,128)(2,1)S(1)}, bf16[1024,384]{1,0:T(8,128)(2,1)}, u32[]{:S(2)}) copy-start(bf16[1024,384]{1,0:T(8,128)(2,1)} %refs_0_.3) | copy-start | bytes 2359300
  44.6 6.9 %collective-permute-start.11 = (bf16[288,384]{1,0:T(8,128)(2,1)S(1)}, bf16[288,384]{1,0:T(8,128)(2,1)S(1)}, u32[]{:S(2)}, u32[]{:S(2)}) collective-permute-start(bf16[288,384]{1,0:T(8,128)(2,1)S(1)} %shard_map.88.refs_4_), channel_id=1, source_target_pairs={{0,2},{1,3},{2,0},{3,1},{4,6},{5,7},{6,4},{7,5},{8,10},{9,11},{10,... | collective-permute-start | bytes 663560 | tf_op jit(solution)/shard_map/ppermute | solution.py:24
  51.5 1.5 %collective-permute-start.10 = (bf16[288,384]{1,0:T(8,128)(2,1)S(1)}, bf16[288,384]{1,0:T(8,128)(2,1)S(1)}, u32[]{:S(2)}, u32[]{:S(2)}) collective-permute-start(bf16[288,384]{1,0:T(8,128)(2,1)S(1)} %shard_map.88.refs_4_), channel_id=1, source_target_pairs={{0,1},{1,0},{2,3},{3,2},{4,5},{5,4},{6,7},{7,6},{8,9},{9,8},{10,11... | collective-permute-start | bytes 663560 | tf_op jit(solution)/shard_map/ppermute | solution.py:24
  52.9 1.5 %collective-permute-start.12 = (bf16[288,384]{1,0:T(8,128)(2,1)S(1)}, bf16[288,384]{1,0:T(8,128)(2,1)S(1)}, u32[]{:S(2)}, u32[]{:S(2)}) collective-permute-start(bf16[288,384]{1,0:T(8,128)(2,1)S(1)} %collective-permute-done.11.refs_6_), channel_id=1, source_target_pairs={{0,1},{1,0},{2,3},{3,2},{4,5},{5,4},{6,7},{7,6},{8,9},{9,8},{10,11... | collective-permute-start | bytes 663560 | tf_op jit(solution)/shard_map/ppermute | solution.py:24
  62.1 10.5 %collective-permute-start.16 = (bf16[272,384]{1,0:T(8,128)(2,1)S(1)}, bf16[272,384]{1,0:T(8,128)(2,1)S(1)}, u32[]{:S(2)}, u32[]{:S(2)}) collective-permute-start(bf16[272,384]{1,0:T(8,128)(2,1)S(1)} %get-tuple-element.77), channel_id=1, source_target_pairs={{0,4},{4,0},{8,12},{12,8},{1,5},{5,1},{9,13},{13,9},{2,6},{6,2},{1... | collective-permute-start | bytes 626696 | tf_op jit(solution)/shard_map/ppermute | solution.py:24
  64.0 18.8 %collective-permute-start.18 = (bf16[272,384]{1,0:T(8,128)(2,1)S(1)}, bf16[272,384]{1,0:T(8,128)(2,1)S(1)}, u32[]{:S(2)}, u32[]{:S(2)}) collective-permute-start(bf16[272,384]{1,0:T(8,128)(2,1)S(1)} %get-tuple-element.79), channel_id=1, source_target_pairs={{0,12},{4,8},{8,4},{12,0},{1,13},{5,9},{9,5},{13,1},{2,14},{6,10},... | collective-permute-start | bytes 626696 | tf_op jit(solution)/shard_map/ppermute | solution.py:24
  64.4 18.4 %collective-permute-start.17 = (bf16[256,384]{1,0:T(8,128)(2,1)S(1)}, bf16[256,384]{1,0:T(8,128)(2,1)S(1)}, u32[]{:S(2)}, u32[]{:S(2)}) collective-permute-start(bf16[256,384]{1,0:T(8,128)(2,1)S(1)} %get-tuple-element.78), channel_id=1, source_target_pairs={{0,8},{4,12},{8,0},{12,4},{1,9},{5,13},{9,1},{13,5},{2,10},{6,14},... | collective-permute-start | bytes 589832 | tf_op jit(solution)/shard_map/ppermute | solution.py:24
  72.6 24.4 %collective-permute-start.23 = (bf16[1024,384]{1,0:T(8,128)(2,1)S(1)}, bf16[1024,384]{1,0:T(8,128)(2,1)S(1)}, u32[]{:S(2)}, u32[]{:S(2)}) collective-permute-start(bf16[1024,384]{1,0:T(8,128)(2,1)S(1)} %collective-permute-done.14.refs_3_), channel_id=1, source_target_pairs={{8,12},{9,13},{10,14},{11,15},{24,28},{25,29},{26,30},{27,31}} | collective-permute-start | bytes 2359304 | tf_op jit(solution)/shard_map/ppermute | solution.py:33
  73.3 23.7 %collective-permute-start.24 = (bf16[1024,384]{1,0:T(8,128)(2,1)S(1)}, bf16[1024,384]{1,0:T(8,128)(2,1)S(1)}, u32[]{:S(2)}, u32[]{:S(2)}) collective-permute-start(bf16[1024,384]{1,0:T(8,128)(2,1)S(1)} %collective-permute-done.15.refs_4_), channel_id=1, source_target_pairs={{4,0},{5,1},{6,2},{7,3},{20,16},{21,17},{22,18},{23,19}} | collective-permute-start | bytes 2359304 | tf_op jit(solution)/shard_map/ppermute | solution.py:33
  82.8 7.0 %collective-permute-start.20 = (bf16[272,384]{1,0:T(8,128)(2,1)S(1)}, bf16[272,384]{1,0:T(8,128)(2,1)S(1)}, u32[]{:S(2)}, u32[]{:S(2)}) collective-permute-start(bf16[272,384]{1,0:T(8,128)(2,1)S(1)} %collective-permute-done.16.refs_4_.refs_5_), channel_id=1, source_target_pairs={{0,2},{1,3},{2,0},{3,1},{4,6},{5,7},{6,4},{7,5},{8,10},{9,11},{10,... | collective-permute-start | bytes 626696 | tf_op jit(solution)/shard_map/ppermute | solution.py:24
  84.3 5.7 %collective-permute-start.21 = (bf16[272,384]{1,0:T(8,128)(2,1)S(1)}, bf16[272,384]{1,0:T(8,128)(2,1)S(1)}, u32[]{:S(2)}, u32[]{:S(2)}) collective-permute-start(bf16[272,384]{1,0:T(8,128)(2,1)S(1)} %collective-permute-done.16.refs_4_.refs_5_), channel_id=1, source_target_pairs={{0,1},{1,0},{2,3},{3,2},{4,5},{5,4},{6,7},{7,6},{8,9},{9,8},{10,11... | collective-permute-start | bytes 626696 | tf_op jit(solution)/shard_map/ppermute | solution.py:24
  84.4 12.7 %collective-permute-start.19 = (bf16[512,384]{1,0:T(8,128)(2,1)S(1)}, bf16[512,384]{1,0:T(8,128)(2,1)S(1)}, u32[]{:S(2)}, u32[]{:S(2)}) collective-permute-start(bf16[512,384]{1,0:T(8,128)(2,1)S(1)} %pad_maximum_fusion), channel_id=1, source_target_pairs={{0,2},{1,3},{2,0},{3,1},{4,6},{5,7},{6,4},{7,5},{8,10},{9,11},{10,... | collective-permute-start | bytes 1179656 | tf_op jit(solution)/shard_map/ppermute | solution.py:24
  89.8 7.3 %collective-permute-start.25 = (bf16[512,384]{1,0:T(8,128)(2,1)S(1)}, bf16[512,384]{1,0:T(8,128)(2,1)S(1)}, u32[]{:S(2)}, u32[]{:S(2)}) collective-permute-start(bf16[512,384]{1,0:T(8,128)(2,1)S(1)} %pad_maximum_fusion), channel_id=1, source_target_pairs={{0,1},{1,0},{2,3},{3,2},{4,5},{5,4},{6,7},{7,6},{8,9},{9,8},{10,11... | collective-permute-start | bytes 1179656 | tf_op jit(solution)/shard_map/ppermute | solution.py:24
  90.0 1.8 %collective-permute-start.22 = (bf16[272,384]{1,0:T(8,128)(2,1)S(1)}, bf16[272,384]{1,0:T(8,128)(2,1)S(1)}, u32[]{:S(2)}, u32[]{:S(2)}) collective-permute-start(bf16[272,384]{1,0:T(8,128)(2,1)S(1)} %collective-permute-done.20.refs_7_), channel_id=1, source_target_pairs={{0,1},{1,0},{2,3},{3,2},{4,5},{5,4},{6,7},{7,6},{8,9},{9,8},{10,11... | collective-permute-start | bytes 626696 | tf_op jit(solution)/shard_map/ppermute | solution.py:24
  97.0 1.7 %collective-permute-start.26 = (bf16[512,384]{1,0:T(8,128)(2,1)S(1)}, bf16[512,384]{1,0:T(8,128)(2,1)S(1)}, u32[]{:S(2)}, u32[]{:S(2)}) collective-permute-start(bf16[512,384]{1,0:T(8,128)(2,1)S(1)} %collective-permute-done.19), channel_id=1, source_target_pairs={{0,1},{1,0},{2,3},{3,2},{4,5},{5,4},{6,7},{7,6},{8,9},{9,8},{10,11... | collective-permute-start | bytes 1179656 | tf_op jit(solution)/shard_map/ppermute | solution.py:24
  (6 other events, 4.7 us)

commit v13 on v12

--- a/solution.py
+++ b/solution.py
@@ -701,6 +701,7 @@
         nseq * rows,
         before=partial,
         vmem=32,
+        stages=[0] * 11 + [1] * 4,
     )
     return (in_grad, w_grad.transpose(1, 0, 2))
 

time: 107 us -> 107 us (level)
  no operation moved by 1% of the time
where the time goes in v13:
time: 107 us
  waiting for transfers between devices  37.3 us (35%)
  starting transfers between devices  32.8 us (31%)
  Pallas kernels  28.6 us (27%)
  local copies, waits for them, and re-layouts  5.99 us (6%)
  other arithmetic  1.12 us (1%)
  between operations  1.12 us (1%)
    ppermute x21, starting transfers between devices, swap(): return lax.ppermute(block, axis, [(i, i ^ flip) for i in range(count)])  24.4 us
    ppermute x21, waiting for transfers between devices, swap(): return lax.ppermute(block, axis, [(i, i ^ flip) for i in range(count)])  22.2 us
    ppermute x6, waiting for transfers between devices, shift(): return lax.ppermute(block, axis, pairs)  15.1 us
    pallas_call x3, Pallas kernels, weight_gradient(): pl.pallas_call(functools.partial(weight_kernel, taps=taps, tile=min(1024,...  13.9 us
    pallas_call x2, Pallas kernels, pieces_gradient(): pl.pallas_call(functools.partial(pieces_kernel, taps=taps, pieces=len(par...  8.51 us
    ppermute x6, starting transfers between devices, shift(): return lax.ppermute(block, axis, pairs)  8.45 us
    unnamed x22, local copies, waits for them, and re-layouts  5.8 us
  transfers between devices with their start and end apart: 27, of which 12 were waited for; matrix products, arithmetic and copies ran while one was open for 1% of the time, Pallas kernels for 17%

profile of v13, /device:TPU:0, one launch (start us, length us, event | category | flops | bytes accessed | tf_op | source)
XLA Modules:
  0.0 106.9 jit_solution(14367671878023300001)
XLA Ops:
  3.1 1.4 %shard_map.86 = (bf16[64,384]{1,0:T(8,128)(2,1)S(1)}, bf16[64,384]{1,0:T(8,128)(2,1)S(1)}, bf16[64,384]{1,0:T(8,128)(2,1)S(1)}, bf16[64,384]{1,0:T(8,128)(2,1)S(1)}) custom-call(s32[16]{0:T(128)S(1)} %copy-done.7, s32[2,16]{1,0:T(2,128)S(1)} %bitcast.12, bf16[1024,384]{1,0:T(8,128)(2,1)S(1)} %copy-done.1), custom_call_target="tpu_custom_call" | custom-call | flops 1000 | bytes 1000 | tf_op jit(solution)/shard_map/pallas_call | solution.py:379
  4.5 3.1 %collective-permute-start = (bf16[64,384]{1,0:T(8,128)(2,1)S(1)}, bf16[64,384]{1,0:T(8,128)(2,1)S(1)}, u32[]{:S(2)}, u32[]{:S(2)}) collective-permute-start(bf16[64,384]{1,0:T(8,128)(2,1)S(1)} %get-tuple-element.54), channel_id=1, source_target_pairs={{0,4},{4,0},{8,12},{12,8},{1,5},{5,1},{9,13},{13,9},{2,6},{6,2},{1... | collective-permute-start | bytes 147464 | tf_op jit(solution)/shard_map/ppermute | solution.py:24
  7.7 2.4 %collective-permute-start.1 = (bf16[64,384]{1,0:T(8,128)(2,1)S(1)}, bf16[64,384]{1,0:T(8,128)(2,1)S(1)}, u32[]{:S(2)}, u32[]{:S(2)}) collective-permute-start(bf16[64,384]{1,0:T(8,128)(2,1)S(1)} %get-tuple-element.55), channel_id=1, source_target_pairs={{0,8},{4,12},{8,0},{12,4},{1,9},{5,13},{9,1},{13,5},{2,10},{6,14},... | collective-permute-start | bytes 147464 | tf_op jit(solution)/shard_map/ppermute | solution.py:24
  10.1 3.0 %collective-permute-start.7 = (bf16[1024,384]{1,0:T(8,128)(2,1)}, bf16[1024,384]{1,0:T(8,128)(2,1)S(1)}, u32[]{:S(2)}, u32[]{:S(2)}) collective-permute-start(bf16[1024,384]{1,0:T(8,128)(2,1)} %refs_0_.3), channel_id=1, source_target_pairs={{0,4},{4,8},{8,12},{1,5},{5,9},{9,13},{2,6},{6,10},{10,14},{3,7},{... | collective-permute-start | bytes 2359304 | tf_op jit(solution)/shard_map/ppermute | solution.py:33
  15.4 1.4 %shard_map.87 = (f32[1024,384]{1,0:T(8,128)S(1)}, bf16[1024,384]{1,0:T(8,128)(2,1)S(1)}) custom-call(bf16[1024,384]{1,0:T(8,128)(2,1)S(1)} %copy-done.1, bf16[512,384]{1,0:T(8,128)(2,1)S(1)} %copy-done.2), custom_call_target="tpu_custom_call" | custom-call | flops 1000 | bytes 1000 | tf_op jit(solution)/shard_map/pallas_call | solution.py:406
  16.9 1.6 %collective-permute-start.4 = (bf16[1024,384]{1,0:T(8,128)(2,1)S(1)}, bf16[1024,384]{1,0:T(8,128)(2,1)S(1)}, u32[]{:S(2)}, u32[]{:S(2)}) collective-permute-start(bf16[1024,384]{1,0:T(8,128)(2,1)S(1)} %get-tuple-element.59.refs_0_), channel_id=1, source_target_pairs={{0,2},{1,3},{2,0},{3,1},{4,6},{5,7},{6,4},{7,5},{8,10},{9,11},{10,... | collective-permute-start | bytes 2359304 | tf_op jit(solution)/shard_map/ppermute | solution.py:24
  19.5 2.7 %collective-permute-start.5 = (bf16[64,384]{1,0:T(8,128)(2,1)S(1)}, bf16[64,384]{1,0:T(8,128)(2,1)S(1)}, u32[]{:S(2)}, u32[]{:S(2)}) collective-permute-start(bf16[64,384]{1,0:T(8,128)(2,1)S(1)} %fusion.1.refs_0_), channel_id=1, source_target_pairs={{0,4},{4,0},{8,12},{12,8},{1,5},{5,1},{9,13},{13,9},{2,6},{6,2},{1... | collective-permute-start | bytes 147464 | tf_op jit(solution)/shard_map/ppermute | solution.py:24
  22.2 3.3 %collective-permute-start.6 = (bf16[64,384]{1,0:T(8,128)(2,1)S(1)}, bf16[64,384]{1,0:T(8,128)(2,1)S(1)}, u32[]{:S(2)}, u32[]{:S(2)}) collective-permute-start(bf16[64,384]{1,0:T(8,128)(2,1)S(1)} %fusion.1.refs_0_), channel_id=1, source_target_pairs={{0,8},{4,12},{8,0},{12,4},{1,9},{5,13},{9,1},{13,5},{2,10},{6,14},... | collective-permute-start | bytes 147464 | tf_op jit(solution)/shard_map/ppermute | solution.py:24
  25.5 4.9 %collective-permute-done.7.refs_1_ = bf16[1024,384]{1,0:T(8,128)(2,1)S(1)} collective-permute-done((bf16[1024,384]{1,0:T(8,128)(2,1)}, bf16[1024,384]{1,0:T(8,128)(2,1)S(1)}, u32[]{:S(2)}, u32[]{:S(2)}) %collective-permute-start.7) | collective-permute-done | bytes 786464 | tf_op jit(solution)/shard_map/ppermute | solution.py:33
  30.4 4.1 %collective-permute-done.8.refs_2_ = bf16[1024,384]{1,0:T(8,128)(2,1)S(1)} collective-permute-done((bf16[1024,384]{1,0:T(8,128)(2,1)}, bf16[1024,384]{1,0:T(8,128)(2,1)S(1)}, u32[]{:S(2)}, u32[]{:S(2)}) %collective-permute-start.8) | collective-permute-done | bytes 786464 | tf_op jit(solution)/shard_map/ppermute | solution.py:33
  34.4 2.8 %collective-permute-start.9 = (bf16[64,384]{1,0:T(8,128)(2,1)S(1)}, bf16[64,384]{1,0:T(8,128)(2,1)S(1)}, u32[]{:S(2)}, u32[]{:S(2)}) collective-permute-start(bf16[64,384]{1,0:T(8,128)(2,1)S(1)} %fusion.1.refs_0_), channel_id=1, source_target_pairs={{0,12},{4,8},{8,4},{12,0},{1,13},{5,9},{9,5},{13,1},{2,14},{6,10},... | collective-permute-start | bytes 147464 | tf_op jit(solution)/shard_map/ppermute | solution.py:24
  42.7 2.0 %shard_map.88.refs_4_ = bf16[288,384]{1,0:T(8,128)(2,1)S(1)} custom-call(s32[16]{0:T(128)S(1)} %copy-done.8, s32[2,16]{1,0:T(2,128)S(1)} %bitcast.13, bf16[512,384]{1,0:T(8,128)(2,1)S(1)} %copy-done.3, f32[1024,384]{1,0:T(8,128)S(1)} %get-tuple-element.60.slope, bf16[64,384]{1,0:T(8,128)(2,1)S(1)} %fusion.1.refs_0_, ...), custom_call_target="tpu_custom_call" | custom-call | flops 4000000000 | bytes 1000 | tf_op jit(solution)/shard_map/pallas_call | solution.py:453
  44.7 1.6 %collective-permute-start.11 = (bf16[288,384]{1,0:T(8,128)(2,1)S(1)}, bf16[288,384]{1,0:T(8,128)(2,1)S(1)}, u32[]{:S(2)}, u32[]{:S(2)}) collective-permute-start(bf16[288,384]{1,0:T(8,128)(2,1)S(1)} %shard_map.88.refs_4_), channel_id=1, source_target_pairs={{0,2},{1,3},{2,0},{3,1},{4,6},{5,7},{6,4},{7,5},{8,10},{9,11},{10,... | collective-permute-start | bytes 663560 | tf_op jit(solution)/shard_map/ppermute | solution.py:24
  46.3 5.4 %collective-permute-done.11.refs_6_ = bf16[288,384]{1,0:T(8,128)(2,1)S(1)} collective-permute-done((bf16[288,384]{1,0:T(8,128)(2,1)S(1)}, bf16[288,384]{1,0:T(8,128)(2,1)S(1)}, u32[]{:S(2)}, u32[]{:S(2)}) %collective-permute-start.11) | collective-permute-done | bytes 221216 | tf_op jit(solution)/shard_map/ppermute | solution.py:24
  51.6 1.5 %collective-permute-done.10.refs_5_ = bf16[288,384]{1,0:T(8,128)(2,1)S(1)} collective-permute-done((bf16[288,384]{1,0:T(8,128)(2,1)S(1)}, bf16[288,384]{1,0:T(8,128)(2,1)S(1)}, u32[]{:S(2)}, u32[]{:S(2)}) %collective-permute-start.10) | collective-permute-done | bytes 221216 | tf_op jit(solution)/shard_map/ppermute | solution.py:24
  53.2 1.3 %collective-permute-done.12.refs_7_ = bf16[288,384]{1,0:T(8,128)(2,1)S(1)} collective-permute-done((bf16[288,384]{1,0:T(8,128)(2,1)S(1)}, bf16[288,384]{1,0:T(8,128)(2,1)S(1)}, u32[]{:S(2)}, u32[]{:S(2)}) %collective-permute-start.12) | collective-permute-done | bytes 221216 | tf_op jit(solution)/shard_map/ppermute | solution.py:24
  54.6 6.2 %collective-permute-done.15.refs_4_ = bf16[1024,384]{1,0:T(8,128)(2,1)S(1)} collective-permute-done((bf16[1024,384]{1,0:T(8,128)(2,1)S(1)}, bf16[1024,384]{1,0:T(8,128)(2,1)S(1)}, u32[]{:S(2)}, u32[]{:S(2)}) %collective-permute-start.15) | collective-permute-done | bytes 786464 | tf_op jit(solution)/shard_map/ppermute | solution.py:33
  60.7 1.4 %shard_map.89 = (bf16[1024,384]{1,0:T(8,128)(2,1)S(1)}, bf16[1024,384]{1,0:T(8,128)(2,1)S(1)}, bf16[1024,384]{1,0:T(8,128)(2,1)S(1)}, bf16[1024,384]{1,0:T(8,128...) custom-call(s32[2,16]{1,0:T(2,128)S(1)} %bitcast.14, ...), custom_call_target="tpu_custom_call", output_to_operand_aliasing={{0}: (1, {}), {1}: (2, {}), {2}: (3, {}), {3}: (4, {})} | custom-call | flops 1000 | bytes 1000 | tf_op jit(solution)/shard_map/pallas_call | solution.py:529
  62.2 1.8 %collective-permute-start.16 = (bf16[272,384]{1,0:T(8,128)(2,1)S(1)}, bf16[272,384]{1,0:T(8,128)(2,1)S(1)}, u32[]{:S(2)}, u32[]{:S(2)}) collective-permute-start(bf16[272,384]{1,0:T(8,128)(2,1)S(1)} %get-tuple-element.77), channel_id=1, source_target_pairs={{0,4},{4,0},{8,12},{12,8},{1,5},{5,1},{9,13},{13,9},{2,6},{6,2},{1... | collective-permute-start | bytes 626696 | tf_op jit(solution)/shard_map/ppermute | solution.py:24
  64.4 1.4 %collective-permute-start.17 = (bf16[256,384]{1,0:T(8,128)(2,1)S(1)}, bf16[256,384]{1,0:T(8,128)(2,1)S(1)}, u32[]{:S(2)}, u32[]{:S(2)}) collective-permute-start(bf16[256,384]{1,0:T(8,128)(2,1)S(1)} %get-tuple-element.78), channel_id=1, source_target_pairs={{0,8},{4,12},{8,0},{12,4},{1,9},{5,13},{9,1},{13,5},{2,10},{6,14},... | collective-permute-start | bytes 589832 | tf_op jit(solution)/shard_map/ppermute | solution.py:24
  65.7 7.0 %collective-permute-done.16.refs_4_.refs_5_ = bf16[272,384]{1,0:T(8,128)(2,1)S(1)} collective-permute-done((bf16[272,384]{1,0:T(8,128)(2,1)S(1)}, bf16[272,384]{1,0:T(8,128)(2,1)S(1)}, u32[]{:S(2)}, u32[]{:S(2)}) %collective-permute-start.16) | collective-permute-done | bytes 208928 | tf_op jit(solution)/shard_map/ppermute | solution.py:24
  73.4 1.5 %collective-permute-start.24 = (bf16[1024,384]{1,0:T(8,128)(2,1)S(1)}, bf16[1024,384]{1,0:T(8,128)(2,1)S(1)}, u32[]{:S(2)}, u32[]{:S(2)}) collective-permute-start(bf16[1024,384]{1,0:T(8,128)(2,1)S(1)} %collective-permute-done.15.refs_4_), channel_id=1, source_target_pairs={{4,0},{5,1},{6,2},{7,3},{20,16},{21,17},{22,18},{23,19}} | collective-permute-start | bytes 2359304 | tf_op jit(solution)/shard_map/ppermute | solution.py:33
  75.0 2.8 %shard_map.90 = (f32[384,1920]{1,0:T(8,128)S(1)}, bf16[1536,1920]{1,0:T(8,128)(2,1)S(1)}) custom-call(bf16[16,384]{1,0:T(8,128)(2,1)S(1)} %slice.44.refs_0_, bf16[1024,384]{1,0:T(8,128)(2,1)S(1)} %copy-done, bf16[16,384]{1,0:T(8,128)(2,1)S(1)} %slice.45.refs_2_, bf16[1024,384]{1,0:T(8,128)(2,1)S(1)} %get-tuple-element.80.refs_3_, ...), custom_call_target="tpu_custom_call" | custom-call | flops 1000 | bytes 1000 | tf_op jit(solution)/shard_map/pallas_call | solution.py:276
  77.8 3.7 %shard_map.91.refs_6_ = bf16[512,384]{1,0:T(8,128)(2,1)S(1)} custom-call(bf16[1024,384]{1,0:T(8,128)(2,1)S(1)} %get-tuple-element.82.refs_0_, bf16[1024,384]{1,0:T(8,128)(2,1)S(1)} %get-tuple-element.83.refs_1_, bf16[1024,384]{1,0:T(8,128)(2,1)S(1)} %get-tuple-element.84.refs_2_, bf16[1024,384]{1,0:T(8,128)(2,1)S(1)} %get-tuple-element.85.refs_3_, ...), custom_call_target="tpu_custom_call" | custom-call | flops 1000 | bytes 1000 | tf_op jit(solution)/shard_map/pallas_call | solution.py:133
  81.5 1.4 %collective-permute-done.17 = bf16[256,384]{1,0:T(8,128)(2,1)S(1)} collective-permute-done((bf16[256,384]{1,0:T(8,128)(2,1)S(1)}, bf16[256,384]{1,0:T(8,128)(2,1)S(1)}, u32[]{:S(2)}, u32[]{:S(2)}) %collective-permute-start.17) | collective-permute-done | bytes 196640 | tf_op jit(solution)/shard_map/ppermute | solution.py:24
  82.9 1.5 %collective-permute-start.20 = (bf16[272,384]{1,0:T(8,128)(2,1)S(1)}, bf16[272,384]{1,0:T(8,128)(2,1)S(1)}, u32[]{:S(2)}, u32[]{:S(2)}) collective-permute-start(bf16[272,384]{1,0:T(8,128)(2,1)S(1)} %collective-permute-done.16.refs_4_.refs_5_), channel_id=1, source_target_pairs={{0,2},{1,3},{2,0},{3,1},{4,6},{5,7},{6,4},{7,5},{8,10},{9,11},{10,... | collective-permute-start | bytes 626696 | tf_op jit(solution)/shard_map/ppermute | solution.py:24
  85.1 4.8 %shard_map.92 = bf16[1024,384]{1,0:T(8,128)(2,1)} custom-call(bf16[1024,384]{1,0:T(8,128)(2,1)S(1)} %get-tuple-element.82.refs_0_, bf16[1024,384]{1,0:T(8,128)(2,1)S(1)} %get-tuple-element.83.refs_1_, bf16[1024,384]{1,0:T(8,128)(2,1)S(1)} %get-tuple-element.84.refs_2_, bf16[1024,384]{1,0:T(8,128)(2,1)S(1)} %get-tuple-element.85.refs_3_, ...), custom_call_target="tpu_custom_call" | custom-call | flops 1000 | bytes 1000 | tf_op jit(solution)/shard_map/pallas_call | solution.py:133
  90.4 1.5 %collective-permute-done.22.refs_8_ = bf16[272,384]{1,0:T(8,128)(2,1)S(1)} collective-permute-done((bf16[272,384]{1,0:T(8,128)(2,1)S(1)}, bf16[272,384]{1,0:T(8,128)(2,1)S(1)}, u32[]{:S(2)}, u32[]{:S(2)}) %collective-permute-start.22) | collective-permute-done | bytes 208928 | tf_op jit(solution)/shard_map/ppermute | solution.py:24
  91.9 3.1 %shard_map.93.refs_15_ = f32[384,1920]{1,0:T(8,128)S(1)} custom-call(bf16[1024,384]{1,0:T(8,128)(2,1)S(1)} %copy-done, bf16[1024,384]{1,0:T(8,128)(2,1)S(1)} %collective-permute-done.7.refs_1_, bf16[1024,384]{1,0:T(8,128)(2,1)S(1)} %collective-permute-done.8.refs_2_, bf16[1024,384]{1,0:T(8,128)(2,1)S(1)} %collective-permute-done.14.refs_3_, ...), custom_call_target="tpu_custom_call" | custom-call | flops 1000 | bytes 1000 | tf_op jit(solution)/shard_map/pallas_call | solution.py:276
  95.1 2.1 %collective-permute-done.19 = bf16[512,384]{1,0:T(8,128)(2,1)S(1)} collective-permute-done((bf16[512,384]{1,0:T(8,128)(2,1)S(1)}, bf16[512,384]{1,0:T(8,128)(2,1)S(1)}, u32[]{:S(2)}, u32[]{:S(2)}) %collective-permute-start.19) | collective-permute-done | bytes 393248 | tf_op jit(solution)/shard_map/ppermute | solution.py:24
  97.2 1.6 %collective-permute-done.26 = bf16[512,384]{1,0:T(8,128)(2,1)S(1)} collective-permute-done((bf16[512,384]{1,0:T(8,128)(2,1)S(1)}, bf16[512,384]{1,0:T(8,128)(2,1)S(1)}, u32[]{:S(2)}, u32[]{:S(2)}) %collective-permute-start.26) | collective-permute-done | bytes 393248 | tf_op jit(solution)/shard_map/ppermute | solution.py:24
  98.9 7.9 %shard_map.94 = bf16[5,384,384]{2,1,0:T(8,128)(2,1)} custom-call(bf16[1024,384]{1,0:T(8,128)(2,1)S(1)} %copy-done, bf16[1024,384]{1,0:T(8,128)(2,1)S(1)} %collective-permute-done.7.refs_1_, bf16[1024,384]{1,0:T(8,128)(2,1)S(1)} %collective-permute-done.8.refs_2_, bf16[1024,384]{1,0:T(8,128)(2,1)S(1)} %collective-permute-done.14.refs_3_, ...), custom_call_target="tpu_custom_call" | custom-call | flops 1000 | bytes 1000 | tf_op jit(solution)/shard_map/pallas_call | solution.py:276
  (63 shorter events, 13.9 us)
Async XLA Ops:
  0.6 1.1 %copy-start.1 = (bf16[1024,384]{1,0:T(8,128)(2,1)S(1)}, bf16[1024,384]{1,0:T(8,128)(2,1)}, u32[]{:S(2)}) copy-start(bf16[1024,384]{1,0:T(8,128)(2,1)} %pre_act.3) | copy-start | bytes 2359300
  4.5 12.3 %collective-permute-start = (bf16[64,384]{1,0:T(8,128)(2,1)S(1)}, bf16[64,384]{1,0:T(8,128)(2,1)S(1)}, u32[]{:S(2)}, u32[]{:S(2)}) collective-permute-start(bf16[64,384]{1,0:T(8,128)(2,1)S(1)} %get-tuple-element.54), channel_id=1, source_target_pairs={{0,4},{4,0},{8,12},{12,8},{1,5},{5,1},{9,13},{13,9},{2,6},{6,2},{1... | collective-permute-start | bytes 147464 | tf_op jit(solution)/shard_map/ppermute | solution.py:24
  7.7 9.2 %collective-permute-start.1 = (bf16[64,384]{1,0:T(8,128)(2,1)S(1)}, bf16[64,384]{1,0:T(8,128)(2,1)S(1)}, u32[]{:S(2)}, u32[]{:S(2)}) collective-permute-start(bf16[64,384]{1,0:T(8,128)(2,1)S(1)} %get-tuple-element.55), channel_id=1, source_target_pairs={{0,8},{4,12},{8,0},{12,4},{1,9},{5,13},{9,1},{13,5},{2,10},{6,14},... | collective-permute-start | bytes 147464 | tf_op jit(solution)/shard_map/ppermute | solution.py:24
  10.0 6.8 %collective-permute-start.2 = (bf16[64,384]{1,0:T(8,128)(2,1)S(1)}, bf16[64,384]{1,0:T(8,128)(2,1)S(1)}, u32[]{:S(2)}, u32[]{:S(2)}) collective-permute-start(bf16[64,384]{1,0:T(8,128)(2,1)S(1)} %get-tuple-element.56), channel_id=1, source_target_pairs={{0,12},{4,8},{8,4},{12,0},{1,13},{5,9},{9,5},{13,1},{2,14},{6,10},... | collective-permute-start | bytes 147464 | tf_op jit(solution)/shard_map/ppermute | solution.py:24
  10.1 20.3 %collective-permute-start.7 = (bf16[1024,384]{1,0:T(8,128)(2,1)}, bf16[1024,384]{1,0:T(8,128)(2,1)S(1)}, u32[]{:S(2)}, u32[]{:S(2)}) collective-permute-start(bf16[1024,384]{1,0:T(8,128)(2,1)} %refs_0_.3), channel_id=1, source_target_pairs={{0,4},{4,8},{8,12},{1,5},{5,9},{9,13},{2,6},{6,10},{10,14},{3,7},{... | collective-permute-start | bytes 2359304 | tf_op jit(solution)/shard_map/ppermute | solution.py:33
  13.1 21.3 %collective-permute-start.8 = (bf16[1024,384]{1,0:T(8,128)(2,1)}, bf16[1024,384]{1,0:T(8,128)(2,1)S(1)}, u32[]{:S(2)}, u32[]{:S(2)}) collective-permute-start(bf16[1024,384]{1,0:T(8,128)(2,1)} %refs_0_.3), channel_id=1, source_target_pairs={{4,0},{8,4},{12,8},{5,1},{9,5},{13,9},{6,2},{10,6},{14,10},{7,3},{... | collective-permute-start | bytes 2359304 | tf_op jit(solution)/shard_map/ppermute | solution.py:33
  16.9 43.9 %copy-start.6 = (s32[16,2]{0,1:T(2,128)S(1)}, s32[16,2]{0,1:T(2,128)}, u32[]{:S(2)}) copy-start(s32[16,2]{0,1:T(2,128)} %param.13) | copy-start | bytes 388
  16.9 22.4 %collective-permute-start.4 = (bf16[1024,384]{1,0:T(8,128)(2,1)S(1)}, bf16[1024,384]{1,0:T(8,128)(2,1)S(1)}, u32[]{:S(2)}, u32[]{:S(2)}) collective-permute-start(bf16[1024,384]{1,0:T(8,128)(2,1)S(1)} %get-tuple-element.59.refs_0_), channel_id=1, source_target_pairs={{0,2},{1,3},{2,0},{3,1},{4,6},{5,7},{6,4},{7,5},{8,10},{9,11},{10,... | collective-permute-start | bytes 2359304 | tf_op jit(solution)/shard_map/ppermute | solution.py:24
  18.4 56.5 %slice-start = ((s8[5898240]{0:T(1024)(128)(4,1)}), s8[4194304]{0:T(1024)(128)(4,1)S(1)}, s32[]{:S(2)}) async-start(s8[5898240]{0:T(1024)(128)(4,1)} %bitcast.9), calls=%async_computation | async-start | bytes 8388608
  19.5 55.5 %slice-start.1 = ((s8[5898240]{0:T(1024)(128)(4,1)}), s8[1703936]{0:T(1024)(128)(4,1)S(1)}, s32[]{:S(2)}) async-start(s8[5898240]{0:T(1024)(128)(4,1)} %bitcast.9), calls=%async_computation.1 | async-start | bytes 3407872
  19.5 17.7 %collective-permute-start.5 = (bf16[64,384]{1,0:T(8,128)(2,1)S(1)}, bf16[64,384]{1,0:T(8,128)(2,1)S(1)}, u32[]{:S(2)}, u32[]{:S(2)}) collective-permute-start(bf16[64,384]{1,0:T(8,128)(2,1)S(1)} %fusion.1.refs_0_), channel_id=1, source_target_pairs={{0,4},{4,0},{8,12},{12,8},{1,5},{5,1},{9,13},{13,9},{2,6},{6,2},{1... | collective-permute-start | bytes 147464 | tf_op jit(solution)/shard_map/ppermute | solution.py:24
  22.2 15.7 %collective-permute-start.6 = (bf16[64,384]{1,0:T(8,128)(2,1)S(1)}, bf16[64,384]{1,0:T(8,128)(2,1)S(1)}, u32[]{:S(2)}, u32[]{:S(2)}) collective-permute-start(bf16[64,384]{1,0:T(8,128)(2,1)S(1)} %fusion.1.refs_0_), channel_id=1, source_target_pairs={{0,8},{4,12},{8,0},{12,4},{1,9},{5,13},{9,1},{13,5},{2,10},{6,14},... | collective-permute-start | bytes 147464 | tf_op jit(solution)/shard_map/ppermute | solution.py:24
  34.4 5.9 %collective-permute-start.9 = (bf16[64,384]{1,0:T(8,128)(2,1)S(1)}, bf16[64,384]{1,0:T(8,128)(2,1)S(1)}, u32[]{:S(2)}, u32[]{:S(2)}) collective-permute-start(bf16[64,384]{1,0:T(8,128)(2,1)S(1)} %fusion.1.refs_0_), channel_id=1, source_target_pairs={{0,12},{4,8},{8,4},{12,0},{1,13},{5,9},{9,5},{13,1},{2,14},{6,10},... | collective-permute-start | bytes 147464 | tf_op jit(solution)/shard_map/ppermute | solution.py:24
  37.2 23.5 %collective-permute-start.3 = (bf16[1024,384]{1,0:T(8,128)(2,1)S(1)}, bf16[1024,384]{1,0:T(8,128)(2,1)S(1)}, u32[]{:S(2)}, u32[]{:S(2)}) collective-permute-start(bf16[1024,384]{1,0:T(8,128)(2,1)S(1)} %get-tuple-element.59.refs_0_), channel_id=1, source_target_pairs={{0,1},{1,0},{2,3},{3,2},{4,5},{5,4},{6,7},{7,6},{8,9},{9,8},{10,11... | collective-permute-start | bytes 2359304 | tf_op jit(solution)/shard_map/ppermute | solution.py:24
  37.3 17.3 %collective-permute-start.14 = (bf16[1024,384]{1,0:T(8,128)(2,1)S(1)}, bf16[1024,384]{1,0:T(8,128)(2,1)S(1)}, u32[]{:S(2)}, u32[]{:S(2)}) collective-permute-start(bf16[1024,384]{1,0:T(8,128)(2,1)S(1)} %collective-permute-done.7.refs_1_), channel_id=1, source_target_pairs={{4,8},{8,12},{5,9},{9,13},{6,10},{10,14},{7,11},{11,15},{20,24},{2... | collective-permute-start | bytes 2359304 | tf_op jit(solution)/shard_map/ppermute | solution.py:33
  38.0 22.8 %collective-permute-start.15 = (bf16[1024,384]{1,0:T(8,128)(2,1)S(1)}, bf16[1024,384]{1,0:T(8,128)(2,1)S(1)}, u32[]{:S(2)}, u32[]{:S(2)}) collective-permute-start(bf16[1024,384]{1,0:T(8,128)(2,1)S(1)} %collective-permute-done.8.refs_2_), channel_id=1, source_target_pairs={{4,0},{8,4},{5,1},{9,5},{6,2},{10,6},{7,3},{11,7},{20,16},{24,20},... | collective-permute-start | bytes 2359304 | tf_op jit(solution)/shard_map/ppermute | solution.py:33
  39.3 21.5 %collective-permute-start.13 = (bf16[1024,384]{1,0:T(8,128)(2,1)S(1)}, bf16[1024,384]{1,0:T(8,128)(2,1)S(1)}, u32[]{:S(2)}, u32[]{:S(2)}) collective-permute-start(bf16[1024,384]{1,0:T(8,128)(2,1)S(1)} %collective-permute-done.4.refs_2_), channel_id=1, source_target_pairs={{0,1},{1,0},{2,3},{3,2},{4,5},{5,4},{6,7},{7,6},{8,9},{9,8},{10,11... | collective-permute-start | bytes 2359304 | tf_op jit(solution)/shard_map/ppermute | solution.py:24
  44.7 30.3 %copy-start = (bf16[1024,384]{1,0:T(8,128)(2,1)S(1)}, bf16[1024,384]{1,0:T(8,128)(2,1)}, u32[]{:S(2)}) copy-start(bf16[1024,384]{1,0:T(8,128)(2,1)} %refs_0_.3) | copy-start | bytes 2359300
  44.7 6.9 %collective-permute-start.11 = (bf16[288,384]{1,0:T(8,128)(2,1)S(1)}, bf16[288,384]{1,0:T(8,128)(2,1)S(1)}, u32[]{:S(2)}, u32[]{:S(2)}) collective-permute-start(bf16[288,384]{1,0:T(8,128)(2,1)S(1)} %shard_map.88.refs_4_), channel_id=1, source_target_pairs={{0,2},{1,3},{2,0},{3,1},{4,6},{5,7},{6,4},{7,5},{8,10},{9,11},{10,... | collective-permute-start | bytes 663560 | tf_op jit(solution)/shard_map/ppermute | solution.py:24
  51.6 1.5 %collective-permute-start.10 = (bf16[288,384]{1,0:T(8,128)(2,1)S(1)}, bf16[288,384]{1,0:T(8,128)(2,1)S(1)}, u32[]{:S(2)}, u32[]{:S(2)}) collective-permute-start(bf16[288,384]{1,0:T(8,128)(2,1)S(1)} %shard_map.88.refs_4_), channel_id=1, source_target_pairs={{0,1},{1,0},{2,3},{3,2},{4,5},{5,4},{6,7},{7,6},{8,9},{9,8},{10,11... | collective-permute-start | bytes 663560 | tf_op jit(solution)/shard_map/ppermute | solution.py:24
  53.1 1.5 %collective-permute-start.12 = (bf16[288,384]{1,0:T(8,128)(2,1)S(1)}, bf16[288,384]{1,0:T(8,128)(2,1)S(1)}, u32[]{:S(2)}, u32[]{:S(2)}) collective-permute-start(bf16[288,384]{1,0:T(8,128)(2,1)S(1)} %collective-permute-done.11.refs_6_), channel_id=1, source_target_pairs={{0,1},{1,0},{2,3},{3,2},{4,5},{5,4},{6,7},{7,6},{8,9},{9,8},{10,11... | collective-permute-start | bytes 663560 | tf_op jit(solution)/shard_map/ppermute | solution.py:24
  62.2 10.6 %collective-permute-start.16 = (bf16[272,384]{1,0:T(8,128)(2,1)S(1)}, bf16[272,384]{1,0:T(8,128)(2,1)S(1)}, u32[]{:S(2)}, u32[]{:S(2)}) collective-permute-start(bf16[272,384]{1,0:T(8,128)(2,1)S(1)} %get-tuple-element.77), channel_id=1, source_target_pairs={{0,4},{4,0},{8,12},{12,8},{1,5},{5,1},{9,13},{13,9},{2,6},{6,2},{1... | collective-permute-start | bytes 626696 | tf_op jit(solution)/shard_map/ppermute | solution.py:24
  64.0 18.9 %collective-permute-start.18 = (bf16[272,384]{1,0:T(8,128)(2,1)S(1)}, bf16[272,384]{1,0:T(8,128)(2,1)S(1)}, u32[]{:S(2)}, u32[]{:S(2)}) collective-permute-start(bf16[272,384]{1,0:T(8,128)(2,1)S(1)} %get-tuple-element.79), channel_id=1, source_target_pairs={{0,12},{4,8},{8,4},{12,0},{1,13},{5,9},{9,5},{13,1},{2,14},{6,10},... | collective-permute-start | bytes 626696 | tf_op jit(solution)/shard_map/ppermute | solution.py:24
  64.4 18.5 %collective-permute-start.17 = (bf16[256,384]{1,0:T(8,128)(2,1)S(1)}, bf16[256,384]{1,0:T(8,128)(2,1)S(1)}, u32[]{:S(2)}, u32[]{:S(2)}) collective-permute-start(bf16[256,384]{1,0:T(8,128)(2,1)S(1)} %get-tuple-element.78), channel_id=1, source_target_pairs={{0,8},{4,12},{8,0},{12,4},{1,9},{5,13},{9,1},{13,5},{2,10},{6,14},... | collective-permute-start | bytes 589832 | tf_op jit(solution)/shard_map/ppermute | solution.py:24
  72.7 24.4 %collective-permute-start.23 = (bf16[1024,384]{1,0:T(8,128)(2,1)S(1)}, bf16[1024,384]{1,0:T(8,128)(2,1)S(1)}, u32[]{:S(2)}, u32[]{:S(2)}) collective-permute-start(bf16[1024,384]{1,0:T(8,128)(2,1)S(1)} %collective-permute-done.14.refs_3_), channel_id=1, source_target_pairs={{8,12},{9,13},{10,14},{11,15},{24,28},{25,29},{26,30},{27,31}} | collective-permute-start | bytes 2359304 | tf_op jit(solution)/shard_map/ppermute | solution.py:33
  73.4 23.7 %collective-permute-start.24 = (bf16[1024,384]{1,0:T(8,128)(2,1)S(1)}, bf16[1024,384]{1,0:T(8,128)(2,1)S(1)}, u32[]{:S(2)}, u32[]{:S(2)}) collective-permute-start(bf16[1024,384]{1,0:T(8,128)(2,1)S(1)} %collective-permute-done.15.refs_4_), channel_id=1, source_target_pairs={{4,0},{5,1},{6,2},{7,3},{20,16},{21,17},{22,18},{23,19}} | collective-permute-start | bytes 2359304 | tf_op jit(solution)/shard_map/ppermute | solution.py:33
  82.9 7.0 %collective-permute-start.20 = (bf16[272,384]{1,0:T(8,128)(2,1)S(1)}, bf16[272,384]{1,0:T(8,128)(2,1)S(1)}, u32[]{:S(2)}, u32[]{:S(2)}) collective-permute-start(bf16[272,384]{1,0:T(8,128)(2,1)S(1)} %collective-permute-done.16.refs_4_.refs_5_), channel_id=1, source_target_pairs={{0,2},{1,3},{2,0},{3,1},{4,6},{5,7},{6,4},{7,5},{8,10},{9,11},{10,... | collective-permute-start | bytes 626696 | tf_op jit(solution)/shard_map/ppermute | solution.py:24
  84.4 5.7 %collective-permute-start.21 = (bf16[272,384]{1,0:T(8,128)(2,1)S(1)}, bf16[272,384]{1,0:T(8,128)(2,1)S(1)}, u32[]{:S(2)}, u32[]{:S(2)}) collective-permute-start(bf16[272,384]{1,0:T(8,128)(2,1)S(1)} %collective-permute-done.16.refs_4_.refs_5_), channel_id=1, source_target_pairs={{0,1},{1,0},{2,3},{3,2},{4,5},{5,4},{6,7},{7,6},{8,9},{9,8},{10,11... | collective-permute-start | bytes 626696 | tf_op jit(solution)/shard_map/ppermute | solution.py:24
  84.5 12.7 %collective-permute-start.19 = (bf16[512,384]{1,0:T(8,128)(2,1)S(1)}, bf16[512,384]{1,0:T(8,128)(2,1)S(1)}, u32[]{:S(2)}, u32[]{:S(2)}) collective-permute-start(bf16[512,384]{1,0:T(8,128)(2,1)S(1)} %pad_maximum_fusion), channel_id=1, source_target_pairs={{0,2},{1,3},{2,0},{3,1},{4,6},{5,7},{6,4},{7,5},{8,10},{9,11},{10,... | collective-permute-start | bytes 1179656 | tf_op jit(solution)/shard_map/ppermute | solution.py:24
  89.9 7.3 %collective-permute-start.25 = (bf16[512,384]{1,0:T(8,128)(2,1)S(1)}, bf16[512,384]{1,0:T(8,128)(2,1)S(1)}, u32[]{:S(2)}, u32[]{:S(2)}) collective-permute-start(bf16[512,384]{1,0:T(8,128)(2,1)S(1)} %pad_maximum_fusion), channel_id=1, source_target_pairs={{0,1},{1,0},{2,3},{3,2},{4,5},{5,4},{6,7},{7,6},{8,9},{9,8},{10,11... | collective-permute-start | bytes 1179656 | tf_op jit(solution)/shard_map/ppermute | solution.py:24
  90.1 1.8 %collective-permute-start.22 = (bf16[272,384]{1,0:T(8,128)(2,1)S(1)}, bf16[272,384]{1,0:T(8,128)(2,1)S(1)}, u32[]{:S(2)}, u32[]{:S(2)}) collective-permute-start(bf16[272,384]{1,0:T(8,128)(2,1)S(1)} %collective-permute-done.20.refs_7_), channel_id=1, source_target_pairs={{0,1},{1,0},{2,3},{3,2},{4,5},{5,4},{6,7},{7,6},{8,9},{9,8},{10,11... | collective-permute-start | bytes 626696 | tf_op jit(solution)/shard_map/ppermute | solution.py:24
  97.1 1.7 %collective-permute-start.26 = (bf16[512,384]{1,0:T(8,128)(2,1)S(1)}, bf16[512,384]{1,0:T(8,128)(2,1)S(1)}, u32[]{:S(2)}, u32[]{:S(2)}) collective-permute-start(bf16[512,384]{1,0:T(8,128)(2,1)S(1)} %collective-permute-done.19), channel_id=1, source_target_pairs={{0,1},{1,0},{2,3},{3,2},{4,5},{5,4},{6,7},{7,6},{8,9},{9,8},{10,11... | collective-permute-start | bytes 1179656 | tf_op jit(solution)/shard_map/ppermute | solution.py:24
  (6 other events, 4.7 us)
